TPU v7x, 256 devices: a whole 4x4x8 slice. The times are simulated.
256 devices in a mesh: space: 64 (over z, x, core), sub: 4 (over y).
Axes of the slice: x: 4, y: 4, z: 8, core: 2. Of those that a mesh axis runs over, the one named last changes fastest.
Arguments:
- trajectories: bfloat16 [300, 131072], P(None, ('space', 'sub')), may hold values from -6 to 6
- kernel_scale: bfloat16 [131072], P(('space', 'sub')), may hold values from 6.90625 to 17.25
- start_vectors: float32 [32, 131072], P(None, ('space', 'sub')), may hold values from -6 to 6
- pair_list: int32 [6144, 2], P(('space', 'sub')), may hold values from 0 to 511, as said below
Outputs:
- subspace: float32 [32, 131072], P(None, ('space', 'sub'))
Inputs may be any that keep to these rules, and one draw needn't show every extreme that they name: `pair_list`: pairs in rows k * 12 * 2 to (k + 1) * 12 * 2 - 1 have their row block a in k * 2 to (k + 1) * 2 - 1, k being a device's index along space+sub. Every block appears once as (a, a). For every other pair, b lies on a device whose space index is that of a's device plus 1 to 3, modulo the size of the space axis. No pair appears twice.
All inputs are finite; a program needn't handle non-finite values.
Results may differ from a plain program's by a relative error of at most 0.0041.
Values may be sent and summed in bfloat16 or wider, within the bound.
No kernel may reach another device: no remote copies, remote signals or barrier semaphores. Data moves between devices by JAX's collectives and lax.ppermute only.
A program may use at most 64 MiB of HBM per device.

v0:
```python
import functools

import jax
import jax.numpy as jnp
from jax import lax
from jax.experimental import pallas as pl
from jax.experimental.pallas import tpu as pltpu
from jax.sharding import PartitionSpec as P

FEAT = 300
BLOCK = 256
LENGTH = 2 * BLOCK
REACH = 3
N_SUB = 4
ROWS = 304
DEPTH = 320
SCALE_ROW = 300
MASK_ROW = 301
PAIRS = 4 * N_SUB
SLOTS = 48
COUNT = SLOTS - 1
NOBODY = 2 * N_SUB
UNROLL = 8
LOG2E = 1.4426950408889634
VMEM_LIMIT = 12 * 1024 * 1024
SMALL_LIMIT = 4 * 1024 * 1024
TRANS_B = (((1,), (1,)), ((), ()))


def shifted(value, axis, steps):
    count = lax.axis_size(axis)
    return lax.ppermute(value, axis, [((at + steps) % count, at) for at in range(count)])


def space_window(value):
    return {h: shifted(value, "space", h) for h in (1, 2, 3, -1, -2, -3)}


def groups_by(key, n_space, n_sub):
    found = {}
    for place in range(n_space * n_sub):
        found.setdefault(key(place // n_sub, place % n_sub), []).append(place)
    return list(found.values())


def summed(value):
    n_space, n_sub = lax.axis_size("space"), lax.axis_size("sub")
    shape = value.shape
    value = value.reshape(-1, 128)
    for key in (lambda s, y: (s // 4, 0), lambda s, y: (s % 4, y)):
        groups = groups_by(key, n_space, n_sub)
        sent = jnp.broadcast_to(value[None], (len(groups[0]),) + value.shape)
        value = jnp.sum(
            lax.all_to_all(sent, ("space", "sub"), 0, 0, axis_index_groups=groups), 0
        )
    return value.reshape(shape)


def pieces(norm):
    high = norm.astype(jnp.bfloat16).astype(jnp.float32)
    rest = norm - high
    middle = rest.astype(jnp.bfloat16).astype(jnp.float32)
    return high, middle, rest - middle


def ones_and_norms(norm, ones_at, norms_at):
    place = lax.broadcasted_iota(jnp.int32, (DEPTH - ROWS, 1), 0)
    tail = jnp.where((place >= ones_at) & (place < ones_at + 3), 1.0, 0.0)
    for k, piece in enumerate(pieces(norm)):
        tail = jnp.where(place == norms_at + k, -piece, tail)
    return tail


def rows_kernel(*refs):
    rows_ref, rate_ref = refs[N_SUB:]
    for e in range(N_SUB):
        wide = refs[e][:FEAT, :].astype(jnp.float32)
        tail = ones_and_norms(jnp.sum(wide * wide, axis=0, keepdims=True), 0, 3)
        tail = tail.astype(jnp.bfloat16)
        rate = LOG2E / refs[e][SCALE_ROW : SCALE_ROW + 1, :].astype(jnp.float32)
        below = lax.broadcasted_iota(jnp.int32, (ROWS, 1), 0) < FEAT
        twice = jnp.where(below, 2.0 * refs[e][...].astype(jnp.float32), 0.0).astype(jnp.bfloat16)
        for r in range(2):
            span = slice(r * BLOCK, (r + 1) * BLOCK)
            rows_ref[2 * e + r, :ROWS] = twice[:, span]
            rows_ref[2 * e + r, ROWS:] = tail[:, span]
            rate_ref[2 * e + r] = jnp.broadcast_to(rate[:, span], (8, BLOCK))


def row_operands(members):
    return pl.pallas_call(
        rows_kernel,
        out_shape=[
            jax.ShapeDtypeStruct((2 * N_SUB, DEPTH, BLOCK), jnp.bfloat16),
            jax.ShapeDtypeStruct((2 * N_SUB, 8, BLOCK), jnp.float32),
        ],
        compiler_params=pltpu.CompilerParams(vmem_limit_bytes=VMEM_LIMIT),
        cost_estimate=pl.CostEstimate(flops=2**22, bytes_accessed=4 * 2**20, transcendentals=0),
    )(*members)


def prepare_columns(data_ref, first, lhs, rate_ref):
    wide = data_ref[...].astype(jnp.float32)
    rate = 1.0 / wide[SCALE_ROW : SCALE_ROW + 1]
    squares = wide[:FEAT] * wide[:FEAT]
    tail = ones_and_norms(jnp.sum(squares, axis=0, keepdims=True), 3, 0)
    full = jnp.concatenate([wide, tail, jnp.zeros((384 - DEPTH, LENGTH), jnp.float32)], 0)
    turned = full.T[:, :DEPTH].astype(jnp.bfloat16)
    rate = jnp.broadcast_to(rate, (128, LENGTH)).T
    for c in range(2):
        lhs[first + c] = turned[c * BLOCK : (c + 1) * BLOCK]
        rate_ref[first + c] = rate[c * BLOCK : (c + 1) * BLOCK]


def list_pairs(mine_ref, theirs_ref, rows_ref, cols_ref, count):
    def member(e, count):
        for side in range(2):
            for r in range(2):
                for c in range(2):
                    if side == 0:
                        used = mine_ref[e * PAIRS + lax.rem(N_SUB - e, N_SUB) * 4 + r * 2 + c]
                    else:
                        used = theirs_ref[e * 4 + c * 2 + r]
                    rows_ref[count] = e * 2 + r
                    cols_ref[count] = side * 2 + c
                    count = count + jnp.where(used > 0.0, 1, 0)
        return count

    count = lax.fori_loop(0, N_SUB, member, count)
    for k in range(8):
        rows_ref[count + k] = NOBODY
        cols_ref[count + k] = 0
    rows_ref[COUNT] = count
    cols_ref[COUNT] = count
    return count


def tile_kernel(
    first, last, mine_ref, theirs_ref, blocks_ref, rate_ref, ahead_ref, behind_ref, extra_ref,
    tile_ref, rows_ref, cols_ref, sums_ref, lhs, col, even, odd, *held
):
    total = held[0] if last else sums_ref
    prepare_columns(ahead_ref, 0, lhs, col)
    prepare_columns(behind_ref, 2, lhs, col)
    count = 0
    if first:
        prepare_columns(extra_ref, 4, lhs, col)
        for r in range(2):
            rows_ref[r] = r
            cols_ref[r] = 4 + r
        count = 2
        total[...] = jnp.zeros_like(total)
    else:
        total[...] = extra_ref[...]
    count = list_pairs(mine_ref, theirs_ref, rows_ref, cols_ref, jnp.int32(count))

    def product(at):
        row = lax.min(rows_ref[at], NOBODY - 1)
        return jnp.dot(lhs[cols_ref[at]], blocks_ref[row], preferred_element_type=jnp.float32)

    def finish(crossed, at):
        row = rows_ref[at]
        rate = col[cols_ref[at]]
        rates = jnp.concatenate([rate, rate], 1) * rate_ref[lax.min(row, NOBODY - 1), :1, :]
        tile = jnp.exp2(crossed * rates).astype(jnp.bfloat16)
        tile_ref[at] = tile
        total[row] += jnp.sum(tile.astype(jnp.float32).reshape(BLOCK // 8, 8, BLOCK), axis=0)

    even[...] = product(0)

    def step(k, _):
        odd[...] = product(2 * k + 1)
        finish(even[...], 2 * k)
        even[...] = product(2 * k + 2)
        finish(odd[...], 2 * k + 1)
        return 0

    lax.fori_loop(0, lax.shift_right_logical(count + 1, 1), step, 0)
    if last:
        for e in range(N_SUB):
            for r in range(2):
                sums = jnp.sum(total[2 * e + r], axis=0, keepdims=True)
                sums_ref[e, :, pl.ds(r * BLOCK, BLOCK)] = jnp.broadcast_to(sums, (8, BLOCK))


def hop_tiles(first, last, mine, theirs, blocks, rate, ahead, behind, extra):
    smem = pl.BlockSpec(memory_space=pltpu.SMEM)
    vmem = pl.BlockSpec(memory_space=pltpu.VMEM)
    columns = 6 if first else 4
    sums = (NOBODY + 1, 8, BLOCK)
    return pl.pallas_call(
        functools.partial(tile_kernel, first, last),
        in_specs=[smem, smem] + [vmem] * 5,
        out_specs=[vmem, smem, smem, vmem],
        out_shape=[
            jax.ShapeDtypeStruct((SLOTS - 4, BLOCK, BLOCK), jnp.bfloat16),
            jax.ShapeDtypeStruct((SLOTS,), jnp.int32),
            jax.ShapeDtypeStruct((SLOTS,), jnp.int32),
            jax.ShapeDtypeStruct((N_SUB, 8, LENGTH) if last else sums, jnp.float32),
        ],
        scratch_shapes=[
            pltpu.VMEM((columns, BLOCK, DEPTH), jnp.bfloat16),
            pltpu.VMEM((columns, BLOCK, 128), jnp.float32),
            pltpu.VMEM((BLOCK, BLOCK), jnp.float32),
            pltpu.VMEM((BLOCK, BLOCK), jnp.float32),
        ]
        + ([pltpu.VMEM(sums, jnp.float32)] if last else []),
        compiler_params=pltpu.CompilerParams(vmem_limit_bytes=VMEM_LIMIT),
        cost_estimate=pl.CostEstimate(
            flops=16 * 2 * DEPTH * BLOCK * BLOCK,
            bytes_accessed=7 * 2**20,
            transcendentals=16 * BLOCK * BLOCK,
        ),
    )(mine, theirs, blocks, rate, ahead, behind, extra)


def stacked(vectors):
    if vectors.dtype == jnp.bfloat16:
        return vectors
    high = vectors.astype(jnp.bfloat16)
    return jnp.concatenate([high, (vectors - high.astype(jnp.float32)).astype(jnp.bfloat16)], 0)


def sweep_kernel(parts, order, *refs):
    list_refs, tile_refs, vector_refs = refs[:6], refs[6:9], refs[9:16]
    out_refs, held, total = refs[16:20], refs[20], refs[21]
    vecs = vector_refs[0].shape[0]
    for k in range(7):
        both = stacked(vector_refs[k][...])
        for c in range(2):
            held[2 * k + c] = both[:, c * BLOCK : (c + 1) * BLOCK]
    total[...] = jnp.zeros_like(total)

    for k, (hop, tile_ref) in enumerate(zip(order, tile_refs)):
        rows_ref, cols_ref = list_refs[2 * k], list_refs[2 * k + 1]

        def product(at, tile_ref=tile_ref, cols_ref=cols_ref, hop=hop):
            block = cols_ref[at]
            block = jnp.where(block >= 4, block - 4, block + 4 * hop - 2)
            return jnp.dot(held[block], tile_ref[at], preferred_element_type=jnp.float32)

        def step(at, _, rows_ref=rows_ref, product=product):
            terms = [product(UNROLL * at + k) for k in range(UNROLL)]
            for k in range(UNROLL):
                total[rows_ref[UNROLL * at + k]] += terms[k]
            return 0

        lax.fori_loop(0, lax.div(rows_ref[COUNT] + (UNROLL - 1), UNROLL), step, 0)

    for e in range(N_SUB):
        for r in range(2):
            result = total[2 * e + r, :vecs]
            for part in range(1, parts):
                result = result + total[2 * e + r, part * vecs : (part + 1) * vecs]
            out_refs[e][:, pl.ds(r * BLOCK, BLOCK)] = result


def sweep(own, near, order, tiles):
    vecs = own.shape[0]
    smem = pl.BlockSpec(memory_space=pltpu.SMEM)
    vmem = pl.BlockSpec(memory_space=pltpu.VMEM)
    parts = 1 if own.dtype == jnp.bfloat16 else 2
    lists = [part for tile in tiles for part in tile[1:]]
    return pl.pallas_call(
        functools.partial(sweep_kernel, parts, order),
        in_specs=[smem] * 6 + [vmem] * 10,
        out_specs=[vmem] * 4,
        out_shape=[jax.ShapeDtypeStruct((vecs, LENGTH), jnp.float32)] * 4,
        scratch_shapes=[
            pltpu.VMEM((14, parts * vecs, BLOCK), jnp.bfloat16),
            pltpu.VMEM((NOBODY + 1, parts * vecs, BLOCK), jnp.float32),
        ],
        compiler_params=pltpu.CompilerParams(vmem_limit_bytes=VMEM_LIMIT),
        cost_estimate=pl.CostEstimate(
            flops=50 * 2 * 128 * BLOCK * BLOCK, bytes_accessed=7 * 2**20, transcendentals=0
        ),
    )(*lists, *[tile[0] for tile in tiles], own, *[near[h] for h in (1, -1, 2, -2, 3, -3)])


def exchanged(parts):
    return [parts[0]] + [shifted(parts[e], "sub", -e) for e in range(1, N_SUB)]


def gram_of(image):
    return lax.dot_general(
        image, image, TRANS_B, precision=lax.Precision.HIGHEST, preferred_element_type=jnp.float32
    )


def solved(gram, image):
    count = gram.shape[0]
    place = lax.broadcasted_iota(jnp.int32, (count, 1), 0)
    across = lax.broadcasted_iota(jnp.int32, (count, count), 1)
    identity = jnp.where(across == place, 1.0, 0.0)
    joined = jnp.concatenate([gram, identity], 1)
    for k in range(count):
        column = jnp.where(place > k, joined[:, k : k + 1], 0.0)
        joined = joined - column * (joined[k : k + 1, :] * (1.0 / joined[k : k + 1, k : k + 1]))
    pivots = jnp.sum(joined[:, :count] * identity, axis=1, keepdims=True)
    inverse = joined[:, count:] / jnp.sqrt(pivots)
    return jnp.dot(
        inverse, image, precision=lax.Precision.HIGHEST, preferred_element_type=jnp.float32
    )


def image_of(root_ref, part_refs):
    first, second, third, fourth = (part_ref[...] for part_ref in part_refs)
    return root_ref[...] * ((first + second) + (third + fourth))


def image_kernel(root_ref, *refs):
    image = image_of(root_ref, refs[:4])
    refs[4][...] = root_ref[...] * image
    refs[5][...] = gram_of(image)


def solve_gram_kernel(gram_ref, root_ref, *refs):
    image = solved(gram_ref[...], image_of(root_ref, refs[:4]))
    refs[4][...] = image
    refs[5][...] = gram_of(image)


def solve_kernel(gram_ref, image_ref, solved_ref):
    solved_ref[...] = solved(gram_ref[...], image_ref[...])


def on_device(trajectories, kernel_scale, start_vectors, pair_list):
    vecs, length = start_vectors.shape
    n_sub = lax.axis_size("sub")
    n_space = lax.axis_size("space")
    space_at = lax.axis_index("space")
    sub_at = lax.axis_index("sub")
    device = space_at * n_sub + sub_at

    row_blk = pair_list[:, 0] - device * 2
    col_dev = pair_list[:, 1] // 2
    hop = jnp.remainder(col_dev // n_sub - space_at, n_space)
    across = jnp.remainder(col_dev % n_sub - sub_at, n_sub)
    place = (((hop - 1) * n_sub + across) * 2 + row_blk) * 2 + pair_list[:, 1] % 2
    place = jnp.where(hop > 0, place, -1)
    used = jnp.any(place[:, None] == jnp.arange(length, dtype=jnp.int32)[None, :], axis=0)
    payload = jnp.concatenate(
        [
            trajectories,
            kernel_scale[None, :],
            used.astype(jnp.bfloat16)[None, :],
            jnp.zeros((ROWS - MASK_ROW - 1, length), jnp.bfloat16),
        ],
        0,
    )

    members = [payload] + [shifted(payload, "sub", e) for e in range(1, N_SUB)]
    near = {h: shifted(payload, "space", h) for h in (2, -2)}
    later, near[2], near[-2] = lax.optimization_barrier((payload, near[2], near[-2]))
    for h, source in ((1, later), (-1, later), (3, near[2]), (-3, near[-2])):
        near[h] = shifted(source, "space", 1 if h > 0 else -1)
    blocks, rate = row_operands(members)
    listed = jnp.stack([member[MASK_ROW, : REACH * PAIRS] for member in members]).astype(jnp.float32)

    order = (2, 1, 3)
    tiles = []
    carried = payload
    for at, h in enumerate(order):
        span = slice((h - 1) * PAIRS, h * PAIRS)
        mine = listed[:, span].reshape(N_SUB * PAIRS)
        theirs = near[-h][MASK_ROW, span].astype(jnp.float32)
        *tile, carried = hop_tiles(
            at == 0, at == REACH - 1, mine, theirs, blocks, rate, near[h], near[-h], carried
        )
        tiles.append(tile)
    degree = carried
    shares = exchanged([degree[e, :1] for e in range(N_SUB)])
    root = lax.rsqrt((shares[0] + shares[1]) + (shares[2] + shares[3]))

    vector_shape = jax.ShapeDtypeStruct((vecs, length), jnp.float32)
    gram_shape = jax.ShapeDtypeStruct((vecs, vecs), jnp.float32)
    light = dict(
        cost_estimate=pl.CostEstimate(flops=2**20, bytes_accessed=2**17, transcendentals=0),
        compiler_params=pltpu.CompilerParams(vmem_limit_bytes=SMALL_LIMIT),
    )

    scaled = (root * start_vectors).astype(jnp.bfloat16)
    shares = exchanged(sweep(scaled, space_window(scaled), order, tiles))
    raw, gram = pl.pallas_call(
        image_kernel, out_shape=[vector_shape, gram_shape], **light
    )(root, *shares)

    near_raw = space_window(raw)
    gram = summed(gram)
    shares = exchanged(sweep(raw, near_raw, order, tiles))
    image, gram = pl.pallas_call(
        solve_gram_kernel, out_shape=[vector_shape, gram_shape], **light
    )(gram, root, *shares)
    return pl.pallas_call(solve_kernel, out_shape=vector_shape, **light)(
        summed(gram), image
    )


def solution(mesh):
    placed = (
        P(None, ("space", "sub")),
        P(("space", "sub")),
        P(None, ("space", "sub")),
        P(("space", "sub"), None),
    )
    return jax.shard_map(
        on_device, mesh=mesh, in_specs=placed, out_specs=P(None, ("space", "sub")), check_vma=False
    )
```

profile of v0, /device:TPU:1, one launch (start us, length us, event | category | flops | bytes accessed | tf_op | source)
XLA Modules:
  0.0 174.9 jit_solution(15357568504361119158)
XLA Ops:
  0.0 0.8 fusion.10
  1.7 1.1 maximum_maximum_fusion.refs_0_.extra_ref
  2.8 2.1 %collective-permute-start.4 = (bf16[304,512]{1,0:T(8,128)(2,1)S(1)}, bf16[304,512]{1,0:T(8,128)(2,1)S(1)}, u32[]{:S(2)}, u32[]{:S(2)}) collective-permute-start(bf16[304,512]{1,0:T(8,128)(2,1)S(1)} %maximum_maximum_fusion.refs_0_.extra_ref), channel_id=1, source_target_pairs={{248,0},{252,4},{0,8},{4,12},{8,16},{12,20},{16,24},{20,28},{24,32... | collective-permute-start | bytes 933896 | tf_op jit(solution)/shard_map/ppermute | solution.py:32
  4.9 6.6 %collective-permute-start.3 = (bf16[304,512]{1,0:T(8,128)(2,1)S(1)}, bf16[304,512]{1,0:T(8,128)(2,1)S(1)}, u32[]{:S(2)}, u32[]{:S(2)}) collective-permute-start(bf16[304,512]{1,0:T(8,128)(2,1)S(1)} %maximum_maximum_fusion.refs_0_.extra_ref), channel_id=1, source_target_pairs={{8,0},{12,4},{16,8},{20,12},{24,16},{28,20},{32,24},{36,28},{40,32... | collective-permute-start | bytes 933896 | tf_op jit(solution)/shard_map/ppermute | solution.py:32
  11.5 1.3 collective-permute-start.2
  12.8 2.6 %collective-permute-start.1 = (bf16[304,512]{1,0:T(8,128)(2,1)S(1)}, bf16[304,512]{1,0:T(8,128)(2,1)S(1)}, u32[]{:S(2)}, u32[]{:S(2)}) collective-permute-start(bf16[304,512]{1,0:T(8,128)(2,1)S(1)} %maximum_maximum_fusion.refs_0_.extra_ref), channel_id=1, source_target_pairs={{2,0},{3,1},{0,2},{1,3},{6,4},{7,5},{4,6},{5,7},{10,8},{11,9},{8,1... | collective-permute-start | bytes 933896 | tf_op jit(solution)/shard_map/ppermute | solution.py:32
  15.5 1.1 collective-permute-start
  16.5 2.0 %collective-permute-done.4.behind_ref = bf16[304,512]{1,0:T(8,128)(2,1)S(1)} collective-permute-done((bf16[304,512]{1,0:T(8,128)(2,1)S(1)}, bf16[304,512]{1,0:T(8,128)(2,1)S(1)}, u32[]{:S(2)}, u32[]{:S(2)}) %collective-permute-start.4) | collective-permute-done | bytes 311328 | tf_op jit(solution)/shard_map/ppermute | solution.py:32
  18.5 1.2 collective-permute-start.8
  20.8 2.7 %collective-permute-start.6 = (bf16[304,512]{1,0:T(8,128)(2,1)S(1)}, bf16[304,512]{1,0:T(8,128)(2,1)S(1)}, u32[]{:S(2)}, u32[]{:S(2)}) collective-permute-start(bf16[304,512]{1,0:T(8,128)(2,1)S(1)} %collective-permute-done.3.ahead_ref), channel_id=1, source_target_pairs={{4,0},{8,4},{12,8},{16,12},{20,16},{24,20},{28,24},{32,28},{36,32}... | collective-permute-start | bytes 933896 | tf_op jit(solution)/shard_map/ppermute | solution.py:32
  23.5 5.1 %collective-permute-done.1.refs_2_ = bf16[304,512]{1,0:T(8,128)(2,1)S(1)} collective-permute-done((bf16[304,512]{1,0:T(8,128)(2,1)S(1)}, bf16[304,512]{1,0:T(8,128)(2,1)S(1)}, u32[]{:S(2)}, u32[]{:S(2)}) %collective-permute-start.1) | collective-permute-done | bytes 311328 | tf_op jit(solution)/shard_map/ppermute | solution.py:32
  29.2 4.6 %shard_map.47 = (bf16[44,256,256]{2,1,0:T(8,128)(2,1)S(1)}, s32[48]{0:T(128)S(1)}, s32[48]{0:T(128)S(1)}, f32[9,8,256]{2,1,0:T(8,128)S(1)}) custom-call(f32[64]{0:T(128)S(1)} %reshape.36.mine_ref, f32[16]{0:T(128)S(1)} %bitcast_convert_fusion.theirs_ref, bf16[8,320,256]{2,1,0:T(8,128)(2,1)S(1)} %get-tuple-element.35.blocks_ref, ...), custom_call_target="tpu_custom_call" | custom-call | flops 671088640 | bytes 7340032 | tf_op jit(solution)/shard_map/pallas_call | solution.py:191
  33.8 2.5 %copy-done = bf16[44,256,256]{2,1,0:T(8,128)(2,1)} copy-done((bf16[44,256,256]{2,1,0:T(8,128)(2,1)}, bf16[44,256,256]{2,1,0:T(8,128)(2,1)S(1)}, u32[]{:S(2)}) %copy-start) | copy-done | bytes 5767192
  37.2 0.8 copy-done.8
  38.0 5.0 %shard_map.48 = (bf16[44,256,256]{2,1,0:T(8,128)(2,1)S(1)}, s32[48]{0:T(128)S(1)}, s32[48]{0:T(128)S(1)}, f32[9,8,256]{2,1,0:T(8,128)S(1)}) custom-call(f32[64]{0:T(128)S(1)} %reshape.35.mine_ref, f32[16]{0:T(128)S(1)} %fusion.8.theirs_ref, bf16[8,320,256]{2,1,0:T(8,128)(2,1)S(1)} %get-tuple-element.35.blocks_ref, f32[8,8,256]{2,1,0:T(8,128)S(1)} %copy-done.8, ...), custom_call_target="tpu_custom_call" | custom-call | flops 671088640 | bytes 7340032 | tf_op jit(solution)/shard_map/pallas_call | solution.py:191
  43.0 0.8 fusion.9.theirs_ref
  43.8 4.8 %shard_map.49 = (bf16[44,256,256]{2,1,0:T(8,128)(2,1)S(1)}, s32[48]{0:T(128)S(1)}, s32[48]{0:T(128)S(1)}, f32[4,8,512]{2,1,0:T(8,128)S(1)}) custom-call(f32[64]{0:T(128)S(1)} %reshape.34.mine_ref, f32[16]{0:T(128)S(1)} %fusion.9.theirs_ref, bf16[8,320,256]{2,1,0:T(8,128)(2,1)S(1)} %get-tuple-element.35.blocks_ref, f32[8,8,256]{2,1,0:T(8,128)S(1)} %copy-done.8, ...), custom_call_target="tpu_custom_call" | custom-call | flops 671088640 | bytes 7340032 | tf_op jit(solution)/shard_map/pallas_call | solution.py:191
  48.5 2.8 %collective-permute-start.11 = (f32[1,512]{1,0:T(1,128)S(1)}, f32[1,512]{1,0:T(1,128)S(1)}, u32[]{:S(2)}, u32[]{:S(2)}) collective-permute-start(f32[1,512]{1,0:T(1,128)S(1)} %get-tuple-element.63), channel_id=1, source_target_pairs={{1,0},{2,1},{3,2},{0,3},{5,4},{6,5},{7,6},{4,7},{9,8},{10,9},{11,1... | collective-permute-start | bytes 6152 | tf_op jit(solution)/shard_map/ppermute | solution.py:32
  51.4 1.3 collective-permute-start.10
  52.7 0.8 collective-permute-start.9
  53.5 1.8 %collective-permute-done.10 = f32[1,512]{1,0:T(1,128)S(1)} collective-permute-done((f32[1,512]{1,0:T(1,128)S(1)}, f32[1,512]{1,0:T(1,128)S(1)}, u32[]{:S(2)}, u32[]{:S(2)}) %collective-permute-start.10) | collective-permute-done | bytes 2080 | tf_op jit(solution)/shard_map/ppermute | solution.py:32
  55.3 1.0 collective-permute-done.9
  56.7 5.1 %collective-permute-start.16 = (bf16[32,512]{1,0:T(8,128)(2,1)S(1)}, bf16[32,512]{1,0:T(8,128)(2,1)S(1)}, u32[]{:S(2)}, u32[]{:S(2)}) collective-permute-start(bf16[32,512]{1,0:T(8,128)(2,1)S(1)} %multiply_convert_fusion.refs_9_), channel_id=1, source_target_pairs={{12,0},{16,4},{20,8},{24,12},{28,16},{32,20},{36,24},{40,28},{44,3... | collective-permute-start | bytes 98312 | tf_op jit(solution)/shard_map/ppermute | solution.py:32
  61.7 4.8 %collective-permute-start.14 = (bf16[32,512]{1,0:T(8,128)(2,1)S(1)}, bf16[32,512]{1,0:T(8,128)(2,1)S(1)}, u32[]{:S(2)}, u32[]{:S(2)}) collective-permute-start(bf16[32,512]{1,0:T(8,128)(2,1)S(1)} %multiply_convert_fusion.refs_9_), channel_id=1, source_target_pairs={{8,0},{12,4},{16,8},{20,12},{24,16},{28,20},{32,24},{36,28},{40,32... | collective-permute-start | bytes 98312 | tf_op jit(solution)/shard_map/ppermute | solution.py:32
  66.5 2.6 %collective-permute-start.12 = (bf16[32,512]{1,0:T(8,128)(2,1)S(1)}, bf16[32,512]{1,0:T(8,128)(2,1)S(1)}, u32[]{:S(2)}, u32[]{:S(2)}) collective-permute-start(bf16[32,512]{1,0:T(8,128)(2,1)S(1)} %multiply_convert_fusion.refs_9_), channel_id=1, source_target_pairs={{4,0},{8,4},{12,8},{16,12},{20,16},{24,20},{28,24},{32,28},{36,32}... | collective-permute-start | bytes 98312 | tf_op jit(solution)/shard_map/ppermute | solution.py:32
  70.2 2.6 %copy-done.1 = bf16[44,256,256]{2,1,0:T(8,128)(2,1)S(1)} copy-done((bf16[44,256,256]{2,1,0:T(8,128)(2,1)S(1)}, bf16[44,256,256]{2,1,0:T(8,128)(2,1)}, u32[]{:S(2)}) %copy-start.1) | copy-done | bytes 5767192
  72.8 2.4 %shard_map.50 = (f32[32,512]{1,0:T(8,128)S(1)}, f32[32,512]{1,0:T(8,128)S(1)}, f32[32,512]{1,0:T(8,128)S(1)}, f32[32,512]{1,0:T(8,128)S(1)}) custom-call(s32[48]{0:T(128)S(1)} %get-tuple-element.42.refs_0_, s32[48]{0:T(128)S(1)} %get-tuple-element.43.refs_1_, s32[48]{0:T(128)S(1)} %get-tuple-element.44.refs_2_, s32[48]{0:T(128)S(1)} %get-tuple-element.45.refs_3_, ...), custom_call_target="tpu_custom_call" | custom-call | flops 838860800 | bytes 7340032 | tf_op jit(solution)/shard_map/pallas_call | solution.py:264
  75.3 2.0 %collective-permute-start.19 = (f32[32,512]{1,0:T(8,128)S(1)}, f32[32,512]{1,0:T(8,128)S(1)}, u32[]{:S(2)}, u32[]{:S(2)}) collective-permute-start(f32[32,512]{1,0:T(8,128)S(1)} %get-tuple-element.53), channel_id=1, source_target_pairs={{2,0},{3,1},{0,2},{1,3},{6,4},{7,5},{4,6},{5,7},{10,8},{11,9},{8,1... | collective-permute-start | bytes 196616 | tf_op jit(solution)/shard_map/ppermute | solution.py:32
  77.3 2.0 %collective-permute-start.20 = (f32[32,512]{1,0:T(8,128)S(1)}, f32[32,512]{1,0:T(8,128)S(1)}, u32[]{:S(2)}, u32[]{:S(2)}) collective-permute-start(f32[32,512]{1,0:T(8,128)S(1)} %get-tuple-element.54), channel_id=1, source_target_pairs={{1,0},{2,1},{3,2},{0,3},{5,4},{6,5},{7,6},{4,7},{9,8},{10,9},{11,1... | collective-permute-start | bytes 196616 | tf_op jit(solution)/shard_map/ppermute | solution.py:32
  79.3 1.0 collective-permute-done.18.refs_1_
  81.2 7.3 %collective-permute-start.25 = (f32[32,512]{1,0:T(8,128)S(1)}, f32[32,512]{1,0:T(8,128)S(1)}, u32[]{:S(2)}, u32[]{:S(2)}) collective-permute-start(f32[32,512]{1,0:T(8,128)S(1)} %get-tuple-element.56.refs_9_), channel_id=1, source_target_pairs={{12,0},{16,4},{20,8},{24,12},{28,16},{32,20},{36,24},{40,28},{44,3... | collective-permute-start | bytes 196616 | tf_op jit(solution)/shard_map/ppermute | solution.py:32
  88.5 1.5 collective-permute-start.24
  89.9 3.5 %collective-permute-start.23 = (f32[32,512]{1,0:T(8,128)S(1)}, f32[32,512]{1,0:T(8,128)S(1)}, u32[]{:S(2)}, u32[]{:S(2)}) collective-permute-start(f32[32,512]{1,0:T(8,128)S(1)} %get-tuple-element.56.refs_9_), channel_id=1, source_target_pairs={{8,0},{12,4},{16,8},{20,12},{24,16},{28,20},{32,24},{36,28},{40,32... | collective-permute-start | bytes 196616 | tf_op jit(solution)/shard_map/ppermute | solution.py:32
  93.5 2.0 %collective-permute-start.22 = (f32[32,512]{1,0:T(8,128)S(1)}, f32[32,512]{1,0:T(8,128)S(1)}, u32[]{:S(2)}, u32[]{:S(2)}) collective-permute-start(f32[32,512]{1,0:T(8,128)S(1)} %get-tuple-element.56.refs_9_), channel_id=1, source_target_pairs={{252,0},{0,4},{4,8},{8,12},{12,16},{16,20},{20,24},{24,28},{28,32}... | collective-permute-start | bytes 196616 | tf_op jit(solution)/shard_map/ppermute | solution.py:32
  95.5 3.7 %collective-permute-start.21 = (f32[32,512]{1,0:T(8,128)S(1)}, f32[32,512]{1,0:T(8,128)S(1)}, u32[]{:S(2)}, u32[]{:S(2)}) collective-permute-start(f32[32,512]{1,0:T(8,128)S(1)} %get-tuple-element.56.refs_9_), channel_id=1, source_target_pairs={{4,0},{8,4},{12,8},{16,12},{20,16},{24,20},{28,24},{32,28},{36,32}... | collective-permute-start | bytes 196616 | tf_op jit(solution)/shard_map/ppermute | solution.py:32
  99.3 14.8 %all_to_all.20 = f32[16,8,128]{2,1,0:T(8,128)S(1)} all-to-all(f32[16,8,128]{2,1,0:T(8,128)S(1)} %broadcast_in_dim.40), channel_id=1, replica_groups={{0,1,2,3,4,5,6,7,8,9,10,11,12,13,14,15},{16,17,18,19,20,21,22,23,24,25,..., dimensions={0} | all-to-all | bytes 131072 | tf_op jit(solution)/shard_map/all_to_all | solution.py:54
  114.8 5.7 %all-to-all-start.1 = ((f32[16,8,128]{2,1,0:T(8,128)}), f32[16,8,128]{2,1,0:T(8,128)S(1)}, u32[]{:S(2)}, u32[]{:S(2)}) async-start(f32[16,8,128]{2,1,0:T(8,128)} %broadcast_in_dim.41), calls=%async_computation.1 | async-start | bytes 131072 | tf_op jit(solution)/shard_map/all_to_all | solution.py:54
  120.5 2.6 %copy-done.2 = bf16[44,256,256]{2,1,0:T(8,128)(2,1)S(1)} copy-done((bf16[44,256,256]{2,1,0:T(8,128)(2,1)S(1)}, bf16[44,256,256]{2,1,0:T(8,128)(2,1)}, u32[]{:S(2)}) %copy-start.2) | copy-done | bytes 5767192
  123.2 2.6 %copy-done.4 = bf16[44,256,256]{2,1,0:T(8,128)(2,1)S(1)} copy-done((bf16[44,256,256]{2,1,0:T(8,128)(2,1)S(1)}, bf16[44,256,256]{2,1,0:T(8,128)(2,1)}, u32[]{:S(2)}) %copy-start.4) | copy-done | bytes 5767192
  125.8 2.6 %copy-done.6 = bf16[44,256,256]{2,1,0:T(8,128)(2,1)S(1)} copy-done((bf16[44,256,256]{2,1,0:T(8,128)(2,1)S(1)}, bf16[44,256,256]{2,1,0:T(8,128)(2,1)}, u32[]{:S(2)}) %copy-start.6) | copy-done | bytes 5767192
  128.4 2.5 %shard_map.52 = (f32[32,512]{1,0:T(8,128)S(1)}, f32[32,512]{1,0:T(8,128)S(1)}, f32[32,512]{1,0:T(8,128)S(1)}, f32[32,512]{1,0:T(8,128)S(1)}) custom-call(s32[48]{0:T(128)S(1)} %get-tuple-element.42.refs_0_, s32[48]{0:T(128)S(1)} %get-tuple-element.43.refs_1_, s32[48]{0:T(128)S(1)} %get-tuple-element.44.refs_2_, s32[48]{0:T(128)S(1)} %get-tuple-element.45.refs_3_, ...), custom_call_target="tpu_custom_call" | custom-call | flops 838860800 | bytes 7340032 | tf_op jit(solution)/shard_map/pallas_call | solution.py:264
  131.6 1.5 collective-permute-start.28
  133.2 1.7 collective-permute-start.29
  135.4 1.6 collective-permute-done.28.refs_2_
  137.0 3.2 %shard_map.53 = (f32[32,512]{1,0:T(8,128)S(1)}, f32[32,32]{1,0:T(8,128)S(1)}) custom-call(f32[32,32]{1,0:T(8,128)S(1)} %reshape.37.gram_ref, f32[1,512]{1,0:T(1,128)S(1)} %fusion.2.root_ref, f32[32,512]{1,0:T(8,128)S(1)} %get-tuple-element.57.refs_0_, f32[32,512]{1,0:T(8,128)S(1)} %collective-permute-done.27.refs_1_, ...), custom_call_target="tpu_custom_call" | custom-call | flops 1048576 | bytes 131072 | tf_op jit(solution)/shard_map/pallas_call | solution.py:391
  140.3 12.0 %all_to_all.21 = f32[16,8,128]{2,1,0:T(8,128)S(1)} all-to-all(f32[16,8,128]{2,1,0:T(8,128)S(1)} %broadcast_in_dim.43), channel_id=1, replica_groups={{0,1,2,3,4,5,6,7,8,9,10,11,12,13,14,15},{16,17,18,19,20,21,22,23,24,25,..., dimensions={0} | all-to-all | bytes 131072 | tf_op jit(solution)/shard_map/all_to_all | solution.py:54
  152.3 18.9 %all_to_all.22 = f32[16,8,128]{2,1,0:T(8,128)S(1)} all-to-all(f32[16,8,128]{2,1,0:T(8,128)S(1)} %broadcast_in_dim.44), channel_id=1, replica_groups={{0,16,32,48,64,80,96,112,128,144,160,176,192,208,224,240},{1,17,33,49,6..., dimensions={0} | all-to-all | bytes 131072 | tf_op jit(solution)/shard_map/all_to_all | solution.py:54
  171.3 3.7 %shard_map.54 = f32[32,512]{1,0:T(8,128)} custom-call(f32[32,32]{1,0:T(8,128)S(1)} %reshape.38.gram_ref, f32[32,512]{1,0:T(8,128)S(1)} %get-tuple-element.62.image_ref), custom_call_target="tpu_custom_call" | custom-call | flops 1048576 | bytes 131072 | tf_op jit(solution)/shard_map/pallas_call | solution.py:394
  (81 shorter events, 7.8 us)
Async XLA Ops:
  2.8 15.8 %collective-permute-start.4 = (bf16[304,512]{1,0:T(8,128)(2,1)S(1)}, bf16[304,512]{1,0:T(8,128)(2,1)S(1)}, u32[]{:S(2)}, u32[]{:S(2)}) collective-permute-start(bf16[304,512]{1,0:T(8,128)(2,1)S(1)} %maximum_maximum_fusion.refs_0_.extra_ref), channel_id=1, source_target_pairs={{248,0},{252,4},{0,8},{4,12},{8,16},{12,20},{16,24},{20,28},{24,32... | collective-permute-start | bytes 933896 | tf_op jit(solution)/shard_map/ppermute | solution.py:32
  4.9 13.6 %collective-permute-start.3 = (bf16[304,512]{1,0:T(8,128)(2,1)S(1)}, bf16[304,512]{1,0:T(8,128)(2,1)S(1)}, u32[]{:S(2)}, u32[]{:S(2)}) collective-permute-start(bf16[304,512]{1,0:T(8,128)(2,1)S(1)} %maximum_maximum_fusion.refs_0_.extra_ref), channel_id=1, source_target_pairs={{8,0},{12,4},{16,8},{20,12},{24,16},{28,20},{32,24},{36,28},{40,32... | collective-permute-start | bytes 933896 | tf_op jit(solution)/shard_map/ppermute | solution.py:32
  11.5 9.2 %collective-permute-start.2 = (bf16[304,512]{1,0:T(8,128)(2,1)S(1)}, bf16[304,512]{1,0:T(8,128)(2,1)S(1)}, u32[]{:S(2)}, u32[]{:S(2)}) collective-permute-start(bf16[304,512]{1,0:T(8,128)(2,1)S(1)} %maximum_maximum_fusion.refs_0_.extra_ref), channel_id=1, source_target_pairs={{3,0},{0,1},{1,2},{2,3},{7,4},{4,5},{5,6},{6,7},{11,8},{8,9},{9,10... | collective-permute-start | bytes 933896 | tf_op jit(solution)/shard_map/ppermute | solution.py:32
  12.8 15.7 %collective-permute-start.1 = (bf16[304,512]{1,0:T(8,128)(2,1)S(1)}, bf16[304,512]{1,0:T(8,128)(2,1)S(1)}, u32[]{:S(2)}, u32[]{:S(2)}) collective-permute-start(bf16[304,512]{1,0:T(8,128)(2,1)S(1)} %maximum_maximum_fusion.refs_0_.extra_ref), channel_id=1, source_target_pairs={{2,0},{3,1},{0,2},{1,3},{6,4},{7,5},{4,6},{5,7},{10,8},{11,9},{8,1... | collective-permute-start | bytes 933896 | tf_op jit(solution)/shard_map/ppermute | solution.py:32
  15.5 13.2 %collective-permute-start = (bf16[304,512]{1,0:T(8,128)(2,1)S(1)}, bf16[304,512]{1,0:T(8,128)(2,1)S(1)}, u32[]{:S(2)}, u32[]{:S(2)}) collective-permute-start(bf16[304,512]{1,0:T(8,128)(2,1)S(1)} %maximum_maximum_fusion.refs_0_.extra_ref), channel_id=1, source_target_pairs={{1,0},{2,1},{3,2},{0,3},{5,4},{6,5},{7,6},{4,7},{9,8},{10,9},{11,1... | collective-permute-start | bytes 933896 | tf_op jit(solution)/shard_map/ppermute | solution.py:32
  18.5 18.6 %collective-permute-start.8 = (bf16[304,512]{1,0:T(8,128)(2,1)S(1)}, bf16[304,512]{1,0:T(8,128)(2,1)}, u32[]{:S(2)}, u32[]{:S(2)}) collective-permute-start(bf16[304,512]{1,0:T(8,128)(2,1)S(1)} %maximum_maximum_fusion.refs_0_.extra_ref), channel_id=1, source_target_pairs={{4,0},{8,4},{12,8},{16,12},{20,16},{24,20},{28,24},{32,28},{36,32}... | collective-permute-start | bytes 933896 | tf_op jit(solution)/shard_map/ppermute | solution.py:32
  19.8 16.7 %collective-permute-start.7 = (bf16[304,512]{1,0:T(8,128)(2,1)S(1)}, bf16[304,512]{1,0:T(8,128)(2,1)}, u32[]{:S(2)}, u32[]{:S(2)}) collective-permute-start(bf16[304,512]{1,0:T(8,128)(2,1)S(1)} %maximum_maximum_fusion.refs_0_.extra_ref), channel_id=1, source_target_pairs={{252,0},{0,4},{4,8},{8,12},{12,16},{16,20},{20,24},{24,28},{28,32}... | collective-permute-start | bytes 933896 | tf_op jit(solution)/shard_map/ppermute | solution.py:32
  20.8 23.0 %collective-permute-start.6 = (bf16[304,512]{1,0:T(8,128)(2,1)S(1)}, bf16[304,512]{1,0:T(8,128)(2,1)S(1)}, u32[]{:S(2)}, u32[]{:S(2)}) collective-permute-start(bf16[304,512]{1,0:T(8,128)(2,1)S(1)} %collective-permute-done.3.ahead_ref), channel_id=1, source_target_pairs={{4,0},{8,4},{12,8},{16,12},{20,16},{24,20},{28,24},{32,28},{36,32}... | collective-permute-start | bytes 933896 | tf_op jit(solution)/shard_map/ppermute | solution.py:32
  28.6 14.4 %collective-permute-start.5 = (bf16[304,512]{1,0:T(8,128)(2,1)S(1)}, bf16[304,512]{1,0:T(8,128)(2,1)}, u32[]{:S(2)}, u32[]{:S(2)}) collective-permute-start(bf16[304,512]{1,0:T(8,128)(2,1)S(1)} %collective-permute-done.4.behind_ref), channel_id=1, source_target_pairs={{252,0},{0,4},{4,8},{8,12},{12,16},{16,20},{20,24},{24,28},{28,32}... | collective-permute-start | bytes 933896 | tf_op jit(solution)/shard_map/ppermute | solution.py:32
  29.2 4.6 %copy-start.7 = (f32[8,8,256]{2,1,0:T(8,128)}, f32[8,8,256]{2,1,0:T(8,128)S(1)}, u32[]{:S(2)}) copy-start(f32[8,8,256]{2,1,0:T(8,128)S(1)} %get-tuple-element.36.rate_ref) | copy-start | bytes 196612
  29.2 27.2 %copy-start.9 = (f32[32,512]{1,0:T(8,128)S(1)}, f32[32,512]{1,0:T(8,128)}, u32[]{:S(2)}) copy-start(f32[32,512]{1,0:T(8,128)} %param.6) | copy-start | bytes 196612
  33.8 2.5 %copy-start = (bf16[44,256,256]{2,1,0:T(8,128)(2,1)}, bf16[44,256,256]{2,1,0:T(8,128)(2,1)S(1)}, u32[]{:S(2)}) copy-start(bf16[44,256,256]{2,1,0:T(8,128)(2,1)S(1)} %get-tuple-element.48.refs_6_) | copy-start | bytes 17301508
  37.2 0.8 copy-start.8
  43.0 32.3 %copy-start.3 = (bf16[44,256,256]{2,1,0:T(8,128)(2,1)}, bf16[44,256,256]{2,1,0:T(8,128)(2,1)S(1)}, u32[]{:S(2)}) copy-start(bf16[44,256,256]{2,1,0:T(8,128)(2,1)S(1)} %get-tuple-element.49.refs_7_) | copy-start | bytes 17301508
  48.5 26.7 %copy-start.5 = (bf16[44,256,256]{2,1,0:T(8,128)(2,1)}, bf16[44,256,256]{2,1,0:T(8,128)(2,1)S(1)}, u32[]{:S(2)}) copy-start(bf16[44,256,256]{2,1,0:T(8,128)(2,1)S(1)} %get-tuple-element.50.refs_8_) | copy-start | bytes 17301508
  48.5 4.9 %collective-permute-start.11 = (f32[1,512]{1,0:T(1,128)S(1)}, f32[1,512]{1,0:T(1,128)S(1)}, u32[]{:S(2)}, u32[]{:S(2)}) collective-permute-start(f32[1,512]{1,0:T(1,128)S(1)} %get-tuple-element.63), channel_id=1, source_target_pairs={{1,0},{2,1},{3,2},{0,3},{5,4},{6,5},{7,6},{4,7},{9,8},{10,9},{11,1... | collective-permute-start | bytes 6152 | tf_op jit(solution)/shard_map/ppermute | solution.py:32
  51.4 3.9 %collective-permute-start.10 = (f32[1,512]{1,0:T(1,128)S(1)}, f32[1,512]{1,0:T(1,128)S(1)}, u32[]{:S(2)}, u32[]{:S(2)}) collective-permute-start(f32[1,512]{1,0:T(1,128)S(1)} %get-tuple-element.64), channel_id=1, source_target_pairs={{2,0},{3,1},{0,2},{1,3},{6,4},{7,5},{4,6},{5,7},{10,8},{11,9},{8,1... | collective-permute-start | bytes 6152 | tf_op jit(solution)/shard_map/ppermute | solution.py:32
  52.7 3.6 %collective-permute-start.9 = (f32[1,512]{1,0:T(1,128)S(1)}, f32[1,512]{1,0:T(1,128)S(1)}, u32[]{:S(2)}, u32[]{:S(2)}) collective-permute-start(f32[1,512]{1,0:T(1,128)S(1)} %get-tuple-element.65), channel_id=1, source_target_pairs={{3,0},{0,1},{1,2},{2,3},{7,4},{4,5},{5,6},{6,7},{11,8},{8,9},{9,10... | collective-permute-start | bytes 6152 | tf_op jit(solution)/shard_map/ppermute | solution.py:32
  56.4 10.1 %collective-permute-start.17 = (bf16[32,512]{1,0:T(8,128)(2,1)S(1)}, bf16[32,512]{1,0:T(8,128)(2,1)S(1)}, u32[]{:S(2)}, u32[]{:S(2)}) collective-permute-start(bf16[32,512]{1,0:T(8,128)(2,1)S(1)} %multiply_convert_fusion.refs_9_), channel_id=1, source_target_pairs={{244,0},{248,4},{252,8},{0,12},{4,16},{8,20},{12,24},{16,28},{20,3... | collective-permute-start | bytes 98312 | tf_op jit(solution)/shard_map/ppermute | solution.py:32
  56.7 12.4 %collective-permute-start.16 = (bf16[32,512]{1,0:T(8,128)(2,1)S(1)}, bf16[32,512]{1,0:T(8,128)(2,1)S(1)}, u32[]{:S(2)}, u32[]{:S(2)}) collective-permute-start(bf16[32,512]{1,0:T(8,128)(2,1)S(1)} %multiply_convert_fusion.refs_9_), channel_id=1, source_target_pairs={{12,0},{16,4},{20,8},{24,12},{28,16},{32,20},{36,24},{40,28},{44,3... | collective-permute-start | bytes 98312 | tf_op jit(solution)/shard_map/ppermute | solution.py:32
  61.7 7.4 %collective-permute-start.15 = (bf16[32,512]{1,0:T(8,128)(2,1)S(1)}, bf16[32,512]{1,0:T(8,128)(2,1)S(1)}, u32[]{:S(2)}, u32[]{:S(2)}) collective-permute-start(bf16[32,512]{1,0:T(8,128)(2,1)S(1)} %multiply_convert_fusion.refs_9_), channel_id=1, source_target_pairs={{248,0},{252,4},{0,8},{4,12},{8,16},{12,20},{16,24},{20,28},{24,32... | collective-permute-start | bytes 98312 | tf_op jit(solution)/shard_map/ppermute | solution.py:32
  61.7 7.4 %collective-permute-start.14 = (bf16[32,512]{1,0:T(8,128)(2,1)S(1)}, bf16[32,512]{1,0:T(8,128)(2,1)S(1)}, u32[]{:S(2)}, u32[]{:S(2)}) collective-permute-start(bf16[32,512]{1,0:T(8,128)(2,1)S(1)} %multiply_convert_fusion.refs_9_), channel_id=1, source_target_pairs={{8,0},{12,4},{16,8},{20,12},{24,16},{28,20},{32,24},{36,28},{40,32... | collective-permute-start | bytes 98312 | tf_op jit(solution)/shard_map/ppermute | solution.py:32
  66.5 3.3 %collective-permute-start.13 = (bf16[32,512]{1,0:T(8,128)(2,1)S(1)}, bf16[32,512]{1,0:T(8,128)(2,1)S(1)}, u32[]{:S(2)}, u32[]{:S(2)}) collective-permute-start(bf16[32,512]{1,0:T(8,128)(2,1)S(1)} %multiply_convert_fusion.refs_9_), channel_id=1, source_target_pairs={{252,0},{0,4},{4,8},{8,12},{12,16},{16,20},{20,24},{24,28},{28,32}... | collective-permute-start | bytes 98312 | tf_op jit(solution)/shard_map/ppermute | solution.py:32
  66.5 3.6 %collective-permute-start.12 = (bf16[32,512]{1,0:T(8,128)(2,1)S(1)}, bf16[32,512]{1,0:T(8,128)(2,1)S(1)}, u32[]{:S(2)}, u32[]{:S(2)}) collective-permute-start(bf16[32,512]{1,0:T(8,128)(2,1)S(1)} %multiply_convert_fusion.refs_9_), channel_id=1, source_target_pairs={{4,0},{8,4},{12,8},{16,12},{20,16},{24,20},{28,24},{32,28},{36,32}... | collective-permute-start | bytes 98312 | tf_op jit(solution)/shard_map/ppermute | solution.py:32
  70.2 2.6 %copy-start.1 = (bf16[44,256,256]{2,1,0:T(8,128)(2,1)S(1)}, bf16[44,256,256]{2,1,0:T(8,128)(2,1)}, u32[]{:S(2)}) copy-start(bf16[44,256,256]{2,1,0:T(8,128)(2,1)} %copy-done) | copy-start | bytes 17301508
  75.2 5.1 %collective-permute-start.18 = (f32[32,512]{1,0:T(8,128)S(1)}, f32[32,512]{1,0:T(8,128)S(1)}, u32[]{:S(2)}, u32[]{:S(2)}) collective-permute-start(f32[32,512]{1,0:T(8,128)S(1)} %get-tuple-element.52), channel_id=1, source_target_pairs={{3,0},{0,1},{1,2},{2,3},{7,4},{4,5},{5,6},{6,7},{11,8},{8,9},{9,10... | collective-permute-start | bytes 196616 | tf_op jit(solution)/shard_map/ppermute | solution.py:32
  75.3 5.0 %collective-permute-start.19 = (f32[32,512]{1,0:T(8,128)S(1)}, f32[32,512]{1,0:T(8,128)S(1)}, u32[]{:S(2)}, u32[]{:S(2)}) collective-permute-start(f32[32,512]{1,0:T(8,128)S(1)} %get-tuple-element.53), channel_id=1, source_target_pairs={{2,0},{3,1},{0,2},{1,3},{6,4},{7,5},{4,6},{5,7},{10,8},{11,9},{8,1... | collective-permute-start | bytes 196616 | tf_op jit(solution)/shard_map/ppermute | solution.py:32
  77.3 3.6 %collective-permute-start.20 = (f32[32,512]{1,0:T(8,128)S(1)}, f32[32,512]{1,0:T(8,128)S(1)}, u32[]{:S(2)}, u32[]{:S(2)}) collective-permute-start(f32[32,512]{1,0:T(8,128)S(1)} %get-tuple-element.54), channel_id=1, source_target_pairs={{1,0},{2,1},{3,2},{0,3},{5,4},{6,5},{7,6},{4,7},{9,8},{10,9},{11,1... | collective-permute-start | bytes 196616 | tf_op jit(solution)/shard_map/ppermute | solution.py:32
  81.1 14.4 %collective-permute-start.26 = (f32[32,512]{1,0:T(8,128)S(1)}, f32[32,512]{1,0:T(8,128)S(1)}, u32[]{:S(2)}, u32[]{:S(2)}) collective-permute-start(f32[32,512]{1,0:T(8,128)S(1)} %get-tuple-element.56.refs_9_), channel_id=1, source_target_pairs={{244,0},{248,4},{252,8},{0,12},{4,16},{8,20},{12,24},{16,28},{20,3... | collective-permute-start | bytes 196616 | tf_op jit(solution)/shard_map/ppermute | solution.py:32
  81.2 39.3 %collective-permute-start.25 = (f32[32,512]{1,0:T(8,128)S(1)}, f32[32,512]{1,0:T(8,128)S(1)}, u32[]{:S(2)}, u32[]{:S(2)}) collective-permute-start(f32[32,512]{1,0:T(8,128)S(1)} %get-tuple-element.56.refs_9_), channel_id=1, source_target_pairs={{12,0},{16,4},{20,8},{24,12},{28,16},{32,20},{36,24},{40,28},{44,3... | collective-permute-start | bytes 196616 | tf_op jit(solution)/shard_map/ppermute | solution.py:32
  88.5 32.0 %collective-permute-start.24 = (f32[32,512]{1,0:T(8,128)S(1)}, f32[32,512]{1,0:T(8,128)S(1)}, u32[]{:S(2)}, u32[]{:S(2)}) collective-permute-start(f32[32,512]{1,0:T(8,128)S(1)} %get-tuple-element.56.refs_9_), channel_id=1, source_target_pairs={{248,0},{252,4},{0,8},{4,12},{8,16},{12,20},{16,24},{20,28},{24,32... | collective-permute-start | bytes 196616 | tf_op jit(solution)/shard_map/ppermute | solution.py:32
  89.9 30.6 %collective-permute-start.23 = (f32[32,512]{1,0:T(8,128)S(1)}, f32[32,512]{1,0:T(8,128)S(1)}, u32[]{:S(2)}, u32[]{:S(2)}) collective-permute-start(f32[32,512]{1,0:T(8,128)S(1)} %get-tuple-element.56.refs_9_), channel_id=1, source_target_pairs={{8,0},{12,4},{16,8},{20,12},{24,16},{28,20},{32,24},{36,28},{40,32... | collective-permute-start | bytes 196616 | tf_op jit(solution)/shard_map/ppermute | solution.py:32
  93.5 27.0 %collective-permute-start.22 = (f32[32,512]{1,0:T(8,128)S(1)}, f32[32,512]{1,0:T(8,128)S(1)}, u32[]{:S(2)}, u32[]{:S(2)}) collective-permute-start(f32[32,512]{1,0:T(8,128)S(1)} %get-tuple-element.56.refs_9_), channel_id=1, source_target_pairs={{252,0},{0,4},{4,8},{8,12},{12,16},{16,20},{20,24},{24,28},{28,32}... | collective-permute-start | bytes 196616 | tf_op jit(solution)/shard_map/ppermute | solution.py:32
  95.5 25.0 %collective-permute-start.21 = (f32[32,512]{1,0:T(8,128)S(1)}, f32[32,512]{1,0:T(8,128)S(1)}, u32[]{:S(2)}, u32[]{:S(2)}) collective-permute-start(f32[32,512]{1,0:T(8,128)S(1)} %get-tuple-element.56.refs_9_), channel_id=1, source_target_pairs={{4,0},{8,4},{12,8},{16,12},{20,16},{24,20},{28,24},{32,28},{36,32}... | collective-permute-start | bytes 196616 | tf_op jit(solution)/shard_map/ppermute | solution.py:32
  114.8 20.1 %all-to-all-start.1 = ((f32[16,8,128]{2,1,0:T(8,128)}), f32[16,8,128]{2,1,0:T(8,128)S(1)}, u32[]{:S(2)}, u32[]{:S(2)}) async-start(f32[16,8,128]{2,1,0:T(8,128)} %broadcast_in_dim.41), calls=%async_computation.1 | async-start | bytes 131072 | tf_op jit(solution)/shard_map/all_to_all | solution.py:54
  120.5 2.6 %copy-start.2 = (bf16[44,256,256]{2,1,0:T(8,128)(2,1)S(1)}, bf16[44,256,256]{2,1,0:T(8,128)(2,1)}, u32[]{:S(2)}) copy-start(bf16[44,256,256]{2,1,0:T(8,128)(2,1)} %copy-done) | copy-start | bytes 17301508
  123.2 2.6 %copy-start.4 = (bf16[44,256,256]{2,1,0:T(8,128)(2,1)S(1)}, bf16[44,256,256]{2,1,0:T(8,128)(2,1)}, u32[]{:S(2)}) copy-start(bf16[44,256,256]{2,1,0:T(8,128)(2,1)} %copy-done.3) | copy-start | bytes 17301508
  125.8 2.6 %copy-start.6 = (bf16[44,256,256]{2,1,0:T(8,128)(2,1)S(1)}, bf16[44,256,256]{2,1,0:T(8,128)(2,1)}, u32[]{:S(2)}) copy-start(bf16[44,256,256]{2,1,0:T(8,128)(2,1)} %copy-done.5) | copy-start | bytes 17301508
  131.0 4.4 %collective-permute-start.27 = (f32[32,512]{1,0:T(8,128)S(1)}, f32[32,512]{1,0:T(8,128)S(1)}, u32[]{:S(2)}, u32[]{:S(2)}) collective-permute-start(f32[32,512]{1,0:T(8,128)S(1)} %get-tuple-element.58), channel_id=1, source_target_pairs={{3,0},{0,1},{1,2},{2,3},{7,4},{4,5},{5,6},{6,7},{11,8},{8,9},{9,10... | collective-permute-start | bytes 196616 | tf_op jit(solution)/shard_map/ppermute | solution.py:32
  131.6 5.3 %collective-permute-start.28 = (f32[32,512]{1,0:T(8,128)S(1)}, f32[32,512]{1,0:T(8,128)S(1)}, u32[]{:S(2)}, u32[]{:S(2)}) collective-permute-start(f32[32,512]{1,0:T(8,128)S(1)} %get-tuple-element.59), channel_id=1, source_target_pairs={{2,0},{3,1},{0,2},{1,3},{6,4},{7,5},{4,6},{5,7},{10,8},{11,9},{8,1... | collective-permute-start | bytes 196616 | tf_op jit(solution)/shard_map/ppermute | solution.py:32
  133.2 3.8 %collective-permute-start.29 = (f32[32,512]{1,0:T(8,128)S(1)}, f32[32,512]{1,0:T(8,128)S(1)}, u32[]{:S(2)}, u32[]{:S(2)}) collective-permute-start(f32[32,512]{1,0:T(8,128)S(1)} %get-tuple-element.60), channel_id=1, source_target_pairs={{1,0},{2,1},{3,2},{0,3},{5,4},{6,5},{7,6},{4,7},{9,8},{10,9},{11,1... | collective-permute-start | bytes 196616 | tf_op jit(solution)/shard_map/ppermute | solution.py:32
where the time goes:
time: 176 us; the launch traced here: 175 us
  starting transfers between devices  67.5 us (38%)
  blocking collectives  45.7 us (26%)
  Pallas kernels  26.6 us (15%)
  local copies, waits for them, and re-layouts  16 us (9%)
  waiting for transfers between devices  15.2 us (9%)
  other arithmetic  3.63 us (2%)
    ppermute x30, starting transfers between devices, shifted(): lax.ppermute(value, axis, [((at + steps) % count, at) for at in range(cou...  61.8 us
    all_to_all x3, blocking collectives, summed(): lax.all_to_all(sent, ('space', 'sub'), 0, 0, axis_index_groups=groups)  45.7 us
    ppermute x30, waiting for transfers between devices, shifted(): lax.ppermute(value, axis, [((at + steps) % count, at) for at in range(cou...  15.2 us
    pallas_call x3, Pallas kernels, hop_tiles(): pl.pallas_call(functools.partial(tile_kernel, first, last), in_specs=[sme...  14.3 us
    unnamed x20, local copies, waits for them, and re-layouts  13.9 us
    all_to_all x1, starting transfers between devices, summed(): lax.all_to_all(sent, ('space', 'sub'), 0, 0, axis_index_groups=groups)  5.67 us
    pallas_call x2, Pallas kernels, sweep(): pl.pallas_call(functools.partial(sweep_kernel, parts, order), in_specs=[s...  4.94 us
    pallas_call x1, Pallas kernels, on_device(): pl.pallas_call(solve_kernel, out_shape=vector_shape, **light)  3.65 us
  transfers between devices with their start and end apart: 31, of which 11 were waited for; matrix products, arithmetic and copies ran while one was open for 2% of the time, Pallas kernels for 7%

commit v1 on v0

--- a/solution.py
+++ b/solution.py
@@ -21,8 +21,11 @@
 COUNT = SLOTS - 1
 NOBODY = 2 * N_SUB
 UNROLL = 8
+STARTS = (0, 5, 9)
+GROUPS = 13
 LOG2E = 1.4426950408889634
 VMEM_LIMIT = 12 * 1024 * 1024
+SWEEP_LIMIT = 24 * 1024 * 1024
 SMALL_LIMIT = 4 * 1024 * 1024
 TRANS_B = (((1,), (1,)), ((), ()))
 
@@ -112,7 +115,7 @@
         rate_ref[first + c] = rate[c * BLOCK : (c + 1) * BLOCK]
 
 
-def list_pairs(mine_ref, theirs_ref, rows_ref, cols_ref, count):
+def list_pairs(mine_ref, theirs, rows_ref, cols_ref, count):
     def member(e, count):
         for side in range(2):
             for r in range(2):
@@ -120,10 +123,10 @@
                     if side == 0:
                         used = mine_ref[e * PAIRS + lax.rem(N_SUB - e, N_SUB) * 4 + r * 2 + c]
                     else:
-                        used = theirs_ref[e * 4 + c * 2 + r]
+                        used = lax.shift_right_logical(theirs, e * 4 + c * 2 + r) & 1
                     rows_ref[count] = e * 2 + r
                     cols_ref[count] = side * 2 + c
-                    count = count + jnp.where(used > 0.0, 1, 0)
+                    count = count + used
         return count
 
     count = lax.fori_loop(0, N_SUB, member, count)
@@ -136,8 +139,8 @@
 
 
 def tile_kernel(
-    first, last, mine_ref, theirs_ref, blocks_ref, rate_ref, ahead_ref, behind_ref, extra_ref,
-    tile_ref, rows_ref, cols_ref, sums_ref, lhs, col, even, odd, *held
+    hop, first, last, mine_ref, blocks_ref, rate_ref, ahead_ref, behind_ref, extra_ref,
+    tile_ref, rows_ref, cols_ref, sums_ref, lhs, col, even, odd, made, sems, *held
 ):
     total = held[0] if last else sums_ref
     prepare_columns(ahead_ref, 0, lhs, col)
@@ -152,7 +155,12 @@
         total[...] = jnp.zeros_like(total)
     else:
         total[...] = extra_ref[...]
-    count = list_pairs(mine_ref, theirs_ref, rows_ref, cols_ref, jnp.int32(count))
+    lane = lax.broadcasted_iota(jnp.int32, (1, 128), 1) - (hop - 1) * PAIRS
+    weight = lax.shift_left(jnp.ones_like(lane), jnp.clip(lane, 0, PAIRS)).astype(jnp.float32)
+    weight = jnp.where((lane >= 0) & (lane < PAIRS), weight, 0.0)
+    theirs = behind_ref[MASK_ROW : MASK_ROW + 1, :128].astype(jnp.float32)
+    theirs = jnp.sum(theirs * weight).astype(jnp.int32)
+    count = list_pairs(mine_ref, theirs, rows_ref, cols_ref, jnp.int32(count))
 
     def product(at):
         row = lax.min(rows_ref[at], NOBODY - 1)
@@ -163,7 +171,7 @@
         rate = col[cols_ref[at]]
         rates = jnp.concatenate([rate, rate], 1) * rate_ref[lax.min(row, NOBODY - 1), :1, :]
         tile = jnp.exp2(crossed * rates).astype(jnp.bfloat16)
-        tile_ref[at] = tile
+        made[at] = tile
         total[row] += jnp.sum(tile.astype(jnp.float32).reshape(BLOCK // 8, 8, BLOCK), axis=0)
 
     even[...] = product(0)
@@ -173,27 +181,49 @@
         finish(even[...], 2 * k)
         even[...] = product(2 * k + 2)
         finish(odd[...], 2 * k + 1)
+
+        @pl.when(lax.rem(k, UNROLL // 2) == UNROLL // 2 - 1)
+        def _():
+            copy(lax.div(k, UNROLL // 2)).start()
+
         return 0
 
-    lax.fori_loop(0, lax.shift_right_logical(count + 1, 1), step, 0)
+    def copy(group):
+        span = pl.ds(group * UNROLL, UNROLL)
+        return pltpu.make_async_copy(made.at[span], tile_ref.at[span], sems.at[group])
+
+    steps = lax.shift_right_logical(count + 1, 1)
+    lax.fori_loop(0, steps, step, 0)
+
+    @pl.when(lax.rem(steps, UNROLL // 2) != 0)
+    def _():
+        copy(lax.div(steps, UNROLL // 2)).start()
+
     if last:
         for e in range(N_SUB):
             for r in range(2):
                 sums = jnp.sum(total[2 * e + r], axis=0, keepdims=True)
                 sums_ref[e, :, pl.ds(r * BLOCK, BLOCK)] = jnp.broadcast_to(sums, (8, BLOCK))
 
-
-def hop_tiles(first, last, mine, theirs, blocks, rate, ahead, behind, extra):
+    def sent(group, _):
+        copy(group).wait()
+        return 0
+
+    lax.fori_loop(0, lax.div(steps + (UNROLL // 2 - 1), UNROLL // 2), sent, 0)
+
+
+def hop_tiles(hop, first, last, mine, blocks, rate, ahead, behind, extra):
     smem = pl.BlockSpec(memory_space=pltpu.SMEM)
     vmem = pl.BlockSpec(memory_space=pltpu.VMEM)
     columns = 6 if first else 4
+    slots = UNROLL * (5 if first else 4)
     sums = (NOBODY + 1, 8, BLOCK)
     return pl.pallas_call(
-        functools.partial(tile_kernel, first, last),
-        in_specs=[smem, smem] + [vmem] * 5,
-        out_specs=[vmem, smem, smem, vmem],
+        functools.partial(tile_kernel, hop, first, last),
+        in_specs=[smem] + [vmem] * 5,
+        out_specs=[pl.BlockSpec(memory_space=pl.ANY), smem, smem, vmem],
         out_shape=[
-            jax.ShapeDtypeStruct((SLOTS - 4, BLOCK, BLOCK), jnp.bfloat16),
+            jax.ShapeDtypeStruct((slots, BLOCK, BLOCK), jnp.bfloat16),
             jax.ShapeDtypeStruct((SLOTS,), jnp.int32),
             jax.ShapeDtypeStruct((SLOTS,), jnp.int32),
             jax.ShapeDtypeStruct((N_SUB, 8, LENGTH) if last else sums, jnp.float32),
@@ -203,6 +233,8 @@
             pltpu.VMEM((columns, BLOCK, 128), jnp.float32),
             pltpu.VMEM((BLOCK, BLOCK), jnp.float32),
             pltpu.VMEM((BLOCK, BLOCK), jnp.float32),
+            pltpu.VMEM((slots, BLOCK, BLOCK), jnp.bfloat16),
+            pltpu.SemaphoreType.DMA((slots // UNROLL,)),
         ]
         + ([pltpu.VMEM(sums, jnp.float32)] if last else []),
         compiler_params=pltpu.CompilerParams(vmem_limit_bytes=VMEM_LIMIT),
@@ -211,7 +243,7 @@
             bytes_accessed=7 * 2**20,
             transcendentals=16 * BLOCK * BLOCK,
         ),
-    )(mine, theirs, blocks, rate, ahead, behind, extra)
+    )(mine, blocks, rate, ahead, behind, extra)
 
 
 def stacked(vectors):
@@ -223,29 +255,44 @@
 
 def sweep_kernel(parts, order, *refs):
     list_refs, tile_refs, vector_refs = refs[:6], refs[6:9], refs[9:16]
-    out_refs, held, total = refs[16:20], refs[20], refs[21]
+    out_refs, (held, total, tiles, sems) = refs[16:20], refs[20:]
     vecs = vector_refs[0].shape[0]
+
+    def copy(k, at):
+        span = pl.ds(at * UNROLL, UNROLL)
+        place = pl.ds((STARTS[k] + at) * UNROLL, UNROLL)
+        return pltpu.make_async_copy(tile_refs[k].at[span], tiles.at[place], sems.at[STARTS[k] + at])
+
+    groups = [lax.div(list_refs[2 * k][COUNT] + (UNROLL - 1), UNROLL) for k in range(REACH)]
+    for k in range(REACH):
+
+        def fetch(at, _, k=k):
+            copy(k, at).start()
+            return 0
+
+        lax.fori_loop(0, groups[k], fetch, 0)
+
     for k in range(7):
         both = stacked(vector_refs[k][...])
         for c in range(2):
             held[2 * k + c] = both[:, c * BLOCK : (c + 1) * BLOCK]
     total[...] = jnp.zeros_like(total)
 
-    for k, (hop, tile_ref) in enumerate(zip(order, tile_refs)):
-        rows_ref, cols_ref = list_refs[2 * k], list_refs[2 * k + 1]
-
-        def product(at, tile_ref=tile_ref, cols_ref=cols_ref, hop=hop):
-            block = cols_ref[at]
-            block = jnp.where(block >= 4, block - 4, block + 4 * hop - 2)
-            return jnp.dot(held[block], tile_ref[at], preferred_element_type=jnp.float32)
-
-        def step(at, _, rows_ref=rows_ref, product=product):
-            terms = [product(UNROLL * at + k) for k in range(UNROLL)]
-            for k in range(UNROLL):
-                total[rows_ref[UNROLL * at + k]] += terms[k]
+    for k, hop in enumerate(order):
+
+        def step(at, _, k=k, hop=hop, rows_ref=list_refs[2 * k], cols_ref=list_refs[2 * k + 1]):
+            copy(k, at).wait()
+            terms = []
+            for n in range(UNROLL):
+                block = cols_ref[UNROLL * at + n]
+                block = jnp.where(block >= 4, block - 4, block + 4 * hop - 2)
+                tile = tiles[(STARTS[k] + at) * UNROLL + n]
+                terms.append(jnp.dot(held[block], tile, preferred_element_type=jnp.float32))
+            for n in range(UNROLL):
+                total[rows_ref[UNROLL * at + n]] += terms[n]
             return 0
 
-        lax.fori_loop(0, lax.div(rows_ref[COUNT] + (UNROLL - 1), UNROLL), step, 0)
+        lax.fori_loop(0, groups[k], step, 0)
 
     for e in range(N_SUB):
         for r in range(2):
@@ -263,14 +310,16 @@
     lists = [part for tile in tiles for part in tile[1:]]
     return pl.pallas_call(
         functools.partial(sweep_kernel, parts, order),
-        in_specs=[smem] * 6 + [vmem] * 10,
+        in_specs=[smem] * 6 + [pl.BlockSpec(memory_space=pl.ANY)] * 3 + [vmem] * 7,
         out_specs=[vmem] * 4,
         out_shape=[jax.ShapeDtypeStruct((vecs, LENGTH), jnp.float32)] * 4,
         scratch_shapes=[
             pltpu.VMEM((14, parts * vecs, BLOCK), jnp.bfloat16),
             pltpu.VMEM((NOBODY + 1, parts * vecs, BLOCK), jnp.float32),
+            pltpu.VMEM((GROUPS * UNROLL, BLOCK, BLOCK), jnp.bfloat16),
+            pltpu.SemaphoreType.DMA((GROUPS,)),
         ],
-        compiler_params=pltpu.CompilerParams(vmem_limit_bytes=VMEM_LIMIT),
+        compiler_params=pltpu.CompilerParams(vmem_limit_bytes=SWEEP_LIMIT),
         cost_estimate=pl.CostEstimate(
             flops=50 * 2 * 128 * BLOCK * BLOCK, bytes_accessed=7 * 2**20, transcendentals=0
         ),
@@ -287,7 +336,7 @@
     )
 
 
-def solved(gram, image):
+def inverse_factor(gram):
     count = gram.shape[0]
     place = lax.broadcasted_iota(jnp.int32, (count, 1), 0)
     across = lax.broadcasted_iota(jnp.int32, (count, count), 1)
@@ -297,10 +346,12 @@
         column = jnp.where(place > k, joined[:, k : k + 1], 0.0)
         joined = joined - column * (joined[k : k + 1, :] * (1.0 / joined[k : k + 1, k : k + 1]))
     pivots = jnp.sum(joined[:, :count] * identity, axis=1, keepdims=True)
-    inverse = joined[:, count:] / jnp.sqrt(pivots)
-    return jnp.dot(
-        inverse, image, precision=lax.Precision.HIGHEST, preferred_element_type=jnp.float32
-    )
+    diagonal = jnp.sum(gram * identity, axis=1, keepdims=True)
+    return joined[:, count:] / jnp.sqrt(pivots), jnp.min(pivots / diagonal)
+
+
+def exact_dot(left, right):
+    return jnp.dot(left, right, precision=lax.Precision.HIGHEST, preferred_element_type=jnp.float32)
 
 
 def image_of(root_ref, part_refs):
@@ -308,20 +359,32 @@
     return root_ref[...] * ((first + second) + (third + fourth))
 
 
-def image_kernel(root_ref, *refs):
+def image_kernel(scaled, root_ref, *refs):
     image = image_of(root_ref, refs[:4])
-    refs[4][...] = root_ref[...] * image
+    refs[4][...] = root_ref[...] * image if scaled else image
     refs[5][...] = gram_of(image)
 
 
-def solve_gram_kernel(gram_ref, root_ref, *refs):
-    image = solved(gram_ref[...], image_of(root_ref, refs[:4]))
-    refs[4][...] = image
-    refs[5][...] = gram_of(image)
+def solve_gram_kernel(gram_ref, image_ref, solved_ref, next_ref):
+    image = exact_dot(inverse_factor(gram_ref[...])[0], image_ref[...])
+    solved_ref[...] = image
+    next_ref[...] = gram_of(image)
 
 
 def solve_kernel(gram_ref, image_ref, solved_ref):
-    solved_ref[...] = solved(gram_ref[...], image_ref[...])
+    solved_ref[...] = exact_dot(inverse_factor(gram_ref[...])[0], image_ref[...])
+
+
+def solve_both_kernel(grams_ref, image_ref, solved_ref, sound_ref):
+    count = image_ref.shape[0]
+    first, quality = inverse_factor(grams_ref[:count])
+    half = lax.dot_general(
+        grams_ref[count:], first, TRANS_B, precision=lax.Precision.HIGHEST,
+        preferred_element_type=jnp.float32,
+    )
+    second, next_quality = inverse_factor(exact_dot(first, half))
+    solved_ref[...] = exact_dot(second, exact_dot(first, image_ref[...]))
+    sound_ref[0] = jnp.where((quality > 0.05) & (next_quality > 0.001), 1, 0)
 
 
 def on_device(trajectories, kernel_scale, start_vectors, pair_list):
@@ -355,7 +418,7 @@
     for h, source in ((1, later), (-1, later), (3, near[2]), (-3, near[-2])):
         near[h] = shifted(source, "space", 1 if h > 0 else -1)
     blocks, rate = row_operands(members)
-    listed = jnp.stack([member[MASK_ROW, : REACH * PAIRS] for member in members]).astype(jnp.float32)
+    listed = jnp.stack([member[MASK_ROW, : REACH * PAIRS] for member in members]).astype(jnp.int32)
 
     order = (2, 1, 3)
     tiles = []
@@ -363,9 +426,8 @@
     for at, h in enumerate(order):
         span = slice((h - 1) * PAIRS, h * PAIRS)
         mine = listed[:, span].reshape(N_SUB * PAIRS)
-        theirs = near[-h][MASK_ROW, span].astype(jnp.float32)
         *tile, carried = hop_tiles(
-            at == 0, at == REACH - 1, mine, theirs, blocks, rate, near[h], near[-h], carried
+            h, at == 0, at == REACH - 1, mine, blocks, rate, near[h], near[-h], carried
         )
         tiles.append(tile)
     degree = carried
@@ -379,21 +441,31 @@
         compiler_params=pltpu.CompilerParams(vmem_limit_bytes=SMALL_LIMIT),
     )
 
+    def imaged(parts, scaled):
+        return pl.pallas_call(
+            functools.partial(image_kernel, scaled), out_shape=[vector_shape, gram_shape], **light
+        )(root, *exchanged(parts))
+
     scaled = (root * start_vectors).astype(jnp.bfloat16)
-    shares = exchanged(sweep(scaled, space_window(scaled), order, tiles))
-    raw, gram = pl.pallas_call(
-        image_kernel, out_shape=[vector_shape, gram_shape], **light
-    )(root, *shares)
-
-    near_raw = space_window(raw)
-    gram = summed(gram)
-    shares = exchanged(sweep(raw, near_raw, order, tiles))
-    image, gram = pl.pallas_call(
-        solve_gram_kernel, out_shape=[vector_shape, gram_shape], **light
-    )(gram, root, *shares)
-    return pl.pallas_call(solve_kernel, out_shape=vector_shape, **light)(
-        summed(gram), image
-    )
+    raw, first_gram = imaged(sweep(scaled, space_window(scaled), order, tiles), True)
+
+    image, second_gram = imaged(sweep(raw, space_window(raw), order, tiles), False)
+    grams = summed(jnp.concatenate([first_gram, second_gram], 0))
+    subspace, sound = pl.pallas_call(
+        solve_both_kernel,
+        in_specs=[pl.BlockSpec(memory_space=pltpu.VMEM)] * 2,
+        out_specs=[pl.BlockSpec(memory_space=pltpu.VMEM), pl.BlockSpec(memory_space=pltpu.SMEM)],
+        out_shape=[vector_shape, jax.ShapeDtypeStruct((1,), jnp.int32)],
+        **light,
+    )(grams, image)
+
+    def directly():
+        solved, gram = pl.pallas_call(
+            solve_gram_kernel, out_shape=[vector_shape, gram_shape], **light
+        )(grams[:vecs], image)
+        return pl.pallas_call(solve_kernel, out_shape=vector_shape, **light)(summed(gram), solved)
+
+    return lax.cond(sound[0] > 0, lambda: subspace, directly)
 
 
 def solution(mesh):

time: 176 us -> 146 us (0.83)
  local copies, waits for them, and re-layouts: 16 us -> 1.92 us
  blocking collectives: 45.7 us -> 33.3 us
  starting transfers between devices: 67.5 us -> 61.4 us
  waiting for transfers between devices: 15.2 us -> 17.8 us
  Pallas kernels: 26.6 us -> 28.5 us
    unnamed x20 -> x4, local copies, waits for them, and re-layouts: 13.9 us -> 0.63 us
    all_to_all x3 -> x2, blocking collectives: 45.7 us -> 33.3 us  [summed(): lax.all_to_all(sent, ('space', 'sub'), 0, 0, axis_index_groups=groups)]
    all_to_all x1 -> x0, starting transfers between devices: 5.67 us -> none  [summed(): lax.all_to_all(sent, ('space', 'sub'), 0, 0, axis_index_groups=groups)]
    ppermute x30, waiting for transfers between devices: 15.2 us -> 17.8 us  [shifted(): lax.ppermute(value, axis, [((at + steps) % count, at) for at in range(cou...]
    pallas_call x2, Pallas kernels: 4.94 us -> 7.09 us  [sweep(): pl.pallas_call(functools.partial(sweep_kernel, parts, order), in_specs=[s...]
  transfers between devices with their start and end apart: 31 -> 30, of which waited for: 11 -> 14; matrix products, arithmetic and copies ran while one was open for 2% -> 0% of each run, Pallas kernels for 7% -> 7%
where the time goes in v1:
time: 146 us
  starting transfers between devices  61.4 us (42%)
  blocking collectives  33.3 us (23%)
  Pallas kernels  28.5 us (20%)
  waiting for transfers between devices  17.8 us (12%)
  other arithmetic  2.07 us (1%)
  local copies, waits for them, and re-layouts  1.92 us (1%)
    ppermute x30, starting transfers between devices, shifted(): lax.ppermute(value, axis, [((at + steps) % count, at) for at in range(cou...  61.4 us
    all_to_all x2, blocking collectives, summed(): lax.all_to_all(sent, ('space', 'sub'), 0, 0, axis_index_groups=groups)  33.3 us
    ppermute x30, waiting for transfers between devices, shifted(): lax.ppermute(value, axis, [((at + steps) % count, at) for at in range(cou...  17.8 us
    pallas_call x3, Pallas kernels, hop_tiles(): pl.pallas_call(functools.partial(tile_kernel, hop, first, last), in_specs...  14.2 us
    pallas_call x2, Pallas kernels, sweep(): pl.pallas_call(functools.partial(sweep_kernel, parts, order), in_specs=[s...  7.09 us
    pallas_call x1, Pallas kernels, on_device(): pl.pallas_call(solve_both_kernel, in_specs=[pl.BlockSpec(memory_space=plt...  6.54 us
  transfers between devices with their start and end apart: 30, of which 14 were waited for; matrix products, arithmetic and copies ran while one was open for 0% of the time, Pallas kernels for 7%

profile of v1, /device:TPU:1, one launch (start us, length us, event | category | flops | bytes accessed | tf_op | source)
XLA Modules:
  0.0 145.9 jit_solution(5514583391980603631)
XLA Ops:
  0.0 0.8 fusion.8
  0.9 0.7 broadcast_in_dim.18
  1.7 1.1 maximum_maximum_fusion.refs_0_.extra_ref
  2.8 2.1 %collective-permute-start.4 = (bf16[304,512]{1,0:T(8,128)(2,1)S(1)}, bf16[304,512]{1,0:T(8,128)(2,1)S(1)}, u32[]{:S(2)}, u32[]{:S(2)}) collective-permute-start(bf16[304,512]{1,0:T(8,128)(2,1)S(1)} %maximum_maximum_fusion.refs_0_.extra_ref), channel_id=1, source_target_pairs={{248,0},{252,4},{0,8},{4,12},{8,16},{12,20},{16,24},{20,28},{24,32... | collective-permute-start | bytes 933896 | tf_op jit(solution)/shard_map/ppermute | solution.py:35
  4.9 6.6 %collective-permute-start.3 = (bf16[304,512]{1,0:T(8,128)(2,1)S(1)}, bf16[304,512]{1,0:T(8,128)(2,1)S(1)}, u32[]{:S(2)}, u32[]{:S(2)}) collective-permute-start(bf16[304,512]{1,0:T(8,128)(2,1)S(1)} %maximum_maximum_fusion.refs_0_.extra_ref), channel_id=1, source_target_pairs={{8,0},{12,4},{16,8},{20,12},{24,16},{28,20},{32,24},{36,28},{40,32... | collective-permute-start | bytes 933896 | tf_op jit(solution)/shard_map/ppermute | solution.py:35
  11.5 1.3 collective-permute-start.2
  12.8 2.6 %collective-permute-start.1 = (bf16[304,512]{1,0:T(8,128)(2,1)S(1)}, bf16[304,512]{1,0:T(8,128)(2,1)S(1)}, u32[]{:S(2)}, u32[]{:S(2)}) collective-permute-start(bf16[304,512]{1,0:T(8,128)(2,1)S(1)} %maximum_maximum_fusion.refs_0_.extra_ref), channel_id=1, source_target_pairs={{2,0},{3,1},{0,2},{1,3},{6,4},{7,5},{4,6},{5,7},{10,8},{11,9},{8,1... | collective-permute-start | bytes 933896 | tf_op jit(solution)/shard_map/ppermute | solution.py:35
  15.5 1.1 collective-permute-start
  16.5 2.0 %collective-permute-done.4.behind_ref = bf16[304,512]{1,0:T(8,128)(2,1)S(1)} collective-permute-done((bf16[304,512]{1,0:T(8,128)(2,1)S(1)}, bf16[304,512]{1,0:T(8,128)(2,1)S(1)}, u32[]{:S(2)}, u32[]{:S(2)}) %collective-permute-start.4) | collective-permute-done | bytes 311328 | tf_op jit(solution)/shard_map/ppermute | solution.py:35
  18.5 1.2 collective-permute-start.7
  19.8 1.0 collective-permute-done.2.refs_3_
  20.8 4.1 %collective-permute-start.5 = (bf16[304,512]{1,0:T(8,128)(2,1)S(1)}, bf16[304,512]{1,0:T(8,128)(2,1)S(1)}, u32[]{:S(2)}, u32[]{:S(2)}) collective-permute-start(bf16[304,512]{1,0:T(8,128)(2,1)S(1)} %collective-permute-done.3.ahead_ref), channel_id=1, source_target_pairs={{4,0},{8,4},{12,8},{16,12},{20,16},{24,20},{28,24},{32,28},{36,32}... | collective-permute-start | bytes 933896 | tf_op jit(solution)/shard_map/ppermute | solution.py:35
  24.8 3.7 %collective-permute-done.1.refs_2_ = bf16[304,512]{1,0:T(8,128)(2,1)S(1)} collective-permute-done((bf16[304,512]{1,0:T(8,128)(2,1)S(1)}, bf16[304,512]{1,0:T(8,128)(2,1)S(1)}, u32[]{:S(2)}, u32[]{:S(2)}) %collective-permute-start.1) | collective-permute-done | bytes 311328 | tf_op jit(solution)/shard_map/ppermute | solution.py:35
  28.9 0.3 shard_map.48
  29.3 5.2 %shard_map.49 = (bf16[40,256,256]{2,1,0:T(8,128)(2,1)S(1)}, s32[48]{0:T(128)S(1)}, s32[48]{0:T(128)S(1)}, f32[9,8,256]{2,1,0:T(8,128)S(1)}) custom-call(s32[64]{0:T(128)S(1)} %reshape.35.mine_ref, bf16[8,320,256]{2,1,0:T(8,128)(2,1)S(1)} %get-tuple-element.48.blocks_ref, f32[8,8,256]{2,1,0:T(8,128)S(1)} %get-tuple-element.49.rate_ref, ...), custom_call_target="tpu_custom_call" | custom-call | flops 671088640 | bytes 7340032 | tf_op jit(solution)/shard_map/pallas_call | solution.py:221
  34.5 4.3 %shard_map.50 = (bf16[32,256,256]{2,1,0:T(8,128)(2,1)S(1)}, s32[48]{0:T(128)S(1)}, s32[48]{0:T(128)S(1)}, f32[9,8,256]{2,1,0:T(8,128)S(1)}) custom-call(s32[64]{0:T(128)S(1)} %reshape.34.mine_ref, bf16[8,320,256]{2,1,0:T(8,128)(2,1)S(1)} %get-tuple-element.48.blocks_ref, f32[8,8,256]{2,1,0:T(8,128)S(1)} %get-tuple-element.49.rate_ref, ...), custom_call_target="tpu_custom_call" | custom-call | flops 671088640 | bytes 7340032 | tf_op jit(solution)/shard_map/pallas_call | solution.py:221
  38.9 4.6 %shard_map.51 = (bf16[32,256,256]{2,1,0:T(8,128)(2,1)S(1)}, s32[48]{0:T(128)S(1)}, s32[48]{0:T(128)S(1)}, f32[4,8,512]{2,1,0:T(8,128)S(1)}) custom-call(s32[64]{0:T(128)S(1)} %reshape.33.mine_ref, bf16[8,320,256]{2,1,0:T(8,128)(2,1)S(1)} %get-tuple-element.48.blocks_ref, f32[8,8,256]{2,1,0:T(8,128)S(1)} %get-tuple-element.49.rate_ref, ...), custom_call_target="tpu_custom_call" | custom-call | flops 671088640 | bytes 7340032 | tf_op jit(solution)/shard_map/pallas_call | solution.py:221
  43.5 3.6 %collective-permute-start.11 = (f32[1,512]{1,0:T(1,128)S(1)}, f32[1,512]{1,0:T(1,128)S(1)}, u32[]{:S(2)}, u32[]{:S(2)}) collective-permute-start(f32[1,512]{1,0:T(1,128)S(1)} %get-tuple-element.80), channel_id=1, source_target_pairs={{1,0},{2,1},{3,2},{0,3},{5,4},{6,5},{7,6},{4,7},{9,8},{10,9},{11,1... | collective-permute-start | bytes 6152 | tf_op jit(solution)/shard_map/ppermute | solution.py:35
  47.1 0.7 collective-permute-start.9
  47.9 3.2 %collective-permute-done.10 = f32[1,512]{1,0:T(1,128)S(1)} collective-permute-done((f32[1,512]{1,0:T(1,128)S(1)}, f32[1,512]{1,0:T(1,128)S(1)}, u32[]{:S(2)}, u32[]{:S(2)}) %collective-permute-start.10) | collective-permute-done | bytes 2080 | tf_op jit(solution)/shard_map/ppermute | solution.py:35
  51.2 5.1 %collective-permute-start.16 = (bf16[32,512]{1,0:T(8,128)(2,1)S(1)}, bf16[32,512]{1,0:T(8,128)(2,1)S(1)}, u32[]{:S(2)}, u32[]{:S(2)}) collective-permute-start(bf16[32,512]{1,0:T(8,128)(2,1)S(1)} %multiply_convert_fusion.refs_9_), channel_id=1, source_target_pairs={{12,0},{16,4},{20,8},{24,12},{28,16},{32,20},{36,24},{40,28},{44,3... | collective-permute-start | bytes 98312 | tf_op jit(solution)/shard_map/ppermute | solution.py:35
  56.3 4.8 %collective-permute-start.14 = (bf16[32,512]{1,0:T(8,128)(2,1)S(1)}, bf16[32,512]{1,0:T(8,128)(2,1)S(1)}, u32[]{:S(2)}, u32[]{:S(2)}) collective-permute-start(bf16[32,512]{1,0:T(8,128)(2,1)S(1)} %multiply_convert_fusion.refs_9_), channel_id=1, source_target_pairs={{8,0},{12,4},{16,8},{20,12},{24,16},{28,20},{32,24},{36,28},{40,32... | collective-permute-start | bytes 98312 | tf_op jit(solution)/shard_map/ppermute | solution.py:35
  61.0 0.3 collective-permute-start.13
  61.3 3.7 %collective-permute-start.12 = (bf16[32,512]{1,0:T(8,128)(2,1)S(1)}, bf16[32,512]{1,0:T(8,128)(2,1)S(1)}, u32[]{:S(2)}, u32[]{:S(2)}) collective-permute-start(bf16[32,512]{1,0:T(8,128)(2,1)S(1)} %multiply_convert_fusion.refs_9_), channel_id=1, source_target_pairs={{4,0},{8,4},{12,8},{16,12},{20,16},{24,20},{28,24},{32,28},{36,32}... | collective-permute-start | bytes 98312 | tf_op jit(solution)/shard_map/ppermute | solution.py:35
  65.0 0.7 collective-permute-done.13.refs_11_
  65.9 3.4 %shard_map.52 = (f32[32,512]{1,0:T(8,128)S(1)}, f32[32,512]{1,0:T(8,128)S(1)}, f32[32,512]{1,0:T(8,128)S(1)}, f32[32,512]{1,0:T(8,128)S(1)}) custom-call(s32[48]{0:T(128)S(1)} %get-tuple-element.56.refs_0_, s32[48]{0:T(128)S(1)} %get-tuple-element.57.refs_1_, s32[48]{0:T(128)S(1)} %get-tuple-element.58.refs_2_, s32[48]{0:T(128)S(1)} %get-tuple-element.59.refs_3_, ...), custom_call_target="tpu_custom_call" | custom-call | flops 838860800 | bytes 7340032 | tf_op jit(solution)/shard_map/pallas_call | solution.py:311
  69.3 1.0 collective-permute-start.19
  70.3 1.6 %collective-permute-start.20 = (f32[32,512]{1,0:T(8,128)S(1)}, f32[32,512]{1,0:T(8,128)S(1)}, u32[]{:S(2)}, u32[]{:S(2)}) collective-permute-start(f32[32,512]{1,0:T(8,128)S(1)} %get-tuple-element.68), channel_id=1, source_target_pairs={{1,0},{2,1},{3,2},{0,3},{5,4},{6,5},{7,6},{4,7},{9,8},{10,9},{11,1... | collective-permute-start | bytes 196616 | tf_op jit(solution)/shard_map/ppermute | solution.py:35
  72.0 2.3 %collective-permute-done.18.refs_1_ = f32[32,512]{1,0:T(8,128)S(1)} collective-permute-done((f32[32,512]{1,0:T(8,128)S(1)}, f32[32,512]{1,0:T(8,128)S(1)}, u32[]{:S(2)}, u32[]{:S(2)}) %collective-permute-start.18) | collective-permute-done | bytes 65568 | tf_op jit(solution)/shard_map/ppermute | solution.py:35
  74.3 0.6 collective-permute-done.20.refs_3_
  74.9 0.2 shard_map.53
  75.2 7.5 %collective-permute-start.25 = (f32[32,512]{1,0:T(8,128)S(1)}, f32[32,512]{1,0:T(8,128)S(1)}, u32[]{:S(2)}, u32[]{:S(2)}) collective-permute-start(f32[32,512]{1,0:T(8,128)S(1)} %get-tuple-element.70.refs_9_), channel_id=1, source_target_pairs={{12,0},{16,4},{20,8},{24,12},{28,16},{32,20},{36,24},{40,28},{44,3... | collective-permute-start | bytes 196616 | tf_op jit(solution)/shard_map/ppermute | solution.py:35
  82.7 0.8 collective-permute-start.24
  83.5 4.3 %collective-permute-start.23 = (f32[32,512]{1,0:T(8,128)S(1)}, f32[32,512]{1,0:T(8,128)S(1)}, u32[]{:S(2)}, u32[]{:S(2)}) collective-permute-start(f32[32,512]{1,0:T(8,128)S(1)} %get-tuple-element.70.refs_9_), channel_id=1, source_target_pairs={{8,0},{12,4},{16,8},{20,12},{24,16},{28,20},{32,24},{36,28},{40,32... | collective-permute-start | bytes 196616 | tf_op jit(solution)/shard_map/ppermute | solution.py:35
  87.8 1.3 collective-permute-start.22
  89.0 3.7 %collective-permute-start.21 = (f32[32,512]{1,0:T(8,128)S(1)}, f32[32,512]{1,0:T(8,128)S(1)}, u32[]{:S(2)}, u32[]{:S(2)}) collective-permute-start(f32[32,512]{1,0:T(8,128)S(1)} %get-tuple-element.70.refs_9_), channel_id=1, source_target_pairs={{4,0},{8,4},{12,8},{16,12},{20,16},{24,20},{28,24},{32,28},{36,32}... | collective-permute-start | bytes 196616 | tf_op jit(solution)/shard_map/ppermute | solution.py:35
  92.8 0.7 collective-permute-done.22.refs_11_
  93.7 3.7 %shard_map.54 = (f32[32,512]{1,0:T(8,128)S(1)}, f32[32,512]{1,0:T(8,128)S(1)}, f32[32,512]{1,0:T(8,128)S(1)}, f32[32,512]{1,0:T(8,128)S(1)}) custom-call(s32[48]{0:T(128)S(1)} %get-tuple-element.56.refs_0_, s32[48]{0:T(128)S(1)} %get-tuple-element.57.refs_1_, s32[48]{0:T(128)S(1)} %get-tuple-element.58.refs_2_, s32[48]{0:T(128)S(1)} %get-tuple-element.59.refs_3_, ...), custom_call_target="tpu_custom_call" | custom-call | flops 838860800 | bytes 7340032 | tf_op jit(solution)/shard_map/pallas_call | solution.py:311
  97.4 0.7 collective-permute-start.27
  98.1 3.1 %collective-permute-start.28 = (f32[32,512]{1,0:T(8,128)S(1)}, f32[32,512]{1,0:T(8,128)S(1)}, u32[]{:S(2)}, u32[]{:S(2)}) collective-permute-start(f32[32,512]{1,0:T(8,128)S(1)} %get-tuple-element.73), channel_id=1, source_target_pairs={{2,0},{3,1},{0,2},{1,3},{6,4},{7,5},{4,6},{5,7},{10,8},{11,9},{8,1... | collective-permute-start | bytes 196616 | tf_op jit(solution)/shard_map/ppermute | solution.py:35
  101.2 0.6 collective-permute-done.27.refs_1_
  101.8 1.8 %collective-permute-done.28.refs_2_ = f32[32,512]{1,0:T(8,128)S(1)} collective-permute-done((f32[32,512]{1,0:T(8,128)S(1)}, f32[32,512]{1,0:T(8,128)S(1)}, u32[]{:S(2)}, u32[]{:S(2)}) %collective-permute-start.28) | collective-permute-done | bytes 65568 | tf_op jit(solution)/shard_map/ppermute | solution.py:35
  103.6 0.8 collective-permute-done.29.refs_3_
  104.3 0.2 shard_map.55
  104.6 16.4 %all_to_all.20 = f32[16,16,128]{2,1,0:T(8,128)S(1)} all-to-all(f32[16,16,128]{2,1,0:T(8,128)S(1)} %broadcast_in_dim.40), channel_id=1, replica_groups={{0,1,2,3,4,5,6,7,8,9,10,11,12,13,14,15},{16,17,18,19,20,21,22,23,24,25,..., dimensions={0} | all-to-all | bytes 262144 | tf_op jit(solution)/shard_map/all_to_all | solution.py:57
  121.1 16.8 %all_to_all.21 = f32[16,16,128]{2,1,0:T(8,128)S(1)} all-to-all(f32[16,16,128]{2,1,0:T(8,128)S(1)} %broadcast_in_dim.41), channel_id=1, replica_groups={{0,16,32,48,64,80,96,112,128,144,160,176,192,208,224,240},{1,17,33,49,6..., dimensions={0} | all-to-all | bytes 262144 | tf_op jit(solution)/shard_map/all_to_all | solution.py:57
  138.0 6.5 %shard_map.56 = (f32[32,512]{1,0:T(8,128)S(1)}, s32[1]{0:T(128)}) custom-call(f32[64,32]{1,0:T(8,128)S(1)} %reshape.36.grams_ref, f32[32,512]{1,0:T(8,128)S(1)} %get-tuple-element.76.image_ref), custom_call_target="tpu_custom_call" | custom-call | flops 1048576 | bytes 131072 | tf_op jit(solution)/shard_map/pallas_call | solution.py:454
  145.3 0.6 copy-done.1
  (55 shorter events, 1.5 us)
Async XLA Ops:
  2.8 15.8 %collective-permute-start.4 = (bf16[304,512]{1,0:T(8,128)(2,1)S(1)}, bf16[304,512]{1,0:T(8,128)(2,1)S(1)}, u32[]{:S(2)}, u32[]{:S(2)}) collective-permute-start(bf16[304,512]{1,0:T(8,128)(2,1)S(1)} %maximum_maximum_fusion.refs_0_.extra_ref), channel_id=1, source_target_pairs={{248,0},{252,4},{0,8},{4,12},{8,16},{12,20},{16,24},{20,28},{24,32... | collective-permute-start | bytes 933896 | tf_op jit(solution)/shard_map/ppermute | solution.py:35
  4.9 13.6 %collective-permute-start.3 = (bf16[304,512]{1,0:T(8,128)(2,1)S(1)}, bf16[304,512]{1,0:T(8,128)(2,1)S(1)}, u32[]{:S(2)}, u32[]{:S(2)}) collective-permute-start(bf16[304,512]{1,0:T(8,128)(2,1)S(1)} %maximum_maximum_fusion.refs_0_.extra_ref), channel_id=1, source_target_pairs={{8,0},{12,4},{16,8},{20,12},{24,16},{28,20},{32,24},{36,28},{40,32... | collective-permute-start | bytes 933896 | tf_op jit(solution)/shard_map/ppermute | solution.py:35
  11.5 9.2 %collective-permute-start.2 = (bf16[304,512]{1,0:T(8,128)(2,1)S(1)}, bf16[304,512]{1,0:T(8,128)(2,1)S(1)}, u32[]{:S(2)}, u32[]{:S(2)}) collective-permute-start(bf16[304,512]{1,0:T(8,128)(2,1)S(1)} %maximum_maximum_fusion.refs_0_.extra_ref), channel_id=1, source_target_pairs={{3,0},{0,1},{1,2},{2,3},{7,4},{4,5},{5,6},{6,7},{11,8},{8,9},{9,10... | collective-permute-start | bytes 933896 | tf_op jit(solution)/shard_map/ppermute | solution.py:35
  12.8 15.7 %collective-permute-start.1 = (bf16[304,512]{1,0:T(8,128)(2,1)S(1)}, bf16[304,512]{1,0:T(8,128)(2,1)S(1)}, u32[]{:S(2)}, u32[]{:S(2)}) collective-permute-start(bf16[304,512]{1,0:T(8,128)(2,1)S(1)} %maximum_maximum_fusion.refs_0_.extra_ref), channel_id=1, source_target_pairs={{2,0},{3,1},{0,2},{1,3},{6,4},{7,5},{4,6},{5,7},{10,8},{11,9},{8,1... | collective-permute-start | bytes 933896 | tf_op jit(solution)/shard_map/ppermute | solution.py:35
  15.5 13.1 %collective-permute-start = (bf16[304,512]{1,0:T(8,128)(2,1)S(1)}, bf16[304,512]{1,0:T(8,128)(2,1)S(1)}, u32[]{:S(2)}, u32[]{:S(2)}) collective-permute-start(bf16[304,512]{1,0:T(8,128)(2,1)S(1)} %maximum_maximum_fusion.refs_0_.extra_ref), channel_id=1, source_target_pairs={{1,0},{2,1},{3,2},{0,3},{5,4},{6,5},{7,6},{4,7},{9,8},{10,9},{11,1... | collective-permute-start | bytes 933896 | tf_op jit(solution)/shard_map/ppermute | solution.py:35
  18.5 15.9 %collective-permute-start.8 = (bf16[304,512]{1,0:T(8,128)(2,1)S(1)}, bf16[304,512]{1,0:T(8,128)(2,1)S(1)}, u32[]{:S(2)}, u32[]{:S(2)}) collective-permute-start(bf16[304,512]{1,0:T(8,128)(2,1)S(1)} %maximum_maximum_fusion.refs_0_.extra_ref), channel_id=1, source_target_pairs={{252,0},{0,4},{4,8},{8,12},{12,16},{16,20},{20,24},{24,28},{28,32}... | collective-permute-start | bytes 933896 | tf_op jit(solution)/shard_map/ppermute | solution.py:35
  18.5 16.0 %collective-permute-start.7 = (bf16[304,512]{1,0:T(8,128)(2,1)S(1)}, bf16[304,512]{1,0:T(8,128)(2,1)S(1)}, u32[]{:S(2)}, u32[]{:S(2)}) collective-permute-start(bf16[304,512]{1,0:T(8,128)(2,1)S(1)} %maximum_maximum_fusion.refs_0_.extra_ref), channel_id=1, source_target_pairs={{4,0},{8,4},{12,8},{16,12},{20,16},{24,20},{28,24},{32,28},{36,32}... | collective-permute-start | bytes 933896 | tf_op jit(solution)/shard_map/ppermute | solution.py:35
  20.8 18.1 %collective-permute-start.5 = (bf16[304,512]{1,0:T(8,128)(2,1)S(1)}, bf16[304,512]{1,0:T(8,128)(2,1)S(1)}, u32[]{:S(2)}, u32[]{:S(2)}) collective-permute-start(bf16[304,512]{1,0:T(8,128)(2,1)S(1)} %collective-permute-done.3.ahead_ref), channel_id=1, source_target_pairs={{4,0},{8,4},{12,8},{16,12},{20,16},{24,20},{28,24},{32,28},{36,32}... | collective-permute-start | bytes 933896 | tf_op jit(solution)/shard_map/ppermute | solution.py:35
  28.6 10.3 %collective-permute-start.6 = (bf16[304,512]{1,0:T(8,128)(2,1)S(1)}, bf16[304,512]{1,0:T(8,128)(2,1)S(1)}, u32[]{:S(2)}, u32[]{:S(2)}) collective-permute-start(bf16[304,512]{1,0:T(8,128)(2,1)S(1)} %collective-permute-done.4.behind_ref), channel_id=1, source_target_pairs={{252,0},{0,4},{4,8},{8,12},{12,16},{16,20},{20,24},{24,28},{28,32}... | collective-permute-start | bytes 933896 | tf_op jit(solution)/shard_map/ppermute | solution.py:35
  28.9 22.1 %copy-start = (f32[32,512]{1,0:T(8,128)S(1)}, f32[32,512]{1,0:T(8,128)}, u32[]{:S(2)}) copy-start(f32[32,512]{1,0:T(8,128)} %param.8) | copy-start | bytes 196612
  43.5 4.3 %collective-permute-start.11 = (f32[1,512]{1,0:T(1,128)S(1)}, f32[1,512]{1,0:T(1,128)S(1)}, u32[]{:S(2)}, u32[]{:S(2)}) collective-permute-start(f32[1,512]{1,0:T(1,128)S(1)} %get-tuple-element.80), channel_id=1, source_target_pairs={{1,0},{2,1},{3,2},{0,3},{5,4},{6,5},{7,6},{4,7},{9,8},{10,9},{11,1... | collective-permute-start | bytes 6152 | tf_op jit(solution)/shard_map/ppermute | solution.py:35
  47.1 3.9 %collective-permute-start.10 = (f32[1,512]{1,0:T(1,128)S(1)}, f32[1,512]{1,0:T(1,128)S(1)}, u32[]{:S(2)}, u32[]{:S(2)}) collective-permute-start(f32[1,512]{1,0:T(1,128)S(1)} %get-tuple-element.81), channel_id=1, source_target_pairs={{2,0},{3,1},{0,2},{1,3},{6,4},{7,5},{4,6},{5,7},{10,8},{11,9},{8,1... | collective-permute-start | bytes 6152 | tf_op jit(solution)/shard_map/ppermute | solution.py:35
  47.1 3.9 %collective-permute-start.9 = (f32[1,512]{1,0:T(1,128)S(1)}, f32[1,512]{1,0:T(1,128)S(1)}, u32[]{:S(2)}, u32[]{:S(2)}) collective-permute-start(f32[1,512]{1,0:T(1,128)S(1)} %get-tuple-element.82), channel_id=1, source_target_pairs={{3,0},{0,1},{1,2},{2,3},{7,4},{4,5},{5,6},{6,7},{11,8},{8,9},{9,10... | collective-permute-start | bytes 6152 | tf_op jit(solution)/shard_map/ppermute | solution.py:35
  51.1 10.2 %collective-permute-start.17 = (bf16[32,512]{1,0:T(8,128)(2,1)S(1)}, bf16[32,512]{1,0:T(8,128)(2,1)S(1)}, u32[]{:S(2)}, u32[]{:S(2)}) collective-permute-start(bf16[32,512]{1,0:T(8,128)(2,1)S(1)} %multiply_convert_fusion.refs_9_), channel_id=1, source_target_pairs={{244,0},{248,4},{252,8},{0,12},{4,16},{8,20},{12,24},{16,28},{20,3... | collective-permute-start | bytes 98312 | tf_op jit(solution)/shard_map/ppermute | solution.py:35
  51.2 13.8 %collective-permute-start.16 = (bf16[32,512]{1,0:T(8,128)(2,1)S(1)}, bf16[32,512]{1,0:T(8,128)(2,1)S(1)}, u32[]{:S(2)}, u32[]{:S(2)}) collective-permute-start(bf16[32,512]{1,0:T(8,128)(2,1)S(1)} %multiply_convert_fusion.refs_9_), channel_id=1, source_target_pairs={{12,0},{16,4},{20,8},{24,12},{28,16},{32,20},{36,24},{40,28},{44,3... | collective-permute-start | bytes 98312 | tf_op jit(solution)/shard_map/ppermute | solution.py:35
  56.3 8.8 %collective-permute-start.15 = (bf16[32,512]{1,0:T(8,128)(2,1)S(1)}, bf16[32,512]{1,0:T(8,128)(2,1)S(1)}, u32[]{:S(2)}, u32[]{:S(2)}) collective-permute-start(bf16[32,512]{1,0:T(8,128)(2,1)S(1)} %multiply_convert_fusion.refs_9_), channel_id=1, source_target_pairs={{248,0},{252,4},{0,8},{4,12},{8,16},{12,20},{16,24},{20,28},{24,32... | collective-permute-start | bytes 98312 | tf_op jit(solution)/shard_map/ppermute | solution.py:35
  56.3 8.8 %collective-permute-start.14 = (bf16[32,512]{1,0:T(8,128)(2,1)S(1)}, bf16[32,512]{1,0:T(8,128)(2,1)S(1)}, u32[]{:S(2)}, u32[]{:S(2)}) collective-permute-start(bf16[32,512]{1,0:T(8,128)(2,1)S(1)} %multiply_convert_fusion.refs_9_), channel_id=1, source_target_pairs={{8,0},{12,4},{16,8},{20,12},{24,16},{28,20},{32,24},{36,28},{40,32... | collective-permute-start | bytes 98312 | tf_op jit(solution)/shard_map/ppermute | solution.py:35
  61.0 4.7 %collective-permute-start.13 = (bf16[32,512]{1,0:T(8,128)(2,1)S(1)}, bf16[32,512]{1,0:T(8,128)(2,1)S(1)}, u32[]{:S(2)}, u32[]{:S(2)}) collective-permute-start(bf16[32,512]{1,0:T(8,128)(2,1)S(1)} %multiply_convert_fusion.refs_9_), channel_id=1, source_target_pairs={{252,0},{0,4},{4,8},{8,12},{12,16},{16,20},{20,24},{24,28},{28,32}... | collective-permute-start | bytes 98312 | tf_op jit(solution)/shard_map/ppermute | solution.py:35
  61.3 4.6 %collective-permute-start.12 = (bf16[32,512]{1,0:T(8,128)(2,1)S(1)}, bf16[32,512]{1,0:T(8,128)(2,1)S(1)}, u32[]{:S(2)}, u32[]{:S(2)}) collective-permute-start(bf16[32,512]{1,0:T(8,128)(2,1)S(1)} %multiply_convert_fusion.refs_9_), channel_id=1, source_target_pairs={{4,0},{8,4},{12,8},{16,12},{20,16},{24,20},{28,24},{32,28},{36,32}... | collective-permute-start | bytes 98312 | tf_op jit(solution)/shard_map/ppermute | solution.py:35
  69.2 5.1 %collective-permute-start.18 = (f32[32,512]{1,0:T(8,128)S(1)}, f32[32,512]{1,0:T(8,128)S(1)}, u32[]{:S(2)}, u32[]{:S(2)}) collective-permute-start(f32[32,512]{1,0:T(8,128)S(1)} %get-tuple-element.66), channel_id=1, source_target_pairs={{3,0},{0,1},{1,2},{2,3},{7,4},{4,5},{5,6},{6,7},{11,8},{8,9},{9,10... | collective-permute-start | bytes 196616 | tf_op jit(solution)/shard_map/ppermute | solution.py:35
  69.3 5.0 %collective-permute-start.19 = (f32[32,512]{1,0:T(8,128)S(1)}, f32[32,512]{1,0:T(8,128)S(1)}, u32[]{:S(2)}, u32[]{:S(2)}) collective-permute-start(f32[32,512]{1,0:T(8,128)S(1)} %get-tuple-element.67), channel_id=1, source_target_pairs={{2,0},{3,1},{0,2},{1,3},{6,4},{7,5},{4,6},{5,7},{10,8},{11,9},{8,1... | collective-permute-start | bytes 196616 | tf_op jit(solution)/shard_map/ppermute | solution.py:35
  70.3 4.6 %collective-permute-start.20 = (f32[32,512]{1,0:T(8,128)S(1)}, f32[32,512]{1,0:T(8,128)S(1)}, u32[]{:S(2)}, u32[]{:S(2)}) collective-permute-start(f32[32,512]{1,0:T(8,128)S(1)} %get-tuple-element.68), channel_id=1, source_target_pairs={{1,0},{2,1},{3,2},{0,3},{5,4},{6,5},{7,6},{4,7},{9,8},{10,9},{11,1... | collective-permute-start | bytes 196616 | tf_op jit(solution)/shard_map/ppermute | solution.py:35
  75.1 13.9 %collective-permute-start.26 = (f32[32,512]{1,0:T(8,128)S(1)}, f32[32,512]{1,0:T(8,128)S(1)}, u32[]{:S(2)}, u32[]{:S(2)}) collective-permute-start(f32[32,512]{1,0:T(8,128)S(1)} %get-tuple-element.70.refs_9_), channel_id=1, source_target_pairs={{244,0},{248,4},{252,8},{0,12},{4,16},{8,20},{12,24},{16,28},{20,3... | collective-permute-start | bytes 196616 | tf_op jit(solution)/shard_map/ppermute | solution.py:35
  75.2 17.6 %collective-permute-start.25 = (f32[32,512]{1,0:T(8,128)S(1)}, f32[32,512]{1,0:T(8,128)S(1)}, u32[]{:S(2)}, u32[]{:S(2)}) collective-permute-start(f32[32,512]{1,0:T(8,128)S(1)} %get-tuple-element.70.refs_9_), channel_id=1, source_target_pairs={{12,0},{16,4},{20,8},{24,12},{28,16},{32,20},{36,24},{40,28},{44,3... | collective-permute-start | bytes 196616 | tf_op jit(solution)/shard_map/ppermute | solution.py:35
  82.7 10.1 %collective-permute-start.24 = (f32[32,512]{1,0:T(8,128)S(1)}, f32[32,512]{1,0:T(8,128)S(1)}, u32[]{:S(2)}, u32[]{:S(2)}) collective-permute-start(f32[32,512]{1,0:T(8,128)S(1)} %get-tuple-element.70.refs_9_), channel_id=1, source_target_pairs={{248,0},{252,4},{0,8},{4,12},{8,16},{12,20},{16,24},{20,28},{24,32... | collective-permute-start | bytes 196616 | tf_op jit(solution)/shard_map/ppermute | solution.py:35
  83.5 9.3 %collective-permute-start.23 = (f32[32,512]{1,0:T(8,128)S(1)}, f32[32,512]{1,0:T(8,128)S(1)}, u32[]{:S(2)}, u32[]{:S(2)}) collective-permute-start(f32[32,512]{1,0:T(8,128)S(1)} %get-tuple-element.70.refs_9_), channel_id=1, source_target_pairs={{8,0},{12,4},{16,8},{20,12},{24,16},{28,20},{32,24},{36,28},{40,32... | collective-permute-start | bytes 196616 | tf_op jit(solution)/shard_map/ppermute | solution.py:35
  87.8 5.7 %collective-permute-start.22 = (f32[32,512]{1,0:T(8,128)S(1)}, f32[32,512]{1,0:T(8,128)S(1)}, u32[]{:S(2)}, u32[]{:S(2)}) collective-permute-start(f32[32,512]{1,0:T(8,128)S(1)} %get-tuple-element.70.refs_9_), channel_id=1, source_target_pairs={{252,0},{0,4},{4,8},{8,12},{12,16},{16,20},{20,24},{24,28},{28,32}... | collective-permute-start | bytes 196616 | tf_op jit(solution)/shard_map/ppermute | solution.py:35
  89.0 4.6 %collective-permute-start.21 = (f32[32,512]{1,0:T(8,128)S(1)}, f32[32,512]{1,0:T(8,128)S(1)}, u32[]{:S(2)}, u32[]{:S(2)}) collective-permute-start(f32[32,512]{1,0:T(8,128)S(1)} %get-tuple-element.70.refs_9_), channel_id=1, source_target_pairs={{4,0},{8,4},{12,8},{16,12},{20,16},{24,20},{28,24},{32,28},{36,32}... | collective-permute-start | bytes 196616 | tf_op jit(solution)/shard_map/ppermute | solution.py:35
  97.4 4.4 %collective-permute-start.27 = (f32[32,512]{1,0:T(8,128)S(1)}, f32[32,512]{1,0:T(8,128)S(1)}, u32[]{:S(2)}, u32[]{:S(2)}) collective-permute-start(f32[32,512]{1,0:T(8,128)S(1)} %get-tuple-element.72), channel_id=1, source_target_pairs={{3,0},{0,1},{1,2},{2,3},{7,4},{4,5},{5,6},{6,7},{11,8},{8,9},{9,10... | collective-permute-start | bytes 196616 | tf_op jit(solution)/shard_map/ppermute | solution.py:35
  98.1 5.4 %collective-permute-start.28 = (f32[32,512]{1,0:T(8,128)S(1)}, f32[32,512]{1,0:T(8,128)S(1)}, u32[]{:S(2)}, u32[]{:S(2)}) collective-permute-start(f32[32,512]{1,0:T(8,128)S(1)} %get-tuple-element.73), channel_id=1, source_target_pairs={{2,0},{3,1},{0,2},{1,3},{6,4},{7,5},{4,6},{5,7},{10,8},{11,9},{8,1... | collective-permute-start | bytes 196616 | tf_op jit(solution)/shard_map/ppermute | solution.py:35
  101.2 3.1 %collective-permute-start.29 = (f32[32,512]{1,0:T(8,128)S(1)}, f32[32,512]{1,0:T(8,128)S(1)}, u32[]{:S(2)}, u32[]{:S(2)}) collective-permute-start(f32[32,512]{1,0:T(8,128)S(1)} %get-tuple-element.74), channel_id=1, source_target_pairs={{1,0},{2,1},{3,2},{0,3},{5,4},{6,5},{7,6},{4,7},{9,8},{10,9},{11,1... | collective-permute-start | bytes 196616 | tf_op jit(solution)/shard_map/ppermute | solution.py:35
  145.3 0.6 copy-start.1

commit v2 on v1

--- a/solution.py
+++ b/solution.py
@@ -36,7 +36,17 @@
 
 
 def space_window(value):
-    return {h: shifted(value, "space", h) for h in (1, 2, 3, -1, -2, -3)}
+    count = lax.axis_size("space")
+    other = lax.ppermute(value, "space", [(at, at ^ 1) for at in range(count)])
+    pair = jnp.stack([value, other])
+    far = [(at, (at + (4 if at % 2 == 0 else -4)) % count) for at in range(count)]
+    return value, other, shifted(pair, "space", 2), shifted(pair, "space", -2), lax.ppermute(other, "space", far)
+
+
+def window_slot(hop, side):
+    odd = lax.rem(lax.axis_index("space"), 2) == 1
+    even_slot, odd_slot = {(1, 0): (1, 3), (1, 1): (5, 1), (2, 0): (2, 2), (2, 1): (4, 4), (3, 0): (3, 6), (3, 1): (6, 5)}[hop, side]
+    return jnp.where(odd, odd_slot, even_slot)
 
 
 def groups_by(key, n_space, n_sub):
@@ -50,7 +60,7 @@
     n_space, n_sub = lax.axis_size("space"), lax.axis_size("sub")
     shape = value.shape
     value = value.reshape(-1, 128)
-    for key in (lambda s, y: (s // 4, 0), lambda s, y: (s % 4, y)):
+    for key in (lambda s, y: (s // 8, 0), lambda s, y: (s % 8, y)):
         groups = groups_by(key, n_space, n_sub)
         sent = jnp.broadcast_to(value[None], (len(groups[0]),) + value.shape)
         value = jnp.sum(
@@ -254,8 +264,8 @@
 
 
 def sweep_kernel(parts, order, *refs):
-    list_refs, tile_refs, vector_refs = refs[:6], refs[6:9], refs[9:16]
-    out_refs, (held, total, tiles, sems) = refs[16:20], refs[20:]
+    list_refs, tile_refs, vector_refs = refs[:6], refs[6:9], refs[9:14]
+    out_refs, (held, total, tiles, sems) = refs[14:18], refs[18:]
     vecs = vector_refs[0].shape[0]
 
     def copy(k, at):
@@ -272,20 +282,25 @@
 
         lax.fori_loop(0, groups[k], fetch, 0)
 
-    for k in range(7):
-        both = stacked(vector_refs[k][...])
+    own, other, ahead, behind, far = vector_refs
+    for k, vectors in enumerate(
+        (own[...], other[...], ahead[0], ahead[1], behind[0], behind[1], far[...])
+    ):
+        both = stacked(vectors)
         for c in range(2):
             held[2 * k + c] = both[:, c * BLOCK : (c + 1) * BLOCK]
     total[...] = jnp.zeros_like(total)
 
     for k, hop in enumerate(order):
-
-        def step(at, _, k=k, hop=hop, rows_ref=list_refs[2 * k], cols_ref=list_refs[2 * k + 1]):
+        slots = [window_slot(hop, side) for side in range(2)]
+
+        def step(at, _, k=k, slots=slots, rows_ref=list_refs[2 * k], cols_ref=list_refs[2 * k + 1]):
             copy(k, at).wait()
             terms = []
             for n in range(UNROLL):
                 block = cols_ref[UNROLL * at + n]
-                block = jnp.where(block >= 4, block - 4, block + 4 * hop - 2)
+                slot = jnp.where(block >= 4, 0, jnp.where(block >= 2, slots[1], slots[0]))
+                block = 2 * slot + (block & 1)
                 tile = tiles[(STARTS[k] + at) * UNROLL + n]
                 terms.append(jnp.dot(held[block], tile, preferred_element_type=jnp.float32))
             for n in range(UNROLL):
@@ -302,7 +317,8 @@
             out_refs[e][:, pl.ds(r * BLOCK, BLOCK)] = result
 
 
-def sweep(own, near, order, tiles):
+def sweep(near, order, tiles):
+    own = near[0]
     vecs = own.shape[0]
     smem = pl.BlockSpec(memory_space=pltpu.SMEM)
     vmem = pl.BlockSpec(memory_space=pltpu.VMEM)
@@ -310,7 +326,7 @@
     lists = [part for tile in tiles for part in tile[1:]]
     return pl.pallas_call(
         functools.partial(sweep_kernel, parts, order),
-        in_specs=[smem] * 6 + [pl.BlockSpec(memory_space=pl.ANY)] * 3 + [vmem] * 7,
+        in_specs=[smem] * 6 + [pl.BlockSpec(memory_space=pl.ANY)] * 3 + [vmem] * 5,
         out_specs=[vmem] * 4,
         out_shape=[jax.ShapeDtypeStruct((vecs, LENGTH), jnp.float32)] * 4,
         scratch_shapes=[
@@ -323,7 +339,7 @@
         cost_estimate=pl.CostEstimate(
             flops=50 * 2 * 128 * BLOCK * BLOCK, bytes_accessed=7 * 2**20, transcendentals=0
         ),
-    )(*lists, *[tile[0] for tile in tiles], own, *[near[h] for h in (1, -1, 2, -2, 3, -3)])
+    )(*lists, *[tile[0] for tile in tiles], *near)
 
 
 def exchanged(parts):
@@ -387,30 +403,43 @@
     sound_ref[0] = jnp.where((quality > 0.05) & (next_quality > 0.001), 1, 0)
 
 
+def payload_kernel(pairs_ref, data_ref, scale_ref, payload_ref):
+    n_space, n_sub = lax.axis_size("space"), lax.axis_size("sub")
+    space_at, sub_at = lax.axis_index("space"), lax.axis_index("sub")
+    lane = lax.broadcasted_iota(jnp.int32, (1, LENGTH), 1)
+    used = jnp.zeros((1, LENGTH), jnp.float32)
+    for k in range(pairs_ref.shape[0]):
+        row, col = pairs_ref[k, 0], pairs_ref[k, 1]
+        device = lax.shift_right_logical(col, 1)
+        hop = lax.rem(lax.div(device, n_sub) - space_at + n_space, n_space)
+        across = lax.rem(lax.rem(device, n_sub) - sub_at + n_sub, n_sub)
+        place = (((hop - 1) * n_sub + across) * 2 + (row & 1)) * 2 + (col & 1)
+        used = jnp.where((lane == place) & (hop > 0), 1.0, used)
+    payload_ref[: ROWS - 16] = data_ref[: ROWS - 16]
+    payload_ref[ROWS - 16 :] = jnp.concatenate(
+        [
+            data_ref[ROWS - 16 : FEAT].astype(jnp.float32),
+            scale_ref[...].astype(jnp.float32),
+            used,
+            jnp.zeros((ROWS - MASK_ROW - 1, LENGTH), jnp.float32),
+        ],
+        0,
+    ).astype(jnp.bfloat16)
+
+
 def on_device(trajectories, kernel_scale, start_vectors, pair_list):
     vecs, length = start_vectors.shape
-    n_sub = lax.axis_size("sub")
-    n_space = lax.axis_size("space")
-    space_at = lax.axis_index("space")
-    sub_at = lax.axis_index("sub")
-    device = space_at * n_sub + sub_at
-
-    row_blk = pair_list[:, 0] - device * 2
-    col_dev = pair_list[:, 1] // 2
-    hop = jnp.remainder(col_dev // n_sub - space_at, n_space)
-    across = jnp.remainder(col_dev % n_sub - sub_at, n_sub)
-    place = (((hop - 1) * n_sub + across) * 2 + row_blk) * 2 + pair_list[:, 1] % 2
-    place = jnp.where(hop > 0, place, -1)
-    used = jnp.any(place[:, None] == jnp.arange(length, dtype=jnp.int32)[None, :], axis=0)
-    payload = jnp.concatenate(
-        [
-            trajectories,
-            kernel_scale[None, :],
-            used.astype(jnp.bfloat16)[None, :],
-            jnp.zeros((ROWS - MASK_ROW - 1, length), jnp.bfloat16),
-        ],
-        0,
+    light = dict(
+        cost_estimate=pl.CostEstimate(flops=2**20, bytes_accessed=2**17, transcendentals=0),
+        compiler_params=pltpu.CompilerParams(vmem_limit_bytes=SMALL_LIMIT),
     )
+
+    payload = pl.pallas_call(
+        payload_kernel,
+        in_specs=[pl.BlockSpec(memory_space=pltpu.SMEM)] + [pl.BlockSpec(memory_space=pltpu.VMEM)] * 2,
+        out_shape=jax.ShapeDtypeStruct((ROWS, length), jnp.bfloat16),
+        **light,
+    )(pair_list, trajectories, kernel_scale[None, :])
 
     members = [payload] + [shifted(payload, "sub", e) for e in range(1, N_SUB)]
     near = {h: shifted(payload, "space", h) for h in (2, -2)}
@@ -436,20 +465,15 @@
 
     vector_shape = jax.ShapeDtypeStruct((vecs, length), jnp.float32)
     gram_shape = jax.ShapeDtypeStruct((vecs, vecs), jnp.float32)
-    light = dict(
-        cost_estimate=pl.CostEstimate(flops=2**20, bytes_accessed=2**17, transcendentals=0),
-        compiler_params=pltpu.CompilerParams(vmem_limit_bytes=SMALL_LIMIT),
-    )
-
     def imaged(parts, scaled):
         return pl.pallas_call(
             functools.partial(image_kernel, scaled), out_shape=[vector_shape, gram_shape], **light
         )(root, *exchanged(parts))
 
     scaled = (root * start_vectors).astype(jnp.bfloat16)
-    raw, first_gram = imaged(sweep(scaled, space_window(scaled), order, tiles), True)
-
-    image, second_gram = imaged(sweep(raw, space_window(raw), order, tiles), False)
+    raw, first_gram = imaged(sweep(space_window(scaled), order, tiles), True)
+
+    image, second_gram = imaged(sweep(space_window(raw), order, tiles), False)
     grams = summed(jnp.concatenate([first_gram, second_gram], 0))
     subspace, sound = pl.pallas_call(
         solve_both_kernel,

time: 146 us -> 139 us (0.952)
  starting transfers between devices: 61.4 us -> 47.6 us
  waiting for transfers between devices: 17.8 us -> 26.2 us
  blocking collectives: 33.3 us -> 30.7 us
  other arithmetic: 2.07 us -> 0.12 us
  local copies, waits for them, and re-layouts: 1.92 us -> 3.55 us
    ppermute x30 -> x22, starting transfers between devices: 61.4 us -> 39.6 us  [shifted(): lax.ppermute(value, axis, [((at + steps) % count, at) for at in range(cou...]
    ppermute x0 -> x4, waiting for transfers between devices: none -> 10.6 us  [the longest x2 8.88 us: space_window(): lax.ppermute(other, 'space', far)]
    ppermute x0 -> x4, starting transfers between devices: none -> 8.01 us  [the longest x2 8 us: space_window(): other = lax.ppermute(value, 'space', [(at, at ^ 1) for at in range(count)])]
    all_to_all x2, blocking collectives: 33.3 us -> 30.7 us  [summed(): lax.all_to_all(sent, ('space', 'sub'), 0, 0, axis_index_groups=groups)]
    ppermute x30 -> x22, waiting for transfers between devices: 17.8 us -> 15.5 us  [shifted(): lax.ppermute(value, axis, [((at + steps) % count, at) for at in range(cou...]
    unnamed x4 -> x7, local copies, waits for them, and re-layouts: 0.63 us -> 2.35 us
  transfers between devices with their start and end apart: 30 -> 26, of which waited for: 14 -> 13; matrix products, arithmetic and copies ran while one was open for 0% -> 0% of each run, Pallas kernels for 7% -> 7%
where the time goes in v2:
time: 139 us
  starting transfers between devices  47.6 us (34%)
  blocking collectives  30.7 us (22%)
  Pallas kernels  29.8 us (21%)
  waiting for transfers between devices  26.2 us (19%)
  local copies, waits for them, and re-layouts  3.55 us (3%)
    ppermute x22, starting transfers between devices, shifted(): lax.ppermute(value, axis, [((at + steps) % count, at) for at in range(cou...  39.6 us
    all_to_all x2, blocking collectives, summed(): lax.all_to_all(sent, ('space', 'sub'), 0, 0, axis_index_groups=groups)  30.7 us
    ppermute x22, waiting for transfers between devices, shifted(): lax.ppermute(value, axis, [((at + steps) % count, at) for at in range(cou...  15.5 us
    pallas_call x3, Pallas kernels, hop_tiles(): pl.pallas_call(functools.partial(tile_kernel, hop, first, last), in_specs...  13.9 us
    ppermute x2, waiting for transfers between devices, space_window(): lax.ppermute(other, 'space', far)  8.88 us
    ppermute x2, starting transfers between devices, space_window(): other = lax.ppermute(value, 'space', [(at, at ^ 1) for at in range(count)])  8 us
    pallas_call x2, Pallas kernels, sweep(): pl.pallas_call(functools.partial(sweep_kernel, parts, order), in_specs=[s...  7.66 us
    pallas_call x1, Pallas kernels, on_device(): pl.pallas_call(solve_both_kernel, in_specs=[pl.BlockSpec(memory_space=plt...  6.54 us
  transfers between devices with their start and end apart: 26, of which 13 were waited for; matrix products, arithmetic and copies ran while one was open for 0% of the time, Pallas kernels for 7%

profile of v2, /device:TPU:1, one launch (start us, length us, event | category | flops | bytes accessed | tf_op | source)
XLA Modules:
  0.0 138.9 jit_solution(2183526506302125718)
XLA Ops:
  0.0 0.7 broadcast_in_dim.14.scale_ref
  0.7 0.8 copy.9.pairs_ref
  1.4 1.0 copy-done
  2.4 1.0 shard_map.48.refs_0_.extra_ref
  3.4 2.1 %collective-permute-start.4 = (bf16[304,512]{1,0:T(8,128)(2,1)S(1)}, bf16[304,512]{1,0:T(8,128)(2,1)S(1)}, u32[]{:S(2)}, u32[]{:S(2)}) collective-permute-start(bf16[304,512]{1,0:T(8,128)(2,1)S(1)} %shard_map.48.refs_0_.extra_ref), channel_id=1, source_target_pairs={{248,0},{252,4},{0,8},{4,12},{8,16},{12,20},{16,24},{20,28},{24,32... | collective-permute-start | bytes 933896 | tf_op jit(solution)/shard_map/ppermute | solution.py:35
  5.5 6.6 %collective-permute-start.3 = (bf16[304,512]{1,0:T(8,128)(2,1)S(1)}, bf16[304,512]{1,0:T(8,128)(2,1)S(1)}, u32[]{:S(2)}, u32[]{:S(2)}) collective-permute-start(bf16[304,512]{1,0:T(8,128)(2,1)S(1)} %shard_map.48.refs_0_.extra_ref), channel_id=1, source_target_pairs={{8,0},{12,4},{16,8},{20,12},{24,16},{28,20},{32,24},{36,28},{40,32... | collective-permute-start | bytes 933896 | tf_op jit(solution)/shard_map/ppermute | solution.py:35
  12.2 1.3 collective-permute-start.2
  13.5 2.6 %collective-permute-start.1 = (bf16[304,512]{1,0:T(8,128)(2,1)S(1)}, bf16[304,512]{1,0:T(8,128)(2,1)S(1)}, u32[]{:S(2)}, u32[]{:S(2)}) collective-permute-start(bf16[304,512]{1,0:T(8,128)(2,1)S(1)} %shard_map.48.refs_0_.extra_ref), channel_id=1, source_target_pairs={{2,0},{3,1},{0,2},{1,3},{6,4},{7,5},{4,6},{5,7},{10,8},{11,9},{8,1... | collective-permute-start | bytes 933896 | tf_op jit(solution)/shard_map/ppermute | solution.py:35
  16.1 1.1 collective-permute-start
  17.2 2.0 %collective-permute-done.4.behind_ref = bf16[304,512]{1,0:T(8,128)(2,1)S(1)} collective-permute-done((bf16[304,512]{1,0:T(8,128)(2,1)S(1)}, bf16[304,512]{1,0:T(8,128)(2,1)S(1)}, u32[]{:S(2)}, u32[]{:S(2)}) %collective-permute-start.4) | collective-permute-done | bytes 311328 | tf_op jit(solution)/shard_map/ppermute | solution.py:35
  19.2 1.2 collective-permute-start.7
  20.4 1.0 collective-permute-done.2.refs_3_
  21.4 4.1 %collective-permute-start.5 = (bf16[304,512]{1,0:T(8,128)(2,1)S(1)}, bf16[304,512]{1,0:T(8,128)(2,1)S(1)}, u32[]{:S(2)}, u32[]{:S(2)}) collective-permute-start(bf16[304,512]{1,0:T(8,128)(2,1)S(1)} %collective-permute-done.3.ahead_ref), channel_id=1, source_target_pairs={{4,0},{8,4},{12,8},{16,12},{20,16},{24,20},{28,24},{32,28},{36,32}... | collective-permute-start | bytes 933896 | tf_op jit(solution)/shard_map/ppermute | solution.py:35
  25.5 3.7 %collective-permute-done.1.refs_2_ = bf16[304,512]{1,0:T(8,128)(2,1)S(1)} collective-permute-done((bf16[304,512]{1,0:T(8,128)(2,1)S(1)}, bf16[304,512]{1,0:T(8,128)(2,1)S(1)}, u32[]{:S(2)}, u32[]{:S(2)}) %collective-permute-start.1) | collective-permute-done | bytes 311328 | tf_op jit(solution)/shard_map/ppermute | solution.py:35
  29.3 0.1 reshape.26.mine_ref
  29.6 0.3 shard_map.49
  29.9 5.2 %shard_map.50 = (bf16[40,256,256]{2,1,0:T(8,128)(2,1)S(1)}, s32[48]{0:T(128)S(1)}, s32[48]{0:T(128)S(1)}, f32[9,8,256]{2,1,0:T(8,128)S(1)}) custom-call(s32[64]{0:T(128)S(1)} %reshape.26.mine_ref, bf16[8,320,256]{2,1,0:T(8,128)(2,1)S(1)} %get-tuple-element.48.blocks_ref, f32[8,8,256]{2,1,0:T(8,128)S(1)} %get-tuple-element.49.rate_ref, ...), custom_call_target="tpu_custom_call" | custom-call | flops 671088640 | bytes 7340032 | tf_op jit(solution)/shard_map/pallas_call | solution.py:231
  35.1 3.7 %shard_map.51 = (bf16[32,256,256]{2,1,0:T(8,128)(2,1)S(1)}, s32[48]{0:T(128)S(1)}, s32[48]{0:T(128)S(1)}, f32[9,8,256]{2,1,0:T(8,128)S(1)}) custom-call(s32[64]{0:T(128)S(1)} %reshape.25.mine_ref, bf16[8,320,256]{2,1,0:T(8,128)(2,1)S(1)} %get-tuple-element.48.blocks_ref, f32[8,8,256]{2,1,0:T(8,128)S(1)} %get-tuple-element.49.rate_ref, ...), custom_call_target="tpu_custom_call" | custom-call | flops 671088640 | bytes 7340032 | tf_op jit(solution)/shard_map/pallas_call | solution.py:231
  38.8 5.0 %shard_map.52 = (bf16[32,256,256]{2,1,0:T(8,128)(2,1)S(1)}, s32[48]{0:T(128)S(1)}, s32[48]{0:T(128)S(1)}, f32[4,8,512]{2,1,0:T(8,128)S(1)}) custom-call(s32[64]{0:T(128)S(1)} %reshape.24.mine_ref, bf16[8,320,256]{2,1,0:T(8,128)(2,1)S(1)} %get-tuple-element.48.blocks_ref, f32[8,8,256]{2,1,0:T(8,128)S(1)} %get-tuple-element.49.rate_ref, ...), custom_call_target="tpu_custom_call" | custom-call | flops 671088640 | bytes 7340032 | tf_op jit(solution)/shard_map/pallas_call | solution.py:231
  43.9 3.1 %collective-permute-start.11 = (f32[1,512]{1,0:T(1,128)S(1)}, f32[1,512]{1,0:T(1,128)S(1)}, u32[]{:S(2)}, u32[]{:S(2)}) collective-permute-start(f32[1,512]{1,0:T(1,128)S(1)} %get-tuple-element.80), channel_id=1, source_target_pairs={{1,0},{2,1},{3,2},{0,3},{5,4},{6,5},{7,6},{4,7},{9,8},{10,9},{11,1... | collective-permute-start | bytes 6152 | tf_op jit(solution)/shard_map/ppermute | solution.py:35
  47.0 1.4 %collective-permute-start.10 = (f32[1,512]{1,0:T(1,128)S(1)}, f32[1,512]{1,0:T(1,128)S(1)}, u32[]{:S(2)}, u32[]{:S(2)}) collective-permute-start(f32[1,512]{1,0:T(1,128)S(1)} %get-tuple-element.81), channel_id=1, source_target_pairs={{2,0},{3,1},{0,2},{1,3},{6,4},{7,5},{4,6},{5,7},{10,8},{11,9},{8,1... | collective-permute-start | bytes 6152 | tf_op jit(solution)/shard_map/ppermute | solution.py:35
  48.4 2.5 %collective-permute-done.10 = f32[1,512]{1,0:T(1,128)S(1)} collective-permute-done((f32[1,512]{1,0:T(1,128)S(1)}, f32[1,512]{1,0:T(1,128)S(1)}, u32[]{:S(2)}, u32[]{:S(2)}) %collective-permute-start.10) | collective-permute-done | bytes 2080 | tf_op jit(solution)/shard_map/ppermute | solution.py:35
  50.9 1.2 collective-permute-done.9
  52.2 2.7 %collective-permute-start.12 = (bf16[32,512]{1,0:T(8,128)(2,1)S(1)}, bf16[32,512]{1,0:T(8,128)(2,1)S(1)}, u32[]{:S(2)}, u32[]{:S(2)}) collective-permute-start(bf16[32,512]{1,0:T(8,128)(2,1)S(1)} %multiply_convert_fusion.refs_9_), channel_id=1, source_target_pairs={{0,4},{4,0},{8,12},{12,8},{16,20},{20,16},{24,28},{28,24},{32,36},... | collective-permute-start | bytes 98312 | tf_op jit(solution)/shard_map/ppermute | solution.py:40
  54.8 0.9 collective-permute-done.12.refs_10_
  55.8 4.8 %collective-permute-start.13 = (bf16[2,32,512]{2,1,0:T(8,128)(2,1)S(1)}, bf16[2,32,512]{2,1,0:T(8,128)(2,1)S(1)}, u32[]{:S(2)}, u32[]{:S(2)}) collective-permute-start(bf16[2,32,512]{2,1,0:T(8,128)(2,1)S(1)} %pad_maximum_fusion.1), channel_id=1, source_target_pairs={{8,0},{12,4},{16,8},{20,12},{24,16},{28,20},{32,24},{36,28},{40,32... | collective-permute-start | bytes 196616 | tf_op jit(solution)/shard_map/ppermute | solution.py:35
  60.5 4.3 %collective-permute-done.15.refs_13_ = bf16[32,512]{1,0:T(8,128)(2,1)S(1)} collective-permute-done((bf16[32,512]{1,0:T(8,128)(2,1)S(1)}, bf16[32,512]{1,0:T(8,128)(2,1)S(1)}, u32[]{:S(2)}, u32[]{:S(2)}) %collective-permute-start.15) | collective-permute-done | bytes 32800 | tf_op jit(solution)/shard_map/ppermute | solution.py:43
  64.8 3.7 %shard_map.53 = (f32[32,512]{1,0:T(8,128)S(1)}, f32[32,512]{1,0:T(8,128)S(1)}, f32[32,512]{1,0:T(8,128)S(1)}, f32[32,512]{1,0:T(8,128)S(1)}) custom-call(s32[48]{0:T(128)S(1)} %get-tuple-element.56.refs_0_, s32[48]{0:T(128)S(1)} %get-tuple-element.57.refs_1_, s32[48]{0:T(128)S(1)} %get-tuple-element.58.refs_2_, s32[48]{0:T(128)S(1)} %get-tuple-element.59.refs_3_, ...), custom_call_target="tpu_custom_call" | custom-call | flops 838860800 | bytes 7340032 | tf_op jit(solution)/shard_map/pallas_call | solution.py:327
  68.7 0.1 collective-permute-start.17
  68.8 2.5 %collective-permute-start.18 = (f32[32,512]{1,0:T(8,128)S(1)}, f32[32,512]{1,0:T(8,128)S(1)}, u32[]{:S(2)}, u32[]{:S(2)}) collective-permute-start(f32[32,512]{1,0:T(8,128)S(1)} %get-tuple-element.68), channel_id=1, source_target_pairs={{1,0},{2,1},{3,2},{0,3},{5,4},{6,5},{7,6},{4,7},{9,8},{10,9},{11,1... | collective-permute-start | bytes 196616 | tf_op jit(solution)/shard_map/ppermute | solution.py:35
  71.3 2.3 %collective-permute-done.16.refs_1_ = f32[32,512]{1,0:T(8,128)S(1)} collective-permute-done((f32[32,512]{1,0:T(8,128)S(1)}, f32[32,512]{1,0:T(8,128)S(1)}, u32[]{:S(2)}, u32[]{:S(2)}) %collective-permute-start.16) | collective-permute-done | bytes 65568 | tf_op jit(solution)/shard_map/ppermute | solution.py:35
  73.7 0.6 collective-permute-done.18.refs_3_
  74.2 0.2 shard_map.54
  74.5 5.3 %collective-permute-start.19 = (f32[32,512]{1,0:T(8,128)S(1)}, f32[32,512]{1,0:T(8,128)S(1)}, u32[]{:S(2)}, u32[]{:S(2)}) collective-permute-start(f32[32,512]{1,0:T(8,128)S(1)} %get-tuple-element.70.refs_9_), channel_id=1, source_target_pairs={{0,4},{4,0},{8,12},{12,8},{16,20},{20,16},{24,28},{28,24},{32,36},... | collective-permute-start | bytes 196616 | tf_op jit(solution)/shard_map/ppermute | solution.py:40
  79.8 0.9 collective-permute-done.19.refs_10_
  80.8 4.8 %collective-permute-start.20 = (f32[2,32,512]{2,1,0:T(8,128)S(1)}, f32[2,32,512]{2,1,0:T(8,128)S(1)}, u32[]{:S(2)}, u32[]{:S(2)}) collective-permute-start(f32[2,32,512]{2,1,0:T(8,128)S(1)} %pad_maximum_fusion), channel_id=1, source_target_pairs={{8,0},{12,4},{16,8},{20,12},{24,16},{28,20},{32,24},{36,28},{40,32... | collective-permute-start | bytes 393224 | tf_op jit(solution)/shard_map/ppermute | solution.py:35
  85.6 4.6 %collective-permute-done.22.refs_13_ = f32[32,512]{1,0:T(8,128)S(1)} collective-permute-done((f32[32,512]{1,0:T(8,128)S(1)}, f32[32,512]{1,0:T(8,128)S(1)}, u32[]{:S(2)}, u32[]{:S(2)}) %collective-permute-start.22) | collective-permute-done | bytes 65568 | tf_op jit(solution)/shard_map/ppermute | solution.py:43
  90.2 3.9 %shard_map.55 = (f32[32,512]{1,0:T(8,128)S(1)}, f32[32,512]{1,0:T(8,128)S(1)}, f32[32,512]{1,0:T(8,128)S(1)}, f32[32,512]{1,0:T(8,128)S(1)}) custom-call(s32[48]{0:T(128)S(1)} %get-tuple-element.56.refs_0_, s32[48]{0:T(128)S(1)} %get-tuple-element.57.refs_1_, s32[48]{0:T(128)S(1)} %get-tuple-element.58.refs_2_, s32[48]{0:T(128)S(1)} %get-tuple-element.59.refs_3_, ...), custom_call_target="tpu_custom_call" | custom-call | flops 838860800 | bytes 7340032 | tf_op jit(solution)/shard_map/pallas_call | solution.py:327
  94.1 1.1 collective-permute-start.23
  95.2 1.5 %collective-permute-start.24 = (f32[32,512]{1,0:T(8,128)S(1)}, f32[32,512]{1,0:T(8,128)S(1)}, u32[]{:S(2)}, u32[]{:S(2)}) collective-permute-start(f32[32,512]{1,0:T(8,128)S(1)} %get-tuple-element.73), channel_id=1, source_target_pairs={{2,0},{3,1},{0,2},{1,3},{6,4},{7,5},{4,6},{5,7},{10,8},{11,9},{8,1... | collective-permute-start | bytes 196616 | tf_op jit(solution)/shard_map/ppermute | solution.py:35
  96.7 1.0 collective-permute-start.25
  97.7 0.8 collective-permute-done.23.refs_1_
  98.5 1.3 collective-permute-done.24.refs_2_
  99.9 0.2 shard_map.56
  100.2 17.9 %all_to_all.20 = f32[32,16,128]{2,1,0:T(8,128)S(1)} all-to-all(f32[32,16,128]{2,1,0:T(8,128)S(1)} %broadcast_in_dim.31), channel_id=1, replica_groups={{0,1,2,3,4,5,6,7,8,9,10,11,12,13,14,15,16,17,18,19,20,21,22,23,24,25,26..., dimensions={0} | all-to-all | bytes 524288 | tf_op jit(solution)/shard_map/all_to_all | solution.py:67
  118.1 12.8 %all_to_all.21 = f32[8,16,128]{2,1,0:T(8,128)S(1)} all-to-all(f32[8,16,128]{2,1,0:T(8,128)S(1)} %broadcast_in_dim.32), channel_id=1, replica_groups={{0,32,64,96,128,160,192,224},{1,33,65,97,129,161,193,225},{2,34,66,98,1..., dimensions={0} | all-to-all | bytes 131072 | tf_op jit(solution)/shard_map/all_to_all | solution.py:67
  131.0 6.5 %shard_map.57 = (f32[32,512]{1,0:T(8,128)S(1)}, s32[1]{0:T(128)}) custom-call(f32[64,32]{1,0:T(8,128)S(1)} %reshape.27.grams_ref, f32[32,512]{1,0:T(8,128)S(1)} %get-tuple-element.76.image_ref), custom_call_target="tpu_custom_call" | custom-call | flops 1048576 | bytes 131072 | tf_op jit(solution)/shard_map/pallas_call | solution.py:478
  138.2 0.6 copy-done.2
  (47 shorter events, 0.8 us)
Async XLA Ops:
  1.4 1.0 copy-start
  3.4 15.8 %collective-permute-start.4 = (bf16[304,512]{1,0:T(8,128)(2,1)S(1)}, bf16[304,512]{1,0:T(8,128)(2,1)S(1)}, u32[]{:S(2)}, u32[]{:S(2)}) collective-permute-start(bf16[304,512]{1,0:T(8,128)(2,1)S(1)} %shard_map.48.refs_0_.extra_ref), channel_id=1, source_target_pairs={{248,0},{252,4},{0,8},{4,12},{8,16},{12,20},{16,24},{20,28},{24,32... | collective-permute-start | bytes 933896 | tf_op jit(solution)/shard_map/ppermute | solution.py:35
  5.5 13.6 %collective-permute-start.3 = (bf16[304,512]{1,0:T(8,128)(2,1)S(1)}, bf16[304,512]{1,0:T(8,128)(2,1)S(1)}, u32[]{:S(2)}, u32[]{:S(2)}) collective-permute-start(bf16[304,512]{1,0:T(8,128)(2,1)S(1)} %shard_map.48.refs_0_.extra_ref), channel_id=1, source_target_pairs={{8,0},{12,4},{16,8},{20,12},{24,16},{28,20},{32,24},{36,28},{40,32... | collective-permute-start | bytes 933896 | tf_op jit(solution)/shard_map/ppermute | solution.py:35
  12.2 9.2 %collective-permute-start.2 = (bf16[304,512]{1,0:T(8,128)(2,1)S(1)}, bf16[304,512]{1,0:T(8,128)(2,1)S(1)}, u32[]{:S(2)}, u32[]{:S(2)}) collective-permute-start(bf16[304,512]{1,0:T(8,128)(2,1)S(1)} %shard_map.48.refs_0_.extra_ref), channel_id=1, source_target_pairs={{3,0},{0,1},{1,2},{2,3},{7,4},{4,5},{5,6},{6,7},{11,8},{8,9},{9,10... | collective-permute-start | bytes 933896 | tf_op jit(solution)/shard_map/ppermute | solution.py:35
  13.5 15.7 %collective-permute-start.1 = (bf16[304,512]{1,0:T(8,128)(2,1)S(1)}, bf16[304,512]{1,0:T(8,128)(2,1)S(1)}, u32[]{:S(2)}, u32[]{:S(2)}) collective-permute-start(bf16[304,512]{1,0:T(8,128)(2,1)S(1)} %shard_map.48.refs_0_.extra_ref), channel_id=1, source_target_pairs={{2,0},{3,1},{0,2},{1,3},{6,4},{7,5},{4,6},{5,7},{10,8},{11,9},{8,1... | collective-permute-start | bytes 933896 | tf_op jit(solution)/shard_map/ppermute | solution.py:35
  16.1 13.1 %collective-permute-start = (bf16[304,512]{1,0:T(8,128)(2,1)S(1)}, bf16[304,512]{1,0:T(8,128)(2,1)S(1)}, u32[]{:S(2)}, u32[]{:S(2)}) collective-permute-start(bf16[304,512]{1,0:T(8,128)(2,1)S(1)} %shard_map.48.refs_0_.extra_ref), channel_id=1, source_target_pairs={{1,0},{2,1},{3,2},{0,3},{5,4},{6,5},{7,6},{4,7},{9,8},{10,9},{11,1... | collective-permute-start | bytes 933896 | tf_op jit(solution)/shard_map/ppermute | solution.py:35
  19.2 15.9 %collective-permute-start.8 = (bf16[304,512]{1,0:T(8,128)(2,1)S(1)}, bf16[304,512]{1,0:T(8,128)(2,1)S(1)}, u32[]{:S(2)}, u32[]{:S(2)}) collective-permute-start(bf16[304,512]{1,0:T(8,128)(2,1)S(1)} %shard_map.48.refs_0_.extra_ref), channel_id=1, source_target_pairs={{252,0},{0,4},{4,8},{8,12},{12,16},{16,20},{20,24},{24,28},{28,32}... | collective-permute-start | bytes 933896 | tf_op jit(solution)/shard_map/ppermute | solution.py:35
  19.2 15.9 %collective-permute-start.7 = (bf16[304,512]{1,0:T(8,128)(2,1)S(1)}, bf16[304,512]{1,0:T(8,128)(2,1)S(1)}, u32[]{:S(2)}, u32[]{:S(2)}) collective-permute-start(bf16[304,512]{1,0:T(8,128)(2,1)S(1)} %shard_map.48.refs_0_.extra_ref), channel_id=1, source_target_pairs={{4,0},{8,4},{12,8},{16,12},{20,16},{24,20},{28,24},{32,28},{36,32}... | collective-permute-start | bytes 933896 | tf_op jit(solution)/shard_map/ppermute | solution.py:35
  21.4 17.4 %collective-permute-start.5 = (bf16[304,512]{1,0:T(8,128)(2,1)S(1)}, bf16[304,512]{1,0:T(8,128)(2,1)S(1)}, u32[]{:S(2)}, u32[]{:S(2)}) collective-permute-start(bf16[304,512]{1,0:T(8,128)(2,1)S(1)} %collective-permute-done.3.ahead_ref), channel_id=1, source_target_pairs={{4,0},{8,4},{12,8},{16,12},{20,16},{24,20},{28,24},{32,28},{36,32}... | collective-permute-start | bytes 933896 | tf_op jit(solution)/shard_map/ppermute | solution.py:35
  29.2 9.6 %collective-permute-start.6 = (bf16[304,512]{1,0:T(8,128)(2,1)S(1)}, bf16[304,512]{1,0:T(8,128)(2,1)S(1)}, u32[]{:S(2)}, u32[]{:S(2)}) collective-permute-start(bf16[304,512]{1,0:T(8,128)(2,1)S(1)} %collective-permute-done.4.behind_ref), channel_id=1, source_target_pairs={{252,0},{0,4},{4,8},{8,12},{12,16},{16,20},{20,24},{24,28},{28,32}... | collective-permute-start | bytes 933896 | tf_op jit(solution)/shard_map/ppermute | solution.py:35
  29.6 22.6 %copy-start.1 = (f32[32,512]{1,0:T(8,128)S(1)}, f32[32,512]{1,0:T(8,128)}, u32[]{:S(2)}) copy-start(f32[32,512]{1,0:T(8,128)} %param.8) | copy-start | bytes 196612
  43.9 4.5 %collective-permute-start.11 = (f32[1,512]{1,0:T(1,128)S(1)}, f32[1,512]{1,0:T(1,128)S(1)}, u32[]{:S(2)}, u32[]{:S(2)}) collective-permute-start(f32[1,512]{1,0:T(1,128)S(1)} %get-tuple-element.80), channel_id=1, source_target_pairs={{1,0},{2,1},{3,2},{0,3},{5,4},{6,5},{7,6},{4,7},{9,8},{10,9},{11,1... | collective-permute-start | bytes 6152 | tf_op jit(solution)/shard_map/ppermute | solution.py:35
  47.0 3.9 %collective-permute-start.10 = (f32[1,512]{1,0:T(1,128)S(1)}, f32[1,512]{1,0:T(1,128)S(1)}, u32[]{:S(2)}, u32[]{:S(2)}) collective-permute-start(f32[1,512]{1,0:T(1,128)S(1)} %get-tuple-element.81), channel_id=1, source_target_pairs={{2,0},{3,1},{0,2},{1,3},{6,4},{7,5},{4,6},{5,7},{10,8},{11,9},{8,1... | collective-permute-start | bytes 6152 | tf_op jit(solution)/shard_map/ppermute | solution.py:35
  48.4 3.7 %collective-permute-start.9 = (f32[1,512]{1,0:T(1,128)S(1)}, f32[1,512]{1,0:T(1,128)S(1)}, u32[]{:S(2)}, u32[]{:S(2)}) collective-permute-start(f32[1,512]{1,0:T(1,128)S(1)} %get-tuple-element.82), channel_id=1, source_target_pairs={{3,0},{0,1},{1,2},{2,3},{7,4},{4,5},{5,6},{6,7},{11,8},{8,9},{9,10... | collective-permute-start | bytes 6152 | tf_op jit(solution)/shard_map/ppermute | solution.py:35
  52.2 3.5 %collective-permute-start.12 = (bf16[32,512]{1,0:T(8,128)(2,1)S(1)}, bf16[32,512]{1,0:T(8,128)(2,1)S(1)}, u32[]{:S(2)}, u32[]{:S(2)}) collective-permute-start(bf16[32,512]{1,0:T(8,128)(2,1)S(1)} %multiply_convert_fusion.refs_9_), channel_id=1, source_target_pairs={{0,4},{4,0},{8,12},{12,8},{16,20},{20,16},{24,28},{28,24},{32,36},... | collective-permute-start | bytes 98312 | tf_op jit(solution)/shard_map/ppermute | solution.py:40
  55.7 9.1 %collective-permute-start.14 = (bf16[2,32,512]{2,1,0:T(8,128)(2,1)S(1)}, bf16[2,32,512]{2,1,0:T(8,128)(2,1)S(1)}, u32[]{:S(2)}, u32[]{:S(2)}) collective-permute-start(bf16[2,32,512]{2,1,0:T(8,128)(2,1)S(1)} %pad_maximum_fusion.1), channel_id=1, source_target_pairs={{248,0},{252,4},{0,8},{4,12},{8,16},{12,20},{16,24},{20,28},{24,32... | collective-permute-start | bytes 196616 | tf_op jit(solution)/shard_map/ppermute | solution.py:35
  55.8 9.0 %collective-permute-start.13 = (bf16[2,32,512]{2,1,0:T(8,128)(2,1)S(1)}, bf16[2,32,512]{2,1,0:T(8,128)(2,1)S(1)}, u32[]{:S(2)}, u32[]{:S(2)}) collective-permute-start(bf16[2,32,512]{2,1,0:T(8,128)(2,1)S(1)} %pad_maximum_fusion.1), channel_id=1, source_target_pairs={{8,0},{12,4},{16,8},{20,12},{24,16},{28,20},{32,24},{36,28},{40,32... | collective-permute-start | bytes 196616 | tf_op jit(solution)/shard_map/ppermute | solution.py:35
  60.5 4.3 %collective-permute-start.15 = (bf16[32,512]{1,0:T(8,128)(2,1)S(1)}, bf16[32,512]{1,0:T(8,128)(2,1)S(1)}, u32[]{:S(2)}, u32[]{:S(2)}) collective-permute-start(bf16[32,512]{1,0:T(8,128)(2,1)S(1)} %collective-permute-done.12.refs_10_), channel_id=1, source_target_pairs={{0,16},{4,244},{8,24},{12,252},{16,32},{20,4},{24,40},{28,12},{32,... | collective-permute-start | bytes 98312 | tf_op jit(solution)/shard_map/ppermute | solution.py:43
  68.6 5.1 %collective-permute-start.16 = (f32[32,512]{1,0:T(8,128)S(1)}, f32[32,512]{1,0:T(8,128)S(1)}, u32[]{:S(2)}, u32[]{:S(2)}) collective-permute-start(f32[32,512]{1,0:T(8,128)S(1)} %get-tuple-element.66), channel_id=1, source_target_pairs={{3,0},{0,1},{1,2},{2,3},{7,4},{4,5},{5,6},{6,7},{11,8},{8,9},{9,10... | collective-permute-start | bytes 196616 | tf_op jit(solution)/shard_map/ppermute | solution.py:35
  68.7 5.0 %collective-permute-start.17 = (f32[32,512]{1,0:T(8,128)S(1)}, f32[32,512]{1,0:T(8,128)S(1)}, u32[]{:S(2)}, u32[]{:S(2)}) collective-permute-start(f32[32,512]{1,0:T(8,128)S(1)} %get-tuple-element.67), channel_id=1, source_target_pairs={{2,0},{3,1},{0,2},{1,3},{6,4},{7,5},{4,6},{5,7},{10,8},{11,9},{8,1... | collective-permute-start | bytes 196616 | tf_op jit(solution)/shard_map/ppermute | solution.py:35
  68.8 5.5 %collective-permute-start.18 = (f32[32,512]{1,0:T(8,128)S(1)}, f32[32,512]{1,0:T(8,128)S(1)}, u32[]{:S(2)}, u32[]{:S(2)}) collective-permute-start(f32[32,512]{1,0:T(8,128)S(1)} %get-tuple-element.68), channel_id=1, source_target_pairs={{1,0},{2,1},{3,2},{0,3},{5,4},{6,5},{7,6},{4,7},{9,8},{10,9},{11,1... | collective-permute-start | bytes 196616 | tf_op jit(solution)/shard_map/ppermute | solution.py:35
  74.5 6.2 %collective-permute-start.19 = (f32[32,512]{1,0:T(8,128)S(1)}, f32[32,512]{1,0:T(8,128)S(1)}, u32[]{:S(2)}, u32[]{:S(2)}) collective-permute-start(f32[32,512]{1,0:T(8,128)S(1)} %get-tuple-element.70.refs_9_), channel_id=1, source_target_pairs={{0,4},{4,0},{8,12},{12,8},{16,20},{20,16},{24,28},{28,24},{32,36},... | collective-permute-start | bytes 196616 | tf_op jit(solution)/shard_map/ppermute | solution.py:40
  80.7 9.5 %collective-permute-start.21 = (f32[2,32,512]{2,1,0:T(8,128)S(1)}, f32[2,32,512]{2,1,0:T(8,128)S(1)}, u32[]{:S(2)}, u32[]{:S(2)}) collective-permute-start(f32[2,32,512]{2,1,0:T(8,128)S(1)} %pad_maximum_fusion), channel_id=1, source_target_pairs={{248,0},{252,4},{0,8},{4,12},{8,16},{12,20},{16,24},{20,28},{24,32... | collective-permute-start | bytes 393224 | tf_op jit(solution)/shard_map/ppermute | solution.py:35
  80.8 9.4 %collective-permute-start.20 = (f32[2,32,512]{2,1,0:T(8,128)S(1)}, f32[2,32,512]{2,1,0:T(8,128)S(1)}, u32[]{:S(2)}, u32[]{:S(2)}) collective-permute-start(f32[2,32,512]{2,1,0:T(8,128)S(1)} %pad_maximum_fusion), channel_id=1, source_target_pairs={{8,0},{12,4},{16,8},{20,12},{24,16},{28,20},{32,24},{36,28},{40,32... | collective-permute-start | bytes 393224 | tf_op jit(solution)/shard_map/ppermute | solution.py:35
  85.6 4.6 %collective-permute-start.22 = (f32[32,512]{1,0:T(8,128)S(1)}, f32[32,512]{1,0:T(8,128)S(1)}, u32[]{:S(2)}, u32[]{:S(2)}) collective-permute-start(f32[32,512]{1,0:T(8,128)S(1)} %collective-permute-done.19.refs_10_), channel_id=1, source_target_pairs={{0,16},{4,244},{8,24},{12,252},{16,32},{20,4},{24,40},{28,12},{32,... | collective-permute-start | bytes 196616 | tf_op jit(solution)/shard_map/ppermute | solution.py:43
  94.1 4.4 %collective-permute-start.23 = (f32[32,512]{1,0:T(8,128)S(1)}, f32[32,512]{1,0:T(8,128)S(1)}, u32[]{:S(2)}, u32[]{:S(2)}) collective-permute-start(f32[32,512]{1,0:T(8,128)S(1)} %get-tuple-element.72), channel_id=1, source_target_pairs={{3,0},{0,1},{1,2},{2,3},{7,4},{4,5},{5,6},{6,7},{11,8},{8,9},{9,10... | collective-permute-start | bytes 196616 | tf_op jit(solution)/shard_map/ppermute | solution.py:35
  95.2 4.6 %collective-permute-start.24 = (f32[32,512]{1,0:T(8,128)S(1)}, f32[32,512]{1,0:T(8,128)S(1)}, u32[]{:S(2)}, u32[]{:S(2)}) collective-permute-start(f32[32,512]{1,0:T(8,128)S(1)} %get-tuple-element.73), channel_id=1, source_target_pairs={{2,0},{3,1},{0,2},{1,3},{6,4},{7,5},{4,6},{5,7},{10,8},{11,9},{8,1... | collective-permute-start | bytes 196616 | tf_op jit(solution)/shard_map/ppermute | solution.py:35
  96.7 3.2 %collective-permute-start.25 = (f32[32,512]{1,0:T(8,128)S(1)}, f32[32,512]{1,0:T(8,128)S(1)}, u32[]{:S(2)}, u32[]{:S(2)}) collective-permute-start(f32[32,512]{1,0:T(8,128)S(1)} %get-tuple-element.74), channel_id=1, source_target_pairs={{1,0},{2,1},{3,2},{0,3},{5,4},{6,5},{7,6},{4,7},{9,8},{10,9},{11,1... | collective-permute-start | bytes 196616 | tf_op jit(solution)/shard_map/ppermute | solution.py:35
  138.2 0.6 copy-start.2

commit v3 on v2

--- a/solution.py
+++ b/solution.py
@@ -17,14 +17,16 @@
 SCALE_ROW = 300
 MASK_ROW = 301
 PAIRS = 4 * N_SUB
-SLOTS = 48
+SLOTS = 80
 COUNT = SLOTS - 1
 NOBODY = 2 * N_SUB
 UNROLL = 8
-STARTS = (0, 5, 9)
+HALF = UNROLL // 2
+HOPS = ((2,), (1, 3))
+STARTS = (0, 5)
 GROUPS = 13
 LOG2E = 1.4426950408889634
-VMEM_LIMIT = 12 * 1024 * 1024
+VMEM_LIMIT = 24 * 1024 * 1024
 SWEEP_LIMIT = 24 * 1024 * 1024
 SMALL_LIMIT = 4 * 1024 * 1024
 TRANS_B = (((1,), (1,)), ((), ()))
@@ -37,10 +39,11 @@
 
 def space_window(value):
     count = lax.axis_size("space")
-    other = lax.ppermute(value, "space", [(at, at ^ 1) for at in range(count)])
-    pair = jnp.stack([value, other])
-    far = [(at, (at + (4 if at % 2 == 0 else -4)) % count) for at in range(count)]
-    return value, other, shifted(pair, "space", 2), shifted(pair, "space", -2), lax.ppermute(other, "space", far)
+    swap = [(at, at ^ 1) for at in range(count)]
+    far = [(at, (at + (3 if at % 2 else -3)) % count) for at in range(count)]
+    other, far = lax.ppermute(value, "space", swap), lax.ppermute(value, "space", far)
+    beside = jnp.stack([shifted(value, "space", 2), shifted(value, "space", -2)])
+    return value, other, beside, lax.ppermute(beside, "space", swap), far
 
 
 def window_slot(hop, side):
@@ -125,22 +128,24 @@
         rate_ref[first + c] = rate[c * BLOCK : (c + 1) * BLOCK]
 
 
-def list_pairs(mine_ref, theirs, rows_ref, cols_ref, count):
+def list_pairs(hops, mine_ref, theirs, rows_ref, cols_ref, count):
     def member(e, count):
-        for side in range(2):
-            for r in range(2):
-                for c in range(2):
-                    if side == 0:
-                        used = mine_ref[e * PAIRS + lax.rem(N_SUB - e, N_SUB) * 4 + r * 2 + c]
-                    else:
-                        used = lax.shift_right_logical(theirs, e * 4 + c * 2 + r) & 1
-                    rows_ref[count] = e * 2 + r
-                    cols_ref[count] = side * 2 + c
-                    count = count + used
+        for k, bits in enumerate(theirs):
+            for side in range(2):
+                for r in range(2):
+                    for c in range(2):
+                        if side == 0:
+                            place = lax.rem(N_SUB - e, N_SUB) * 4 + r * 2 + c
+                            used = mine_ref[(e * REACH + hops[k] - 1) * PAIRS + place]
+                        else:
+                            used = lax.shift_right_logical(bits, e * 4 + c * 2 + r) & 1
+                        rows_ref[count] = e * 2 + r
+                        cols_ref[count] = k * 4 + side * 2 + c
+                        count = count + used
         return count
 
     count = lax.fori_loop(0, N_SUB, member, count)
-    for k in range(8):
+    for k in range(UNROLL + HALF):
         rows_ref[count + k] = NOBODY
         cols_ref[count + k] = 0
     rows_ref[COUNT] = count
@@ -148,67 +153,66 @@
     return count
 
 
-def tile_kernel(
-    hop, first, last, mine_ref, blocks_ref, rate_ref, ahead_ref, behind_ref, extra_ref,
-    tile_ref, rows_ref, cols_ref, sums_ref, lhs, col, even, odd, made, sems, *held
-):
+def listed_behind(data_ref, hop):
+    lane = lax.broadcasted_iota(jnp.int32, (1, 128), 1) - (hop - 1) * PAIRS
+    weight = lax.shift_left(jnp.ones_like(lane), jnp.clip(lane, 0, PAIRS)).astype(jnp.float32)
+    weight = jnp.where((lane >= 0) & (lane < PAIRS), weight, 0.0)
+    used = data_ref[MASK_ROW : MASK_ROW + 1, :128].astype(jnp.float32)
+    return jnp.sum(used * weight).astype(jnp.int32)
+
+
+def tile_kernel(hops, first, last, mine_ref, blocks_ref, rate_ref, *refs):
+    window_refs, extra_ref, refs = refs[: 2 * len(hops)], refs[2 * len(hops)], refs[2 * len(hops) + 1 :]
+    tile_ref, rows_ref, cols_ref, sums_ref, lhs, col, even, odd, made, sems, *held = refs
     total = held[0] if last else sums_ref
-    prepare_columns(ahead_ref, 0, lhs, col)
-    prepare_columns(behind_ref, 2, lhs, col)
+    for k, window_ref in enumerate(window_refs):
+        prepare_columns(window_ref, 2 * k, lhs, col)
     count = 0
     if first:
-        prepare_columns(extra_ref, 4, lhs, col)
+        prepare_columns(extra_ref, 4 * len(hops), lhs, col)
         for r in range(2):
             rows_ref[r] = r
-            cols_ref[r] = 4 + r
+            cols_ref[r] = 4 * len(hops) + r
         count = 2
         total[...] = jnp.zeros_like(total)
     else:
         total[...] = extra_ref[...]
-    lane = lax.broadcasted_iota(jnp.int32, (1, 128), 1) - (hop - 1) * PAIRS
-    weight = lax.shift_left(jnp.ones_like(lane), jnp.clip(lane, 0, PAIRS)).astype(jnp.float32)
-    weight = jnp.where((lane >= 0) & (lane < PAIRS), weight, 0.0)
-    theirs = behind_ref[MASK_ROW : MASK_ROW + 1, :128].astype(jnp.float32)
-    theirs = jnp.sum(theirs * weight).astype(jnp.int32)
-    count = list_pairs(mine_ref, theirs, rows_ref, cols_ref, jnp.int32(count))
-
-    def product(at):
-        row = lax.min(rows_ref[at], NOBODY - 1)
-        return jnp.dot(lhs[cols_ref[at]], blocks_ref[row], preferred_element_type=jnp.float32)
-
-    def finish(crossed, at):
-        row = rows_ref[at]
-        rate = col[cols_ref[at]]
-        rates = jnp.concatenate([rate, rate], 1) * rate_ref[lax.min(row, NOBODY - 1), :1, :]
-        tile = jnp.exp2(crossed * rates).astype(jnp.bfloat16)
-        made[at] = tile
-        total[row] += jnp.sum(tile.astype(jnp.float32).reshape(BLOCK // 8, 8, BLOCK), axis=0)
-
-    even[...] = product(0)
-
-    def step(k, _):
-        odd[...] = product(2 * k + 1)
-        finish(even[...], 2 * k)
-        even[...] = product(2 * k + 2)
-        finish(odd[...], 2 * k + 1)
-
-        @pl.when(lax.rem(k, UNROLL // 2) == UNROLL // 2 - 1)
-        def _():
-            copy(lax.div(k, UNROLL // 2)).start()
-
-        return 0
+    theirs = [listed_behind(window_refs[2 * k + 1], hop) for k, hop in enumerate(hops)]
+    count = list_pairs(hops, mine_ref, theirs, rows_ref, cols_ref, jnp.int32(count))
+
+    def products(buffer, base):
+        for n in range(HALF):
+            row = lax.min(rows_ref[base + n], NOBODY - 1)
+            buffer[n] = jnp.dot(
+                lhs[cols_ref[base + n]], blocks_ref[row], preferred_element_type=jnp.float32
+            )
+
+    def finish(buffer, base):
+        for n in range(HALF):
+            at = base + n
+            row = rows_ref[at]
+            rate = col[cols_ref[at]]
+            rates = jnp.concatenate([rate, rate], 1) * rate_ref[lax.min(row, NOBODY - 1), :1, :]
+            tile = jnp.exp2(buffer[n] * rates).astype(jnp.bfloat16)
+            made[at] = tile
+            total[row] += jnp.sum(tile.astype(jnp.float32).reshape(BLOCK // 8, 8, BLOCK), axis=0)
 
     def copy(group):
         span = pl.ds(group * UNROLL, UNROLL)
         return pltpu.make_async_copy(made.at[span], tile_ref.at[span], sems.at[group])
 
-    steps = lax.shift_right_logical(count + 1, 1)
-    lax.fori_loop(0, steps, step, 0)
-
-    @pl.when(lax.rem(steps, UNROLL // 2) != 0)
-    def _():
-        copy(lax.div(steps, UNROLL // 2)).start()
-
+    products(even, 0)
+
+    def step(group, _):
+        products(odd, UNROLL * group + HALF)
+        finish(even, UNROLL * group)
+        products(even, UNROLL * group + UNROLL)
+        finish(odd, UNROLL * group + HALF)
+        copy(group).start()
+        return 0
+
+    groups = lax.div(count + (UNROLL - 1), UNROLL)
+    lax.fori_loop(0, groups, step, 0)
     if last:
         for e in range(N_SUB):
             for r in range(2):
@@ -219,18 +223,18 @@
         copy(group).wait()
         return 0
 
-    lax.fori_loop(0, lax.div(steps + (UNROLL // 2 - 1), UNROLL // 2), sent, 0)
-
-
-def hop_tiles(hop, first, last, mine, blocks, rate, ahead, behind, extra):
+    lax.fori_loop(0, groups, sent, 0)
+
+
+def hop_tiles(hops, first, last, mine, blocks, rate, windows, extra):
     smem = pl.BlockSpec(memory_space=pltpu.SMEM)
     vmem = pl.BlockSpec(memory_space=pltpu.VMEM)
-    columns = 6 if first else 4
-    slots = UNROLL * (5 if first else 4)
+    columns = 4 * len(hops) + (2 if first else 0)
+    slots = 2 * len(hops) * PAIRS + (UNROLL if first else 0)
     sums = (NOBODY + 1, 8, BLOCK)
     return pl.pallas_call(
-        functools.partial(tile_kernel, hop, first, last),
-        in_specs=[smem] + [vmem] * 5,
+        functools.partial(tile_kernel, hops, first, last),
+        in_specs=[smem] + [vmem] * (3 + len(windows)),
         out_specs=[pl.BlockSpec(memory_space=pl.ANY), smem, smem, vmem],
         out_shape=[
             jax.ShapeDtypeStruct((slots, BLOCK, BLOCK), jnp.bfloat16),
@@ -241,19 +245,19 @@
         scratch_shapes=[
             pltpu.VMEM((columns, BLOCK, DEPTH), jnp.bfloat16),
             pltpu.VMEM((columns, BLOCK, 128), jnp.float32),
-            pltpu.VMEM((BLOCK, BLOCK), jnp.float32),
-            pltpu.VMEM((BLOCK, BLOCK), jnp.float32),
+            pltpu.VMEM((HALF, BLOCK, BLOCK), jnp.float32),
+            pltpu.VMEM((HALF, BLOCK, BLOCK), jnp.float32),
             pltpu.VMEM((slots, BLOCK, BLOCK), jnp.bfloat16),
             pltpu.SemaphoreType.DMA((slots // UNROLL,)),
         ]
         + ([pltpu.VMEM(sums, jnp.float32)] if last else []),
         compiler_params=pltpu.CompilerParams(vmem_limit_bytes=VMEM_LIMIT),
         cost_estimate=pl.CostEstimate(
-            flops=16 * 2 * DEPTH * BLOCK * BLOCK,
+            flops=16 * len(hops) * 2 * DEPTH * BLOCK * BLOCK,
             bytes_accessed=7 * 2**20,
-            transcendentals=16 * BLOCK * BLOCK,
+            transcendentals=16 * len(hops) * BLOCK * BLOCK,
         ),
-    )(mine, blocks, rate, ahead, behind, extra)
+    )(mine, blocks, rate, *windows, extra)
 
 
 def stacked(vectors):
@@ -263,9 +267,9 @@
     return jnp.concatenate([high, (vectors - high.astype(jnp.float32)).astype(jnp.bfloat16)], 0)
 
 
-def sweep_kernel(parts, order, *refs):
-    list_refs, tile_refs, vector_refs = refs[:6], refs[6:9], refs[9:14]
-    out_refs, (held, total, tiles, sems) = refs[14:18], refs[18:]
+def sweep_kernel(parts, *refs):
+    list_refs, tile_refs, vector_refs = refs[:4], refs[4:6], refs[6:11]
+    out_refs, (held, total, tiles, sems) = refs[11:15], refs[15:]
     vecs = vector_refs[0].shape[0]
 
     def copy(k, at):
@@ -273,8 +277,8 @@
         place = pl.ds((STARTS[k] + at) * UNROLL, UNROLL)
         return pltpu.make_async_copy(tile_refs[k].at[span], tiles.at[place], sems.at[STARTS[k] + at])
 
-    groups = [lax.div(list_refs[2 * k][COUNT] + (UNROLL - 1), UNROLL) for k in range(REACH)]
-    for k in range(REACH):
+    groups = [lax.div(list_refs[2 * k][COUNT] + (UNROLL - 1), UNROLL) for k in range(len(HOPS))]
+    for k in range(len(HOPS)):
 
         def fetch(at, _, k=k):
             copy(k, at).start()
@@ -282,24 +286,26 @@
 
         lax.fori_loop(0, groups[k], fetch, 0)
 
-    own, other, ahead, behind, far = vector_refs
+    own, other, beside, swapped, far = vector_refs
     for k, vectors in enumerate(
-        (own[...], other[...], ahead[0], ahead[1], behind[0], behind[1], far[...])
+        (own[...], other[...], beside[0], swapped[0], beside[1], swapped[1], far[...])
     ):
         both = stacked(vectors)
         for c in range(2):
             held[2 * k + c] = both[:, c * BLOCK : (c + 1) * BLOCK]
     total[...] = jnp.zeros_like(total)
 
-    for k, hop in enumerate(order):
-        slots = [window_slot(hop, side) for side in range(2)]
+    for k, hops in enumerate(HOPS):
+        slots = [window_slot(hop, side) for hop in hops for side in range(2)]
 
         def step(at, _, k=k, slots=slots, rows_ref=list_refs[2 * k], cols_ref=list_refs[2 * k + 1]):
             copy(k, at).wait()
             terms = []
             for n in range(UNROLL):
                 block = cols_ref[UNROLL * at + n]
-                slot = jnp.where(block >= 4, 0, jnp.where(block >= 2, slots[1], slots[0]))
+                slot = 0
+                for at_slot, found in enumerate(slots):
+                    slot = jnp.where(lax.shift_right_logical(block, 1) == at_slot, found, slot)
                 block = 2 * slot + (block & 1)
                 tile = tiles[(STARTS[k] + at) * UNROLL + n]
                 terms.append(jnp.dot(held[block], tile, preferred_element_type=jnp.float32))
@@ -317,7 +323,7 @@
             out_refs[e][:, pl.ds(r * BLOCK, BLOCK)] = result
 
 
-def sweep(near, order, tiles):
+def sweep(near, tiles):
     own = near[0]
     vecs = own.shape[0]
     smem = pl.BlockSpec(memory_space=pltpu.SMEM)
@@ -325,8 +331,8 @@
     parts = 1 if own.dtype == jnp.bfloat16 else 2
     lists = [part for tile in tiles for part in tile[1:]]
     return pl.pallas_call(
-        functools.partial(sweep_kernel, parts, order),
-        in_specs=[smem] * 6 + [pl.BlockSpec(memory_space=pl.ANY)] * 3 + [vmem] * 5,
+        functools.partial(sweep_kernel, parts),
+        in_specs=[smem] * 4 + [pl.BlockSpec(memory_space=pl.ANY)] * 2 + [vmem] * 5,
         out_specs=[vmem] * 4,
         out_shape=[jax.ShapeDtypeStruct((vecs, LENGTH), jnp.float32)] * 4,
         scratch_shapes=[
@@ -448,15 +454,14 @@
         near[h] = shifted(source, "space", 1 if h > 0 else -1)
     blocks, rate = row_operands(members)
     listed = jnp.stack([member[MASK_ROW, : REACH * PAIRS] for member in members]).astype(jnp.int32)
-
-    order = (2, 1, 3)
+    listed = listed.reshape(N_SUB * REACH * PAIRS)
+
     tiles = []
     carried = payload
-    for at, h in enumerate(order):
-        span = slice((h - 1) * PAIRS, h * PAIRS)
-        mine = listed[:, span].reshape(N_SUB * PAIRS)
+    for at, hops in enumerate(HOPS):
+        windows = [near[side * h] for h in hops for side in (1, -1)]
         *tile, carried = hop_tiles(
-            h, at == 0, at == REACH - 1, mine, blocks, rate, near[h], near[-h], carried
+            hops, at == 0, at == len(HOPS) - 1, listed, blocks, rate, windows, carried
         )
         tiles.append(tile)
     degree = carried
@@ -471,9 +476,9 @@
         )(root, *exchanged(parts))
 
     scaled = (root * start_vectors).astype(jnp.bfloat16)
-    raw, first_gram = imaged(sweep(space_window(scaled), order, tiles), True)
-
-    image, second_gram = imaged(sweep(space_window(raw), order, tiles), False)
+    raw, first_gram = imaged(sweep(space_window(scaled), tiles), True)
+
+    image, second_gram = imaged(sweep(space_window(raw), tiles), False)
     grams = summed(jnp.concatenate([first_gram, second_gram], 0))
     subspace, sound = pl.pallas_call(
         solve_both_kernel,

time: 139 us -> 140 us (level)
  starting transfers between devices: 47.6 us -> 53.3 us
  Pallas kernels: 29.8 us -> 27.7 us
  waiting for transfers between devices: 26.2 us -> 24.6 us
    ppermute x4 -> x6, starting transfers between devices: 8.01 us -> 13.1 us  [the longest x2 9.38 us: space_window(): return (value, other, beside, lax.ppermute(beside, 'space', swap), far)]
    ppermute x4 -> x6, waiting for transfers between devices: 10.6 us -> 6.35 us  [the longest x2 6.34 us: space_window(): lax.ppermute(value, 'space', far)]
    ppermute x22, waiting for transfers between devices: 15.5 us -> 18.2 us  [shifted(): lax.ppermute(value, axis, [((at + steps) % count, at) for at in range(cou...]
    pallas_call x5 -> x4, Pallas kernels: 21.6 us -> 19.5 us  [the longest x2 11.9 us: hop_tiles(): pl.pallas_call(functools.partial(tile_kernel, hops, first, last), in_spec...]
    all_to_all x2, blocking collectives: 30.7 us -> 29.3 us  [summed(): lax.all_to_all(sent, ('space', 'sub'), 0, 0, axis_index_groups=groups)]
  transfers between devices with their start and end apart: 26 -> 28, of which waited for: 13 -> 14; matrix products, arithmetic and copies ran while one was open for 0% -> 0% of each run, Pallas kernels for 7% -> 4%
where the time goes in v3:
time: 140 us; the launch traced here: 139 us
  starting transfers between devices  53.3 us (38%)
  blocking collectives  29.3 us (21%)
  Pallas kernels  27.7 us (20%)
  waiting for transfers between devices  24.6 us (18%)
  local copies, waits for them, and re-layouts  3.32 us (2%)
    ppermute x22, starting transfers between devices, shifted(): lax.ppermute(value, axis, [((at + steps) % count, at) for at in range(cou...  40.2 us
    all_to_all x2, blocking collectives, summed(): lax.all_to_all(sent, ('space', 'sub'), 0, 0, axis_index_groups=groups)  29.3 us
    ppermute x22, waiting for transfers between devices, shifted(): lax.ppermute(value, axis, [((at + steps) % count, at) for at in range(cou...  18.2 us
    pallas_call x2, Pallas kernels, hop_tiles(): pl.pallas_call(functools.partial(tile_kernel, hops, first, last), in_spec...  11.9 us
    ppermute x2, starting transfers between devices, space_window(): return (value, other, beside, lax.ppermute(beside, 'space', swap), far)  9.38 us
    pallas_call x2, Pallas kernels, sweep(): pl.pallas_call(functools.partial(sweep_kernel, parts), in_specs=[smem] *...  7.62 us
    pallas_call x1, Pallas kernels, on_device(): pl.pallas_call(solve_both_kernel, in_specs=[pl.BlockSpec(memory_space=plt...  6.55 us
    ppermute x2, waiting for transfers between devices, space_window(): lax.ppermute(value, 'space', far)  6.34 us
  transfers between devices with their start and end apart: 28, of which 14 were waited for; matrix products, arithmetic and copies ran while one was open for 0% of the time, Pallas kernels for 4%

profile of v3, /device:TPU:1, one launch (start us, length us, event | category | flops | bytes accessed | tf_op | source)
XLA Modules:
  0.0 139.2 jit_solution(14067517712444155524)
XLA Ops:
  0.0 0.7 broadcast_in_dim.14.scale_ref
  0.7 0.8 copy.9.pairs_ref
  1.4 1.0 copy-done
  2.4 1.0 shard_map.48.refs_0_.refs_2_
  3.4 2.1 %collective-permute-start.4 = (bf16[304,512]{1,0:T(8,128)(2,1)S(1)}, bf16[304,512]{1,0:T(8,128)(2,1)S(1)}, u32[]{:S(2)}, u32[]{:S(2)}) collective-permute-start(bf16[304,512]{1,0:T(8,128)(2,1)S(1)} %shard_map.48.refs_0_.refs_2_), channel_id=1, source_target_pairs={{248,0},{252,4},{0,8},{4,12},{8,16},{12,20},{16,24},{20,28},{24,32... | collective-permute-start | bytes 933896 | tf_op jit(solution)/shard_map/ppermute | solution.py:37
  5.5 6.6 %collective-permute-start.3 = (bf16[304,512]{1,0:T(8,128)(2,1)S(1)}, bf16[304,512]{1,0:T(8,128)(2,1)S(1)}, u32[]{:S(2)}, u32[]{:S(2)}) collective-permute-start(bf16[304,512]{1,0:T(8,128)(2,1)S(1)} %shard_map.48.refs_0_.refs_2_), channel_id=1, source_target_pairs={{8,0},{12,4},{16,8},{20,12},{24,16},{28,20},{32,24},{36,28},{40,32... | collective-permute-start | bytes 933896 | tf_op jit(solution)/shard_map/ppermute | solution.py:37
  12.2 1.3 collective-permute-start.2
  13.5 2.6 %collective-permute-start.1 = (bf16[304,512]{1,0:T(8,128)(2,1)S(1)}, bf16[304,512]{1,0:T(8,128)(2,1)S(1)}, u32[]{:S(2)}, u32[]{:S(2)}) collective-permute-start(bf16[304,512]{1,0:T(8,128)(2,1)S(1)} %shard_map.48.refs_0_.refs_2_), channel_id=1, source_target_pairs={{2,0},{3,1},{0,2},{1,3},{6,4},{7,5},{4,6},{5,7},{10,8},{11,9},{8,1... | collective-permute-start | bytes 933896 | tf_op jit(solution)/shard_map/ppermute | solution.py:37
  16.1 1.1 collective-permute-start
  17.2 2.0 %collective-permute-done.4.refs_1_ = bf16[304,512]{1,0:T(8,128)(2,1)S(1)} collective-permute-done((bf16[304,512]{1,0:T(8,128)(2,1)S(1)}, bf16[304,512]{1,0:T(8,128)(2,1)S(1)}, u32[]{:S(2)}, u32[]{:S(2)}) %collective-permute-start.4) | collective-permute-done | bytes 311328 | tf_op jit(solution)/shard_map/ppermute | solution.py:37
  19.2 1.2 collective-permute-start.5
  20.4 1.0 collective-permute-done.2.refs_3_
  21.4 4.1 %collective-permute-start.7 = (bf16[304,512]{1,0:T(8,128)(2,1)S(1)}, bf16[304,512]{1,0:T(8,128)(2,1)S(1)}, u32[]{:S(2)}, u32[]{:S(2)}) collective-permute-start(bf16[304,512]{1,0:T(8,128)(2,1)S(1)} %collective-permute-done.3.refs_0_), channel_id=1, source_target_pairs={{4,0},{8,4},{12,8},{16,12},{20,16},{24,20},{28,24},{32,28},{36,32}... | collective-permute-start | bytes 933896 | tf_op jit(solution)/shard_map/ppermute | solution.py:37
  25.5 3.7 %collective-permute-done.1.refs_2_ = bf16[304,512]{1,0:T(8,128)(2,1)S(1)} collective-permute-done((bf16[304,512]{1,0:T(8,128)(2,1)S(1)}, bf16[304,512]{1,0:T(8,128)(2,1)S(1)}, u32[]{:S(2)}, u32[]{:S(2)}) %collective-permute-start.1) | collective-permute-done | bytes 311328 | tf_op jit(solution)/shard_map/ppermute | solution.py:37
  29.4 0.3 shard_map.49
  29.7 4.9 %shard_map.50 = (bf16[40,256,256]{2,1,0:T(8,128)(2,1)S(1)}, s32[80]{0:T(128)S(1)}, s32[80]{0:T(128)S(1)}, f32[9,8,256]{2,1,0:T(8,128)S(1)}) custom-call(s32[192]{0:T(256)S(1)} %reshape.20.mine_ref, bf16[8,320,256]{2,1,0:T(8,128)(2,1)S(1)} %get-tuple-element.44.blocks_ref, f32[8,8,256]{2,1,0:T(8,128)S(1)} %get-tuple-element.45.rate_ref, ...), custom_call_target="tpu_custom_call" | custom-call | flops 671088640 | bytes 7340032 | tf_op jit(solution)/shard_map/pallas_call | solution.py:235
  34.6 7.0 %shard_map.51 = (bf16[64,256,256]{2,1,0:T(8,128)(2,1)S(1)}, s32[80]{0:T(128)S(1)}, s32[80]{0:T(128)S(1)}, f32[4,8,512]{2,1,0:T(8,128)S(1)}) custom-call(s32[192]{0:T(256)S(1)} %reshape.20.mine_ref, bf16[8,320,256]{2,1,0:T(8,128)(2,1)S(1)} %get-tuple-element.44.blocks_ref, f32[8,8,256]{2,1,0:T(8,128)S(1)} %get-tuple-element.45.rate_ref, ...), custom_call_target="tpu_custom_call" | custom-call | flops 1342177280 | bytes 7340032 | tf_op jit(solution)/shard_map/pallas_call | solution.py:235
  41.6 0.6 collective-permute-start.11
  42.2 1.2 collective-permute-start.10
  43.5 0.6 collective-permute-start.9
  44.1 2.0 %collective-permute-done.10 = f32[1,512]{1,0:T(1,128)S(1)} collective-permute-done((f32[1,512]{1,0:T(1,128)S(1)}, f32[1,512]{1,0:T(1,128)S(1)}, u32[]{:S(2)}, u32[]{:S(2)}) %collective-permute-start.10) | collective-permute-done | bytes 2080 | tf_op jit(solution)/shard_map/ppermute | solution.py:37
  46.2 0.9 collective-permute-done.9
  47.2 5.2 %collective-permute-start.13 = (bf16[32,512]{1,0:T(8,128)(2,1)S(1)}, bf16[32,512]{1,0:T(8,128)(2,1)S(1)}, u32[]{:S(2)}, u32[]{:S(2)}) collective-permute-start(bf16[32,512]{1,0:T(8,128)(2,1)S(1)} %multiply_convert_fusion.refs_6_), channel_id=1, source_target_pairs={{8,0},{12,4},{16,8},{20,12},{24,16},{28,20},{32,24},{36,28},{40,32... | collective-permute-start | bytes 98312 | tf_op jit(solution)/shard_map/ppermute | solution.py:37
  52.4 1.2 collective-permute-done.14
  53.6 7.0 %collective-permute-start.15 = (bf16[2,32,512]{2,1,0:T(8,128)(2,1)S(1)}, bf16[2,32,512]{2,1,0:T(8,128)(2,1)S(1)}, u32[]{:S(2)}, u32[]{:S(2)}) collective-permute-start(bf16[2,32,512]{2,1,0:T(8,128)(2,1)S(1)} %pad_maximum_fusion.1.refs_8_), channel_id=1, source_target_pairs={{0,4},{4,0},{8,12},{12,8},{16,20},{20,16},{24,28},{28,24},{32,36},... | collective-permute-start | bytes 196616 | tf_op jit(solution)/shard_map/ppermute | solution.py:46
  60.6 1.6 %collective-permute-start.12 = (bf16[32,512]{1,0:T(8,128)(2,1)S(1)}, bf16[32,512]{1,0:T(8,128)(2,1)S(1)}, u32[]{:S(2)}, u32[]{:S(2)}) collective-permute-start(bf16[32,512]{1,0:T(8,128)(2,1)S(1)} %multiply_convert_fusion.refs_6_), channel_id=1, source_target_pairs={{0,4},{4,0},{8,12},{12,8},{16,20},{20,16},{24,28},{28,24},{32,36},... | collective-permute-start | bytes 98312 | tf_op jit(solution)/shard_map/ppermute | solution.py:44
  62.2 3.3 %collective-permute-done.16.refs_10_ = bf16[32,512]{1,0:T(8,128)(2,1)S(1)} collective-permute-done((bf16[32,512]{1,0:T(8,128)(2,1)S(1)}, bf16[32,512]{1,0:T(8,128)(2,1)S(1)}, u32[]{:S(2)}, u32[]{:S(2)}) %collective-permute-start.16) | collective-permute-done | bytes 32800 | tf_op jit(solution)/shard_map/ppermute | solution.py:44
  65.5 3.7 %shard_map.52 = (f32[32,512]{1,0:T(8,128)S(1)}, f32[32,512]{1,0:T(8,128)S(1)}, f32[32,512]{1,0:T(8,128)S(1)}, f32[32,512]{1,0:T(8,128)S(1)}) custom-call(s32[80]{0:T(128)S(1)} %get-tuple-element.51.refs_0_, s32[80]{0:T(128)S(1)} %get-tuple-element.52.refs_1_, s32[80]{0:T(128)S(1)} %get-tuple-element.53.refs_2_, s32[80]{0:T(128)S(1)} %get-tuple-element.54.refs_3_, ...), custom_call_target="tpu_custom_call" | custom-call | flops 838860800 | bytes 7340032 | tf_op jit(solution)/shard_map/pallas_call | solution.py:333
  69.3 1.8 %collective-permute-start.18 = (f32[32,512]{1,0:T(8,128)S(1)}, f32[32,512]{1,0:T(8,128)S(1)}, u32[]{:S(2)}, u32[]{:S(2)}) collective-permute-start(f32[32,512]{1,0:T(8,128)S(1)} %get-tuple-element.59), channel_id=1, source_target_pairs={{2,0},{3,1},{0,2},{1,3},{6,4},{7,5},{4,6},{5,7},{10,8},{11,9},{8,1... | collective-permute-start | bytes 196616 | tf_op jit(solution)/shard_map/ppermute | solution.py:37
  71.1 0.9 collective-permute-start.19
  72.0 2.3 %collective-permute-done.17.refs_1_ = f32[32,512]{1,0:T(8,128)S(1)} collective-permute-done((f32[32,512]{1,0:T(8,128)S(1)}, f32[32,512]{1,0:T(8,128)S(1)}, u32[]{:S(2)}, u32[]{:S(2)}) %collective-permute-start.17) | collective-permute-done | bytes 65568 | tf_op jit(solution)/shard_map/ppermute | solution.py:37
  74.3 0.6 collective-permute-done.19.refs_3_
  74.9 0.2 shard_map.53
  75.1 3.1 %collective-permute-start.22 = (f32[32,512]{1,0:T(8,128)S(1)}, f32[32,512]{1,0:T(8,128)S(1)}, u32[]{:S(2)}, u32[]{:S(2)}) collective-permute-start(f32[32,512]{1,0:T(8,128)S(1)} %get-tuple-element.62.refs_6_), channel_id=1, source_target_pairs={{248,0},{252,4},{0,8},{4,12},{8,16},{12,20},{16,24},{20,28},{24,32... | collective-permute-start | bytes 196616 | tf_op jit(solution)/shard_map/ppermute | solution.py:37
  78.2 4.7 %collective-permute-start.21 = (f32[32,512]{1,0:T(8,128)S(1)}, f32[32,512]{1,0:T(8,128)S(1)}, u32[]{:S(2)}, u32[]{:S(2)}) collective-permute-start(f32[32,512]{1,0:T(8,128)S(1)} %get-tuple-element.62.refs_6_), channel_id=1, source_target_pairs={{8,0},{12,4},{16,8},{20,12},{24,16},{28,20},{32,24},{36,28},{40,32... | collective-permute-start | bytes 196616 | tf_op jit(solution)/shard_map/ppermute | solution.py:37
  82.9 1.6 %collective-permute-done.22 = f32[32,512]{1,0:T(8,128)S(1)} collective-permute-done((f32[32,512]{1,0:T(8,128)S(1)}, f32[32,512]{1,0:T(8,128)S(1)}, u32[]{:S(2)}, u32[]{:S(2)}) %collective-permute-start.22) | collective-permute-done | bytes 65568 | tf_op jit(solution)/shard_map/ppermute | solution.py:37
  84.4 2.4 %collective-permute-start.23 = (f32[2,32,512]{2,1,0:T(8,128)S(1)}, f32[2,32,512]{2,1,0:T(8,128)S(1)}, u32[]{:S(2)}, u32[]{:S(2)}) collective-permute-start(f32[2,32,512]{2,1,0:T(8,128)S(1)} %pad_maximum_fusion.refs_8_), channel_id=1, source_target_pairs={{0,4},{4,0},{8,12},{12,8},{16,20},{20,16},{24,28},{28,24},{32,36},... | collective-permute-start | bytes 393224 | tf_op jit(solution)/shard_map/ppermute | solution.py:46
  86.8 2.1 %collective-permute-start.20 = (f32[32,512]{1,0:T(8,128)S(1)}, f32[32,512]{1,0:T(8,128)S(1)}, u32[]{:S(2)}, u32[]{:S(2)}) collective-permute-start(f32[32,512]{1,0:T(8,128)S(1)} %get-tuple-element.62.refs_6_), channel_id=1, source_target_pairs={{0,4},{4,0},{8,12},{12,8},{16,20},{20,16},{24,28},{28,24},{32,36},... | collective-permute-start | bytes 196616 | tf_op jit(solution)/shard_map/ppermute | solution.py:44
  89.0 3.1 %collective-permute-done.24.refs_10_ = f32[32,512]{1,0:T(8,128)S(1)} collective-permute-done((f32[32,512]{1,0:T(8,128)S(1)}, f32[32,512]{1,0:T(8,128)S(1)}, u32[]{:S(2)}, u32[]{:S(2)}) %collective-permute-start.24) | collective-permute-done | bytes 65568 | tf_op jit(solution)/shard_map/ppermute | solution.py:44
  92.0 3.9 %shard_map.54 = (f32[32,512]{1,0:T(8,128)S(1)}, f32[32,512]{1,0:T(8,128)S(1)}, f32[32,512]{1,0:T(8,128)S(1)}, f32[32,512]{1,0:T(8,128)S(1)}) custom-call(s32[80]{0:T(128)S(1)} %get-tuple-element.51.refs_0_, s32[80]{0:T(128)S(1)} %get-tuple-element.52.refs_1_, s32[80]{0:T(128)S(1)} %get-tuple-element.53.refs_2_, s32[80]{0:T(128)S(1)} %get-tuple-element.54.refs_3_, ...), custom_call_target="tpu_custom_call" | custom-call | flops 838860800 | bytes 7340032 | tf_op jit(solution)/shard_map/pallas_call | solution.py:333
  96.0 1.6 %collective-permute-start.26 = (f32[32,512]{1,0:T(8,128)S(1)}, f32[32,512]{1,0:T(8,128)S(1)}, u32[]{:S(2)}, u32[]{:S(2)}) collective-permute-start(f32[32,512]{1,0:T(8,128)S(1)} %get-tuple-element.65), channel_id=1, source_target_pairs={{2,0},{3,1},{0,2},{1,3},{6,4},{7,5},{4,6},{5,7},{10,8},{11,9},{8,1... | collective-permute-start | bytes 196616 | tf_op jit(solution)/shard_map/ppermute | solution.py:37
  97.7 1.3 collective-permute-start.27
  98.9 2.1 %collective-permute-done.25.refs_1_ = f32[32,512]{1,0:T(8,128)S(1)} collective-permute-done((f32[32,512]{1,0:T(8,128)S(1)}, f32[32,512]{1,0:T(8,128)S(1)}, u32[]{:S(2)}, u32[]{:S(2)}) %collective-permute-start.25) | collective-permute-done | bytes 65568 | tf_op jit(solution)/shard_map/ppermute | solution.py:37
  101.0 0.6 collective-permute-done.27.refs_3_
  101.9 16.2 %all_to_all.20 = f32[32,16,128]{2,1,0:T(8,128)S(1)} all-to-all(f32[32,16,128]{2,1,0:T(8,128)S(1)} %broadcast_in_dim.31), channel_id=1, replica_groups={{0,1,2,3,4,5,6,7,8,9,10,11,12,13,14,15,16,17,18,19,20,21,22,23,24,25,26..., dimensions={0} | all-to-all | bytes 524288 | tf_op jit(solution)/shard_map/all_to_all | solution.py:70
  118.2 13.1 %all_to_all.21 = f32[8,16,128]{2,1,0:T(8,128)S(1)} all-to-all(f32[8,16,128]{2,1,0:T(8,128)S(1)} %broadcast_in_dim.32), channel_id=1, replica_groups={{0,32,64,96,128,160,192,224},{1,33,65,97,129,161,193,225},{2,34,66,98,1..., dimensions={0} | all-to-all | bytes 131072 | tf_op jit(solution)/shard_map/all_to_all | solution.py:70
  131.3 6.5 %shard_map.56 = (f32[32,512]{1,0:T(8,128)S(1)}, s32[1]{0:T(128)}) custom-call(f32[64,32]{1,0:T(8,128)S(1)} %reshape.19.grams_ref, f32[32,512]{1,0:T(8,128)S(1)} %get-tuple-element.68.image_ref), custom_call_target="tpu_custom_call" | custom-call | flops 1048576 | bytes 131072 | tf_op jit(solution)/shard_map/pallas_call | solution.py:483
  138.6 0.6 copy-done.2
  (46 shorter events, 1.0 us)
Async XLA Ops:
  1.4 1.0 copy-start
  2.4 44.7 %copy-start.1 = (f32[32,512]{1,0:T(8,128)S(1)}, f32[32,512]{1,0:T(8,128)}, u32[]{:S(2)}) copy-start(f32[32,512]{1,0:T(8,128)} %param.8) | copy-start | bytes 196612
  3.4 15.8 %collective-permute-start.4 = (bf16[304,512]{1,0:T(8,128)(2,1)S(1)}, bf16[304,512]{1,0:T(8,128)(2,1)S(1)}, u32[]{:S(2)}, u32[]{:S(2)}) collective-permute-start(bf16[304,512]{1,0:T(8,128)(2,1)S(1)} %shard_map.48.refs_0_.refs_2_), channel_id=1, source_target_pairs={{248,0},{252,4},{0,8},{4,12},{8,16},{12,20},{16,24},{20,28},{24,32... | collective-permute-start | bytes 933896 | tf_op jit(solution)/shard_map/ppermute | solution.py:37
  5.5 13.6 %collective-permute-start.3 = (bf16[304,512]{1,0:T(8,128)(2,1)S(1)}, bf16[304,512]{1,0:T(8,128)(2,1)S(1)}, u32[]{:S(2)}, u32[]{:S(2)}) collective-permute-start(bf16[304,512]{1,0:T(8,128)(2,1)S(1)} %shard_map.48.refs_0_.refs_2_), channel_id=1, source_target_pairs={{8,0},{12,4},{16,8},{20,12},{24,16},{28,20},{32,24},{36,28},{40,32... | collective-permute-start | bytes 933896 | tf_op jit(solution)/shard_map/ppermute | solution.py:37
  12.2 9.2 %collective-permute-start.2 = (bf16[304,512]{1,0:T(8,128)(2,1)S(1)}, bf16[304,512]{1,0:T(8,128)(2,1)S(1)}, u32[]{:S(2)}, u32[]{:S(2)}) collective-permute-start(bf16[304,512]{1,0:T(8,128)(2,1)S(1)} %shard_map.48.refs_0_.refs_2_), channel_id=1, source_target_pairs={{3,0},{0,1},{1,2},{2,3},{7,4},{4,5},{5,6},{6,7},{11,8},{8,9},{9,10... | collective-permute-start | bytes 933896 | tf_op jit(solution)/shard_map/ppermute | solution.py:37
  13.5 15.7 %collective-permute-start.1 = (bf16[304,512]{1,0:T(8,128)(2,1)S(1)}, bf16[304,512]{1,0:T(8,128)(2,1)S(1)}, u32[]{:S(2)}, u32[]{:S(2)}) collective-permute-start(bf16[304,512]{1,0:T(8,128)(2,1)S(1)} %shard_map.48.refs_0_.refs_2_), channel_id=1, source_target_pairs={{2,0},{3,1},{0,2},{1,3},{6,4},{7,5},{4,6},{5,7},{10,8},{11,9},{8,1... | collective-permute-start | bytes 933896 | tf_op jit(solution)/shard_map/ppermute | solution.py:37
  16.1 13.2 %collective-permute-start = (bf16[304,512]{1,0:T(8,128)(2,1)S(1)}, bf16[304,512]{1,0:T(8,128)(2,1)S(1)}, u32[]{:S(2)}, u32[]{:S(2)}) collective-permute-start(bf16[304,512]{1,0:T(8,128)(2,1)S(1)} %shard_map.48.refs_0_.refs_2_), channel_id=1, source_target_pairs={{1,0},{2,1},{3,2},{0,3},{5,4},{6,5},{7,6},{4,7},{9,8},{10,9},{11,1... | collective-permute-start | bytes 933896 | tf_op jit(solution)/shard_map/ppermute | solution.py:37
  19.2 15.4 %collective-permute-start.6 = (bf16[304,512]{1,0:T(8,128)(2,1)S(1)}, bf16[304,512]{1,0:T(8,128)(2,1)S(1)}, u32[]{:S(2)}, u32[]{:S(2)}) collective-permute-start(bf16[304,512]{1,0:T(8,128)(2,1)S(1)} %shard_map.48.refs_0_.refs_2_), channel_id=1, source_target_pairs={{252,0},{0,4},{4,8},{8,12},{12,16},{16,20},{20,24},{24,28},{28,32}... | collective-permute-start | bytes 933896 | tf_op jit(solution)/shard_map/ppermute | solution.py:37
  19.2 15.4 %collective-permute-start.5 = (bf16[304,512]{1,0:T(8,128)(2,1)S(1)}, bf16[304,512]{1,0:T(8,128)(2,1)S(1)}, u32[]{:S(2)}, u32[]{:S(2)}) collective-permute-start(bf16[304,512]{1,0:T(8,128)(2,1)S(1)} %shard_map.48.refs_0_.refs_2_), channel_id=1, source_target_pairs={{4,0},{8,4},{12,8},{16,12},{20,16},{24,20},{28,24},{32,28},{36,32}... | collective-permute-start | bytes 933896 | tf_op jit(solution)/shard_map/ppermute | solution.py:37
  21.4 13.2 %collective-permute-start.7 = (bf16[304,512]{1,0:T(8,128)(2,1)S(1)}, bf16[304,512]{1,0:T(8,128)(2,1)S(1)}, u32[]{:S(2)}, u32[]{:S(2)}) collective-permute-start(bf16[304,512]{1,0:T(8,128)(2,1)S(1)} %collective-permute-done.3.refs_0_), channel_id=1, source_target_pairs={{4,0},{8,4},{12,8},{16,12},{20,16},{24,20},{28,24},{32,28},{36,32}... | collective-permute-start | bytes 933896 | tf_op jit(solution)/shard_map/ppermute | solution.py:37
  29.2 5.4 %collective-permute-start.8 = (bf16[304,512]{1,0:T(8,128)(2,1)S(1)}, bf16[304,512]{1,0:T(8,128)(2,1)S(1)}, u32[]{:S(2)}, u32[]{:S(2)}) collective-permute-start(bf16[304,512]{1,0:T(8,128)(2,1)S(1)} %collective-permute-done.4.refs_1_), channel_id=1, source_target_pairs={{252,0},{0,4},{4,8},{8,12},{12,16},{16,20},{20,24},{24,28},{28,32}... | collective-permute-start | bytes 933896 | tf_op jit(solution)/shard_map/ppermute | solution.py:37
  41.6 2.5 %collective-permute-start.11 = (f32[1,512]{1,0:T(1,128)S(1)}, f32[1,512]{1,0:T(1,128)S(1)}, u32[]{:S(2)}, u32[]{:S(2)}) collective-permute-start(f32[1,512]{1,0:T(1,128)S(1)} %get-tuple-element.72), channel_id=1, source_target_pairs={{1,0},{2,1},{3,2},{0,3},{5,4},{6,5},{7,6},{4,7},{9,8},{10,9},{11,1... | collective-permute-start | bytes 6152 | tf_op jit(solution)/shard_map/ppermute | solution.py:37
  42.2 3.9 %collective-permute-start.10 = (f32[1,512]{1,0:T(1,128)S(1)}, f32[1,512]{1,0:T(1,128)S(1)}, u32[]{:S(2)}, u32[]{:S(2)}) collective-permute-start(f32[1,512]{1,0:T(1,128)S(1)} %get-tuple-element.73), channel_id=1, source_target_pairs={{2,0},{3,1},{0,2},{1,3},{6,4},{7,5},{4,6},{5,7},{10,8},{11,9},{8,1... | collective-permute-start | bytes 6152 | tf_op jit(solution)/shard_map/ppermute | solution.py:37
  43.5 3.6 %collective-permute-start.9 = (f32[1,512]{1,0:T(1,128)S(1)}, f32[1,512]{1,0:T(1,128)S(1)}, u32[]{:S(2)}, u32[]{:S(2)}) collective-permute-start(f32[1,512]{1,0:T(1,128)S(1)} %get-tuple-element.74), channel_id=1, source_target_pairs={{3,0},{0,1},{1,2},{2,3},{7,4},{4,5},{5,6},{6,7},{11,8},{8,9},{9,10... | collective-permute-start | bytes 6152 | tf_op jit(solution)/shard_map/ppermute | solution.py:37
  47.2 6.5 %collective-permute-start.14 = (bf16[32,512]{1,0:T(8,128)(2,1)S(1)}, bf16[32,512]{1,0:T(8,128)(2,1)S(1)}, u32[]{:S(2)}, u32[]{:S(2)}) collective-permute-start(bf16[32,512]{1,0:T(8,128)(2,1)S(1)} %multiply_convert_fusion.refs_6_), channel_id=1, source_target_pairs={{248,0},{252,4},{0,8},{4,12},{8,16},{12,20},{16,24},{20,28},{24,32... | collective-permute-start | bytes 98312 | tf_op jit(solution)/shard_map/ppermute | solution.py:37
  47.2 6.4 %collective-permute-start.13 = (bf16[32,512]{1,0:T(8,128)(2,1)S(1)}, bf16[32,512]{1,0:T(8,128)(2,1)S(1)}, u32[]{:S(2)}, u32[]{:S(2)}) collective-permute-start(bf16[32,512]{1,0:T(8,128)(2,1)S(1)} %multiply_convert_fusion.refs_6_), channel_id=1, source_target_pairs={{8,0},{12,4},{16,8},{20,12},{24,16},{28,20},{32,24},{36,28},{40,32... | collective-permute-start | bytes 98312 | tf_op jit(solution)/shard_map/ppermute | solution.py:37
  53.6 11.8 %collective-permute-start.15 = (bf16[2,32,512]{2,1,0:T(8,128)(2,1)S(1)}, bf16[2,32,512]{2,1,0:T(8,128)(2,1)S(1)}, u32[]{:S(2)}, u32[]{:S(2)}) collective-permute-start(bf16[2,32,512]{2,1,0:T(8,128)(2,1)S(1)} %pad_maximum_fusion.1.refs_8_), channel_id=1, source_target_pairs={{0,4},{4,0},{8,12},{12,8},{16,20},{20,16},{24,28},{28,24},{32,36},... | collective-permute-start | bytes 196616 | tf_op jit(solution)/shard_map/ppermute | solution.py:46
  60.6 4.8 %collective-permute-start.16 = (bf16[32,512]{1,0:T(8,128)(2,1)S(1)}, bf16[32,512]{1,0:T(8,128)(2,1)S(1)}, u32[]{:S(2)}, u32[]{:S(2)}) collective-permute-start(bf16[32,512]{1,0:T(8,128)(2,1)S(1)} %multiply_convert_fusion.refs_6_), channel_id=1, source_target_pairs={{0,244},{4,16},{8,252},{12,24},{16,4},{20,32},{24,12},{28,40},{32,... | collective-permute-start | bytes 98312 | tf_op jit(solution)/shard_map/ppermute | solution.py:44
  60.6 4.8 %collective-permute-start.12 = (bf16[32,512]{1,0:T(8,128)(2,1)S(1)}, bf16[32,512]{1,0:T(8,128)(2,1)S(1)}, u32[]{:S(2)}, u32[]{:S(2)}) collective-permute-start(bf16[32,512]{1,0:T(8,128)(2,1)S(1)} %multiply_convert_fusion.refs_6_), channel_id=1, source_target_pairs={{0,4},{4,0},{8,12},{12,8},{16,20},{20,16},{24,28},{28,24},{32,36},... | collective-permute-start | bytes 98312 | tf_op jit(solution)/shard_map/ppermute | solution.py:44
  69.2 5.1 %collective-permute-start.17 = (f32[32,512]{1,0:T(8,128)S(1)}, f32[32,512]{1,0:T(8,128)S(1)}, u32[]{:S(2)}, u32[]{:S(2)}) collective-permute-start(f32[32,512]{1,0:T(8,128)S(1)} %get-tuple-element.58), channel_id=1, source_target_pairs={{3,0},{0,1},{1,2},{2,3},{7,4},{4,5},{5,6},{6,7},{11,8},{8,9},{9,10... | collective-permute-start | bytes 196616 | tf_op jit(solution)/shard_map/ppermute | solution.py:37
  69.3 5.0 %collective-permute-start.18 = (f32[32,512]{1,0:T(8,128)S(1)}, f32[32,512]{1,0:T(8,128)S(1)}, u32[]{:S(2)}, u32[]{:S(2)}) collective-permute-start(f32[32,512]{1,0:T(8,128)S(1)} %get-tuple-element.59), channel_id=1, source_target_pairs={{2,0},{3,1},{0,2},{1,3},{6,4},{7,5},{4,6},{5,7},{10,8},{11,9},{8,1... | collective-permute-start | bytes 196616 | tf_op jit(solution)/shard_map/ppermute | solution.py:37
  71.1 3.8 %collective-permute-start.19 = (f32[32,512]{1,0:T(8,128)S(1)}, f32[32,512]{1,0:T(8,128)S(1)}, u32[]{:S(2)}, u32[]{:S(2)}) collective-permute-start(f32[32,512]{1,0:T(8,128)S(1)} %get-tuple-element.60), channel_id=1, source_target_pairs={{1,0},{2,1},{3,2},{0,3},{5,4},{6,5},{7,6},{4,7},{9,8},{10,9},{11,1... | collective-permute-start | bytes 196616 | tf_op jit(solution)/shard_map/ppermute | solution.py:37
  75.1 9.3 %collective-permute-start.22 = (f32[32,512]{1,0:T(8,128)S(1)}, f32[32,512]{1,0:T(8,128)S(1)}, u32[]{:S(2)}, u32[]{:S(2)}) collective-permute-start(f32[32,512]{1,0:T(8,128)S(1)} %get-tuple-element.62.refs_6_), channel_id=1, source_target_pairs={{248,0},{252,4},{0,8},{4,12},{8,16},{12,20},{16,24},{20,28},{24,32... | collective-permute-start | bytes 196616 | tf_op jit(solution)/shard_map/ppermute | solution.py:37
  78.2 6.2 %collective-permute-start.21 = (f32[32,512]{1,0:T(8,128)S(1)}, f32[32,512]{1,0:T(8,128)S(1)}, u32[]{:S(2)}, u32[]{:S(2)}) collective-permute-start(f32[32,512]{1,0:T(8,128)S(1)} %get-tuple-element.62.refs_6_), channel_id=1, source_target_pairs={{8,0},{12,4},{16,8},{20,12},{24,16},{28,20},{32,24},{36,28},{40,32... | collective-permute-start | bytes 196616 | tf_op jit(solution)/shard_map/ppermute | solution.py:37
  84.4 7.6 %collective-permute-start.23 = (f32[2,32,512]{2,1,0:T(8,128)S(1)}, f32[2,32,512]{2,1,0:T(8,128)S(1)}, u32[]{:S(2)}, u32[]{:S(2)}) collective-permute-start(f32[2,32,512]{2,1,0:T(8,128)S(1)} %pad_maximum_fusion.refs_8_), channel_id=1, source_target_pairs={{0,4},{4,0},{8,12},{12,8},{16,20},{20,16},{24,28},{28,24},{32,36},... | collective-permute-start | bytes 393224 | tf_op jit(solution)/shard_map/ppermute | solution.py:46
  86.8 5.2 %collective-permute-start.24 = (f32[32,512]{1,0:T(8,128)S(1)}, f32[32,512]{1,0:T(8,128)S(1)}, u32[]{:S(2)}, u32[]{:S(2)}) collective-permute-start(f32[32,512]{1,0:T(8,128)S(1)} %get-tuple-element.62.refs_6_), channel_id=1, source_target_pairs={{0,244},{4,16},{8,252},{12,24},{16,4},{20,32},{24,12},{28,40},{32,... | collective-permute-start | bytes 196616 | tf_op jit(solution)/shard_map/ppermute | solution.py:44
  86.8 5.2 %collective-permute-start.20 = (f32[32,512]{1,0:T(8,128)S(1)}, f32[32,512]{1,0:T(8,128)S(1)}, u32[]{:S(2)}, u32[]{:S(2)}) collective-permute-start(f32[32,512]{1,0:T(8,128)S(1)} %get-tuple-element.62.refs_6_), channel_id=1, source_target_pairs={{0,4},{4,0},{8,12},{12,8},{16,20},{20,16},{24,28},{28,24},{32,36},... | collective-permute-start | bytes 196616 | tf_op jit(solution)/shard_map/ppermute | solution.py:44
  95.9 5.1 %collective-permute-start.25 = (f32[32,512]{1,0:T(8,128)S(1)}, f32[32,512]{1,0:T(8,128)S(1)}, u32[]{:S(2)}, u32[]{:S(2)}) collective-permute-start(f32[32,512]{1,0:T(8,128)S(1)} %get-tuple-element.64), channel_id=1, source_target_pairs={{3,0},{0,1},{1,2},{2,3},{7,4},{4,5},{5,6},{6,7},{11,8},{8,9},{9,10... | collective-permute-start | bytes 196616 | tf_op jit(solution)/shard_map/ppermute | solution.py:37
  96.0 5.0 %collective-permute-start.26 = (f32[32,512]{1,0:T(8,128)S(1)}, f32[32,512]{1,0:T(8,128)S(1)}, u32[]{:S(2)}, u32[]{:S(2)}) collective-permute-start(f32[32,512]{1,0:T(8,128)S(1)} %get-tuple-element.65), channel_id=1, source_target_pairs={{2,0},{3,1},{0,2},{1,3},{6,4},{7,5},{4,6},{5,7},{10,8},{11,9},{8,1... | collective-permute-start | bytes 196616 | tf_op jit(solution)/shard_map/ppermute | solution.py:37
  97.7 3.9 %collective-permute-start.27 = (f32[32,512]{1,0:T(8,128)S(1)}, f32[32,512]{1,0:T(8,128)S(1)}, u32[]{:S(2)}, u32[]{:S(2)}) collective-permute-start(f32[32,512]{1,0:T(8,128)S(1)} %get-tuple-element.66), channel_id=1, source_target_pairs={{1,0},{2,1},{3,2},{0,3},{5,4},{6,5},{7,6},{4,7},{9,8},{10,9},{11,1... | collective-permute-start | bytes 196616 | tf_op jit(solution)/shard_map/ppermute | solution.py:37
  138.6 0.6 copy-start.2

commit v4 on v3

--- a/solution.py
+++ b/solution.py
@@ -21,6 +21,7 @@
 COUNT = SLOTS - 1
 NOBODY = 2 * N_SUB
 UNROLL = 8
+AT_ONCE = 16
 HALF = UNROLL // 2
 HOPS = ((2,), (1, 3))
 STARTS = (0, 5)
@@ -41,8 +42,15 @@
     count = lax.axis_size("space")
     swap = [(at, at ^ 1) for at in range(count)]
     far = [(at, (at + (3 if at % 2 else -3)) % count) for at in range(count)]
-    other, far = lax.ppermute(value, "space", swap), lax.ppermute(value, "space", far)
-    beside = jnp.stack([shifted(value, "space", 2), shifted(value, "space", -2)])
+    other, far, ahead, behind = lax.optimization_barrier(
+        (
+            lax.ppermute(value, "space", swap),
+            lax.ppermute(value, "space", far),
+            shifted(value, "space", 2),
+            shifted(value, "space", -2),
+        )
+    )
+    beside = jnp.stack([ahead, behind])
     return value, other, beside, lax.ppermute(beside, "space", swap), far
 
 
@@ -364,9 +372,18 @@
     across = lax.broadcasted_iota(jnp.int32, (count, count), 1)
     identity = jnp.where(across == place, 1.0, 0.0)
     joined = jnp.concatenate([gram, identity], 1)
-    for k in range(count):
-        column = jnp.where(place > k, joined[:, k : k + 1], 0.0)
-        joined = joined - column * (joined[k : k + 1, :] * (1.0 / joined[k : k + 1, k : k + 1]))
+    for k in range(0, count, AT_ONCE):
+        columns = [
+            jnp.broadcast_to(joined[:, k + n : k + n + 1], joined.shape) for n in range(AT_ONCE)
+        ]
+        rows = [joined[k + n : k + n + 1, :] for n in range(AT_ONCE)]
+        for n in range(AT_ONCE):
+            at = slice(k + n, k + n + 1)
+            factor = jnp.where(place > k + n, columns[n] * (1.0 / columns[n][at]), 0.0)
+            for m in range(n + 1, AT_ONCE):
+                columns[m] = columns[m] - factor * columns[m][at]
+                rows[m] = rows[m] - factor[k + m : k + m + 1] * rows[n]
+            joined = joined - factor * rows[n]
     pivots = jnp.sum(joined[:, :count] * identity, axis=1, keepdims=True)
     diagonal = jnp.sum(gram * identity, axis=1, keepdims=True)
     return joined[:, count:] / jnp.sqrt(pivots), jnp.min(pivots / diagonal)
@@ -414,8 +431,8 @@
     space_at, sub_at = lax.axis_index("space"), lax.axis_index("sub")
     lane = lax.broadcasted_iota(jnp.int32, (1, LENGTH), 1)
     used = jnp.zeros((1, LENGTH), jnp.float32)
-    for k in range(pairs_ref.shape[0]):
-        row, col = pairs_ref[k, 0], pairs_ref[k, 1]
+    for k in range(pairs_ref.shape[1]):
+        row, col = pairs_ref[0, k], pairs_ref[1, k]
         device = lax.shift_right_logical(col, 1)
         hop = lax.rem(lax.div(device, n_sub) - space_at + n_space, n_space)
         across = lax.rem(lax.rem(device, n_sub) - sub_at + n_sub, n_sub)
@@ -425,7 +442,7 @@
     payload_ref[ROWS - 16 :] = jnp.concatenate(
         [
             data_ref[ROWS - 16 : FEAT].astype(jnp.float32),
-            scale_ref[...].astype(jnp.float32),
+            scale_ref[...].astype(jnp.float32).reshape(1, LENGTH),
             used,
             jnp.zeros((ROWS - MASK_ROW - 1, LENGTH), jnp.float32),
         ],
@@ -445,7 +462,7 @@
         in_specs=[pl.BlockSpec(memory_space=pltpu.SMEM)] + [pl.BlockSpec(memory_space=pltpu.VMEM)] * 2,
         out_shape=jax.ShapeDtypeStruct((ROWS, length), jnp.bfloat16),
         **light,
-    )(pair_list, trajectories, kernel_scale[None, :])
+    )(pair_list.T, trajectories, kernel_scale)
 
     members = [payload] + [shifted(payload, "sub", e) for e in range(1, N_SUB)]
     near = {h: shifted(payload, "space", h) for h in (2, -2)}

time: 140 us -> 133 us (0.950)
  Pallas kernels: 27.7 us -> 23.6 us
  blocking collectives: 29.3 us -> 25.6 us
    pallas_call x1, Pallas kernels: 6.55 us -> 2.6 us  [on_device(): pl.pallas_call(solve_both_kernel, in_specs=[pl.BlockSpec(memory_space=plt...]
    all_to_all x2, blocking collectives: 29.3 us -> 25.6 us  [summed(): lax.all_to_all(sent, ('space', 'sub'), 0, 0, axis_index_groups=groups)]
    ppermute x2, starting transfers between devices: 3.69 us -> 6.7 us  [space_window(): lax.ppermute(value, 'space', swap)]
    ppermute x2, waiting for transfers between devices: 6.34 us -> 3.54 us  [space_window(): lax.ppermute(value, 'space', far)]
    ppermute x22, starting transfers between devices: 40.2 us -> 37.4 us  [shifted(): lax.ppermute(value, axis, [((at + steps) % count, at) for at in range(cou...]
    ppermute x2, waiting for transfers between devices: 0.01 us -> 1.89 us  [space_window(): return (value, other, beside, lax.ppermute(beside, 'space', swap), far)]
    unnamed x7 -> x10, local copies, waits for them, and re-layouts: 2.35 us -> 2.95 us
where the time goes in v4:
time: 133 us; the launch traced here: 132 us
  starting transfers between devices  53.9 us (41%)
  blocking collectives  25.6 us (19%)
  waiting for transfers between devices  25.2 us (19%)
  Pallas kernels  23.6 us (18%)
  local copies, waits for them, and re-layouts  3.24 us (2%)
    ppermute x22, starting transfers between devices, shifted(): lax.ppermute(value, axis, [((at + steps) % count, at) for at in range(cou...  37.4 us
    all_to_all x2, blocking collectives, summed(): lax.all_to_all(sent, ('space', 'sub'), 0, 0, axis_index_groups=groups)  25.6 us
    ppermute x22, waiting for transfers between devices, shifted(): lax.ppermute(value, axis, [((at + steps) % count, at) for at in range(cou...  18.9 us
    pallas_call x2, Pallas kernels, hop_tiles(): pl.pallas_call(functools.partial(tile_kernel, hops, first, last), in_spec...  11.9 us
    ppermute x2, starting transfers between devices, space_window(): return (value, other, beside, lax.ppermute(beside, 'space', swap), far)  9.72 us
    pallas_call x2, Pallas kernels, sweep(): pl.pallas_call(functools.partial(sweep_kernel, parts), in_specs=[smem] *...  7.6 us
    ppermute x2, starting transfers between devices, space_window(): lax.ppermute(value, 'space', swap)  6.7 us
    ppermute x2, waiting for transfers between devices, space_window(): lax.ppermute(value, 'space', far)  3.54 us
  transfers between devices with their start and end apart: 28, of which 14 were waited for; matrix products, arithmetic and copies ran while one was open for 0% of the time, Pallas kernels for 4%

profile of v4, /device:TPU:1, one launch (start us, length us, event | category | flops | bytes accessed | tf_op | source)
XLA Modules:
  0.0 132.5 jit_solution(14161889498430342466)
XLA Ops:
  0.0 1.0 copy-done
  1.0 0.7 copy-done.1
  1.6 0.7 copy-done.2
  2.3 0.8 shard_map.48.refs_0_.refs_2_
  3.1 2.1 %collective-permute-start.4 = (bf16[304,512]{1,0:T(8,128)(2,1)S(1)}, bf16[304,512]{1,0:T(8,128)(2,1)S(1)}, u32[]{:S(2)}, u32[]{:S(2)}) collective-permute-start(bf16[304,512]{1,0:T(8,128)(2,1)S(1)} %shard_map.48.refs_0_.refs_2_), channel_id=1, source_target_pairs={{248,0},{252,4},{0,8},{4,12},{8,16},{12,20},{16,24},{20,28},{24,32... | collective-permute-start | bytes 933896 | tf_op jit(solution)/shard_map/ppermute | solution.py:38
  5.3 6.6 %collective-permute-start.3 = (bf16[304,512]{1,0:T(8,128)(2,1)S(1)}, bf16[304,512]{1,0:T(8,128)(2,1)S(1)}, u32[]{:S(2)}, u32[]{:S(2)}) collective-permute-start(bf16[304,512]{1,0:T(8,128)(2,1)S(1)} %shard_map.48.refs_0_.refs_2_), channel_id=1, source_target_pairs={{8,0},{12,4},{16,8},{20,12},{24,16},{28,20},{32,24},{36,28},{40,32... | collective-permute-start | bytes 933896 | tf_op jit(solution)/shard_map/ppermute | solution.py:38
  11.9 1.3 collective-permute-start.2
  13.2 2.6 %collective-permute-start.1 = (bf16[304,512]{1,0:T(8,128)(2,1)S(1)}, bf16[304,512]{1,0:T(8,128)(2,1)S(1)}, u32[]{:S(2)}, u32[]{:S(2)}) collective-permute-start(bf16[304,512]{1,0:T(8,128)(2,1)S(1)} %shard_map.48.refs_0_.refs_2_), channel_id=1, source_target_pairs={{2,0},{3,1},{0,2},{1,3},{6,4},{7,5},{4,6},{5,7},{10,8},{11,9},{8,1... | collective-permute-start | bytes 933896 | tf_op jit(solution)/shard_map/ppermute | solution.py:38
  15.8 1.1 collective-permute-start
  16.9 2.0 %collective-permute-done.4.refs_1_ = bf16[304,512]{1,0:T(8,128)(2,1)S(1)} collective-permute-done((bf16[304,512]{1,0:T(8,128)(2,1)S(1)}, bf16[304,512]{1,0:T(8,128)(2,1)S(1)}, u32[]{:S(2)}, u32[]{:S(2)}) %collective-permute-start.4) | collective-permute-done | bytes 311328 | tf_op jit(solution)/shard_map/ppermute | solution.py:38
  18.9 1.2 collective-permute-start.5
  20.1 1.0 collective-permute-done.2.refs_3_
  21.1 4.1 %collective-permute-start.7 = (bf16[304,512]{1,0:T(8,128)(2,1)S(1)}, bf16[304,512]{1,0:T(8,128)(2,1)S(1)}, u32[]{:S(2)}, u32[]{:S(2)}) collective-permute-start(bf16[304,512]{1,0:T(8,128)(2,1)S(1)} %collective-permute-done.3.refs_0_), channel_id=1, source_target_pairs={{4,0},{8,4},{12,8},{16,12},{20,16},{24,20},{28,24},{32,28},{36,32}... | collective-permute-start | bytes 933896 | tf_op jit(solution)/shard_map/ppermute | solution.py:38
  25.2 3.7 %collective-permute-done.1.refs_2_ = bf16[304,512]{1,0:T(8,128)(2,1)S(1)} collective-permute-done((bf16[304,512]{1,0:T(8,128)(2,1)S(1)}, bf16[304,512]{1,0:T(8,128)(2,1)S(1)}, u32[]{:S(2)}, u32[]{:S(2)}) %collective-permute-start.1) | collective-permute-done | bytes 311328 | tf_op jit(solution)/shard_map/ppermute | solution.py:38
  29.1 0.3 shard_map.49
  29.4 4.9 %shard_map.50 = (bf16[40,256,256]{2,1,0:T(8,128)(2,1)S(1)}, s32[80]{0:T(128)S(1)}, s32[80]{0:T(128)S(1)}, f32[9,8,256]{2,1,0:T(8,128)S(1)}) custom-call(s32[192]{0:T(256)S(1)} %reshape.20.mine_ref, bf16[8,320,256]{2,1,0:T(8,128)(2,1)S(1)} %get-tuple-element.52.blocks_ref, f32[8,8,256]{2,1,0:T(8,128)S(1)} %get-tuple-element.53.rate_ref, ...), custom_call_target="tpu_custom_call" | custom-call | flops 671088640 | bytes 7340032 | tf_op jit(solution)/shard_map/pallas_call | solution.py:243
  34.4 7.0 %shard_map.51 = (bf16[64,256,256]{2,1,0:T(8,128)(2,1)S(1)}, s32[80]{0:T(128)S(1)}, s32[80]{0:T(128)S(1)}, f32[4,8,512]{2,1,0:T(8,128)S(1)}) custom-call(s32[192]{0:T(256)S(1)} %reshape.20.mine_ref, bf16[8,320,256]{2,1,0:T(8,128)(2,1)S(1)} %get-tuple-element.52.blocks_ref, f32[8,8,256]{2,1,0:T(8,128)S(1)} %get-tuple-element.53.rate_ref, ...), custom_call_target="tpu_custom_call" | custom-call | flops 1342177280 | bytes 7340032 | tf_op jit(solution)/shard_map/pallas_call | solution.py:243
  41.4 1.5 %collective-permute-start.11 = (f32[1,512]{1,0:T(1,128)S(1)}, f32[1,512]{1,0:T(1,128)S(1)}, u32[]{:S(2)}, u32[]{:S(2)}) collective-permute-start(f32[1,512]{1,0:T(1,128)S(1)} %get-tuple-element.88), channel_id=1, source_target_pairs={{1,0},{2,1},{3,2},{0,3},{5,4},{6,5},{7,6},{4,7},{9,8},{10,9},{11,1... | collective-permute-start | bytes 6152 | tf_op jit(solution)/shard_map/ppermute | solution.py:38
  42.8 0.9 collective-permute-start.10
  43.9 2.9 %collective-permute-done.10 = f32[1,512]{1,0:T(1,128)S(1)} collective-permute-done((f32[1,512]{1,0:T(1,128)S(1)}, f32[1,512]{1,0:T(1,128)S(1)}, u32[]{:S(2)}, u32[]{:S(2)}) %collective-permute-start.10) | collective-permute-done | bytes 2080 | tf_op jit(solution)/shard_map/ppermute | solution.py:38
  46.8 0.6 collective-permute-done.9
  47.5 5.5 %collective-permute-start.14 = (bf16[32,512]{1,0:T(8,128)(2,1)S(1)}, bf16[32,512]{1,0:T(8,128)(2,1)S(1)}, u32[]{:S(2)}, u32[]{:S(2)}) collective-permute-start(bf16[32,512]{1,0:T(8,128)(2,1)S(1)} %multiply_convert_fusion.refs_6_), channel_id=1, source_target_pairs={{8,0},{12,4},{16,8},{20,12},{24,16},{28,20},{32,24},{36,28},{40,32... | collective-permute-start | bytes 98312 | tf_op jit(solution)/shard_map/ppermute | solution.py:38
  53.0 5.4 %collective-permute-start.12 = (bf16[32,512]{1,0:T(8,128)(2,1)S(1)}, bf16[32,512]{1,0:T(8,128)(2,1)S(1)}, u32[]{:S(2)}, u32[]{:S(2)}) collective-permute-start(bf16[32,512]{1,0:T(8,128)(2,1)S(1)} %multiply_convert_fusion.refs_6_), channel_id=1, source_target_pairs={{0,4},{4,0},{8,12},{12,8},{16,20},{20,16},{24,28},{28,24},{32,36},... | collective-permute-start | bytes 98312 | tf_op jit(solution)/shard_map/ppermute | solution.py:47
  58.4 0.8 collective-permute-done.12.refs_7_
  59.2 6.2 %collective-permute-start.16 = (bf16[2,32,512]{2,1,0:T(8,128)(2,1)S(1)}, bf16[2,32,512]{2,1,0:T(8,128)(2,1)S(1)}, u32[]{:S(2)}, u32[]{:S(2)}) collective-permute-start(bf16[2,32,512]{2,1,0:T(8,128)(2,1)S(1)} %pad_maximum_fusion.1.refs_8_), channel_id=1, source_target_pairs={{0,4},{4,0},{8,12},{12,8},{16,20},{20,16},{24,28},{28,24},{32,36},... | collective-permute-start | bytes 196616 | tf_op jit(solution)/shard_map/ppermute | solution.py:54
  65.4 0.9 collective-permute-done.16.refs_9_
  66.3 3.7 %shard_map.52 = (f32[32,512]{1,0:T(8,128)S(1)}, f32[32,512]{1,0:T(8,128)S(1)}, f32[32,512]{1,0:T(8,128)S(1)}, f32[32,512]{1,0:T(8,128)S(1)}) custom-call(s32[80]{0:T(128)S(1)} %get-tuple-element.59.refs_0_, s32[80]{0:T(128)S(1)} %get-tuple-element.60.refs_1_, s32[80]{0:T(128)S(1)} %get-tuple-element.61.refs_2_, s32[80]{0:T(128)S(1)} %get-tuple-element.62.refs_3_, ...), custom_call_target="tpu_custom_call" | custom-call | flops 838860800 | bytes 7340032 | tf_op jit(solution)/shard_map/pallas_call | solution.py:341
  70.0 0.3 collective-permute-start.17
  70.3 2.0 %collective-permute-start.18 = (f32[32,512]{1,0:T(8,128)S(1)}, f32[32,512]{1,0:T(8,128)S(1)}, u32[]{:S(2)}, u32[]{:S(2)}) collective-permute-start(f32[32,512]{1,0:T(8,128)S(1)} %get-tuple-element.71), channel_id=1, source_target_pairs={{2,0},{3,1},{0,2},{1,3},{6,4},{7,5},{4,6},{5,7},{10,8},{11,9},{8,1... | collective-permute-start | bytes 196616 | tf_op jit(solution)/shard_map/ppermute | solution.py:38
  72.3 0.5 collective-permute-start.19
  72.8 3.9 %collective-permute-done.17.refs_1_ = f32[32,512]{1,0:T(8,128)S(1)} collective-permute-done((f32[32,512]{1,0:T(8,128)S(1)}, f32[32,512]{1,0:T(8,128)S(1)}, u32[]{:S(2)}, u32[]{:S(2)}) %collective-permute-start.17) | collective-permute-done | bytes 65568 | tf_op jit(solution)/shard_map/ppermute | solution.py:38
  76.8 0.3 collective-permute-done.19.refs_3_
  77.1 0.2 shard_map.53
  77.4 4.8 %collective-permute-start.22 = (f32[32,512]{1,0:T(8,128)S(1)}, f32[32,512]{1,0:T(8,128)S(1)}, u32[]{:S(2)}, u32[]{:S(2)}) collective-permute-start(f32[32,512]{1,0:T(8,128)S(1)} %get-tuple-element.74.refs_6_), channel_id=1, source_target_pairs={{8,0},{12,4},{16,8},{20,12},{24,16},{28,20},{32,24},{36,28},{40,32... | collective-permute-start | bytes 196616 | tf_op jit(solution)/shard_map/ppermute | solution.py:38
  82.1 1.3 %collective-permute-start.20 = (f32[32,512]{1,0:T(8,128)S(1)}, f32[32,512]{1,0:T(8,128)S(1)}, u32[]{:S(2)}, u32[]{:S(2)}) collective-permute-start(f32[32,512]{1,0:T(8,128)S(1)} %get-tuple-element.74.refs_6_), channel_id=1, source_target_pairs={{0,4},{4,0},{8,12},{12,8},{16,20},{20,16},{24,28},{28,24},{32,36},... | collective-permute-start | bytes 196616 | tf_op jit(solution)/shard_map/ppermute | solution.py:47
  83.5 0.3 collective-permute-done.23
  83.8 3.5 %collective-permute-done.21.refs_10_ = f32[32,512]{1,0:T(8,128)S(1)} collective-permute-done((f32[32,512]{1,0:T(8,128)S(1)}, f32[32,512]{1,0:T(8,128)S(1)}, u32[]{:S(2)}, u32[]{:S(2)}) %collective-permute-start.21) | collective-permute-done | bytes 65568 | tf_op jit(solution)/shard_map/ppermute | solution.py:48
  87.4 3.5 %collective-permute-start.24 = (f32[2,32,512]{2,1,0:T(8,128)S(1)}, f32[2,32,512]{2,1,0:T(8,128)S(1)}, u32[]{:S(2)}, u32[]{:S(2)}) collective-permute-start(f32[2,32,512]{2,1,0:T(8,128)S(1)} %pad_maximum_fusion.refs_8_), channel_id=1, source_target_pairs={{0,4},{4,0},{8,12},{12,8},{16,20},{20,16},{24,28},{28,24},{32,36},... | collective-permute-start | bytes 393224 | tf_op jit(solution)/shard_map/ppermute | solution.py:54
  90.9 1.0 collective-permute-done.24.refs_9_
  91.9 3.9 %shard_map.54 = (f32[32,512]{1,0:T(8,128)S(1)}, f32[32,512]{1,0:T(8,128)S(1)}, f32[32,512]{1,0:T(8,128)S(1)}, f32[32,512]{1,0:T(8,128)S(1)}) custom-call(s32[80]{0:T(128)S(1)} %get-tuple-element.59.refs_0_, s32[80]{0:T(128)S(1)} %get-tuple-element.60.refs_1_, s32[80]{0:T(128)S(1)} %get-tuple-element.61.refs_2_, s32[80]{0:T(128)S(1)} %get-tuple-element.62.refs_3_, ...), custom_call_target="tpu_custom_call" | custom-call | flops 838860800 | bytes 7340032 | tf_op jit(solution)/shard_map/pallas_call | solution.py:341
  95.9 2.5 %collective-permute-start.26 = (f32[32,512]{1,0:T(8,128)S(1)}, f32[32,512]{1,0:T(8,128)S(1)}, u32[]{:S(2)}, u32[]{:S(2)}) collective-permute-start(f32[32,512]{1,0:T(8,128)S(1)} %get-tuple-element.81), channel_id=1, source_target_pairs={{2,0},{3,1},{0,2},{1,3},{6,4},{7,5},{4,6},{5,7},{10,8},{11,9},{8,1... | collective-permute-start | bytes 196616 | tf_op jit(solution)/shard_map/ppermute | solution.py:38
  98.3 0.2 collective-permute-start.27
  98.5 4.0 %collective-permute-done.25.refs_1_ = f32[32,512]{1,0:T(8,128)S(1)} collective-permute-done((f32[32,512]{1,0:T(8,128)S(1)}, f32[32,512]{1,0:T(8,128)S(1)}, u32[]{:S(2)}, u32[]{:S(2)}) %collective-permute-start.25) | collective-permute-done | bytes 65568 | tf_op jit(solution)/shard_map/ppermute | solution.py:38
  102.5 0.2 shard_map.55
  102.8 13.4 %all_to_all.20 = f32[32,16,128]{2,1,0:T(8,128)S(1)} all-to-all(f32[32,16,128]{2,1,0:T(8,128)S(1)} %broadcast_in_dim.13), channel_id=1, replica_groups={{0,1,2,3,4,5,6,7,8,9,10,11,12,13,14,15,16,17,18,19,20,21,22,23,24,25,26..., dimensions={0} | all-to-all | bytes 524288 | tf_op jit(solution)/shard_map/all_to_all | solution.py:78
  116.3 12.2 %all_to_all.21 = f32[8,16,128]{2,1,0:T(8,128)S(1)} all-to-all(f32[8,16,128]{2,1,0:T(8,128)S(1)} %broadcast_in_dim.28), channel_id=1, replica_groups={{0,32,64,96,128,160,192,224},{1,33,65,97,129,161,193,225},{2,34,66,98,1..., dimensions={0} | all-to-all | bytes 131072 | tf_op jit(solution)/shard_map/all_to_all | solution.py:78
  128.6 2.6 %shard_map.56 = (f32[32,512]{1,0:T(8,128)S(1)}, s32[1]{0:T(128)}) custom-call(f32[64,32]{1,0:T(8,128)S(1)} %reshape.19.grams_ref, f32[32,512]{1,0:T(8,128)S(1)} %get-tuple-element.84.image_ref), custom_call_target="tpu_custom_call" | custom-call | flops 1048576 | bytes 131072 | tf_op jit(solution)/shard_map/pallas_call | solution.py:500
  131.9 0.6 copy-done.4
  (48 shorter events, 0.9 us)
Async XLA Ops:
  0.0 1.0 copy-start
  1.0 0.7 copy-start.1
  1.6 0.7 copy-start.2
  2.3 45.0 %copy-start.3 = (f32[32,512]{1,0:T(8,128)S(1)}, f32[32,512]{1,0:T(8,128)}, u32[]{:S(2)}) copy-start(f32[32,512]{1,0:T(8,128)} %param.8) | copy-start | bytes 196612
  3.1 15.8 %collective-permute-start.4 = (bf16[304,512]{1,0:T(8,128)(2,1)S(1)}, bf16[304,512]{1,0:T(8,128)(2,1)S(1)}, u32[]{:S(2)}, u32[]{:S(2)}) collective-permute-start(bf16[304,512]{1,0:T(8,128)(2,1)S(1)} %shard_map.48.refs_0_.refs_2_), channel_id=1, source_target_pairs={{248,0},{252,4},{0,8},{4,12},{8,16},{12,20},{16,24},{20,28},{24,32... | collective-permute-start | bytes 933896 | tf_op jit(solution)/shard_map/ppermute | solution.py:38
  5.3 13.6 %collective-permute-start.3 = (bf16[304,512]{1,0:T(8,128)(2,1)S(1)}, bf16[304,512]{1,0:T(8,128)(2,1)S(1)}, u32[]{:S(2)}, u32[]{:S(2)}) collective-permute-start(bf16[304,512]{1,0:T(8,128)(2,1)S(1)} %shard_map.48.refs_0_.refs_2_), channel_id=1, source_target_pairs={{8,0},{12,4},{16,8},{20,12},{24,16},{28,20},{32,24},{36,28},{40,32... | collective-permute-start | bytes 933896 | tf_op jit(solution)/shard_map/ppermute | solution.py:38
  11.9 9.2 %collective-permute-start.2 = (bf16[304,512]{1,0:T(8,128)(2,1)S(1)}, bf16[304,512]{1,0:T(8,128)(2,1)S(1)}, u32[]{:S(2)}, u32[]{:S(2)}) collective-permute-start(bf16[304,512]{1,0:T(8,128)(2,1)S(1)} %shard_map.48.refs_0_.refs_2_), channel_id=1, source_target_pairs={{3,0},{0,1},{1,2},{2,3},{7,4},{4,5},{5,6},{6,7},{11,8},{8,9},{9,10... | collective-permute-start | bytes 933896 | tf_op jit(solution)/shard_map/ppermute | solution.py:38
  13.2 15.7 %collective-permute-start.1 = (bf16[304,512]{1,0:T(8,128)(2,1)S(1)}, bf16[304,512]{1,0:T(8,128)(2,1)S(1)}, u32[]{:S(2)}, u32[]{:S(2)}) collective-permute-start(bf16[304,512]{1,0:T(8,128)(2,1)S(1)} %shard_map.48.refs_0_.refs_2_), channel_id=1, source_target_pairs={{2,0},{3,1},{0,2},{1,3},{6,4},{7,5},{4,6},{5,7},{10,8},{11,9},{8,1... | collective-permute-start | bytes 933896 | tf_op jit(solution)/shard_map/ppermute | solution.py:38
  15.8 13.2 %collective-permute-start = (bf16[304,512]{1,0:T(8,128)(2,1)S(1)}, bf16[304,512]{1,0:T(8,128)(2,1)S(1)}, u32[]{:S(2)}, u32[]{:S(2)}) collective-permute-start(bf16[304,512]{1,0:T(8,128)(2,1)S(1)} %shard_map.48.refs_0_.refs_2_), channel_id=1, source_target_pairs={{1,0},{2,1},{3,2},{0,3},{5,4},{6,5},{7,6},{4,7},{9,8},{10,9},{11,1... | collective-permute-start | bytes 933896 | tf_op jit(solution)/shard_map/ppermute | solution.py:38
  18.9 15.4 %collective-permute-start.6 = (bf16[304,512]{1,0:T(8,128)(2,1)S(1)}, bf16[304,512]{1,0:T(8,128)(2,1)S(1)}, u32[]{:S(2)}, u32[]{:S(2)}) collective-permute-start(bf16[304,512]{1,0:T(8,128)(2,1)S(1)} %shard_map.48.refs_0_.refs_2_), channel_id=1, source_target_pairs={{252,0},{0,4},{4,8},{8,12},{12,16},{16,20},{20,24},{24,28},{28,32}... | collective-permute-start | bytes 933896 | tf_op jit(solution)/shard_map/ppermute | solution.py:38
  18.9 15.5 %collective-permute-start.5 = (bf16[304,512]{1,0:T(8,128)(2,1)S(1)}, bf16[304,512]{1,0:T(8,128)(2,1)S(1)}, u32[]{:S(2)}, u32[]{:S(2)}) collective-permute-start(bf16[304,512]{1,0:T(8,128)(2,1)S(1)} %shard_map.48.refs_0_.refs_2_), channel_id=1, source_target_pairs={{4,0},{8,4},{12,8},{16,12},{20,16},{24,20},{28,24},{32,28},{36,32}... | collective-permute-start | bytes 933896 | tf_op jit(solution)/shard_map/ppermute | solution.py:38
  21.1 13.2 %collective-permute-start.7 = (bf16[304,512]{1,0:T(8,128)(2,1)S(1)}, bf16[304,512]{1,0:T(8,128)(2,1)S(1)}, u32[]{:S(2)}, u32[]{:S(2)}) collective-permute-start(bf16[304,512]{1,0:T(8,128)(2,1)S(1)} %collective-permute-done.3.refs_0_), channel_id=1, source_target_pairs={{4,0},{8,4},{12,8},{16,12},{20,16},{24,20},{28,24},{32,28},{36,32}... | collective-permute-start | bytes 933896 | tf_op jit(solution)/shard_map/ppermute | solution.py:38
  28.9 5.4 %collective-permute-start.8 = (bf16[304,512]{1,0:T(8,128)(2,1)S(1)}, bf16[304,512]{1,0:T(8,128)(2,1)S(1)}, u32[]{:S(2)}, u32[]{:S(2)}) collective-permute-start(bf16[304,512]{1,0:T(8,128)(2,1)S(1)} %collective-permute-done.4.refs_1_), channel_id=1, source_target_pairs={{252,0},{0,4},{4,8},{8,12},{12,16},{16,20},{20,24},{24,28},{28,32}... | collective-permute-start | bytes 933896 | tf_op jit(solution)/shard_map/ppermute | solution.py:38
  41.4 2.5 %collective-permute-start.11 = (f32[1,512]{1,0:T(1,128)S(1)}, f32[1,512]{1,0:T(1,128)S(1)}, u32[]{:S(2)}, u32[]{:S(2)}) collective-permute-start(f32[1,512]{1,0:T(1,128)S(1)} %get-tuple-element.88), channel_id=1, source_target_pairs={{1,0},{2,1},{3,2},{0,3},{5,4},{6,5},{7,6},{4,7},{9,8},{10,9},{11,1... | collective-permute-start | bytes 6152 | tf_op jit(solution)/shard_map/ppermute | solution.py:38
  42.8 3.9 %collective-permute-start.10 = (f32[1,512]{1,0:T(1,128)S(1)}, f32[1,512]{1,0:T(1,128)S(1)}, u32[]{:S(2)}, u32[]{:S(2)}) collective-permute-start(f32[1,512]{1,0:T(1,128)S(1)} %get-tuple-element.89), channel_id=1, source_target_pairs={{2,0},{3,1},{0,2},{1,3},{6,4},{7,5},{4,6},{5,7},{10,8},{11,9},{8,1... | collective-permute-start | bytes 6152 | tf_op jit(solution)/shard_map/ppermute | solution.py:38
  43.7 3.6 %collective-permute-start.9 = (f32[1,512]{1,0:T(1,128)S(1)}, f32[1,512]{1,0:T(1,128)S(1)}, u32[]{:S(2)}, u32[]{:S(2)}) collective-permute-start(f32[1,512]{1,0:T(1,128)S(1)} %get-tuple-element.90), channel_id=1, source_target_pairs={{3,0},{0,1},{1,2},{2,3},{7,4},{4,5},{5,6},{6,7},{11,8},{8,9},{9,10... | collective-permute-start | bytes 6152 | tf_op jit(solution)/shard_map/ppermute | solution.py:38
  47.4 11.0 %collective-permute-start.15 = (bf16[32,512]{1,0:T(8,128)(2,1)S(1)}, bf16[32,512]{1,0:T(8,128)(2,1)S(1)}, u32[]{:S(2)}, u32[]{:S(2)}) collective-permute-start(bf16[32,512]{1,0:T(8,128)(2,1)S(1)} %multiply_convert_fusion.refs_6_), channel_id=1, source_target_pairs={{248,0},{252,4},{0,8},{4,12},{8,16},{12,20},{16,24},{20,28},{24,32... | collective-permute-start | bytes 98312 | tf_op jit(solution)/shard_map/ppermute | solution.py:38
  47.5 10.9 %collective-permute-start.14 = (bf16[32,512]{1,0:T(8,128)(2,1)S(1)}, bf16[32,512]{1,0:T(8,128)(2,1)S(1)}, u32[]{:S(2)}, u32[]{:S(2)}) collective-permute-start(bf16[32,512]{1,0:T(8,128)(2,1)S(1)} %multiply_convert_fusion.refs_6_), channel_id=1, source_target_pairs={{8,0},{12,4},{16,8},{20,12},{24,16},{28,20},{32,24},{36,28},{40,32... | collective-permute-start | bytes 98312 | tf_op jit(solution)/shard_map/ppermute | solution.py:38
  53.0 5.4 %collective-permute-start.13 = (bf16[32,512]{1,0:T(8,128)(2,1)S(1)}, bf16[32,512]{1,0:T(8,128)(2,1)S(1)}, u32[]{:S(2)}, u32[]{:S(2)}) collective-permute-start(bf16[32,512]{1,0:T(8,128)(2,1)S(1)} %multiply_convert_fusion.refs_6_), channel_id=1, source_target_pairs={{0,244},{4,16},{8,252},{12,24},{16,4},{20,32},{24,12},{28,40},{32,... | collective-permute-start | bytes 98312 | tf_op jit(solution)/shard_map/ppermute | solution.py:48
  53.0 6.2 %collective-permute-start.12 = (bf16[32,512]{1,0:T(8,128)(2,1)S(1)}, bf16[32,512]{1,0:T(8,128)(2,1)S(1)}, u32[]{:S(2)}, u32[]{:S(2)}) collective-permute-start(bf16[32,512]{1,0:T(8,128)(2,1)S(1)} %multiply_convert_fusion.refs_6_), channel_id=1, source_target_pairs={{0,4},{4,0},{8,12},{12,8},{16,20},{20,16},{24,28},{28,24},{32,36},... | collective-permute-start | bytes 98312 | tf_op jit(solution)/shard_map/ppermute | solution.py:47
  59.2 7.1 %collective-permute-start.16 = (bf16[2,32,512]{2,1,0:T(8,128)(2,1)S(1)}, bf16[2,32,512]{2,1,0:T(8,128)(2,1)S(1)}, u32[]{:S(2)}, u32[]{:S(2)}) collective-permute-start(bf16[2,32,512]{2,1,0:T(8,128)(2,1)S(1)} %pad_maximum_fusion.1.refs_8_), channel_id=1, source_target_pairs={{0,4},{4,0},{8,12},{12,8},{16,20},{20,16},{24,28},{28,24},{32,36},... | collective-permute-start | bytes 196616 | tf_op jit(solution)/shard_map/ppermute | solution.py:54
  70.0 6.7 %collective-permute-start.17 = (f32[32,512]{1,0:T(8,128)S(1)}, f32[32,512]{1,0:T(8,128)S(1)}, u32[]{:S(2)}, u32[]{:S(2)}) collective-permute-start(f32[32,512]{1,0:T(8,128)S(1)} %get-tuple-element.70), channel_id=1, source_target_pairs={{3,0},{0,1},{1,2},{2,3},{7,4},{4,5},{5,6},{6,7},{11,8},{8,9},{9,10... | collective-permute-start | bytes 196616 | tf_op jit(solution)/shard_map/ppermute | solution.py:38
  70.3 6.4 %collective-permute-start.18 = (f32[32,512]{1,0:T(8,128)S(1)}, f32[32,512]{1,0:T(8,128)S(1)}, u32[]{:S(2)}, u32[]{:S(2)}) collective-permute-start(f32[32,512]{1,0:T(8,128)S(1)} %get-tuple-element.71), channel_id=1, source_target_pairs={{2,0},{3,1},{0,2},{1,3},{6,4},{7,5},{4,6},{5,7},{10,8},{11,9},{8,1... | collective-permute-start | bytes 196616 | tf_op jit(solution)/shard_map/ppermute | solution.py:38
  72.3 4.8 %collective-permute-start.19 = (f32[32,512]{1,0:T(8,128)S(1)}, f32[32,512]{1,0:T(8,128)S(1)}, u32[]{:S(2)}, u32[]{:S(2)}) collective-permute-start(f32[32,512]{1,0:T(8,128)S(1)} %get-tuple-element.72), channel_id=1, source_target_pairs={{1,0},{2,1},{3,2},{0,3},{5,4},{6,5},{7,6},{4,7},{9,8},{10,9},{11,1... | collective-permute-start | bytes 196616 | tf_op jit(solution)/shard_map/ppermute | solution.py:38
  77.3 6.5 %collective-permute-start.23 = (f32[32,512]{1,0:T(8,128)S(1)}, f32[32,512]{1,0:T(8,128)S(1)}, u32[]{:S(2)}, u32[]{:S(2)}) collective-permute-start(f32[32,512]{1,0:T(8,128)S(1)} %get-tuple-element.74.refs_6_), channel_id=1, source_target_pairs={{248,0},{252,4},{0,8},{4,12},{8,16},{12,20},{16,24},{20,28},{24,32... | collective-permute-start | bytes 196616 | tf_op jit(solution)/shard_map/ppermute | solution.py:38
  77.4 6.4 %collective-permute-start.22 = (f32[32,512]{1,0:T(8,128)S(1)}, f32[32,512]{1,0:T(8,128)S(1)}, u32[]{:S(2)}, u32[]{:S(2)}) collective-permute-start(f32[32,512]{1,0:T(8,128)S(1)} %get-tuple-element.74.refs_6_), channel_id=1, source_target_pairs={{8,0},{12,4},{16,8},{20,12},{24,16},{28,20},{32,24},{36,28},{40,32... | collective-permute-start | bytes 196616 | tf_op jit(solution)/shard_map/ppermute | solution.py:38
  82.1 5.2 %collective-permute-start.21 = (f32[32,512]{1,0:T(8,128)S(1)}, f32[32,512]{1,0:T(8,128)S(1)}, u32[]{:S(2)}, u32[]{:S(2)}) collective-permute-start(f32[32,512]{1,0:T(8,128)S(1)} %get-tuple-element.74.refs_6_), channel_id=1, source_target_pairs={{0,244},{4,16},{8,252},{12,24},{16,4},{20,32},{24,12},{28,40},{32,... | collective-permute-start | bytes 196616 | tf_op jit(solution)/shard_map/ppermute | solution.py:48
  82.1 5.2 %collective-permute-start.20 = (f32[32,512]{1,0:T(8,128)S(1)}, f32[32,512]{1,0:T(8,128)S(1)}, u32[]{:S(2)}, u32[]{:S(2)}) collective-permute-start(f32[32,512]{1,0:T(8,128)S(1)} %get-tuple-element.74.refs_6_), channel_id=1, source_target_pairs={{0,4},{4,0},{8,12},{12,8},{16,20},{20,16},{24,28},{28,24},{32,36},... | collective-permute-start | bytes 196616 | tf_op jit(solution)/shard_map/ppermute | solution.py:47
  87.4 4.5 %collective-permute-start.24 = (f32[2,32,512]{2,1,0:T(8,128)S(1)}, f32[2,32,512]{2,1,0:T(8,128)S(1)}, u32[]{:S(2)}, u32[]{:S(2)}) collective-permute-start(f32[2,32,512]{2,1,0:T(8,128)S(1)} %pad_maximum_fusion.refs_8_), channel_id=1, source_target_pairs={{0,4},{4,0},{8,12},{12,8},{16,20},{20,16},{24,28},{28,24},{32,36},... | collective-permute-start | bytes 393224 | tf_op jit(solution)/shard_map/ppermute | solution.py:54
  95.8 6.7 %collective-permute-start.25 = (f32[32,512]{1,0:T(8,128)S(1)}, f32[32,512]{1,0:T(8,128)S(1)}, u32[]{:S(2)}, u32[]{:S(2)}) collective-permute-start(f32[32,512]{1,0:T(8,128)S(1)} %get-tuple-element.80), channel_id=1, source_target_pairs={{3,0},{0,1},{1,2},{2,3},{7,4},{4,5},{5,6},{6,7},{11,8},{8,9},{9,10... | collective-permute-start | bytes 196616 | tf_op jit(solution)/shard_map/ppermute | solution.py:38
  95.9 6.6 %collective-permute-start.26 = (f32[32,512]{1,0:T(8,128)S(1)}, f32[32,512]{1,0:T(8,128)S(1)}, u32[]{:S(2)}, u32[]{:S(2)}) collective-permute-start(f32[32,512]{1,0:T(8,128)S(1)} %get-tuple-element.81), channel_id=1, source_target_pairs={{2,0},{3,1},{0,2},{1,3},{6,4},{7,5},{4,6},{5,7},{10,8},{11,9},{8,1... | collective-permute-start | bytes 196616 | tf_op jit(solution)/shard_map/ppermute | solution.py:38
  98.3 4.2 %collective-permute-start.27 = (f32[32,512]{1,0:T(8,128)S(1)}, f32[32,512]{1,0:T(8,128)S(1)}, u32[]{:S(2)}, u32[]{:S(2)}) collective-permute-start(f32[32,512]{1,0:T(8,128)S(1)} %get-tuple-element.82), channel_id=1, source_target_pairs={{1,0},{2,1},{3,2},{0,3},{5,4},{6,5},{7,6},{4,7},{9,8},{10,9},{11,1... | collective-permute-start | bytes 196616 | tf_op jit(solution)/shard_map/ppermute | solution.py:38
  131.9 0.6 copy-start.4

commit v5 on v4

--- a/solution.py
+++ b/solution.py
@@ -42,16 +42,15 @@
     count = lax.axis_size("space")
     swap = [(at, at ^ 1) for at in range(count)]
     far = [(at, (at + (3 if at % 2 else -3)) % count) for at in range(count)]
-    other, far, ahead, behind = lax.optimization_barrier(
+    far, ahead, behind = lax.optimization_barrier(
         (
-            lax.ppermute(value, "space", swap),
             lax.ppermute(value, "space", far),
             shifted(value, "space", 2),
             shifted(value, "space", -2),
         )
     )
-    beside = jnp.stack([ahead, behind])
-    return value, other, beside, lax.ppermute(beside, "space", swap), far
+    held = jnp.stack([value, ahead, behind])
+    return held, lax.ppermute(held, "space", swap), far
 
 
 def window_slot(hop, side):
@@ -276,9 +275,9 @@
 
 
 def sweep_kernel(parts, *refs):
-    list_refs, tile_refs, vector_refs = refs[:4], refs[4:6], refs[6:11]
-    out_refs, (held, total, tiles, sems) = refs[11:15], refs[15:]
-    vecs = vector_refs[0].shape[0]
+    list_refs, tile_refs, vector_refs = refs[:4], refs[4:6], refs[6:9]
+    out_refs, (held, total, tiles, sems) = refs[9:13], refs[13:]
+    vecs = vector_refs[0].shape[1]
 
     def copy(k, at):
         span = pl.ds(at * UNROLL, UNROLL)
@@ -294,9 +293,9 @@
 
         lax.fori_loop(0, groups[k], fetch, 0)
 
-    own, other, beside, swapped, far = vector_refs
+    here, there, far = vector_refs
     for k, vectors in enumerate(
-        (own[...], other[...], beside[0], swapped[0], beside[1], swapped[1], far[...])
+        (here[0], there[0], here[1], there[1], here[2], there[2], far[...])
     ):
         both = stacked(vectors)
         for c in range(2):
@@ -333,14 +332,14 @@
 
 def sweep(near, tiles):
     own = near[0]
-    vecs = own.shape[0]
+    vecs = own.shape[1]
     smem = pl.BlockSpec(memory_space=pltpu.SMEM)
     vmem = pl.BlockSpec(memory_space=pltpu.VMEM)
     parts = 1 if own.dtype == jnp.bfloat16 else 2
     lists = [part for tile in tiles for part in tile[1:]]
     return pl.pallas_call(
         functools.partial(sweep_kernel, parts),
-        in_specs=[smem] * 4 + [pl.BlockSpec(memory_space=pl.ANY)] * 2 + [vmem] * 5,
+        in_specs=[smem] * 4 + [pl.BlockSpec(memory_space=pl.ANY)] * 2 + [vmem] * 3,
         out_specs=[vmem] * 4,
         out_shape=[jax.ShapeDtypeStruct((vecs, LENGTH), jnp.float32)] * 4,
         scratch_shapes=[

time: 133 us -> 128 us (0.962)
  starting transfers between devices: 53.9 us -> 43.1 us
  waiting for transfers between devices: 25.2 us -> 33.5 us
  Pallas kernels: 23.6 us -> 21.6 us
    ppermute x4 -> x2, starting transfers between devices: 16.4 us -> 4.22 us  [space_window(): return (held, lax.ppermute(held, 'space', swap), far)]
    ppermute x22, waiting for transfers between devices: 18.9 us -> 23.7 us  [shifted(): lax.ppermute(value, axis, [((at + steps) % count, at) for at in range(cou...]
    ppermute x2, waiting for transfers between devices: 3.54 us -> 7.36 us  [space_window(): lax.ppermute(value, 'space', far)]
    ppermute x4 -> x2, waiting for transfers between devices: 2.74 us -> 2.36 us  [space_window(): return (held, lax.ppermute(held, 'space', swap), far)]
  transfers between devices with their start and end apart: 28 -> 26, of which waited for: 14 -> 18; matrix products, arithmetic and copies ran while one was open for 0% -> 0% of each run, Pallas kernels for 4% -> 4%
where the time goes in v5:
time: 128 us
  starting transfers between devices  43.1 us (34%)
  waiting for transfers between devices  33.5 us (26%)
  blocking collectives  25.8 us (20%)
  Pallas kernels  21.6 us (17%)
  local copies, waits for them, and re-layouts  3.24 us (3%)
    ppermute x22, starting transfers between devices, shifted(): lax.ppermute(value, axis, [((at + steps) % count, at) for at in range(cou...  38 us
    all_to_all x2, blocking collectives, summed(): lax.all_to_all(sent, ('space', 'sub'), 0, 0, axis_index_groups=groups)  25.8 us
    ppermute x22, waiting for transfers between devices, shifted(): lax.ppermute(value, axis, [((at + steps) % count, at) for at in range(cou...  23.7 us
    pallas_call x2, Pallas kernels, hop_tiles(): pl.pallas_call(functools.partial(tile_kernel, hops, first, last), in_spec...  10.6 us
    ppermute x2, waiting for transfers between devices, space_window(): lax.ppermute(value, 'space', far)  7.36 us
    pallas_call x2, Pallas kernels, sweep(): pl.pallas_call(functools.partial(sweep_kernel, parts), in_specs=[smem] *...  6.85 us
    ppermute x2, starting transfers between devices, space_window(): return (held, lax.ppermute(held, 'space', swap), far)  4.22 us
    unnamed x10, local copies, waits for them, and re-layouts  2.95 us
  transfers between devices with their start and end apart: 26, of which 18 were waited for; matrix products, arithmetic and copies ran while one was open for 0% of the time, Pallas kernels for 4%

profile of v5, /device:TPU:1, one launch (start us, length us, event | category | flops | bytes accessed | tf_op | source)
XLA Modules:
  0.0 128.2 jit_solution(1700472923120686842)
XLA Ops:
  0.0 1.0 copy-done
  1.0 0.7 copy-done.1
  1.6 0.7 copy-done.2
  2.3 0.8 shard_map.48.refs_0_.refs_2_
  3.1 2.1 %collective-permute-start.4 = (bf16[304,512]{1,0:T(8,128)(2,1)S(1)}, bf16[304,512]{1,0:T(8,128)(2,1)S(1)}, u32[]{:S(2)}, u32[]{:S(2)}) collective-permute-start(bf16[304,512]{1,0:T(8,128)(2,1)S(1)} %shard_map.48.refs_0_.refs_2_), channel_id=1, source_target_pairs={{248,0},{252,4},{0,8},{4,12},{8,16},{12,20},{16,24},{20,28},{24,32... | collective-permute-start | bytes 933896 | tf_op jit(solution)/shard_map/ppermute | solution.py:38
  5.3 6.6 %collective-permute-start.3 = (bf16[304,512]{1,0:T(8,128)(2,1)S(1)}, bf16[304,512]{1,0:T(8,128)(2,1)S(1)}, u32[]{:S(2)}, u32[]{:S(2)}) collective-permute-start(bf16[304,512]{1,0:T(8,128)(2,1)S(1)} %shard_map.48.refs_0_.refs_2_), channel_id=1, source_target_pairs={{8,0},{12,4},{16,8},{20,12},{24,16},{28,20},{32,24},{36,28},{40,32... | collective-permute-start | bytes 933896 | tf_op jit(solution)/shard_map/ppermute | solution.py:38
  11.9 1.3 %collective-permute-start.2 = (bf16[304,512]{1,0:T(8,128)(2,1)S(1)}, bf16[304,512]{1,0:T(8,128)(2,1)S(1)}, u32[]{:S(2)}, u32[]{:S(2)}) collective-permute-start(bf16[304,512]{1,0:T(8,128)(2,1)S(1)} %shard_map.48.refs_0_.refs_2_), channel_id=1, source_target_pairs={{3,0},{0,1},{1,2},{2,3},{7,4},{4,5},{5,6},{6,7},{11,8},{8,9},{9,10... | collective-permute-start | bytes 933896 | tf_op jit(solution)/shard_map/ppermute | solution.py:38
  13.2 2.6 %collective-permute-start.1 = (bf16[304,512]{1,0:T(8,128)(2,1)S(1)}, bf16[304,512]{1,0:T(8,128)(2,1)S(1)}, u32[]{:S(2)}, u32[]{:S(2)}) collective-permute-start(bf16[304,512]{1,0:T(8,128)(2,1)S(1)} %shard_map.48.refs_0_.refs_2_), channel_id=1, source_target_pairs={{2,0},{3,1},{0,2},{1,3},{6,4},{7,5},{4,6},{5,7},{10,8},{11,9},{8,1... | collective-permute-start | bytes 933896 | tf_op jit(solution)/shard_map/ppermute | solution.py:38
  15.8 1.1 collective-permute-start
  16.9 2.0 %collective-permute-done.4.refs_1_ = bf16[304,512]{1,0:T(8,128)(2,1)S(1)} collective-permute-done((bf16[304,512]{1,0:T(8,128)(2,1)S(1)}, bf16[304,512]{1,0:T(8,128)(2,1)S(1)}, u32[]{:S(2)}, u32[]{:S(2)}) %collective-permute-start.4) | collective-permute-done | bytes 311328 | tf_op jit(solution)/shard_map/ppermute | solution.py:38
  18.9 1.2 collective-permute-start.5
  20.1 1.0 collective-permute-done.2.refs_3_
  21.1 4.1 %collective-permute-start.7 = (bf16[304,512]{1,0:T(8,128)(2,1)S(1)}, bf16[304,512]{1,0:T(8,128)(2,1)S(1)}, u32[]{:S(2)}, u32[]{:S(2)}) collective-permute-start(bf16[304,512]{1,0:T(8,128)(2,1)S(1)} %collective-permute-done.3.refs_0_), channel_id=1, source_target_pairs={{4,0},{8,4},{12,8},{16,12},{20,16},{24,20},{28,24},{32,28},{36,32}... | collective-permute-start | bytes 933896 | tf_op jit(solution)/shard_map/ppermute | solution.py:38
  25.2 3.7 %collective-permute-done.1.refs_2_ = bf16[304,512]{1,0:T(8,128)(2,1)S(1)} collective-permute-done((bf16[304,512]{1,0:T(8,128)(2,1)S(1)}, bf16[304,512]{1,0:T(8,128)(2,1)S(1)}, u32[]{:S(2)}, u32[]{:S(2)}) %collective-permute-start.1) | collective-permute-done | bytes 311328 | tf_op jit(solution)/shard_map/ppermute | solution.py:38
  29.4 4.8 %shard_map.50 = (bf16[40,256,256]{2,1,0:T(8,128)(2,1)S(1)}, s32[80]{0:T(128)S(1)}, s32[80]{0:T(128)S(1)}, f32[9,8,256]{2,1,0:T(8,128)S(1)}) custom-call(s32[192]{0:T(256)S(1)} %reshape.20.mine_ref, bf16[8,320,256]{2,1,0:T(8,128)(2,1)S(1)} %get-tuple-element.50.blocks_ref, f32[8,8,256]{2,1,0:T(8,128)S(1)} %get-tuple-element.51.rate_ref, ...), custom_call_target="tpu_custom_call" | custom-call | flops 671088640 | bytes 7340032 | tf_op jit(solution)/shard_map/pallas_call | solution.py:242
  34.2 5.9 %shard_map.51 = (bf16[64,256,256]{2,1,0:T(8,128)(2,1)S(1)}, s32[80]{0:T(128)S(1)}, s32[80]{0:T(128)S(1)}, f32[4,8,512]{2,1,0:T(8,128)S(1)}) custom-call(s32[192]{0:T(256)S(1)} %reshape.20.mine_ref, bf16[8,320,256]{2,1,0:T(8,128)(2,1)S(1)} %get-tuple-element.50.blocks_ref, f32[8,8,256]{2,1,0:T(8,128)S(1)} %get-tuple-element.51.rate_ref, ...), custom_call_target="tpu_custom_call" | custom-call | flops 1342177280 | bytes 7340032 | tf_op jit(solution)/shard_map/pallas_call | solution.py:242
  40.1 2.4 %collective-permute-start.11 = (f32[1,512]{1,0:T(1,128)S(1)}, f32[1,512]{1,0:T(1,128)S(1)}, u32[]{:S(2)}, u32[]{:S(2)}) collective-permute-start(f32[1,512]{1,0:T(1,128)S(1)} %get-tuple-element.84), channel_id=1, source_target_pairs={{1,0},{2,1},{3,2},{0,3},{5,4},{6,5},{7,6},{4,7},{9,8},{10,9},{11,1... | collective-permute-start | bytes 6152 | tf_op jit(solution)/shard_map/ppermute | solution.py:38
  42.5 0.8 collective-permute-start.10
  43.3 3.1 %collective-permute-done.10 = f32[1,512]{1,0:T(1,128)S(1)} collective-permute-done((f32[1,512]{1,0:T(1,128)S(1)}, f32[1,512]{1,0:T(1,128)S(1)}, u32[]{:S(2)}, u32[]{:S(2)}) %collective-permute-start.10) | collective-permute-done | bytes 2080 | tf_op jit(solution)/shard_map/ppermute | solution.py:38
  46.4 0.5 collective-permute-done.9
  47.0 4.7 %collective-permute-start.13 = (bf16[32,512]{1,0:T(8,128)(2,1)S(1)}, bf16[32,512]{1,0:T(8,128)(2,1)S(1)}, u32[]{:S(2)}, u32[]{:S(2)}) collective-permute-start(bf16[32,512]{1,0:T(8,128)(2,1)S(1)} %multiply_convert_fusion), channel_id=1, source_target_pairs={{8,0},{12,4},{16,8},{20,12},{24,16},{28,20},{32,24},{36,28},{40,32... | collective-permute-start | bytes 98312 | tf_op jit(solution)/shard_map/ppermute | solution.py:38
  51.7 0.9 collective-permute-start.12
  52.7 3.8 %collective-permute-done.12.refs_8_ = bf16[32,512]{1,0:T(8,128)(2,1)S(1)} collective-permute-done((bf16[32,512]{1,0:T(8,128)(2,1)S(1)}, bf16[32,512]{1,0:T(8,128)(2,1)S(1)}, u32[]{:S(2)}, u32[]{:S(2)}) %collective-permute-start.12) | collective-permute-done | bytes 32800 | tf_op jit(solution)/shard_map/ppermute | solution.py:47
  56.5 4.1 %collective-permute-done.14 = bf16[32,512]{1,0:T(8,128)(2,1)S(1)} collective-permute-done((bf16[32,512]{1,0:T(8,128)(2,1)S(1)}, bf16[32,512]{1,0:T(8,128)(2,1)S(1)}, u32[]{:S(2)}, u32[]{:S(2)}) %collective-permute-start.14) | collective-permute-done | bytes 32800 | tf_op jit(solution)/shard_map/ppermute | solution.py:38
  60.7 1.3 %collective-permute-done.15.refs_7_ = bf16[3,32,512]{2,1,0:T(8,128)(2,1)S(1)} collective-permute-done((bf16[3,32,512]{2,1,0:T(8,128)(2,1)S(1)}, bf16[3,32,512]{2,1,0:T(8,128)(2,1)S(1)}, u32[]{:S(2)}, u32[]{:S(2)}) %collective-permute-start.15) | collective-permute-done | bytes 98336 | tf_op jit(solution)/shard_map/ppermute | solution.py:53
  62.0 3.4 %shard_map.52 = (f32[32,512]{1,0:T(8,128)S(1)}, f32[32,512]{1,0:T(8,128)S(1)}, f32[32,512]{1,0:T(8,128)S(1)}, f32[32,512]{1,0:T(8,128)S(1)}) custom-call(s32[80]{0:T(128)S(1)} %get-tuple-element.57.refs_0_, s32[80]{0:T(128)S(1)} %get-tuple-element.58.refs_1_, s32[80]{0:T(128)S(1)} %get-tuple-element.59.refs_2_, s32[80]{0:T(128)S(1)} %get-tuple-element.60.refs_3_, ...), custom_call_target="tpu_custom_call" | custom-call | flops 838860800 | bytes 7340032 | tf_op jit(solution)/shard_map/pallas_call | solution.py:340
  65.3 0.7 collective-permute-start.16
  66.0 2.0 %collective-permute-start.17 = (f32[32,512]{1,0:T(8,128)S(1)}, f32[32,512]{1,0:T(8,128)S(1)}, u32[]{:S(2)}, u32[]{:S(2)}) collective-permute-start(f32[32,512]{1,0:T(8,128)S(1)} %get-tuple-element.68), channel_id=1, source_target_pairs={{2,0},{3,1},{0,2},{1,3},{6,4},{7,5},{4,6},{5,7},{10,8},{11,9},{8,1... | collective-permute-start | bytes 196616 | tf_op jit(solution)/shard_map/ppermute | solution.py:38
  68.0 0.5 collective-permute-start.18
  68.5 1.7 %collective-permute-done.16.refs_1_ = f32[32,512]{1,0:T(8,128)S(1)} collective-permute-done((f32[32,512]{1,0:T(8,128)S(1)}, f32[32,512]{1,0:T(8,128)S(1)}, u32[]{:S(2)}, u32[]{:S(2)}) %collective-permute-start.16) | collective-permute-done | bytes 65568 | tf_op jit(solution)/shard_map/ppermute | solution.py:38
  70.2 1.4 %collective-permute-done.17.refs_2_ = f32[32,512]{1,0:T(8,128)S(1)} collective-permute-done((f32[32,512]{1,0:T(8,128)S(1)}, f32[32,512]{1,0:T(8,128)S(1)}, u32[]{:S(2)}, u32[]{:S(2)}) %collective-permute-start.17) | collective-permute-done | bytes 65568 | tf_op jit(solution)/shard_map/ppermute | solution.py:38
  71.6 0.3 collective-permute-done.18.refs_3_
  72.1 0.7 collective-permute-start.21
  72.9 4.1 %collective-permute-start.20 = (f32[32,512]{1,0:T(8,128)S(1)}, f32[32,512]{1,0:T(8,128)S(1)}, u32[]{:S(2)}, u32[]{:S(2)}) collective-permute-start(f32[32,512]{1,0:T(8,128)S(1)} %get-tuple-element.71), channel_id=1, source_target_pairs={{8,0},{12,4},{16,8},{20,12},{24,16},{28,20},{32,24},{36,28},{40,32... | collective-permute-start | bytes 196616 | tf_op jit(solution)/shard_map/ppermute | solution.py:38
  77.0 1.6 %collective-permute-done.21 = f32[32,512]{1,0:T(8,128)S(1)} collective-permute-done((f32[32,512]{1,0:T(8,128)S(1)}, f32[32,512]{1,0:T(8,128)S(1)}, u32[]{:S(2)}, u32[]{:S(2)}) %collective-permute-start.21) | collective-permute-done | bytes 65568 | tf_op jit(solution)/shard_map/ppermute | solution.py:38
  78.6 3.5 %collective-permute-done.19.refs_8_ = f32[32,512]{1,0:T(8,128)S(1)} collective-permute-done((f32[32,512]{1,0:T(8,128)S(1)}, f32[32,512]{1,0:T(8,128)S(1)}, u32[]{:S(2)}, u32[]{:S(2)}) %collective-permute-start.19) | collective-permute-done | bytes 65568 | tf_op jit(solution)/shard_map/ppermute | solution.py:47
  82.2 4.1 %collective-permute-start.22 = (f32[3,32,512]{2,1,0:T(8,128)S(1)}, f32[3,32,512]{2,1,0:T(8,128)S(1)}, u32[]{:S(2)}, u32[]{:S(2)}) collective-permute-start(f32[3,32,512]{2,1,0:T(8,128)S(1)} %pad_maximum_fusion.refs_6_), channel_id=1, source_target_pairs={{0,4},{4,0},{8,12},{12,8},{16,20},{20,16},{24,28},{28,24},{32,36},... | collective-permute-start | bytes 589832 | tf_op jit(solution)/shard_map/ppermute | solution.py:53
  86.3 1.1 collective-permute-done.22.refs_7_
  87.4 3.5 %shard_map.54 = (f32[32,512]{1,0:T(8,128)S(1)}, f32[32,512]{1,0:T(8,128)S(1)}, f32[32,512]{1,0:T(8,128)S(1)}, f32[32,512]{1,0:T(8,128)S(1)}) custom-call(s32[80]{0:T(128)S(1)} %get-tuple-element.57.refs_0_, s32[80]{0:T(128)S(1)} %get-tuple-element.58.refs_1_, s32[80]{0:T(128)S(1)} %get-tuple-element.59.refs_2_, s32[80]{0:T(128)S(1)} %get-tuple-element.60.refs_3_, ...), custom_call_target="tpu_custom_call" | custom-call | flops 838860800 | bytes 7340032 | tf_op jit(solution)/shard_map/pallas_call | solution.py:340
  90.9 0.5 collective-permute-start.23
  91.4 2.5 %collective-permute-start.24 = (f32[32,512]{1,0:T(8,128)S(1)}, f32[32,512]{1,0:T(8,128)S(1)}, u32[]{:S(2)}, u32[]{:S(2)}) collective-permute-start(f32[32,512]{1,0:T(8,128)S(1)} %get-tuple-element.77), channel_id=1, source_target_pairs={{2,0},{3,1},{0,2},{1,3},{6,4},{7,5},{4,6},{5,7},{10,8},{11,9},{8,1... | collective-permute-start | bytes 196616 | tf_op jit(solution)/shard_map/ppermute | solution.py:38
  94.0 1.3 %collective-permute-done.23.refs_1_ = f32[32,512]{1,0:T(8,128)S(1)} collective-permute-done((f32[32,512]{1,0:T(8,128)S(1)}, f32[32,512]{1,0:T(8,128)S(1)}, u32[]{:S(2)}, u32[]{:S(2)}) %collective-permute-start.23) | collective-permute-done | bytes 65568 | tf_op jit(solution)/shard_map/ppermute | solution.py:38
  95.3 1.2 collective-permute-done.24.refs_2_
  96.5 1.5 %collective-permute-done.25.refs_3_ = f32[32,512]{1,0:T(8,128)S(1)} collective-permute-done((f32[32,512]{1,0:T(8,128)S(1)}, f32[32,512]{1,0:T(8,128)S(1)}, u32[]{:S(2)}, u32[]{:S(2)}) %collective-permute-start.25) | collective-permute-done | bytes 65568 | tf_op jit(solution)/shard_map/ppermute | solution.py:38
  98.3 13.4 %all_to_all.20 = f32[32,16,128]{2,1,0:T(8,128)S(1)} all-to-all(f32[32,16,128]{2,1,0:T(8,128)S(1)} %broadcast_in_dim.13), channel_id=1, replica_groups={{0,1,2,3,4,5,6,7,8,9,10,11,12,13,14,15,16,17,18,19,20,21,22,23,24,25,26..., dimensions={0} | all-to-all | bytes 524288 | tf_op jit(solution)/shard_map/all_to_all | solution.py:77
  111.8 12.4 %all_to_all.21 = f32[8,16,128]{2,1,0:T(8,128)S(1)} all-to-all(f32[8,16,128]{2,1,0:T(8,128)S(1)} %broadcast_in_dim.28), channel_id=1, replica_groups={{0,32,64,96,128,160,192,224},{1,33,65,97,129,161,193,225},{2,34,66,98,1..., dimensions={0} | all-to-all | bytes 131072 | tf_op jit(solution)/shard_map/all_to_all | solution.py:77
  124.3 2.6 %shard_map.56 = (f32[32,512]{1,0:T(8,128)S(1)}, s32[1]{0:T(128)}) custom-call(f32[64,32]{1,0:T(8,128)S(1)} %reshape.19.grams_ref, f32[32,512]{1,0:T(8,128)S(1)} %get-tuple-element.80.image_ref), custom_call_target="tpu_custom_call" | custom-call | flops 1048576 | bytes 131072 | tf_op jit(solution)/shard_map/pallas_call | solution.py:499
  127.6 0.6 copy-done.4
  (45 shorter events, 1.4 us)
Async XLA Ops:
  0.0 1.0 copy-start
  1.0 0.7 copy-start.1
  1.6 0.7 copy-start.2
  2.3 44.6 %copy-start.3 = (f32[32,512]{1,0:T(8,128)S(1)}, f32[32,512]{1,0:T(8,128)}, u32[]{:S(2)}) copy-start(f32[32,512]{1,0:T(8,128)} %param.8) | copy-start | bytes 196612
  3.1 15.8 %collective-permute-start.4 = (bf16[304,512]{1,0:T(8,128)(2,1)S(1)}, bf16[304,512]{1,0:T(8,128)(2,1)S(1)}, u32[]{:S(2)}, u32[]{:S(2)}) collective-permute-start(bf16[304,512]{1,0:T(8,128)(2,1)S(1)} %shard_map.48.refs_0_.refs_2_), channel_id=1, source_target_pairs={{248,0},{252,4},{0,8},{4,12},{8,16},{12,20},{16,24},{20,28},{24,32... | collective-permute-start | bytes 933896 | tf_op jit(solution)/shard_map/ppermute | solution.py:38
  5.3 13.6 %collective-permute-start.3 = (bf16[304,512]{1,0:T(8,128)(2,1)S(1)}, bf16[304,512]{1,0:T(8,128)(2,1)S(1)}, u32[]{:S(2)}, u32[]{:S(2)}) collective-permute-start(bf16[304,512]{1,0:T(8,128)(2,1)S(1)} %shard_map.48.refs_0_.refs_2_), channel_id=1, source_target_pairs={{8,0},{12,4},{16,8},{20,12},{24,16},{28,20},{32,24},{36,28},{40,32... | collective-permute-start | bytes 933896 | tf_op jit(solution)/shard_map/ppermute | solution.py:38
  11.9 9.2 %collective-permute-start.2 = (bf16[304,512]{1,0:T(8,128)(2,1)S(1)}, bf16[304,512]{1,0:T(8,128)(2,1)S(1)}, u32[]{:S(2)}, u32[]{:S(2)}) collective-permute-start(bf16[304,512]{1,0:T(8,128)(2,1)S(1)} %shard_map.48.refs_0_.refs_2_), channel_id=1, source_target_pairs={{3,0},{0,1},{1,2},{2,3},{7,4},{4,5},{5,6},{6,7},{11,8},{8,9},{9,10... | collective-permute-start | bytes 933896 | tf_op jit(solution)/shard_map/ppermute | solution.py:38
  13.2 15.7 %collective-permute-start.1 = (bf16[304,512]{1,0:T(8,128)(2,1)S(1)}, bf16[304,512]{1,0:T(8,128)(2,1)S(1)}, u32[]{:S(2)}, u32[]{:S(2)}) collective-permute-start(bf16[304,512]{1,0:T(8,128)(2,1)S(1)} %shard_map.48.refs_0_.refs_2_), channel_id=1, source_target_pairs={{2,0},{3,1},{0,2},{1,3},{6,4},{7,5},{4,6},{5,7},{10,8},{11,9},{8,1... | collective-permute-start | bytes 933896 | tf_op jit(solution)/shard_map/ppermute | solution.py:38
  15.8 13.2 %collective-permute-start = (bf16[304,512]{1,0:T(8,128)(2,1)S(1)}, bf16[304,512]{1,0:T(8,128)(2,1)S(1)}, u32[]{:S(2)}, u32[]{:S(2)}) collective-permute-start(bf16[304,512]{1,0:T(8,128)(2,1)S(1)} %shard_map.48.refs_0_.refs_2_), channel_id=1, source_target_pairs={{1,0},{2,1},{3,2},{0,3},{5,4},{6,5},{7,6},{4,7},{9,8},{10,9},{11,1... | collective-permute-start | bytes 933896 | tf_op jit(solution)/shard_map/ppermute | solution.py:38
  18.9 15.3 %collective-permute-start.6 = (bf16[304,512]{1,0:T(8,128)(2,1)S(1)}, bf16[304,512]{1,0:T(8,128)(2,1)S(1)}, u32[]{:S(2)}, u32[]{:S(2)}) collective-permute-start(bf16[304,512]{1,0:T(8,128)(2,1)S(1)} %shard_map.48.refs_0_.refs_2_), channel_id=1, source_target_pairs={{252,0},{0,4},{4,8},{8,12},{12,16},{16,20},{20,24},{24,28},{28,32}... | collective-permute-start | bytes 933896 | tf_op jit(solution)/shard_map/ppermute | solution.py:38
  18.9 15.3 %collective-permute-start.5 = (bf16[304,512]{1,0:T(8,128)(2,1)S(1)}, bf16[304,512]{1,0:T(8,128)(2,1)S(1)}, u32[]{:S(2)}, u32[]{:S(2)}) collective-permute-start(bf16[304,512]{1,0:T(8,128)(2,1)S(1)} %shard_map.48.refs_0_.refs_2_), channel_id=1, source_target_pairs={{4,0},{8,4},{12,8},{16,12},{20,16},{24,20},{28,24},{32,28},{36,32}... | collective-permute-start | bytes 933896 | tf_op jit(solution)/shard_map/ppermute | solution.py:38
  21.1 13.1 %collective-permute-start.7 = (bf16[304,512]{1,0:T(8,128)(2,1)S(1)}, bf16[304,512]{1,0:T(8,128)(2,1)S(1)}, u32[]{:S(2)}, u32[]{:S(2)}) collective-permute-start(bf16[304,512]{1,0:T(8,128)(2,1)S(1)} %collective-permute-done.3.refs_0_), channel_id=1, source_target_pairs={{4,0},{8,4},{12,8},{16,12},{20,16},{24,20},{28,24},{32,28},{36,32}... | collective-permute-start | bytes 933896 | tf_op jit(solution)/shard_map/ppermute | solution.py:38
  28.9 5.3 %collective-permute-start.8 = (bf16[304,512]{1,0:T(8,128)(2,1)S(1)}, bf16[304,512]{1,0:T(8,128)(2,1)S(1)}, u32[]{:S(2)}, u32[]{:S(2)}) collective-permute-start(bf16[304,512]{1,0:T(8,128)(2,1)S(1)} %collective-permute-done.4.refs_1_), channel_id=1, source_target_pairs={{252,0},{0,4},{4,8},{8,12},{12,16},{16,20},{20,24},{24,28},{28,32}... | collective-permute-start | bytes 933896 | tf_op jit(solution)/shard_map/ppermute | solution.py:38
  40.1 3.2 %collective-permute-start.11 = (f32[1,512]{1,0:T(1,128)S(1)}, f32[1,512]{1,0:T(1,128)S(1)}, u32[]{:S(2)}, u32[]{:S(2)}) collective-permute-start(f32[1,512]{1,0:T(1,128)S(1)} %get-tuple-element.84), channel_id=1, source_target_pairs={{1,0},{2,1},{3,2},{0,3},{5,4},{6,5},{7,6},{4,7},{9,8},{10,9},{11,1... | collective-permute-start | bytes 6152 | tf_op jit(solution)/shard_map/ppermute | solution.py:38
  42.5 3.9 %collective-permute-start.10 = (f32[1,512]{1,0:T(1,128)S(1)}, f32[1,512]{1,0:T(1,128)S(1)}, u32[]{:S(2)}, u32[]{:S(2)}) collective-permute-start(f32[1,512]{1,0:T(1,128)S(1)} %get-tuple-element.85), channel_id=1, source_target_pairs={{2,0},{3,1},{0,2},{1,3},{6,4},{7,5},{4,6},{5,7},{10,8},{11,9},{8,1... | collective-permute-start | bytes 6152 | tf_op jit(solution)/shard_map/ppermute | solution.py:38
  43.3 3.6 %collective-permute-start.9 = (f32[1,512]{1,0:T(1,128)S(1)}, f32[1,512]{1,0:T(1,128)S(1)}, u32[]{:S(2)}, u32[]{:S(2)}) collective-permute-start(f32[1,512]{1,0:T(1,128)S(1)} %get-tuple-element.86), channel_id=1, source_target_pairs={{3,0},{0,1},{1,2},{2,3},{7,4},{4,5},{5,6},{6,7},{11,8},{8,9},{9,10... | collective-permute-start | bytes 6152 | tf_op jit(solution)/shard_map/ppermute | solution.py:38
  47.0 5.7 %collective-permute-start.13 = (bf16[32,512]{1,0:T(8,128)(2,1)S(1)}, bf16[32,512]{1,0:T(8,128)(2,1)S(1)}, u32[]{:S(2)}, u32[]{:S(2)}) collective-permute-start(bf16[32,512]{1,0:T(8,128)(2,1)S(1)} %multiply_convert_fusion), channel_id=1, source_target_pairs={{8,0},{12,4},{16,8},{20,12},{24,16},{28,20},{32,24},{36,28},{40,32... | collective-permute-start | bytes 98312 | tf_op jit(solution)/shard_map/ppermute | solution.py:38
  51.7 4.8 %collective-permute-start.12 = (bf16[32,512]{1,0:T(8,128)(2,1)S(1)}, bf16[32,512]{1,0:T(8,128)(2,1)S(1)}, u32[]{:S(2)}, u32[]{:S(2)}) collective-permute-start(bf16[32,512]{1,0:T(8,128)(2,1)S(1)} %multiply_convert_fusion), channel_id=1, source_target_pairs={{0,244},{4,16},{8,252},{12,24},{16,4},{20,32},{24,12},{28,40},{32,... | collective-permute-start | bytes 98312 | tf_op jit(solution)/shard_map/ppermute | solution.py:47
  52.5 8.0 %collective-permute-start.14 = (bf16[32,512]{1,0:T(8,128)(2,1)S(1)}, bf16[32,512]{1,0:T(8,128)(2,1)S(1)}, u32[]{:S(2)}, u32[]{:S(2)}) collective-permute-start(bf16[32,512]{1,0:T(8,128)(2,1)S(1)} %multiply_convert_fusion), channel_id=1, source_target_pairs={{248,0},{252,4},{0,8},{4,12},{8,16},{12,20},{16,24},{20,28},{24,32... | collective-permute-start | bytes 98312 | tf_op jit(solution)/shard_map/ppermute | solution.py:38
  60.6 1.4 %collective-permute-start.15 = (bf16[3,32,512]{2,1,0:T(8,128)(2,1)S(1)}, bf16[3,32,512]{2,1,0:T(8,128)(2,1)S(1)}, u32[]{:S(2)}, u32[]{:S(2)}) collective-permute-start(bf16[3,32,512]{2,1,0:T(8,128)(2,1)S(1)} %pad_maximum_fusion.1.refs_6_), channel_id=1, source_target_pairs={{0,4},{4,0},{8,12},{12,8},{16,20},{20,16},{24,28},{28,24},{32,36},... | collective-permute-start | bytes 294920 | tf_op jit(solution)/shard_map/ppermute | solution.py:53
  65.3 4.8 %collective-permute-start.16 = (f32[32,512]{1,0:T(8,128)S(1)}, f32[32,512]{1,0:T(8,128)S(1)}, u32[]{:S(2)}, u32[]{:S(2)}) collective-permute-start(f32[32,512]{1,0:T(8,128)S(1)} %get-tuple-element.67), channel_id=1, source_target_pairs={{3,0},{0,1},{1,2},{2,3},{7,4},{4,5},{5,6},{6,7},{11,8},{8,9},{9,10... | collective-permute-start | bytes 196616 | tf_op jit(solution)/shard_map/ppermute | solution.py:38
  66.0 5.6 %collective-permute-start.17 = (f32[32,512]{1,0:T(8,128)S(1)}, f32[32,512]{1,0:T(8,128)S(1)}, u32[]{:S(2)}, u32[]{:S(2)}) collective-permute-start(f32[32,512]{1,0:T(8,128)S(1)} %get-tuple-element.68), channel_id=1, source_target_pairs={{2,0},{3,1},{0,2},{1,3},{6,4},{7,5},{4,6},{5,7},{10,8},{11,9},{8,1... | collective-permute-start | bytes 196616 | tf_op jit(solution)/shard_map/ppermute | solution.py:38
  68.0 4.0 %collective-permute-start.18 = (f32[32,512]{1,0:T(8,128)S(1)}, f32[32,512]{1,0:T(8,128)S(1)}, u32[]{:S(2)}, u32[]{:S(2)}) collective-permute-start(f32[32,512]{1,0:T(8,128)S(1)} %get-tuple-element.69), channel_id=1, source_target_pairs={{1,0},{2,1},{3,2},{0,3},{5,4},{6,5},{7,6},{4,7},{9,8},{10,9},{11,1... | collective-permute-start | bytes 196616 | tf_op jit(solution)/shard_map/ppermute | solution.py:38
  72.1 6.5 %collective-permute-start.21 = (f32[32,512]{1,0:T(8,128)S(1)}, f32[32,512]{1,0:T(8,128)S(1)}, u32[]{:S(2)}, u32[]{:S(2)}) collective-permute-start(f32[32,512]{1,0:T(8,128)S(1)} %get-tuple-element.71), channel_id=1, source_target_pairs={{248,0},{252,4},{0,8},{4,12},{8,16},{12,20},{16,24},{20,28},{24,32... | collective-permute-start | bytes 196616 | tf_op jit(solution)/shard_map/ppermute | solution.py:38
  72.9 5.7 %collective-permute-start.20 = (f32[32,512]{1,0:T(8,128)S(1)}, f32[32,512]{1,0:T(8,128)S(1)}, u32[]{:S(2)}, u32[]{:S(2)}) collective-permute-start(f32[32,512]{1,0:T(8,128)S(1)} %get-tuple-element.71), channel_id=1, source_target_pairs={{8,0},{12,4},{16,8},{20,12},{24,16},{28,20},{32,24},{36,28},{40,32... | collective-permute-start | bytes 196616 | tf_op jit(solution)/shard_map/ppermute | solution.py:38
  77.0 5.2 %collective-permute-start.19 = (f32[32,512]{1,0:T(8,128)S(1)}, f32[32,512]{1,0:T(8,128)S(1)}, u32[]{:S(2)}, u32[]{:S(2)}) collective-permute-start(f32[32,512]{1,0:T(8,128)S(1)} %get-tuple-element.71), channel_id=1, source_target_pairs={{0,244},{4,16},{8,252},{12,24},{16,4},{20,32},{24,12},{28,40},{32,... | collective-permute-start | bytes 196616 | tf_op jit(solution)/shard_map/ppermute | solution.py:47
  82.2 5.2 %collective-permute-start.22 = (f32[3,32,512]{2,1,0:T(8,128)S(1)}, f32[3,32,512]{2,1,0:T(8,128)S(1)}, u32[]{:S(2)}, u32[]{:S(2)}) collective-permute-start(f32[3,32,512]{2,1,0:T(8,128)S(1)} %pad_maximum_fusion.refs_6_), channel_id=1, source_target_pairs={{0,4},{4,0},{8,12},{12,8},{16,20},{20,16},{24,28},{28,24},{32,36},... | collective-permute-start | bytes 589832 | tf_op jit(solution)/shard_map/ppermute | solution.py:53
  90.9 4.4 %collective-permute-start.23 = (f32[32,512]{1,0:T(8,128)S(1)}, f32[32,512]{1,0:T(8,128)S(1)}, u32[]{:S(2)}, u32[]{:S(2)}) collective-permute-start(f32[32,512]{1,0:T(8,128)S(1)} %get-tuple-element.76), channel_id=1, source_target_pairs={{3,0},{0,1},{1,2},{2,3},{7,4},{4,5},{5,6},{6,7},{11,8},{8,9},{9,10... | collective-permute-start | bytes 196616 | tf_op jit(solution)/shard_map/ppermute | solution.py:38
  91.4 5.1 %collective-permute-start.24 = (f32[32,512]{1,0:T(8,128)S(1)}, f32[32,512]{1,0:T(8,128)S(1)}, u32[]{:S(2)}, u32[]{:S(2)}) collective-permute-start(f32[32,512]{1,0:T(8,128)S(1)} %get-tuple-element.77), channel_id=1, source_target_pairs={{2,0},{3,1},{0,2},{1,3},{6,4},{7,5},{4,6},{5,7},{10,8},{11,9},{8,1... | collective-permute-start | bytes 196616 | tf_op jit(solution)/shard_map/ppermute | solution.py:38
  94.0 4.0 %collective-permute-start.25 = (f32[32,512]{1,0:T(8,128)S(1)}, f32[32,512]{1,0:T(8,128)S(1)}, u32[]{:S(2)}, u32[]{:S(2)}) collective-permute-start(f32[32,512]{1,0:T(8,128)S(1)} %get-tuple-element.78), channel_id=1, source_target_pairs={{1,0},{2,1},{3,2},{0,3},{5,4},{6,5},{7,6},{4,7},{9,8},{10,9},{11,1... | collective-permute-start | bytes 196616 | tf_op jit(solution)/shard_map/ppermute | solution.py:38
  127.6 0.6 copy-start.4

commit v6 on v5

--- a/solution.py
+++ b/solution.py
@@ -23,7 +23,9 @@
 UNROLL = 8
 AT_ONCE = 16
 HALF = UNROLL // 2
-HOPS = ((2,), (1, 3))
+WINDOWS = (((2, 2), (-2, -2)), ((1, -1), (3, 1), (-1, -3), (-3, 3)))
+PLACES = ((2, 4, 0), (1, 3, 5, 6))
+WIDE = 320
 STARTS = (0, 5)
 GROUPS = 13
 LOG2E = 1.4426950408889634
@@ -38,25 +40,24 @@
     return lax.ppermute(value, axis, [((at + steps) % count, at) for at in range(count)])
 
 
+def far_pairs(count):
+    return [(at, (at + (3 if at % 2 else -3)) % count) for at in range(count)]
+
+
+def swapped(value):
+    return lax.ppermute(value, "space", [(at, at ^ 1) for at in range(lax.axis_size("space"))])
+
+
 def space_window(value):
-    count = lax.axis_size("space")
-    swap = [(at, at ^ 1) for at in range(count)]
-    far = [(at, (at + (3 if at % 2 else -3)) % count) for at in range(count)]
     far, ahead, behind = lax.optimization_barrier(
         (
-            lax.ppermute(value, "space", far),
+            lax.ppermute(value, "space", far_pairs(lax.axis_size("space"))),
             shifted(value, "space", 2),
             shifted(value, "space", -2),
         )
     )
-    held = jnp.stack([value, ahead, behind])
-    return held, lax.ppermute(held, "space", swap), far
-
-
-def window_slot(hop, side):
-    odd = lax.rem(lax.axis_index("space"), 2) == 1
-    even_slot, odd_slot = {(1, 0): (1, 3), (1, 1): (5, 1), (2, 0): (2, 2), (2, 1): (4, 4), (3, 0): (3, 6), (3, 1): (6, 5)}[hop, side]
-    return jnp.where(odd, odd_slot, even_slot)
+    here = jnp.stack([value, ahead, behind])
+    return here, swapped(here), far
 
 
 def groups_by(key, n_space, n_sub):
@@ -102,7 +103,7 @@
         tail = tail.astype(jnp.bfloat16)
         rate = LOG2E / refs[e][SCALE_ROW : SCALE_ROW + 1, :].astype(jnp.float32)
         below = lax.broadcasted_iota(jnp.int32, (ROWS, 1), 0) < FEAT
-        twice = jnp.where(below, 2.0 * refs[e][...].astype(jnp.float32), 0.0).astype(jnp.bfloat16)
+        twice = jnp.where(below, 2.0 * refs[e][:ROWS, :].astype(jnp.float32), 0.0).astype(jnp.bfloat16)
         for r in range(2):
             span = slice(r * BLOCK, (r + 1) * BLOCK)
             rows_ref[2 * e + r, :ROWS] = twice[:, span]
@@ -137,18 +138,15 @@
 
 def list_pairs(hops, mine_ref, theirs, rows_ref, cols_ref, count):
     def member(e, count):
-        for k, bits in enumerate(theirs):
-            for side in range(2):
-                for r in range(2):
-                    for c in range(2):
-                        if side == 0:
-                            place = lax.rem(N_SUB - e, N_SUB) * 4 + r * 2 + c
-                            used = mine_ref[(e * REACH + hops[k] - 1) * PAIRS + place]
-                        else:
-                            used = lax.shift_right_logical(bits, e * 4 + c * 2 + r) & 1
-                        rows_ref[count] = e * 2 + r
-                        cols_ref[count] = k * 4 + side * 2 + c
-                        count = count + used
+        for k, (hop, bits) in enumerate(zip(hops, theirs)):
+            base = (e * REACH + lax.abs(hop) - 1) * PAIRS + lax.rem(N_SUB - e, N_SUB) * 4
+            for r in range(2):
+                for c in range(2):
+                    behind = lax.shift_right_logical(bits, e * 4 + c * 2 + r) & 1
+                    used = jnp.where(hop > 0, mine_ref[base + r * 2 + c], behind)
+                    rows_ref[count] = e * 2 + r
+                    cols_ref[count] = k * 2 + c
+                    count = count + used
         return count
 
     count = lax.fori_loop(0, N_SUB, member, count)
@@ -161,30 +159,35 @@
 
 
 def listed_behind(data_ref, hop):
-    lane = lax.broadcasted_iota(jnp.int32, (1, 128), 1) - (hop - 1) * PAIRS
+    lane = lax.broadcasted_iota(jnp.int32, (1, 128), 1) - (lax.abs(hop) - 1) * PAIRS
     weight = lax.shift_left(jnp.ones_like(lane), jnp.clip(lane, 0, PAIRS)).astype(jnp.float32)
     weight = jnp.where((lane >= 0) & (lane < PAIRS), weight, 0.0)
     used = data_ref[MASK_ROW : MASK_ROW + 1, :128].astype(jnp.float32)
     return jnp.sum(used * weight).astype(jnp.int32)
 
 
-def tile_kernel(hops, first, last, mine_ref, blocks_ref, rate_ref, *refs):
-    window_refs, extra_ref, refs = refs[: 2 * len(hops)], refs[2 * len(hops)], refs[2 * len(hops) + 1 :]
+def tile_kernel(windows, first, last, mine_ref, blocks_ref, rate_ref, *refs):
+    ahead_ref, behind_ref, extra_ref, refs = *refs[:3], refs[3:]
+    window_refs = [ahead_ref, behind_ref]
+    if not first:
+        window_refs = [ahead_ref.at[k] for k in range(3)] + [behind_ref]
+    odd_place = lax.rem(lax.axis_index("space"), 2) == 1
+    hops = [jnp.where(odd_place, odd_hop, even_hop) for even_hop, odd_hop in windows]
     tile_ref, rows_ref, cols_ref, sums_ref, lhs, col, even, odd, made, sems, *held = refs
     total = held[0] if last else sums_ref
     for k, window_ref in enumerate(window_refs):
         prepare_columns(window_ref, 2 * k, lhs, col)
     count = 0
     if first:
-        prepare_columns(extra_ref, 4 * len(hops), lhs, col)
+        prepare_columns(extra_ref, 2 * len(hops), lhs, col)
         for r in range(2):
             rows_ref[r] = r
-            cols_ref[r] = 4 * len(hops) + r
+            cols_ref[r] = 2 * len(hops) + r
         count = 2
         total[...] = jnp.zeros_like(total)
     else:
         total[...] = extra_ref[...]
-    theirs = [listed_behind(window_refs[2 * k + 1], hop) for k, hop in enumerate(hops)]
+    theirs = [listed_behind(ref, hop) for ref, hop in zip(window_refs, hops)]
     count = list_pairs(hops, mine_ref, theirs, rows_ref, cols_ref, jnp.int32(count))
 
     def products(buffer, base):
@@ -233,15 +236,15 @@
     lax.fori_loop(0, groups, sent, 0)
 
 
-def hop_tiles(hops, first, last, mine, blocks, rate, windows, extra):
+def hop_tiles(windows, first, last, mine, blocks, rate, ahead, behind, extra):
     smem = pl.BlockSpec(memory_space=pltpu.SMEM)
     vmem = pl.BlockSpec(memory_space=pltpu.VMEM)
-    columns = 4 * len(hops) + (2 if first else 0)
-    slots = 2 * len(hops) * PAIRS + (UNROLL if first else 0)
+    columns = 2 * len(windows) + (2 if first else 0)
+    slots = len(windows) * PAIRS + (UNROLL if first else 0)
     sums = (NOBODY + 1, 8, BLOCK)
     return pl.pallas_call(
-        functools.partial(tile_kernel, hops, first, last),
-        in_specs=[smem] + [vmem] * (3 + len(windows)),
+        functools.partial(tile_kernel, windows, first, last),
+        in_specs=[smem] + [vmem] * 5,
         out_specs=[pl.BlockSpec(memory_space=pl.ANY), smem, smem, vmem],
         out_shape=[
             jax.ShapeDtypeStruct((slots, BLOCK, BLOCK), jnp.bfloat16),
@@ -260,11 +263,11 @@
         + ([pltpu.VMEM(sums, jnp.float32)] if last else []),
         compiler_params=pltpu.CompilerParams(vmem_limit_bytes=VMEM_LIMIT),
         cost_estimate=pl.CostEstimate(
-            flops=16 * len(hops) * 2 * DEPTH * BLOCK * BLOCK,
+            flops=8 * len(windows) * 2 * DEPTH * BLOCK * BLOCK,
             bytes_accessed=7 * 2**20,
-            transcendentals=16 * len(hops) * BLOCK * BLOCK,
+            transcendentals=8 * len(windows) * BLOCK * BLOCK,
         ),
-    )(mine, blocks, rate, *windows, extra)
+    )(mine, blocks, rate, ahead, behind, extra)
 
 
 def stacked(vectors):
@@ -284,8 +287,8 @@
         place = pl.ds((STARTS[k] + at) * UNROLL, UNROLL)
         return pltpu.make_async_copy(tile_refs[k].at[span], tiles.at[place], sems.at[STARTS[k] + at])
 
-    groups = [lax.div(list_refs[2 * k][COUNT] + (UNROLL - 1), UNROLL) for k in range(len(HOPS))]
-    for k in range(len(HOPS)):
+    groups = [lax.div(list_refs[2 * k][COUNT] + (UNROLL - 1), UNROLL) for k in range(len(WINDOWS))]
+    for k in range(len(WINDOWS)):
 
         def fetch(at, _, k=k):
             copy(k, at).start()
@@ -302,8 +305,7 @@
             held[2 * k + c] = both[:, c * BLOCK : (c + 1) * BLOCK]
     total[...] = jnp.zeros_like(total)
 
-    for k, hops in enumerate(HOPS):
-        slots = [window_slot(hop, side) for hop in hops for side in range(2)]
+    for k, slots in enumerate(PLACES):
 
         def step(at, _, k=k, slots=slots, rows_ref=list_refs[2 * k], cols_ref=list_refs[2 * k + 1]):
             copy(k, at).wait()
@@ -425,7 +427,7 @@
     sound_ref[0] = jnp.where((quality > 0.05) & (next_quality > 0.001), 1, 0)
 
 
-def payload_kernel(pairs_ref, data_ref, scale_ref, payload_ref):
+def payload_kernel(pairs_ref, data_ref, scale_ref, payload_ref, wide_ref):
     n_space, n_sub = lax.axis_size("space"), lax.axis_size("sub")
     space_at, sub_at = lax.axis_index("space"), lax.axis_index("sub")
     lane = lax.broadcasted_iota(jnp.int32, (1, LENGTH), 1)
@@ -438,7 +440,8 @@
         place = (((hop - 1) * n_sub + across) * 2 + (row & 1)) * 2 + (col & 1)
         used = jnp.where((lane == place) & (hop > 0), 1.0, used)
     payload_ref[: ROWS - 16] = data_ref[: ROWS - 16]
-    payload_ref[ROWS - 16 :] = jnp.concatenate(
+    wide_ref[: ROWS - 16] = data_ref[: ROWS - 16]
+    last = jnp.concatenate(
         [
             data_ref[ROWS - 16 : FEAT].astype(jnp.float32),
             scale_ref[...].astype(jnp.float32).reshape(1, LENGTH),
@@ -447,6 +450,9 @@
         ],
         0,
     ).astype(jnp.bfloat16)
+    payload_ref[ROWS - 16 :] = last
+    wide_ref[ROWS - 16 : ROWS] = last
+    wide_ref[ROWS:] = jnp.zeros((WIDE - ROWS, LENGTH), jnp.bfloat16)
 
 
 def on_device(trajectories, kernel_scale, start_vectors, pair_list):
@@ -456,28 +462,28 @@
         compiler_params=pltpu.CompilerParams(vmem_limit_bytes=SMALL_LIMIT),
     )
 
-    payload = pl.pallas_call(
+    payload, wide = pl.pallas_call(
         payload_kernel,
         in_specs=[pl.BlockSpec(memory_space=pltpu.SMEM)] + [pl.BlockSpec(memory_space=pltpu.VMEM)] * 2,
-        out_shape=jax.ShapeDtypeStruct((ROWS, length), jnp.bfloat16),
+        out_shape=[jax.ShapeDtypeStruct((rows, length), jnp.bfloat16) for rows in (ROWS, WIDE)],
         **light,
     )(pair_list.T, trajectories, kernel_scale)
 
-    members = [payload] + [shifted(payload, "sub", e) for e in range(1, N_SUB)]
-    near = {h: shifted(payload, "space", h) for h in (2, -2)}
-    later, near[2], near[-2] = lax.optimization_barrier((payload, near[2], near[-2]))
-    for h, source in ((1, later), (-1, later), (3, near[2]), (-3, near[-2])):
-        near[h] = shifted(source, "space", 1 if h > 0 else -1)
+    far = lax.ppermute(payload, "space", far_pairs(lax.axis_size("space")))
+    ahead, behind = shifted(payload, "space", 2), shifted(payload, "space", -2)
+    members = [shifted(wide, "sub", e) for e in range(1, N_SUB)]
+    far, ahead, behind, *members = lax.optimization_barrier((far, ahead, behind, *members))
+    members = [wide] + members
+    there = swapped(jnp.stack([payload, ahead, behind]))
     blocks, rate = row_operands(members)
     listed = jnp.stack([member[MASK_ROW, : REACH * PAIRS] for member in members]).astype(jnp.int32)
     listed = listed.reshape(N_SUB * REACH * PAIRS)
 
     tiles = []
     carried = payload
-    for at, hops in enumerate(HOPS):
-        windows = [near[side * h] for h in hops for side in (1, -1)]
+    for at, sources in enumerate(((ahead, behind), (there, far))):
         *tile, carried = hop_tiles(
-            hops, at == 0, at == len(HOPS) - 1, listed, blocks, rate, windows, carried
+            WINDOWS[at], at == 0, at == len(WINDOWS) - 1, listed, blocks, rate, *sources, carried
         )
         tiles.append(tile)
     degree = carried

time: 128 us -> 131 us (1.023)
  waiting for transfers between devices: 33.5 us -> 35.9 us
  Pallas kernels: 21.6 us -> 20 us
    ppermute x4 -> x6, waiting for transfers between devices: 9.72 us -> 17.4 us  [the longest x1 8.04 us: on_device(): far = lax.ppermute(payload, 'space', far_pairs(lax.axis_size('space')))]
    ppermute x22 -> x18, waiting for transfers between devices: 23.7 us -> 18.5 us  [shifted(): lax.ppermute(value, axis, [((at + steps) % count, at) for at in range(cou...]
    ppermute x4 -> x6, starting transfers between devices: 5.09 us -> 8.25 us  [the longest x3 8.25 us: swapped(): lax.ppermute(value, 'space', [(at, at ^ 1) for at in range(lax.axis_size(...]
    ppermute x22 -> x18, starting transfers between devices: 38 us -> 35.7 us  [shifted(): lax.ppermute(value, axis, [((at + steps) % count, at) for at in range(cou...]
  transfers between devices with their start and end apart: 26 -> 24, of which waited for: 18 -> 17; matrix products, arithmetic and copies ran while one was open for 0% -> 0% of each run, Pallas kernels for 4% -> 3%
where the time goes in v6:
time: 131 us; the launch traced here: 130 us
  starting transfers between devices  44 us (34%)
  waiting for transfers between devices  35.9 us (27%)
  blocking collectives  25.1 us (19%)
  Pallas kernels  20 us (15%)
  local copies, waits for them, and re-layouts  3.23 us (2%)
    ppermute x18, starting transfers between devices, shifted(): lax.ppermute(value, axis, [((at + steps) % count, at) for at in range(cou...  35.7 us
    all_to_all x2, blocking collectives, summed(): lax.all_to_all(sent, ('space', 'sub'), 0, 0, axis_index_groups=groups)  25.1 us
    ppermute x18, waiting for transfers between devices, shifted(): lax.ppermute(value, axis, [((at + steps) % count, at) for at in range(cou...  18.5 us
    pallas_call x2, Pallas kernels, hop_tiles(): pl.pallas_call(functools.partial(tile_kernel, windows, first, last), in_s...  9.84 us
    ppermute x3, starting transfers between devices, swapped(): lax.ppermute(value, 'space', [(at, at ^ 1) for at in range(lax.axis_size(...  8.25 us
    ppermute x1, waiting for transfers between devices, on_device(): far = lax.ppermute(payload, 'space', far_pairs(lax.axis_size('space')))  8.04 us
    ppermute x2, waiting for transfers between devices, space_window(): lax.ppermute(value, 'space', far_pairs(lax.axis_size('space')))  7.36 us
    pallas_call x2, Pallas kernels, sweep(): pl.pallas_call(functools.partial(sweep_kernel, parts), in_specs=[smem] *...  6.07 us
  transfers between devices with their start and end apart: 24, of which 17 were waited for; matrix products, arithmetic and copies ran while one was open for 0% of the time, Pallas kernels for 3%

profile of v6, /device:TPU:1, one launch (start us, length us, event | category | flops | bytes accessed | tf_op | source)
XLA Modules:
  0.0 130.3 jit_solution(12601536453769466773)
XLA Ops:
  0.0 1.0 copy-done
  1.0 0.7 copy-done.1
  1.6 0.7 copy-done.2
  2.3 0.8 shard_map.48
  3.1 2.1 %collective-permute-start.2 = (bf16[304,512]{1,0:T(8,128)(2,1)S(1)}, bf16[304,512]{1,0:T(8,128)(2,1)S(1)}, u32[]{:S(2)}, u32[]{:S(2)}) collective-permute-start(bf16[304,512]{1,0:T(8,128)(2,1)S(1)} %get-tuple-element.56.refs_2_), channel_id=1, source_target_pairs={{248,0},{252,4},{0,8},{4,12},{8,16},{12,20},{16,24},{20,28},{24,32... | collective-permute-start | bytes 933896 | tf_op jit(solution)/shard_map/ppermute | solution.py:40
  5.3 1.3 collective-permute-start.5
  6.6 2.6 %collective-permute-start.4 = (bf16[320,512]{1,0:T(8,128)(2,1)S(1)}, bf16[320,512]{1,0:T(8,128)(2,1)S(1)}, u32[]{:S(2)}, u32[]{:S(2)}) collective-permute-start(bf16[320,512]{1,0:T(8,128)(2,1)S(1)} %get-tuple-element.55.refs_0_), channel_id=1, source_target_pairs={{2,0},{3,1},{0,2},{1,3},{6,4},{7,5},{4,6},{5,7},{10,8},{11,9},{8,1... | collective-permute-start | bytes 983048 | tf_op jit(solution)/shard_map/ppermute | solution.py:40
  9.2 1.1 collective-permute-start.3
  10.3 6.6 %collective-permute-start.1 = (bf16[304,512]{1,0:T(8,128)(2,1)S(1)}, bf16[304,512]{1,0:T(8,128)(2,1)S(1)}, u32[]{:S(2)}, u32[]{:S(2)}) collective-permute-start(bf16[304,512]{1,0:T(8,128)(2,1)S(1)} %get-tuple-element.56.refs_2_), channel_id=1, source_target_pairs={{8,0},{12,4},{16,8},{20,12},{24,16},{28,20},{32,24},{36,28},{40,32... | collective-permute-start | bytes 933896 | tf_op jit(solution)/shard_map/ppermute | solution.py:40
  16.9 2.0 %collective-permute-done.2.refs_1_ = bf16[304,512]{1,0:T(8,128)(2,1)S(1)} collective-permute-done((bf16[304,512]{1,0:T(8,128)(2,1)S(1)}, bf16[304,512]{1,0:T(8,128)(2,1)S(1)}, u32[]{:S(2)}, u32[]{:S(2)}) %collective-permute-start.2) | collective-permute-done | bytes 311328 | tf_op jit(solution)/shard_map/ppermute | solution.py:40
  18.9 3.1 %collective-permute-done.1.refs_0_ = bf16[304,512]{1,0:T(8,128)(2,1)S(1)} collective-permute-done((bf16[304,512]{1,0:T(8,128)(2,1)S(1)}, bf16[304,512]{1,0:T(8,128)(2,1)S(1)}, u32[]{:S(2)}, u32[]{:S(2)}) %collective-permute-start.1) | collective-permute-done | bytes 311328 | tf_op jit(solution)/shard_map/ppermute | solution.py:40
  22.0 8.0 %collective-permute-done.refs_1_ = bf16[304,512]{1,0:T(8,128)(2,1)S(1)} collective-permute-done((bf16[304,512]{1,0:T(8,128)(2,1)S(1)}, bf16[304,512]{1,0:T(8,128)(2,1)S(1)}, u32[]{:S(2)}, u32[]{:S(2)}) %collective-permute-start) | collective-permute-done | bytes 311328 | tf_op jit(solution)/shard_map/ppermute | solution.py:472
  30.1 1.1 pad_maximum_fusion
  31.4 0.3 shard_map.49
  31.7 3.9 %shard_map.50 = (bf16[40,256,256]{2,1,0:T(8,128)(2,1)S(1)}, s32[80]{0:T(128)S(1)}, s32[80]{0:T(128)S(1)}, f32[9,8,256]{2,1,0:T(8,128)S(1)}) custom-call(s32[192]{0:T(256)S(1)} %reshape.20.mine_ref, bf16[8,320,256]{2,1,0:T(8,128)(2,1)S(1)} %get-tuple-element.60.blocks_ref, f32[8,8,256]{2,1,0:T(8,128)S(1)} %get-tuple-element.61.rate_ref, ...), custom_call_target="tpu_custom_call" | custom-call | flops 671088640 | bytes 7340032 | tf_op jit(solution)/shard_map/pallas_call | solution.py:245
  35.7 5.9 %shard_map.51 = (bf16[64,256,256]{2,1,0:T(8,128)(2,1)S(1)}, s32[80]{0:T(128)S(1)}, s32[80]{0:T(128)S(1)}, f32[4,8,512]{2,1,0:T(8,128)S(1)}) custom-call(s32[192]{0:T(256)S(1)} %reshape.20.mine_ref, bf16[8,320,256]{2,1,0:T(8,128)(2,1)S(1)} %get-tuple-element.60.blocks_ref, f32[8,8,256]{2,1,0:T(8,128)S(1)} %get-tuple-element.61.rate_ref, ...), custom_call_target="tpu_custom_call" | custom-call | flops 1342177280 | bytes 7340032 | tf_op jit(solution)/shard_map/pallas_call | solution.py:245
  41.6 2.8 %collective-permute-start.9 = (f32[1,512]{1,0:T(1,128)S(1)}, f32[1,512]{1,0:T(1,128)S(1)}, u32[]{:S(2)}, u32[]{:S(2)}) collective-permute-start(f32[1,512]{1,0:T(1,128)S(1)} %get-tuple-element.94), channel_id=1, source_target_pairs={{1,0},{2,1},{3,2},{0,3},{5,4},{6,5},{7,6},{4,7},{9,8},{10,9},{11,1... | collective-permute-start | bytes 6152 | tf_op jit(solution)/shard_map/ppermute | solution.py:40
  44.4 1.1 collective-permute-start.8
  45.5 0.8 collective-permute-start.7
  46.3 2.1 %collective-permute-done.8 = f32[1,512]{1,0:T(1,128)S(1)} collective-permute-done((f32[1,512]{1,0:T(1,128)S(1)}, f32[1,512]{1,0:T(1,128)S(1)}, u32[]{:S(2)}, u32[]{:S(2)}) %collective-permute-start.8) | collective-permute-done | bytes 2080 | tf_op jit(solution)/shard_map/ppermute | solution.py:40
  48.4 0.8 collective-permute-done.7
  49.2 5.7 %collective-permute-start.11 = (bf16[32,512]{1,0:T(8,128)(2,1)S(1)}, bf16[32,512]{1,0:T(8,128)(2,1)S(1)}, u32[]{:S(2)}, u32[]{:S(2)}) collective-permute-start(bf16[32,512]{1,0:T(8,128)(2,1)S(1)} %multiply_convert_fusion), channel_id=1, source_target_pairs={{8,0},{12,4},{16,8},{20,12},{24,16},{28,20},{32,24},{36,28},{40,32... | collective-permute-start | bytes 98312 | tf_op jit(solution)/shard_map/ppermute | solution.py:40
  55.0 1.0 collective-permute-done.11
  56.0 3.8 %collective-permute-done.10.refs_8_ = bf16[32,512]{1,0:T(8,128)(2,1)S(1)} collective-permute-done((bf16[32,512]{1,0:T(8,128)(2,1)S(1)}, bf16[32,512]{1,0:T(8,128)(2,1)S(1)}, u32[]{:S(2)}, u32[]{:S(2)}) %collective-permute-start.10) | collective-permute-done | bytes 32800 | tf_op jit(solution)/shard_map/ppermute | solution.py:54
  59.8 1.2 collective-permute-done.12
  61.0 3.3 %collective-permute-start.13 = (bf16[3,32,512]{2,1,0:T(8,128)(2,1)S(1)}, bf16[3,32,512]{2,1,0:T(8,128)(2,1)S(1)}, u32[]{:S(2)}, u32[]{:S(2)}) collective-permute-start(bf16[3,32,512]{2,1,0:T(8,128)(2,1)S(1)} %pad_maximum_fusion.2.refs_6_), channel_id=1, source_target_pairs={{0,4},{4,0},{8,12},{12,8},{16,20},{20,16},{24,28},{28,24},{32,36},... | collective-permute-start | bytes 294920 | tf_op jit(solution)/shard_map/ppermute | solution.py:48
  64.3 0.9 collective-permute-done.13.refs_7_
  65.3 3.0 %shard_map.52 = (f32[32,512]{1,0:T(8,128)S(1)}, f32[32,512]{1,0:T(8,128)S(1)}, f32[32,512]{1,0:T(8,128)S(1)}, f32[32,512]{1,0:T(8,128)S(1)}) custom-call(s32[80]{0:T(128)S(1)} %get-tuple-element.67.refs_0_, s32[80]{0:T(128)S(1)} %get-tuple-element.68.refs_1_, s32[80]{0:T(128)S(1)} %get-tuple-element.69.refs_2_, s32[80]{0:T(128)S(1)} %get-tuple-element.70.refs_3_, ...), custom_call_target="tpu_custom_call" | custom-call | flops 838860800 | bytes 7340032 | tf_op jit(solution)/shard_map/pallas_call | solution.py:342
  68.4 2.3 %collective-permute-start.15 = (f32[32,512]{1,0:T(8,128)S(1)}, f32[32,512]{1,0:T(8,128)S(1)}, u32[]{:S(2)}, u32[]{:S(2)}) collective-permute-start(f32[32,512]{1,0:T(8,128)S(1)} %get-tuple-element.78), channel_id=1, source_target_pairs={{2,0},{3,1},{0,2},{1,3},{6,4},{7,5},{4,6},{5,7},{10,8},{11,9},{8,1... | collective-permute-start | bytes 196616 | tf_op jit(solution)/shard_map/ppermute | solution.py:40
  70.8 0.4 collective-permute-start.16
  71.2 2.6 %collective-permute-done.14.refs_1_ = f32[32,512]{1,0:T(8,128)S(1)} collective-permute-done((f32[32,512]{1,0:T(8,128)S(1)}, f32[32,512]{1,0:T(8,128)S(1)}, u32[]{:S(2)}, u32[]{:S(2)}) %collective-permute-start.14) | collective-permute-done | bytes 65568 | tf_op jit(solution)/shard_map/ppermute | solution.py:40
  73.8 0.5 collective-permute-done.16.refs_3_
  74.5 4.8 %collective-permute-start.18 = (f32[32,512]{1,0:T(8,128)S(1)}, f32[32,512]{1,0:T(8,128)S(1)}, u32[]{:S(2)}, u32[]{:S(2)}) collective-permute-start(f32[32,512]{1,0:T(8,128)S(1)} %get-tuple-element.81), channel_id=1, source_target_pairs={{8,0},{12,4},{16,8},{20,12},{24,16},{28,20},{32,24},{36,28},{40,32... | collective-permute-start | bytes 196616 | tf_op jit(solution)/shard_map/ppermute | solution.py:40
  79.3 1.6 %collective-permute-done.19 = f32[32,512]{1,0:T(8,128)S(1)} collective-permute-done((f32[32,512]{1,0:T(8,128)S(1)}, f32[32,512]{1,0:T(8,128)S(1)}, u32[]{:S(2)}, u32[]{:S(2)}) %collective-permute-start.19) | collective-permute-done | bytes 65568 | tf_op jit(solution)/shard_map/ppermute | solution.py:40
  80.9 3.5 %collective-permute-done.17.refs_8_ = f32[32,512]{1,0:T(8,128)S(1)} collective-permute-done((f32[32,512]{1,0:T(8,128)S(1)}, f32[32,512]{1,0:T(8,128)S(1)}, u32[]{:S(2)}, u32[]{:S(2)}) %collective-permute-start.17) | collective-permute-done | bytes 65568 | tf_op jit(solution)/shard_map/ppermute | solution.py:54
  84.5 4.8 %collective-permute-start.20 = (f32[3,32,512]{2,1,0:T(8,128)S(1)}, f32[3,32,512]{2,1,0:T(8,128)S(1)}, u32[]{:S(2)}, u32[]{:S(2)}) collective-permute-start(f32[3,32,512]{2,1,0:T(8,128)S(1)} %pad_maximum_fusion.1.refs_6_), channel_id=1, source_target_pairs={{0,4},{4,0},{8,12},{12,8},{16,20},{20,16},{24,28},{28,24},{32,36},... | collective-permute-start | bytes 589832 | tf_op jit(solution)/shard_map/ppermute | solution.py:48
  89.3 1.1 collective-permute-done.20.refs_7_
  90.4 3.1 %shard_map.54 = (f32[32,512]{1,0:T(8,128)S(1)}, f32[32,512]{1,0:T(8,128)S(1)}, f32[32,512]{1,0:T(8,128)S(1)}, f32[32,512]{1,0:T(8,128)S(1)}) custom-call(s32[80]{0:T(128)S(1)} %get-tuple-element.67.refs_0_, s32[80]{0:T(128)S(1)} %get-tuple-element.68.refs_1_, s32[80]{0:T(128)S(1)} %get-tuple-element.69.refs_2_, s32[80]{0:T(128)S(1)} %get-tuple-element.70.refs_3_, ...), custom_call_target="tpu_custom_call" | custom-call | flops 838860800 | bytes 7340032 | tf_op jit(solution)/shard_map/pallas_call | solution.py:342
  93.5 0.9 collective-permute-start.21
  94.4 2.4 %collective-permute-start.22 = (f32[32,512]{1,0:T(8,128)S(1)}, f32[32,512]{1,0:T(8,128)S(1)}, u32[]{:S(2)}, u32[]{:S(2)}) collective-permute-start(f32[32,512]{1,0:T(8,128)S(1)} %get-tuple-element.87), channel_id=1, source_target_pairs={{2,0},{3,1},{0,2},{1,3},{6,4},{7,5},{4,6},{5,7},{10,8},{11,9},{8,1... | collective-permute-start | bytes 196616 | tf_op jit(solution)/shard_map/ppermute | solution.py:40
  96.8 0.5 collective-permute-start.23
  97.3 0.6 collective-permute-done.21.refs_1_
  97.9 1.4 %collective-permute-done.22.refs_2_ = f32[32,512]{1,0:T(8,128)S(1)} collective-permute-done((f32[32,512]{1,0:T(8,128)S(1)}, f32[32,512]{1,0:T(8,128)S(1)}, u32[]{:S(2)}, u32[]{:S(2)}) %collective-permute-start.22) | collective-permute-done | bytes 65568 | tf_op jit(solution)/shard_map/ppermute | solution.py:40
  99.3 1.5 %collective-permute-done.23.refs_3_ = f32[32,512]{1,0:T(8,128)S(1)} collective-permute-done((f32[32,512]{1,0:T(8,128)S(1)}, f32[32,512]{1,0:T(8,128)S(1)}, u32[]{:S(2)}, u32[]{:S(2)}) %collective-permute-start.23) | collective-permute-done | bytes 65568 | tf_op jit(solution)/shard_map/ppermute | solution.py:40
  101.2 13.6 %all_to_all.20 = f32[32,16,128]{2,1,0:T(8,128)S(1)} all-to-all(f32[32,16,128]{2,1,0:T(8,128)S(1)} %broadcast_in_dim.13), channel_id=1, replica_groups={{0,1,2,3,4,5,6,7,8,9,10,11,12,13,14,15,16,17,18,19,20,21,22,23,24,25,26..., dimensions={0} | all-to-all | bytes 524288 | tf_op jit(solution)/shard_map/all_to_all | solution.py:78
  114.8 11.5 %all_to_all.21 = f32[8,16,128]{2,1,0:T(8,128)S(1)} all-to-all(f32[8,16,128]{2,1,0:T(8,128)S(1)} %broadcast_in_dim.28), channel_id=1, replica_groups={{0,32,64,96,128,160,192,224},{1,33,65,97,129,161,193,225},{2,34,66,98,1..., dimensions={0} | all-to-all | bytes 131072 | tf_op jit(solution)/shard_map/all_to_all | solution.py:78
  126.4 2.6 %shard_map.56 = (f32[32,512]{1,0:T(8,128)S(1)}, s32[1]{0:T(128)}) custom-call(f32[64,32]{1,0:T(8,128)S(1)} %reshape.19.grams_ref, f32[32,512]{1,0:T(8,128)S(1)} %get-tuple-element.90.image_ref), custom_call_target="tpu_custom_call" | custom-call | flops 1048576 | bytes 131072 | tf_op jit(solution)/shard_map/pallas_call | solution.py:505
  129.7 0.6 copy-done.4
  (42 shorter events, 1.2 us)
Async XLA Ops:
  0.0 1.0 copy-start
  1.0 0.7 copy-start.1
  1.6 0.7 copy-start.2
  3.1 15.8 %collective-permute-start.2 = (bf16[304,512]{1,0:T(8,128)(2,1)S(1)}, bf16[304,512]{1,0:T(8,128)(2,1)S(1)}, u32[]{:S(2)}, u32[]{:S(2)}) collective-permute-start(bf16[304,512]{1,0:T(8,128)(2,1)S(1)} %get-tuple-element.56.refs_2_), channel_id=1, source_target_pairs={{248,0},{252,4},{0,8},{4,12},{8,16},{12,20},{16,24},{20,28},{24,32... | collective-permute-start | bytes 933896 | tf_op jit(solution)/shard_map/ppermute | solution.py:40
  5.3 24.8 %collective-permute-start.5 = (bf16[320,512]{1,0:T(8,128)(2,1)S(1)}, bf16[320,512]{1,0:T(8,128)(2,1)S(1)}, u32[]{:S(2)}, u32[]{:S(2)}) collective-permute-start(bf16[320,512]{1,0:T(8,128)(2,1)S(1)} %get-tuple-element.55.refs_0_), channel_id=1, source_target_pairs={{3,0},{0,1},{1,2},{2,3},{7,4},{4,5},{5,6},{6,7},{11,8},{8,9},{9,10... | collective-permute-start | bytes 983048 | tf_op jit(solution)/shard_map/ppermute | solution.py:40
  6.6 23.5 %collective-permute-start.4 = (bf16[320,512]{1,0:T(8,128)(2,1)S(1)}, bf16[320,512]{1,0:T(8,128)(2,1)S(1)}, u32[]{:S(2)}, u32[]{:S(2)}) collective-permute-start(bf16[320,512]{1,0:T(8,128)(2,1)S(1)} %get-tuple-element.55.refs_0_), channel_id=1, source_target_pairs={{2,0},{3,1},{0,2},{1,3},{6,4},{7,5},{4,6},{5,7},{10,8},{11,9},{8,1... | collective-permute-start | bytes 983048 | tf_op jit(solution)/shard_map/ppermute | solution.py:40
  9.2 20.9 %collective-permute-start.3 = (bf16[320,512]{1,0:T(8,128)(2,1)S(1)}, bf16[320,512]{1,0:T(8,128)(2,1)S(1)}, u32[]{:S(2)}, u32[]{:S(2)}) collective-permute-start(bf16[320,512]{1,0:T(8,128)(2,1)S(1)} %get-tuple-element.55.refs_0_), channel_id=1, source_target_pairs={{1,0},{2,1},{3,2},{0,3},{5,4},{6,5},{7,6},{4,7},{9,8},{10,9},{11,1... | collective-permute-start | bytes 983048 | tf_op jit(solution)/shard_map/ppermute | solution.py:40
  10.3 11.8 %collective-permute-start.1 = (bf16[304,512]{1,0:T(8,128)(2,1)S(1)}, bf16[304,512]{1,0:T(8,128)(2,1)S(1)}, u32[]{:S(2)}, u32[]{:S(2)}) collective-permute-start(bf16[304,512]{1,0:T(8,128)(2,1)S(1)} %get-tuple-element.56.refs_2_), channel_id=1, source_target_pairs={{8,0},{12,4},{16,8},{20,12},{24,16},{28,20},{32,24},{36,28},{40,32... | collective-permute-start | bytes 933896 | tf_op jit(solution)/shard_map/ppermute | solution.py:40
  18.9 11.2 %collective-permute-start = (bf16[304,512]{1,0:T(8,128)(2,1)S(1)}, bf16[304,512]{1,0:T(8,128)(2,1)S(1)}, u32[]{:S(2)}, u32[]{:S(2)}) collective-permute-start(bf16[304,512]{1,0:T(8,128)(2,1)S(1)} %get-tuple-element.56.refs_2_), channel_id=1, source_target_pairs={{0,244},{4,16},{8,252},{12,24},{16,4},{20,32},{24,12},{28,40},{32,... | collective-permute-start | bytes 933896 | tf_op jit(solution)/shard_map/ppermute | solution.py:472
  31.1 4.5 %collective-permute-start.6 = (bf16[3,304,512]{2,1,0:T(8,128)(2,1)}, bf16[3,304,512]{2,1,0:T(8,128)(2,1)S(1)}, u32[]{:S(2)}, u32[]{:S(2)}) collective-permute-start(bf16[3,304,512]{2,1,0:T(8,128)(2,1)} %pad_maximum_fusion), channel_id=1, source_target_pairs={{0,4},{4,0},{8,12},{12,8},{16,20},{20,16},{24,28},{28,24},{32,36},... | collective-permute-start | bytes 2801672 | tf_op jit(solution)/shard_map/ppermute | solution.py:48
  31.4 17.8 %copy-start.3 = (f32[32,512]{1,0:T(8,128)S(1)}, f32[32,512]{1,0:T(8,128)}, u32[]{:S(2)}) copy-start(f32[32,512]{1,0:T(8,128)} %param.8) | copy-start | bytes 196612
  41.6 4.7 %collective-permute-start.9 = (f32[1,512]{1,0:T(1,128)S(1)}, f32[1,512]{1,0:T(1,128)S(1)}, u32[]{:S(2)}, u32[]{:S(2)}) collective-permute-start(f32[1,512]{1,0:T(1,128)S(1)} %get-tuple-element.94), channel_id=1, source_target_pairs={{1,0},{2,1},{3,2},{0,3},{5,4},{6,5},{7,6},{4,7},{9,8},{10,9},{11,1... | collective-permute-start | bytes 6152 | tf_op jit(solution)/shard_map/ppermute | solution.py:40
  44.4 3.9 %collective-permute-start.8 = (f32[1,512]{1,0:T(1,128)S(1)}, f32[1,512]{1,0:T(1,128)S(1)}, u32[]{:S(2)}, u32[]{:S(2)}) collective-permute-start(f32[1,512]{1,0:T(1,128)S(1)} %get-tuple-element.95), channel_id=1, source_target_pairs={{2,0},{3,1},{0,2},{1,3},{6,4},{7,5},{4,6},{5,7},{10,8},{11,9},{8,1... | collective-permute-start | bytes 6152 | tf_op jit(solution)/shard_map/ppermute | solution.py:40
  45.5 3.6 %collective-permute-start.7 = (f32[1,512]{1,0:T(1,128)S(1)}, f32[1,512]{1,0:T(1,128)S(1)}, u32[]{:S(2)}, u32[]{:S(2)}) collective-permute-start(f32[1,512]{1,0:T(1,128)S(1)} %get-tuple-element.96), channel_id=1, source_target_pairs={{3,0},{0,1},{1,2},{2,3},{7,4},{4,5},{5,6},{6,7},{11,8},{8,9},{9,10... | collective-permute-start | bytes 6152 | tf_op jit(solution)/shard_map/ppermute | solution.py:40
  49.2 6.8 %collective-permute-start.11 = (bf16[32,512]{1,0:T(8,128)(2,1)S(1)}, bf16[32,512]{1,0:T(8,128)(2,1)S(1)}, u32[]{:S(2)}, u32[]{:S(2)}) collective-permute-start(bf16[32,512]{1,0:T(8,128)(2,1)S(1)} %multiply_convert_fusion), channel_id=1, source_target_pairs={{8,0},{12,4},{16,8},{20,12},{24,16},{28,20},{32,24},{36,28},{40,32... | collective-permute-start | bytes 98312 | tf_op jit(solution)/shard_map/ppermute | solution.py:40
  54.9 4.8 %collective-permute-start.10 = (bf16[32,512]{1,0:T(8,128)(2,1)S(1)}, bf16[32,512]{1,0:T(8,128)(2,1)S(1)}, u32[]{:S(2)}, u32[]{:S(2)}) collective-permute-start(bf16[32,512]{1,0:T(8,128)(2,1)S(1)} %multiply_convert_fusion), channel_id=1, source_target_pairs={{0,244},{4,16},{8,252},{12,24},{16,4},{20,32},{24,12},{28,40},{32,... | collective-permute-start | bytes 98312 | tf_op jit(solution)/shard_map/ppermute | solution.py:54
  54.9 6.1 %collective-permute-start.12 = (bf16[32,512]{1,0:T(8,128)(2,1)S(1)}, bf16[32,512]{1,0:T(8,128)(2,1)S(1)}, u32[]{:S(2)}, u32[]{:S(2)}) collective-permute-start(bf16[32,512]{1,0:T(8,128)(2,1)S(1)} %multiply_convert_fusion), channel_id=1, source_target_pairs={{248,0},{252,4},{0,8},{4,12},{8,16},{12,20},{16,24},{20,28},{24,32... | collective-permute-start | bytes 98312 | tf_op jit(solution)/shard_map/ppermute | solution.py:40
  61.0 4.2 %collective-permute-start.13 = (bf16[3,32,512]{2,1,0:T(8,128)(2,1)S(1)}, bf16[3,32,512]{2,1,0:T(8,128)(2,1)S(1)}, u32[]{:S(2)}, u32[]{:S(2)}) collective-permute-start(bf16[3,32,512]{2,1,0:T(8,128)(2,1)S(1)} %pad_maximum_fusion.2.refs_6_), channel_id=1, source_target_pairs={{0,4},{4,0},{8,12},{12,8},{16,20},{20,16},{24,28},{28,24},{32,36},... | collective-permute-start | bytes 294920 | tf_op jit(solution)/shard_map/ppermute | solution.py:48
  68.3 5.5 %collective-permute-start.14 = (f32[32,512]{1,0:T(8,128)S(1)}, f32[32,512]{1,0:T(8,128)S(1)}, u32[]{:S(2)}, u32[]{:S(2)}) collective-permute-start(f32[32,512]{1,0:T(8,128)S(1)} %get-tuple-element.77), channel_id=1, source_target_pairs={{3,0},{0,1},{1,2},{2,3},{7,4},{4,5},{5,6},{6,7},{11,8},{8,9},{9,10... | collective-permute-start | bytes 196616 | tf_op jit(solution)/shard_map/ppermute | solution.py:40
  68.4 5.3 %collective-permute-start.15 = (f32[32,512]{1,0:T(8,128)S(1)}, f32[32,512]{1,0:T(8,128)S(1)}, u32[]{:S(2)}, u32[]{:S(2)}) collective-permute-start(f32[32,512]{1,0:T(8,128)S(1)} %get-tuple-element.78), channel_id=1, source_target_pairs={{2,0},{3,1},{0,2},{1,3},{6,4},{7,5},{4,6},{5,7},{10,8},{11,9},{8,1... | collective-permute-start | bytes 196616 | tf_op jit(solution)/shard_map/ppermute | solution.py:40
  70.8 3.5 %collective-permute-start.16 = (f32[32,512]{1,0:T(8,128)S(1)}, f32[32,512]{1,0:T(8,128)S(1)}, u32[]{:S(2)}, u32[]{:S(2)}) collective-permute-start(f32[32,512]{1,0:T(8,128)S(1)} %get-tuple-element.79), channel_id=1, source_target_pairs={{1,0},{2,1},{3,2},{0,3},{5,4},{6,5},{7,6},{4,7},{9,8},{10,9},{11,1... | collective-permute-start | bytes 196616 | tf_op jit(solution)/shard_map/ppermute | solution.py:40
  74.5 6.5 %collective-permute-start.19 = (f32[32,512]{1,0:T(8,128)S(1)}, f32[32,512]{1,0:T(8,128)S(1)}, u32[]{:S(2)}, u32[]{:S(2)}) collective-permute-start(f32[32,512]{1,0:T(8,128)S(1)} %get-tuple-element.81), channel_id=1, source_target_pairs={{248,0},{252,4},{0,8},{4,12},{8,16},{12,20},{16,24},{20,28},{24,32... | collective-permute-start | bytes 196616 | tf_op jit(solution)/shard_map/ppermute | solution.py:40
  74.5 6.4 %collective-permute-start.18 = (f32[32,512]{1,0:T(8,128)S(1)}, f32[32,512]{1,0:T(8,128)S(1)}, u32[]{:S(2)}, u32[]{:S(2)}) collective-permute-start(f32[32,512]{1,0:T(8,128)S(1)} %get-tuple-element.81), channel_id=1, source_target_pairs={{8,0},{12,4},{16,8},{20,12},{24,16},{28,20},{32,24},{36,28},{40,32... | collective-permute-start | bytes 196616 | tf_op jit(solution)/shard_map/ppermute | solution.py:40
  79.3 5.2 %collective-permute-start.17 = (f32[32,512]{1,0:T(8,128)S(1)}, f32[32,512]{1,0:T(8,128)S(1)}, u32[]{:S(2)}, u32[]{:S(2)}) collective-permute-start(f32[32,512]{1,0:T(8,128)S(1)} %get-tuple-element.81), channel_id=1, source_target_pairs={{0,244},{4,16},{8,252},{12,24},{16,4},{20,32},{24,12},{28,40},{32,... | collective-permute-start | bytes 196616 | tf_op jit(solution)/shard_map/ppermute | solution.py:54
  84.5 5.9 %collective-permute-start.20 = (f32[3,32,512]{2,1,0:T(8,128)S(1)}, f32[3,32,512]{2,1,0:T(8,128)S(1)}, u32[]{:S(2)}, u32[]{:S(2)}) collective-permute-start(f32[3,32,512]{2,1,0:T(8,128)S(1)} %pad_maximum_fusion.1.refs_6_), channel_id=1, source_target_pairs={{0,4},{4,0},{8,12},{12,8},{16,20},{20,16},{24,28},{28,24},{32,36},... | collective-permute-start | bytes 589832 | tf_op jit(solution)/shard_map/ppermute | solution.py:48
  93.5 4.4 %collective-permute-start.21 = (f32[32,512]{1,0:T(8,128)S(1)}, f32[32,512]{1,0:T(8,128)S(1)}, u32[]{:S(2)}, u32[]{:S(2)}) collective-permute-start(f32[32,512]{1,0:T(8,128)S(1)} %get-tuple-element.86), channel_id=1, source_target_pairs={{3,0},{0,1},{1,2},{2,3},{7,4},{4,5},{5,6},{6,7},{11,8},{8,9},{9,10... | collective-permute-start | bytes 196616 | tf_op jit(solution)/shard_map/ppermute | solution.py:40
  94.4 4.9 %collective-permute-start.22 = (f32[32,512]{1,0:T(8,128)S(1)}, f32[32,512]{1,0:T(8,128)S(1)}, u32[]{:S(2)}, u32[]{:S(2)}) collective-permute-start(f32[32,512]{1,0:T(8,128)S(1)} %get-tuple-element.87), channel_id=1, source_target_pairs={{2,0},{3,1},{0,2},{1,3},{6,4},{7,5},{4,6},{5,7},{10,8},{11,9},{8,1... | collective-permute-start | bytes 196616 | tf_op jit(solution)/shard_map/ppermute | solution.py:40
  96.8 4.0 %collective-permute-start.23 = (f32[32,512]{1,0:T(8,128)S(1)}, f32[32,512]{1,0:T(8,128)S(1)}, u32[]{:S(2)}, u32[]{:S(2)}) collective-permute-start(f32[32,512]{1,0:T(8,128)S(1)} %get-tuple-element.88), channel_id=1, source_target_pairs={{1,0},{2,1},{3,2},{0,3},{5,4},{6,5},{7,6},{4,7},{9,8},{10,9},{11,1... | collective-permute-start | bytes 196616 | tf_op jit(solution)/shard_map/ppermute | solution.py:40
  129.7 0.6 copy-start.4

commit v7 on v6

--- a/solution.py
+++ b/solution.py
@@ -167,10 +167,7 @@
 
 
 def tile_kernel(windows, first, last, mine_ref, blocks_ref, rate_ref, *refs):
-    ahead_ref, behind_ref, extra_ref, refs = *refs[:3], refs[3:]
-    window_refs = [ahead_ref, behind_ref]
-    if not first:
-        window_refs = [ahead_ref.at[k] for k in range(3)] + [behind_ref]
+    window_refs, extra_ref, refs = refs[: len(windows)], refs[len(windows)], refs[len(windows) + 1 :]
     odd_place = lax.rem(lax.axis_index("space"), 2) == 1
     hops = [jnp.where(odd_place, odd_hop, even_hop) for even_hop, odd_hop in windows]
     tile_ref, rows_ref, cols_ref, sums_ref, lhs, col, even, odd, made, sems, *held = refs
@@ -236,7 +233,7 @@
     lax.fori_loop(0, groups, sent, 0)
 
 
-def hop_tiles(windows, first, last, mine, blocks, rate, ahead, behind, extra):
+def hop_tiles(windows, first, last, mine, blocks, rate, sources, extra):
     smem = pl.BlockSpec(memory_space=pltpu.SMEM)
     vmem = pl.BlockSpec(memory_space=pltpu.VMEM)
     columns = 2 * len(windows) + (2 if first else 0)
@@ -244,7 +241,7 @@
     sums = (NOBODY + 1, 8, BLOCK)
     return pl.pallas_call(
         functools.partial(tile_kernel, windows, first, last),
-        in_specs=[smem] + [vmem] * 5,
+        in_specs=[smem] + [vmem] * (3 + len(sources)),
         out_specs=[pl.BlockSpec(memory_space=pl.ANY), smem, smem, vmem],
         out_shape=[
             jax.ShapeDtypeStruct((slots, BLOCK, BLOCK), jnp.bfloat16),
@@ -267,7 +264,7 @@
             bytes_accessed=7 * 2**20,
             transcendentals=8 * len(windows) * BLOCK * BLOCK,
         ),
-    )(mine, blocks, rate, ahead, behind, extra)
+    )(mine, blocks, rate, *sources, extra)
 
 
 def stacked(vectors):
@@ -469,21 +466,20 @@
         **light,
     )(pair_list.T, trajectories, kernel_scale)
 
-    far = lax.ppermute(payload, "space", far_pairs(lax.axis_size("space")))
+    members = [wide] + [shifted(wide, "sub", e) for e in range(1, N_SUB)]
     ahead, behind = shifted(payload, "space", 2), shifted(payload, "space", -2)
-    members = [shifted(wide, "sub", e) for e in range(1, N_SUB)]
-    far, ahead, behind, *members = lax.optimization_barrier((far, ahead, behind, *members))
-    members = [wide] + members
-    there = swapped(jnp.stack([payload, ahead, behind]))
+    later, ahead, behind = lax.optimization_barrier((payload, ahead, behind))
+    there = swapped(later), swapped(ahead), swapped(behind)
+    far = lax.ppermute(later, "space", far_pairs(lax.axis_size("space")))
     blocks, rate = row_operands(members)
     listed = jnp.stack([member[MASK_ROW, : REACH * PAIRS] for member in members]).astype(jnp.int32)
     listed = listed.reshape(N_SUB * REACH * PAIRS)
 
     tiles = []
     carried = payload
-    for at, sources in enumerate(((ahead, behind), (there, far))):
+    for at, sources in enumerate(((ahead, behind), (*there, far))):
         *tile, carried = hop_tiles(
-            WINDOWS[at], at == 0, at == len(WINDOWS) - 1, listed, blocks, rate, *sources, carried
+            WINDOWS[at], at == 0, at == len(WINDOWS) - 1, listed, blocks, rate, sources, carried
         )
         tiles.append(tile)
     degree = carried

time: 131 us -> 128 us (0.977)
  waiting for transfers between devices: 35.9 us -> 28.5 us
  starting transfers between devices: 44 us -> 49.5 us
    ppermute x1, waiting for transfers between devices: 8.04 us -> 0.72 us  [on_device(): far = lax.ppermute(later, 'space', far_pairs(lax.axis_size('space')))]
    ppermute x3 -> x5, starting transfers between devices: 8.25 us -> 12.4 us  [swapped(): lax.ppermute(value, 'space', [(at, at ^ 1) for at in range(lax.axis_size(...]
    ppermute x18, starting transfers between devices: 35.7 us -> 37.1 us  [shifted(): lax.ppermute(value, axis, [((at + steps) % count, at) for at in range(cou...]
  transfers between devices with their start and end apart: 24 -> 26, of which waited for: 17 -> 17; matrix products, arithmetic and copies ran while one was open for 0% -> 0% of each run, Pallas kernels for 3% -> 3%
where the time goes in v7:
time: 128 us; the launch traced here: 127 us
  starting transfers between devices  49.5 us (39%)
  waiting for transfers between devices  28.5 us (22%)
  blocking collectives  25.1 us (20%)
  Pallas kernels  20.1 us (16%)
  local copies, waits for them, and re-layouts  3.23 us (3%)
    ppermute x18, starting transfers between devices, shifted(): lax.ppermute(value, axis, [((at + steps) % count, at) for at in range(cou...  37.1 us
    all_to_all x2, blocking collectives, summed(): lax.all_to_all(sent, ('space', 'sub'), 0, 0, axis_index_groups=groups)  25.1 us
    ppermute x18, waiting for transfers between devices, shifted(): lax.ppermute(value, axis, [((at + steps) % count, at) for at in range(cou...  18.4 us
    ppermute x5, starting transfers between devices, swapped(): lax.ppermute(value, 'space', [(at, at ^ 1) for at in range(lax.axis_size(...  12.4 us
    pallas_call x2, Pallas kernels, hop_tiles(): pl.pallas_call(functools.partial(tile_kernel, windows, first, last), in_s...  9.87 us
    ppermute x2, waiting for transfers between devices, space_window(): lax.ppermute(value, 'space', far_pairs(lax.axis_size('space')))  7.36 us
    pallas_call x2, Pallas kernels, sweep(): pl.pallas_call(functools.partial(sweep_kernel, parts), in_specs=[smem] *...  6.08 us
    unnamed x10, local copies, waits for them, and re-layouts  2.95 us
  transfers between devices with their start and end apart: 26, of which 17 were waited for; matrix products, arithmetic and copies ran while one was open for 0% of the time, Pallas kernels for 3%

profile of v7, /device:TPU:1, one launch (start us, length us, event | category | flops | bytes accessed | tf_op | source)
XLA Modules:
  0.0 127.4 jit_solution(13239803891191255772)
XLA Ops:
  0.0 1.0 copy-done
  1.0 0.7 copy-done.1
  1.6 0.7 copy-done.2
  2.3 0.8 shard_map.48
  3.1 2.2 %collective-permute-start.2 = (bf16[320,512]{1,0:T(8,128)(2,1)S(1)}, bf16[320,512]{1,0:T(8,128)(2,1)S(1)}, u32[]{:S(2)}, u32[]{:S(2)}) collective-permute-start(bf16[320,512]{1,0:T(8,128)(2,1)S(1)} %get-tuple-element.52.refs_0_), channel_id=1, source_target_pairs={{3,0},{0,1},{1,2},{2,3},{7,4},{4,5},{5,6},{6,7},{11,8},{8,9},{9,10... | collective-permute-start | bytes 983048 | tf_op jit(solution)/shard_map/ppermute | solution.py:40
  5.4 2.6 %collective-permute-start.1 = (bf16[320,512]{1,0:T(8,128)(2,1)S(1)}, bf16[320,512]{1,0:T(8,128)(2,1)S(1)}, u32[]{:S(2)}, u32[]{:S(2)}) collective-permute-start(bf16[320,512]{1,0:T(8,128)(2,1)S(1)} %get-tuple-element.52.refs_0_), channel_id=1, source_target_pairs={{2,0},{3,1},{0,2},{1,3},{6,4},{7,5},{4,6},{5,7},{10,8},{11,9},{8,1... | collective-permute-start | bytes 983048 | tf_op jit(solution)/shard_map/ppermute | solution.py:40
  8.0 1.2 collective-permute-start.4
  9.2 6.6 %collective-permute-start.3 = (bf16[304,512]{1,0:T(8,128)(2,1)S(1)}, bf16[304,512]{1,0:T(8,128)(2,1)S(1)}, u32[]{:S(2)}, u32[]{:S(2)}) collective-permute-start(bf16[304,512]{1,0:T(8,128)(2,1)S(1)} %get-tuple-element.56.refs_2_), channel_id=1, source_target_pairs={{8,0},{12,4},{16,8},{20,12},{24,16},{28,20},{32,24},{36,28},{40,32... | collective-permute-start | bytes 933896 | tf_op jit(solution)/shard_map/ppermute | solution.py:40
  15.7 1.1 collective-permute-start
  16.8 5.4 %collective-permute-done.4.refs_1_ = bf16[304,512]{1,0:T(8,128)(2,1)S(1)} collective-permute-done((bf16[304,512]{1,0:T(8,128)(2,1)S(1)}, bf16[304,512]{1,0:T(8,128)(2,1)S(1)}, u32[]{:S(2)}, u32[]{:S(2)}) %collective-permute-start.4) | collective-permute-done | bytes 311328 | tf_op jit(solution)/shard_map/ppermute | solution.py:40
  22.2 2.5 %collective-permute-start.5 = (bf16[304,512]{1,0:T(8,128)(2,1)S(1)}, bf16[304,512]{1,0:T(8,128)(2,1)S(1)}, u32[]{:S(2)}, u32[]{:S(2)}) collective-permute-start(bf16[304,512]{1,0:T(8,128)(2,1)S(1)} %get-tuple-element.56.refs_2_), channel_id=1, source_target_pairs={{0,4},{4,0},{8,12},{12,8},{16,20},{20,16},{24,28},{28,24},{32,36},... | collective-permute-start | bytes 933896 | tf_op jit(solution)/shard_map/ppermute | solution.py:48
  24.7 0.5 collective-permute-start.7
  25.3 0.3 shard_map.49
  25.6 4.0 %shard_map.50 = (bf16[40,256,256]{2,1,0:T(8,128)(2,1)S(1)}, s32[80]{0:T(128)S(1)}, s32[80]{0:T(128)S(1)}, f32[9,8,256]{2,1,0:T(8,128)S(1)}) custom-call(s32[192]{0:T(256)S(1)} %reshape.20.mine_ref, bf16[8,320,256]{2,1,0:T(8,128)(2,1)S(1)} %get-tuple-element.53.blocks_ref, f32[8,8,256]{2,1,0:T(8,128)S(1)} %get-tuple-element.54.rate_ref, ...), custom_call_target="tpu_custom_call" | custom-call | flops 671088640 | bytes 7340032 | tf_op jit(solution)/shard_map/pallas_call | solution.py:242
  29.6 0.7 collective-permute-done.8.refs_3_
  30.3 5.9 %shard_map.51 = (bf16[64,256,256]{2,1,0:T(8,128)(2,1)S(1)}, s32[80]{0:T(128)S(1)}, s32[80]{0:T(128)S(1)}, f32[4,8,512]{2,1,0:T(8,128)S(1)}) custom-call(s32[192]{0:T(256)S(1)} %reshape.20.mine_ref, bf16[8,320,256]{2,1,0:T(8,128)(2,1)S(1)} %get-tuple-element.53.blocks_ref, f32[8,8,256]{2,1,0:T(8,128)S(1)} %get-tuple-element.54.rate_ref, ...), custom_call_target="tpu_custom_call" | custom-call | flops 1342177280 | bytes 7340032 | tf_op jit(solution)/shard_map/pallas_call | solution.py:242
  36.3 1.2 collective-permute-start.11
  37.4 3.5 %collective-permute-start.10 = (f32[1,512]{1,0:T(1,128)S(1)}, f32[1,512]{1,0:T(1,128)S(1)}, u32[]{:S(2)}, u32[]{:S(2)}) collective-permute-start(f32[1,512]{1,0:T(1,128)S(1)} %get-tuple-element.89), channel_id=1, source_target_pairs={{2,0},{3,1},{0,2},{1,3},{6,4},{7,5},{4,6},{5,7},{10,8},{11,9},{8,1... | collective-permute-start | bytes 6152 | tf_op jit(solution)/shard_map/ppermute | solution.py:40
  41.0 1.0 collective-permute-done.10
  41.9 2.7 %collective-permute-done.9 = f32[1,512]{1,0:T(1,128)S(1)} collective-permute-done((f32[1,512]{1,0:T(1,128)S(1)}, f32[1,512]{1,0:T(1,128)S(1)}, u32[]{:S(2)}, u32[]{:S(2)}) %collective-permute-start.9) | collective-permute-done | bytes 2080 | tf_op jit(solution)/shard_map/ppermute | solution.py:40
  44.6 5.6 %collective-permute-start.13 = (bf16[32,512]{1,0:T(8,128)(2,1)S(1)}, bf16[32,512]{1,0:T(8,128)(2,1)S(1)}, u32[]{:S(2)}, u32[]{:S(2)}) collective-permute-start(bf16[32,512]{1,0:T(8,128)(2,1)S(1)} %multiply_convert_fusion), channel_id=1, source_target_pairs={{8,0},{12,4},{16,8},{20,12},{24,16},{28,20},{32,24},{36,28},{40,32... | collective-permute-start | bytes 98312 | tf_op jit(solution)/shard_map/ppermute | solution.py:40
  50.2 1.0 collective-permute-done.13
  51.2 3.8 %collective-permute-done.12.refs_8_ = bf16[32,512]{1,0:T(8,128)(2,1)S(1)} collective-permute-done((bf16[32,512]{1,0:T(8,128)(2,1)S(1)}, bf16[32,512]{1,0:T(8,128)(2,1)S(1)}, u32[]{:S(2)}, u32[]{:S(2)}) %collective-permute-start.12) | collective-permute-done | bytes 32800 | tf_op jit(solution)/shard_map/ppermute | solution.py:54
  55.0 1.2 collective-permute-done.14
  56.3 4.8 %collective-permute-start.15 = (bf16[3,32,512]{2,1,0:T(8,128)(2,1)S(1)}, bf16[3,32,512]{2,1,0:T(8,128)(2,1)S(1)}, u32[]{:S(2)}, u32[]{:S(2)}) collective-permute-start(bf16[3,32,512]{2,1,0:T(8,128)(2,1)S(1)} %pad_maximum_fusion.1.refs_6_), channel_id=1, source_target_pairs={{0,4},{4,0},{8,12},{12,8},{16,20},{20,16},{24,28},{28,24},{32,36},... | collective-permute-start | bytes 294920 | tf_op jit(solution)/shard_map/ppermute | solution.py:48
  61.1 0.9 collective-permute-done.15.refs_7_
  62.0 3.0 %shard_map.52 = (f32[32,512]{1,0:T(8,128)S(1)}, f32[32,512]{1,0:T(8,128)S(1)}, f32[32,512]{1,0:T(8,128)S(1)}, f32[32,512]{1,0:T(8,128)S(1)}) custom-call(s32[80]{0:T(128)S(1)} %get-tuple-element.61.refs_0_, s32[80]{0:T(128)S(1)} %get-tuple-element.62.refs_1_, s32[80]{0:T(128)S(1)} %get-tuple-element.63.refs_2_, s32[80]{0:T(128)S(1)} %get-tuple-element.64.refs_3_, ...), custom_call_target="tpu_custom_call" | custom-call | flops 838860800 | bytes 7340032 | tf_op jit(solution)/shard_map/pallas_call | solution.py:339
  65.1 1.9 %collective-permute-start.17 = (f32[32,512]{1,0:T(8,128)S(1)}, f32[32,512]{1,0:T(8,128)S(1)}, u32[]{:S(2)}, u32[]{:S(2)}) collective-permute-start(f32[32,512]{1,0:T(8,128)S(1)} %get-tuple-element.72), channel_id=1, source_target_pairs={{2,0},{3,1},{0,2},{1,3},{6,4},{7,5},{4,6},{5,7},{10,8},{11,9},{8,1... | collective-permute-start | bytes 196616 | tf_op jit(solution)/shard_map/ppermute | solution.py:40
  67.0 1.9 %collective-permute-start.18 = (f32[32,512]{1,0:T(8,128)S(1)}, f32[32,512]{1,0:T(8,128)S(1)}, u32[]{:S(2)}, u32[]{:S(2)}) collective-permute-start(f32[32,512]{1,0:T(8,128)S(1)} %get-tuple-element.73), channel_id=1, source_target_pairs={{1,0},{2,1},{3,2},{0,3},{5,4},{6,5},{7,6},{4,7},{9,8},{10,9},{11,1... | collective-permute-start | bytes 196616 | tf_op jit(solution)/shard_map/ppermute | solution.py:40
  68.9 0.9 collective-permute-done.16.refs_1_
  69.8 0.7 collective-permute-done.17.refs_2_
  70.4 0.5 collective-permute-done.18.refs_3_
  71.0 0.2 shard_map.53
  71.3 4.8 %collective-permute-start.20 = (f32[32,512]{1,0:T(8,128)S(1)}, f32[32,512]{1,0:T(8,128)S(1)}, u32[]{:S(2)}, u32[]{:S(2)}) collective-permute-start(f32[32,512]{1,0:T(8,128)S(1)} %get-tuple-element.75), channel_id=1, source_target_pairs={{8,0},{12,4},{16,8},{20,12},{24,16},{28,20},{32,24},{36,28},{40,32... | collective-permute-start | bytes 196616 | tf_op jit(solution)/shard_map/ppermute | solution.py:40
  76.0 1.6 %collective-permute-done.21 = f32[32,512]{1,0:T(8,128)S(1)} collective-permute-done((f32[32,512]{1,0:T(8,128)S(1)}, f32[32,512]{1,0:T(8,128)S(1)}, u32[]{:S(2)}, u32[]{:S(2)}) %collective-permute-start.21) | collective-permute-done | bytes 65568 | tf_op jit(solution)/shard_map/ppermute | solution.py:40
  77.7 3.5 %collective-permute-done.19.refs_8_ = f32[32,512]{1,0:T(8,128)S(1)} collective-permute-done((f32[32,512]{1,0:T(8,128)S(1)}, f32[32,512]{1,0:T(8,128)S(1)}, u32[]{:S(2)}, u32[]{:S(2)}) %collective-permute-start.19) | collective-permute-done | bytes 65568 | tf_op jit(solution)/shard_map/ppermute | solution.py:54
  81.2 4.6 %collective-permute-start.22 = (f32[3,32,512]{2,1,0:T(8,128)S(1)}, f32[3,32,512]{2,1,0:T(8,128)S(1)}, u32[]{:S(2)}, u32[]{:S(2)}) collective-permute-start(f32[3,32,512]{2,1,0:T(8,128)S(1)} %pad_maximum_fusion.refs_6_), channel_id=1, source_target_pairs={{0,4},{4,0},{8,12},{12,8},{16,20},{20,16},{24,28},{28,24},{32,36},... | collective-permute-start | bytes 589832 | tf_op jit(solution)/shard_map/ppermute | solution.py:48
  85.9 1.1 collective-permute-done.22.refs_7_
  86.9 3.1 %shard_map.54 = (f32[32,512]{1,0:T(8,128)S(1)}, f32[32,512]{1,0:T(8,128)S(1)}, f32[32,512]{1,0:T(8,128)S(1)}, f32[32,512]{1,0:T(8,128)S(1)}) custom-call(s32[80]{0:T(128)S(1)} %get-tuple-element.61.refs_0_, s32[80]{0:T(128)S(1)} %get-tuple-element.62.refs_1_, s32[80]{0:T(128)S(1)} %get-tuple-element.63.refs_2_, s32[80]{0:T(128)S(1)} %get-tuple-element.64.refs_3_, ...), custom_call_target="tpu_custom_call" | custom-call | flops 838860800 | bytes 7340032 | tf_op jit(solution)/shard_map/pallas_call | solution.py:339
  90.0 2.0 %collective-permute-start.23 = (f32[32,512]{1,0:T(8,128)S(1)}, f32[32,512]{1,0:T(8,128)S(1)}, u32[]{:S(2)}, u32[]{:S(2)}) collective-permute-start(f32[32,512]{1,0:T(8,128)S(1)} %get-tuple-element.80), channel_id=1, source_target_pairs={{3,0},{0,1},{1,2},{2,3},{7,4},{4,5},{5,6},{6,7},{11,8},{8,9},{9,10... | collective-permute-start | bytes 196616 | tf_op jit(solution)/shard_map/ppermute | solution.py:40
  92.0 2.5 %collective-permute-start.24 = (f32[32,512]{1,0:T(8,128)S(1)}, f32[32,512]{1,0:T(8,128)S(1)}, u32[]{:S(2)}, u32[]{:S(2)}) collective-permute-start(f32[32,512]{1,0:T(8,128)S(1)} %get-tuple-element.81), channel_id=1, source_target_pairs={{2,0},{3,1},{0,2},{1,3},{6,4},{7,5},{4,6},{5,7},{10,8},{11,9},{8,1... | collective-permute-start | bytes 196616 | tf_op jit(solution)/shard_map/ppermute | solution.py:40
  94.5 0.5 collective-permute-done.23.refs_1_
  95.0 2.0 %collective-permute-done.24.refs_2_ = f32[32,512]{1,0:T(8,128)S(1)} collective-permute-done((f32[32,512]{1,0:T(8,128)S(1)}, f32[32,512]{1,0:T(8,128)S(1)}, u32[]{:S(2)}, u32[]{:S(2)}) %collective-permute-start.24) | collective-permute-done | bytes 65568 | tf_op jit(solution)/shard_map/ppermute | solution.py:40
  97.0 0.9 collective-permute-done.25.refs_3_
  98.2 13.9 %all_to_all.20 = f32[32,16,128]{2,1,0:T(8,128)S(1)} all-to-all(f32[32,16,128]{2,1,0:T(8,128)S(1)} %broadcast_in_dim.13), channel_id=1, replica_groups={{0,1,2,3,4,5,6,7,8,9,10,11,12,13,14,15,16,17,18,19,20,21,22,23,24,25,26..., dimensions={0} | all-to-all | bytes 524288 | tf_op jit(solution)/shard_map/all_to_all | solution.py:78
  112.2 11.2 %all_to_all.21 = f32[8,16,128]{2,1,0:T(8,128)S(1)} all-to-all(f32[8,16,128]{2,1,0:T(8,128)S(1)} %broadcast_in_dim.28), channel_id=1, replica_groups={{0,32,64,96,128,160,192,224},{1,33,65,97,129,161,193,225},{2,34,66,98,1..., dimensions={0} | all-to-all | bytes 131072 | tf_op jit(solution)/shard_map/all_to_all | solution.py:78
  123.5 2.6 %shard_map.56 = (f32[32,512]{1,0:T(8,128)S(1)}, s32[1]{0:T(128)}) custom-call(f32[64,32]{1,0:T(8,128)S(1)} %reshape.19.grams_ref, f32[32,512]{1,0:T(8,128)S(1)} %get-tuple-element.84.image_ref), custom_call_target="tpu_custom_call" | custom-call | flops 1048576 | bytes 131072 | tf_op jit(solution)/shard_map/pallas_call | solution.py:501
  126.8 0.6 copy-done.4
  (45 shorter events, 0.8 us)
Async XLA Ops:
  0.0 1.0 copy-start
  1.0 0.7 copy-start.1
  1.6 0.7 copy-start.2
  3.1 21.5 %collective-permute-start.2 = (bf16[320,512]{1,0:T(8,128)(2,1)S(1)}, bf16[320,512]{1,0:T(8,128)(2,1)S(1)}, u32[]{:S(2)}, u32[]{:S(2)}) collective-permute-start(bf16[320,512]{1,0:T(8,128)(2,1)S(1)} %get-tuple-element.52.refs_0_), channel_id=1, source_target_pairs={{3,0},{0,1},{1,2},{2,3},{7,4},{4,5},{5,6},{6,7},{11,8},{8,9},{9,10... | collective-permute-start | bytes 983048 | tf_op jit(solution)/shard_map/ppermute | solution.py:40
  5.4 19.3 %collective-permute-start.1 = (bf16[320,512]{1,0:T(8,128)(2,1)S(1)}, bf16[320,512]{1,0:T(8,128)(2,1)S(1)}, u32[]{:S(2)}, u32[]{:S(2)}) collective-permute-start(bf16[320,512]{1,0:T(8,128)(2,1)S(1)} %get-tuple-element.52.refs_0_), channel_id=1, source_target_pairs={{2,0},{3,1},{0,2},{1,3},{6,4},{7,5},{4,6},{5,7},{10,8},{11,9},{8,1... | collective-permute-start | bytes 983048 | tf_op jit(solution)/shard_map/ppermute | solution.py:40
  8.0 14.2 %collective-permute-start.4 = (bf16[304,512]{1,0:T(8,128)(2,1)S(1)}, bf16[304,512]{1,0:T(8,128)(2,1)S(1)}, u32[]{:S(2)}, u32[]{:S(2)}) collective-permute-start(bf16[304,512]{1,0:T(8,128)(2,1)S(1)} %get-tuple-element.56.refs_2_), channel_id=1, source_target_pairs={{248,0},{252,4},{0,8},{4,12},{8,16},{12,20},{16,24},{20,28},{24,32... | collective-permute-start | bytes 933896 | tf_op jit(solution)/shard_map/ppermute | solution.py:40
  9.2 13.0 %collective-permute-start.3 = (bf16[304,512]{1,0:T(8,128)(2,1)S(1)}, bf16[304,512]{1,0:T(8,128)(2,1)S(1)}, u32[]{:S(2)}, u32[]{:S(2)}) collective-permute-start(bf16[304,512]{1,0:T(8,128)(2,1)S(1)} %get-tuple-element.56.refs_2_), channel_id=1, source_target_pairs={{8,0},{12,4},{16,8},{20,12},{24,16},{28,20},{32,24},{36,28},{40,32... | collective-permute-start | bytes 933896 | tf_op jit(solution)/shard_map/ppermute | solution.py:40
  15.7 9.5 %collective-permute-start = (bf16[320,512]{1,0:T(8,128)(2,1)S(1)}, bf16[320,512]{1,0:T(8,128)(2,1)S(1)}, u32[]{:S(2)}, u32[]{:S(2)}) collective-permute-start(bf16[320,512]{1,0:T(8,128)(2,1)S(1)} %get-tuple-element.52.refs_0_), channel_id=1, source_target_pairs={{1,0},{2,1},{3,2},{0,3},{5,4},{6,5},{7,6},{4,7},{9,8},{10,9},{11,1... | collective-permute-start | bytes 983048 | tf_op jit(solution)/shard_map/ppermute | solution.py:40
  22.2 8.1 %collective-permute-start.8 = (bf16[304,512]{1,0:T(8,128)(2,1)S(1)}, bf16[304,512]{1,0:T(8,128)(2,1)S(1)}, u32[]{:S(2)}, u32[]{:S(2)}) collective-permute-start(bf16[304,512]{1,0:T(8,128)(2,1)S(1)} %get-tuple-element.56.refs_2_), channel_id=1, source_target_pairs={{0,244},{4,16},{8,252},{12,24},{16,4},{20,32},{24,12},{28,40},{32,... | collective-permute-start | bytes 933896 | tf_op jit(solution)/shard_map/ppermute | solution.py:473
  22.2 8.1 %collective-permute-start.5 = (bf16[304,512]{1,0:T(8,128)(2,1)S(1)}, bf16[304,512]{1,0:T(8,128)(2,1)S(1)}, u32[]{:S(2)}, u32[]{:S(2)}) collective-permute-start(bf16[304,512]{1,0:T(8,128)(2,1)S(1)} %get-tuple-element.56.refs_2_), channel_id=1, source_target_pairs={{0,4},{4,0},{8,12},{12,8},{16,20},{20,16},{24,28},{28,24},{32,36},... | collective-permute-start | bytes 933896 | tf_op jit(solution)/shard_map/ppermute | solution.py:48
  24.7 5.7 %collective-permute-start.6 = (bf16[304,512]{1,0:T(8,128)(2,1)S(1)}, bf16[304,512]{1,0:T(8,128)(2,1)S(1)}, u32[]{:S(2)}, u32[]{:S(2)}) collective-permute-start(bf16[304,512]{1,0:T(8,128)(2,1)S(1)} %collective-permute-done.3.refs_0_), channel_id=1, source_target_pairs={{0,4},{4,0},{8,12},{12,8},{16,20},{20,16},{24,28},{28,24},{32,36},... | collective-permute-start | bytes 933896 | tf_op jit(solution)/shard_map/ppermute | solution.py:48
  24.7 5.7 %collective-permute-start.7 = (bf16[304,512]{1,0:T(8,128)(2,1)S(1)}, bf16[304,512]{1,0:T(8,128)(2,1)S(1)}, u32[]{:S(2)}, u32[]{:S(2)}) collective-permute-start(bf16[304,512]{1,0:T(8,128)(2,1)S(1)} %collective-permute-done.4.refs_1_), channel_id=1, source_target_pairs={{0,4},{4,0},{8,12},{12,8},{16,20},{20,16},{24,28},{28,24},{32,36},... | collective-permute-start | bytes 933896 | tf_op jit(solution)/shard_map/ppermute | solution.py:48
  25.3 19.3 %copy-start.3 = (f32[32,512]{1,0:T(8,128)S(1)}, f32[32,512]{1,0:T(8,128)}, u32[]{:S(2)}) copy-start(f32[32,512]{1,0:T(8,128)} %param.8) | copy-start | bytes 196612
  36.3 4.7 %collective-permute-start.11 = (f32[1,512]{1,0:T(1,128)S(1)}, f32[1,512]{1,0:T(1,128)S(1)}, u32[]{:S(2)}, u32[]{:S(2)}) collective-permute-start(f32[1,512]{1,0:T(1,128)S(1)} %get-tuple-element.88), channel_id=1, source_target_pairs={{1,0},{2,1},{3,2},{0,3},{5,4},{6,5},{7,6},{4,7},{9,8},{10,9},{11,1... | collective-permute-start | bytes 6152 | tf_op jit(solution)/shard_map/ppermute | solution.py:40
  37.4 4.5 %collective-permute-start.10 = (f32[1,512]{1,0:T(1,128)S(1)}, f32[1,512]{1,0:T(1,128)S(1)}, u32[]{:S(2)}, u32[]{:S(2)}) collective-permute-start(f32[1,512]{1,0:T(1,128)S(1)} %get-tuple-element.89), channel_id=1, source_target_pairs={{2,0},{3,1},{0,2},{1,3},{6,4},{7,5},{4,6},{5,7},{10,8},{11,9},{8,1... | collective-permute-start | bytes 6152 | tf_op jit(solution)/shard_map/ppermute | solution.py:40
  41.0 3.6 %collective-permute-start.9 = (f32[1,512]{1,0:T(1,128)S(1)}, f32[1,512]{1,0:T(1,128)S(1)}, u32[]{:S(2)}, u32[]{:S(2)}) collective-permute-start(f32[1,512]{1,0:T(1,128)S(1)} %get-tuple-element.90), channel_id=1, source_target_pairs={{3,0},{0,1},{1,2},{2,3},{7,4},{4,5},{5,6},{6,7},{11,8},{8,9},{9,10... | collective-permute-start | bytes 6152 | tf_op jit(solution)/shard_map/ppermute | solution.py:40
  44.6 6.6 %collective-permute-start.13 = (bf16[32,512]{1,0:T(8,128)(2,1)S(1)}, bf16[32,512]{1,0:T(8,128)(2,1)S(1)}, u32[]{:S(2)}, u32[]{:S(2)}) collective-permute-start(bf16[32,512]{1,0:T(8,128)(2,1)S(1)} %multiply_convert_fusion), channel_id=1, source_target_pairs={{8,0},{12,4},{16,8},{20,12},{24,16},{28,20},{32,24},{36,28},{40,32... | collective-permute-start | bytes 98312 | tf_op jit(solution)/shard_map/ppermute | solution.py:40
  50.2 4.8 %collective-permute-start.12 = (bf16[32,512]{1,0:T(8,128)(2,1)S(1)}, bf16[32,512]{1,0:T(8,128)(2,1)S(1)}, u32[]{:S(2)}, u32[]{:S(2)}) collective-permute-start(bf16[32,512]{1,0:T(8,128)(2,1)S(1)} %multiply_convert_fusion), channel_id=1, source_target_pairs={{0,244},{4,16},{8,252},{12,24},{16,4},{20,32},{24,12},{28,40},{32,... | collective-permute-start | bytes 98312 | tf_op jit(solution)/shard_map/ppermute | solution.py:54
  50.2 6.1 %collective-permute-start.14 = (bf16[32,512]{1,0:T(8,128)(2,1)S(1)}, bf16[32,512]{1,0:T(8,128)(2,1)S(1)}, u32[]{:S(2)}, u32[]{:S(2)}) collective-permute-start(bf16[32,512]{1,0:T(8,128)(2,1)S(1)} %multiply_convert_fusion), channel_id=1, source_target_pairs={{248,0},{252,4},{0,8},{4,12},{8,16},{12,20},{16,24},{20,28},{24,32... | collective-permute-start | bytes 98312 | tf_op jit(solution)/shard_map/ppermute | solution.py:40
  56.3 5.7 %collective-permute-start.15 = (bf16[3,32,512]{2,1,0:T(8,128)(2,1)S(1)}, bf16[3,32,512]{2,1,0:T(8,128)(2,1)S(1)}, u32[]{:S(2)}, u32[]{:S(2)}) collective-permute-start(bf16[3,32,512]{2,1,0:T(8,128)(2,1)S(1)} %pad_maximum_fusion.1.refs_6_), channel_id=1, source_target_pairs={{0,4},{4,0},{8,12},{12,8},{16,20},{20,16},{24,28},{28,24},{32,36},... | collective-permute-start | bytes 294920 | tf_op jit(solution)/shard_map/ppermute | solution.py:48
  65.0 4.8 %collective-permute-start.16 = (f32[32,512]{1,0:T(8,128)S(1)}, f32[32,512]{1,0:T(8,128)S(1)}, u32[]{:S(2)}, u32[]{:S(2)}) collective-permute-start(f32[32,512]{1,0:T(8,128)S(1)} %get-tuple-element.71), channel_id=1, source_target_pairs={{3,0},{0,1},{1,2},{2,3},{7,4},{4,5},{5,6},{6,7},{11,8},{8,9},{9,10... | collective-permute-start | bytes 196616 | tf_op jit(solution)/shard_map/ppermute | solution.py:40
  65.1 5.4 %collective-permute-start.17 = (f32[32,512]{1,0:T(8,128)S(1)}, f32[32,512]{1,0:T(8,128)S(1)}, u32[]{:S(2)}, u32[]{:S(2)}) collective-permute-start(f32[32,512]{1,0:T(8,128)S(1)} %get-tuple-element.72), channel_id=1, source_target_pairs={{2,0},{3,1},{0,2},{1,3},{6,4},{7,5},{4,6},{5,7},{10,8},{11,9},{8,1... | collective-permute-start | bytes 196616 | tf_op jit(solution)/shard_map/ppermute | solution.py:40
  67.0 4.0 %collective-permute-start.18 = (f32[32,512]{1,0:T(8,128)S(1)}, f32[32,512]{1,0:T(8,128)S(1)}, u32[]{:S(2)}, u32[]{:S(2)}) collective-permute-start(f32[32,512]{1,0:T(8,128)S(1)} %get-tuple-element.73), channel_id=1, source_target_pairs={{1,0},{2,1},{3,2},{0,3},{5,4},{6,5},{7,6},{4,7},{9,8},{10,9},{11,1... | collective-permute-start | bytes 196616 | tf_op jit(solution)/shard_map/ppermute | solution.py:40
  71.2 6.5 %collective-permute-start.21 = (f32[32,512]{1,0:T(8,128)S(1)}, f32[32,512]{1,0:T(8,128)S(1)}, u32[]{:S(2)}, u32[]{:S(2)}) collective-permute-start(f32[32,512]{1,0:T(8,128)S(1)} %get-tuple-element.75), channel_id=1, source_target_pairs={{248,0},{252,4},{0,8},{4,12},{8,16},{12,20},{16,24},{20,28},{24,32... | collective-permute-start | bytes 196616 | tf_op jit(solution)/shard_map/ppermute | solution.py:40
  71.3 6.4 %collective-permute-start.20 = (f32[32,512]{1,0:T(8,128)S(1)}, f32[32,512]{1,0:T(8,128)S(1)}, u32[]{:S(2)}, u32[]{:S(2)}) collective-permute-start(f32[32,512]{1,0:T(8,128)S(1)} %get-tuple-element.75), channel_id=1, source_target_pairs={{8,0},{12,4},{16,8},{20,12},{24,16},{28,20},{32,24},{36,28},{40,32... | collective-permute-start | bytes 196616 | tf_op jit(solution)/shard_map/ppermute | solution.py:40
  76.0 5.2 %collective-permute-start.19 = (f32[32,512]{1,0:T(8,128)S(1)}, f32[32,512]{1,0:T(8,128)S(1)}, u32[]{:S(2)}, u32[]{:S(2)}) collective-permute-start(f32[32,512]{1,0:T(8,128)S(1)} %get-tuple-element.75), channel_id=1, source_target_pairs={{0,244},{4,16},{8,252},{12,24},{16,4},{20,32},{24,12},{28,40},{32,... | collective-permute-start | bytes 196616 | tf_op jit(solution)/shard_map/ppermute | solution.py:54
  81.2 5.7 %collective-permute-start.22 = (f32[3,32,512]{2,1,0:T(8,128)S(1)}, f32[3,32,512]{2,1,0:T(8,128)S(1)}, u32[]{:S(2)}, u32[]{:S(2)}) collective-permute-start(f32[3,32,512]{2,1,0:T(8,128)S(1)} %pad_maximum_fusion.refs_6_), channel_id=1, source_target_pairs={{0,4},{4,0},{8,12},{12,8},{16,20},{20,16},{24,28},{28,24},{32,36},... | collective-permute-start | bytes 589832 | tf_op jit(solution)/shard_map/ppermute | solution.py:48
  90.0 4.9 %collective-permute-start.23 = (f32[32,512]{1,0:T(8,128)S(1)}, f32[32,512]{1,0:T(8,128)S(1)}, u32[]{:S(2)}, u32[]{:S(2)}) collective-permute-start(f32[32,512]{1,0:T(8,128)S(1)} %get-tuple-element.80), channel_id=1, source_target_pairs={{3,0},{0,1},{1,2},{2,3},{7,4},{4,5},{5,6},{6,7},{11,8},{8,9},{9,10... | collective-permute-start | bytes 196616 | tf_op jit(solution)/shard_map/ppermute | solution.py:40
  92.0 5.0 %collective-permute-start.24 = (f32[32,512]{1,0:T(8,128)S(1)}, f32[32,512]{1,0:T(8,128)S(1)}, u32[]{:S(2)}, u32[]{:S(2)}) collective-permute-start(f32[32,512]{1,0:T(8,128)S(1)} %get-tuple-element.81), channel_id=1, source_target_pairs={{2,0},{3,1},{0,2},{1,3},{6,4},{7,5},{4,6},{5,7},{10,8},{11,9},{8,1... | collective-permute-start | bytes 196616 | tf_op jit(solution)/shard_map/ppermute | solution.py:40
  94.5 3.4 %collective-permute-start.25 = (f32[32,512]{1,0:T(8,128)S(1)}, f32[32,512]{1,0:T(8,128)S(1)}, u32[]{:S(2)}, u32[]{:S(2)}) collective-permute-start(f32[32,512]{1,0:T(8,128)S(1)} %get-tuple-element.82), channel_id=1, source_target_pairs={{1,0},{2,1},{3,2},{0,3},{5,4},{6,5},{7,6},{4,7},{9,8},{10,9},{11,1... | collective-permute-start | bytes 196616 | tf_op jit(solution)/shard_map/ppermute | solution.py:40
  126.8 0.6 copy-start.4

commit v8 on v7

--- a/solution.py
+++ b/solution.py
@@ -32,6 +32,7 @@
 VMEM_LIMIT = 24 * 1024 * 1024
 SWEEP_LIMIT = 24 * 1024 * 1024
 SMALL_LIMIT = 4 * 1024 * 1024
+PAYLOAD_LIMIT = 60 * 1024 * 1024
 TRANS_B = (((1,), (1,)), ((), ()))
 
 
@@ -463,7 +464,8 @@
         payload_kernel,
         in_specs=[pl.BlockSpec(memory_space=pltpu.SMEM)] + [pl.BlockSpec(memory_space=pltpu.VMEM)] * 2,
         out_shape=[jax.ShapeDtypeStruct((rows, length), jnp.bfloat16) for rows in (ROWS, WIDE)],
-        **light,
+        cost_estimate=light["cost_estimate"],
+        compiler_params=pltpu.CompilerParams(vmem_limit_bytes=PAYLOAD_LIMIT),
     )(pair_list.T, trajectories, kernel_scale)
 
     members = [wide] + [shifted(wide, "sub", e) for e in range(1, N_SUB)]

time: 128 us -> 127 us (level)
  starting transfers between devices: 49.5 us -> 45.7 us
  waiting for transfers between devices: 28.5 us -> 29.9 us
  Pallas kernels: 20.1 us -> 21.4 us
    ppermute x18, starting transfers between devices: 37.1 us -> 34 us  [shifted(): lax.ppermute(value, axis, [((at + steps) % count, at) for at in range(cou...]
    ppermute x18, waiting for transfers between devices: 18.4 us -> 20.5 us  [shifted(): lax.ppermute(value, axis, [((at + steps) % count, at) for at in range(cou...]
    pallas_call x1, Pallas kernels: 0.81 us -> 2.1 us  [on_device(): pl.pallas_call(payload_kernel, in_specs=[pl.BlockSpec(memory_space=pltpu....]
    unnamed x10 -> x8, local copies, waits for them, and re-layouts: 2.95 us -> 2.56 us
  transfers between devices with their start and end apart: 26 -> 26, of which waited for: 17 -> 16; matrix products, arithmetic and copies ran while one was open for 0% -> 1% of each run, Pallas kernels for 3% -> 3%
where the time goes in v8:
time: 127 us
  starting transfers between devices  45.7 us (36%)
  waiting for transfers between devices  29.9 us (24%)
  blocking collectives  25.4 us (20%)
  Pallas kernels  21.4 us (17%)
  local copies, waits for them, and re-layouts  3.52 us (3%)
    ppermute x18, starting transfers between devices, shifted(): lax.ppermute(value, axis, [((at + steps) % count, at) for at in range(cou...  34 us
    all_to_all x2, blocking collectives, summed(): lax.all_to_all(sent, ('space', 'sub'), 0, 0, axis_index_groups=groups)  25.4 us
    ppermute x18, waiting for transfers between devices, shifted(): lax.ppermute(value, axis, [((at + steps) % count, at) for at in range(cou...  20.5 us
    ppermute x5, starting transfers between devices, swapped(): lax.ppermute(value, 'space', [(at, at ^ 1) for at in range(lax.axis_size(...  11.5 us
    pallas_call x2, Pallas kernels, hop_tiles(): pl.pallas_call(functools.partial(tile_kernel, windows, first, last), in_s...  9.86 us
    ppermute x2, waiting for transfers between devices, space_window(): lax.ppermute(value, 'space', far_pairs(lax.axis_size('space')))  7.36 us
    pallas_call x2, Pallas kernels, sweep(): pl.pallas_call(functools.partial(sweep_kernel, parts), in_specs=[smem] *...  6.08 us
    pallas_call x1, Pallas kernels, on_device(): pl.pallas_call(solve_both_kernel, in_specs=[pl.BlockSpec(memory_space=plt...  2.6 us
  transfers between devices with their start and end apart: 26, of which 16 were waited for; matrix products, arithmetic and copies ran while one was open for 1% of the time, Pallas kernels for 3%

profile of v8, /device:TPU:1, one launch (start us, length us, event | category | flops | bytes accessed | tf_op | source)
XLA Modules:
  0.0 126.9 jit_solution(1806125946065431403)
XLA Ops:
  0.0 2.1 %shard_map.48 = (bf16[304,512]{1,0:T(8,128)(2,1)}, bf16[320,512]{1,0:T(8,128)(2,1)}) custom-call(s32[2,24]{1,0:T(2,128)} %bitcast.29, bf16[300,512]{1,0:T(8,128)(2,1)} %data_ref.1, bf16[512]{0:T(512)(128)(2,1)} %scale_ref.1), custom_call_target="tpu_custom_call" | custom-call | flops 1048576 | bytes 131072 | tf_op jit(solution)/shard_map/pallas_call | solution.py:463
  2.1 2.1 %collective-permute-start.2 = (bf16[320,512]{1,0:T(8,128)(2,1)}, bf16[320,512]{1,0:T(8,128)(2,1)S(1)}, u32[]{:S(2)}, u32[]{:S(2)}) collective-permute-start(bf16[320,512]{1,0:T(8,128)(2,1)} %get-tuple-element.52.refs_0_), channel_id=1, source_target_pairs={{3,0},{0,1},{1,2},{2,3},{7,4},{4,5},{5,6},{6,7},{11,8},{8,9},{9,10... | collective-permute-start | bytes 983048 | tf_op jit(solution)/shard_map/ppermute | solution.py:41
  4.2 2.6 %collective-permute-start.1 = (bf16[320,512]{1,0:T(8,128)(2,1)}, bf16[320,512]{1,0:T(8,128)(2,1)S(1)}, u32[]{:S(2)}, u32[]{:S(2)}) collective-permute-start(bf16[320,512]{1,0:T(8,128)(2,1)} %get-tuple-element.52.refs_0_), channel_id=1, source_target_pairs={{2,0},{3,1},{0,2},{1,3},{6,4},{7,5},{4,6},{5,7},{10,8},{11,9},{8,1... | collective-permute-start | bytes 983048 | tf_op jit(solution)/shard_map/ppermute | solution.py:41
  6.8 1.2 collective-permute-start.4
  8.1 6.6 %collective-permute-start.3 = (bf16[304,512]{1,0:T(8,128)(2,1)}, bf16[304,512]{1,0:T(8,128)(2,1)S(1)}, u32[]{:S(2)}, u32[]{:S(2)}) collective-permute-start(bf16[304,512]{1,0:T(8,128)(2,1)} %get-tuple-element.56.refs_2_), channel_id=1, source_target_pairs={{8,0},{12,4},{16,8},{20,12},{24,16},{28,20},{32,24},{36,28},{40,32... | collective-permute-start | bytes 933896 | tf_op jit(solution)/shard_map/ppermute | solution.py:41
  14.6 1.1 collective-permute-start
  15.7 5.6 %collective-permute-done.4.refs_1_ = bf16[304,512]{1,0:T(8,128)(2,1)S(1)} collective-permute-done((bf16[304,512]{1,0:T(8,128)(2,1)}, bf16[304,512]{1,0:T(8,128)(2,1)S(1)}, u32[]{:S(2)}, u32[]{:S(2)}) %collective-permute-start.4) | collective-permute-done | bytes 311328 | tf_op jit(solution)/shard_map/ppermute | solution.py:41
  21.3 2.5 %collective-permute-start.5 = (bf16[304,512]{1,0:T(8,128)(2,1)}, bf16[304,512]{1,0:T(8,128)(2,1)S(1)}, u32[]{:S(2)}, u32[]{:S(2)}) collective-permute-start(bf16[304,512]{1,0:T(8,128)(2,1)} %get-tuple-element.56.refs_2_), channel_id=1, source_target_pairs={{0,4},{4,0},{8,12},{12,8},{16,20},{20,16},{24,28},{28,24},{32,36},... | collective-permute-start | bytes 933896 | tf_op jit(solution)/shard_map/ppermute | solution.py:49
  23.8 0.5 collective-permute-start.7
  24.3 0.7 slice.27
  25.1 1.0 copy-done
  26.1 0.3 shard_map.49
  26.4 1.0 copy-done.1
  27.3 3.9 %shard_map.50 = (bf16[40,256,256]{2,1,0:T(8,128)(2,1)S(1)}, s32[80]{0:T(128)S(1)}, s32[80]{0:T(128)S(1)}, f32[9,8,256]{2,1,0:T(8,128)S(1)}) custom-call(s32[192]{0:T(256)S(1)} %reshape.20.mine_ref, bf16[8,320,256]{2,1,0:T(8,128)(2,1)S(1)} %get-tuple-element.53.blocks_ref, f32[8,8,256]{2,1,0:T(8,128)S(1)} %get-tuple-element.54.rate_ref, ...), custom_call_target="tpu_custom_call" | custom-call | flops 671088640 | bytes 7340032 | tf_op jit(solution)/shard_map/pallas_call | solution.py:243
  31.3 5.9 %shard_map.51 = (bf16[64,256,256]{2,1,0:T(8,128)(2,1)S(1)}, s32[80]{0:T(128)S(1)}, s32[80]{0:T(128)S(1)}, f32[4,8,512]{2,1,0:T(8,128)S(1)}) custom-call(s32[192]{0:T(256)S(1)} %reshape.20.mine_ref, bf16[8,320,256]{2,1,0:T(8,128)(2,1)S(1)} %get-tuple-element.53.blocks_ref, f32[8,8,256]{2,1,0:T(8,128)S(1)} %get-tuple-element.54.rate_ref, ...), custom_call_target="tpu_custom_call" | custom-call | flops 1342177280 | bytes 7340032 | tf_op jit(solution)/shard_map/pallas_call | solution.py:243
  37.3 2.0 %collective-permute-start.11 = (f32[1,512]{1,0:T(1,128)S(1)}, f32[1,512]{1,0:T(1,128)S(1)}, u32[]{:S(2)}, u32[]{:S(2)}) collective-permute-start(f32[1,512]{1,0:T(1,128)S(1)} %get-tuple-element.88), channel_id=1, source_target_pairs={{1,0},{2,1},{3,2},{0,3},{5,4},{6,5},{7,6},{4,7},{9,8},{10,9},{11,1... | collective-permute-start | bytes 6152 | tf_op jit(solution)/shard_map/ppermute | solution.py:41
  39.2 1.7 %collective-permute-start.10 = (f32[1,512]{1,0:T(1,128)S(1)}, f32[1,512]{1,0:T(1,128)S(1)}, u32[]{:S(2)}, u32[]{:S(2)}) collective-permute-start(f32[1,512]{1,0:T(1,128)S(1)} %get-tuple-element.89), channel_id=1, source_target_pairs={{2,0},{3,1},{0,2},{1,3},{6,4},{7,5},{4,6},{5,7},{10,8},{11,9},{8,1... | collective-permute-start | bytes 6152 | tf_op jit(solution)/shard_map/ppermute | solution.py:41
  41.0 2.2 %collective-permute-done.10 = f32[1,512]{1,0:T(1,128)S(1)} collective-permute-done((f32[1,512]{1,0:T(1,128)S(1)}, f32[1,512]{1,0:T(1,128)S(1)}, u32[]{:S(2)}, u32[]{:S(2)}) %collective-permute-start.10) | collective-permute-done | bytes 2080 | tf_op jit(solution)/shard_map/ppermute | solution.py:41
  43.2 1.4 %collective-permute-done.9 = f32[1,512]{1,0:T(1,128)S(1)} collective-permute-done((f32[1,512]{1,0:T(1,128)S(1)}, f32[1,512]{1,0:T(1,128)S(1)}, u32[]{:S(2)}, u32[]{:S(2)}) %collective-permute-start.9) | collective-permute-done | bytes 2080 | tf_op jit(solution)/shard_map/ppermute | solution.py:41
  44.6 5.1 %collective-permute-start.13 = (bf16[32,512]{1,0:T(8,128)(2,1)S(1)}, bf16[32,512]{1,0:T(8,128)(2,1)S(1)}, u32[]{:S(2)}, u32[]{:S(2)}) collective-permute-start(bf16[32,512]{1,0:T(8,128)(2,1)S(1)} %multiply_convert_fusion), channel_id=1, source_target_pairs={{8,0},{12,4},{16,8},{20,12},{24,16},{28,20},{32,24},{36,28},{40,32... | collective-permute-start | bytes 98312 | tf_op jit(solution)/shard_map/ppermute | solution.py:41
  50.0 0.9 collective-permute-done.13
  50.8 3.8 %collective-permute-done.12.refs_8_ = bf16[32,512]{1,0:T(8,128)(2,1)S(1)} collective-permute-done((bf16[32,512]{1,0:T(8,128)(2,1)S(1)}, bf16[32,512]{1,0:T(8,128)(2,1)S(1)}, u32[]{:S(2)}, u32[]{:S(2)}) %collective-permute-start.12) | collective-permute-done | bytes 32800 | tf_op jit(solution)/shard_map/ppermute | solution.py:55
  54.6 1.4 %collective-permute-done.14 = bf16[32,512]{1,0:T(8,128)(2,1)S(1)} collective-permute-done((bf16[32,512]{1,0:T(8,128)(2,1)S(1)}, bf16[32,512]{1,0:T(8,128)(2,1)S(1)}, u32[]{:S(2)}, u32[]{:S(2)}) %collective-permute-start.14) | collective-permute-done | bytes 32800 | tf_op jit(solution)/shard_map/ppermute | solution.py:41
  56.0 4.4 %collective-permute-start.15 = (bf16[3,32,512]{2,1,0:T(8,128)(2,1)S(1)}, bf16[3,32,512]{2,1,0:T(8,128)(2,1)S(1)}, u32[]{:S(2)}, u32[]{:S(2)}) collective-permute-start(bf16[3,32,512]{2,1,0:T(8,128)(2,1)S(1)} %pad_maximum_fusion.1.refs_6_), channel_id=1, source_target_pairs={{0,4},{4,0},{8,12},{12,8},{16,20},{20,16},{24,28},{28,24},{32,36},... | collective-permute-start | bytes 294920 | tf_op jit(solution)/shard_map/ppermute | solution.py:49
  60.5 0.9 collective-permute-done.15.refs_7_
  61.4 3.0 %shard_map.52 = (f32[32,512]{1,0:T(8,128)S(1)}, f32[32,512]{1,0:T(8,128)S(1)}, f32[32,512]{1,0:T(8,128)S(1)}, f32[32,512]{1,0:T(8,128)S(1)}) custom-call(s32[80]{0:T(128)S(1)} %get-tuple-element.61.refs_0_, s32[80]{0:T(128)S(1)} %get-tuple-element.62.refs_1_, s32[80]{0:T(128)S(1)} %get-tuple-element.63.refs_2_, s32[80]{0:T(128)S(1)} %get-tuple-element.64.refs_3_, ...), custom_call_target="tpu_custom_call" | custom-call | flops 838860800 | bytes 7340032 | tf_op jit(solution)/shard_map/pallas_call | solution.py:340
  64.4 0.9 collective-permute-start.16
  65.3 2.3 %collective-permute-start.17 = (f32[32,512]{1,0:T(8,128)S(1)}, f32[32,512]{1,0:T(8,128)S(1)}, u32[]{:S(2)}, u32[]{:S(2)}) collective-permute-start(f32[32,512]{1,0:T(8,128)S(1)} %get-tuple-element.72), channel_id=1, source_target_pairs={{2,0},{3,1},{0,2},{1,3},{6,4},{7,5},{4,6},{5,7},{10,8},{11,9},{8,1... | collective-permute-start | bytes 196616 | tf_op jit(solution)/shard_map/ppermute | solution.py:41
  67.8 1.0 collective-permute-done.16.refs_1_
  68.8 1.8 %collective-permute-done.17.refs_2_ = f32[32,512]{1,0:T(8,128)S(1)} collective-permute-done((f32[32,512]{1,0:T(8,128)S(1)}, f32[32,512]{1,0:T(8,128)S(1)}, u32[]{:S(2)}, u32[]{:S(2)}) %collective-permute-start.17) | collective-permute-done | bytes 65568 | tf_op jit(solution)/shard_map/ppermute | solution.py:41
  70.6 0.9 collective-permute-done.18.refs_3_
  71.5 0.2 shard_map.53
  71.8 4.8 %collective-permute-start.20 = (f32[32,512]{1,0:T(8,128)S(1)}, f32[32,512]{1,0:T(8,128)S(1)}, u32[]{:S(2)}, u32[]{:S(2)}) collective-permute-start(f32[32,512]{1,0:T(8,128)S(1)} %get-tuple-element.75), channel_id=1, source_target_pairs={{8,0},{12,4},{16,8},{20,12},{24,16},{28,20},{32,24},{36,28},{40,32... | collective-permute-start | bytes 196616 | tf_op jit(solution)/shard_map/ppermute | solution.py:41
  76.5 1.6 %collective-permute-done.21 = f32[32,512]{1,0:T(8,128)S(1)} collective-permute-done((f32[32,512]{1,0:T(8,128)S(1)}, f32[32,512]{1,0:T(8,128)S(1)}, u32[]{:S(2)}, u32[]{:S(2)}) %collective-permute-start.21) | collective-permute-done | bytes 65568 | tf_op jit(solution)/shard_map/ppermute | solution.py:41
  78.2 3.5 %collective-permute-done.19.refs_8_ = f32[32,512]{1,0:T(8,128)S(1)} collective-permute-done((f32[32,512]{1,0:T(8,128)S(1)}, f32[32,512]{1,0:T(8,128)S(1)}, u32[]{:S(2)}, u32[]{:S(2)}) %collective-permute-start.19) | collective-permute-done | bytes 65568 | tf_op jit(solution)/shard_map/ppermute | solution.py:55
  81.7 4.1 %collective-permute-start.22 = (f32[3,32,512]{2,1,0:T(8,128)S(1)}, f32[3,32,512]{2,1,0:T(8,128)S(1)}, u32[]{:S(2)}, u32[]{:S(2)}) collective-permute-start(f32[3,32,512]{2,1,0:T(8,128)S(1)} %pad_maximum_fusion.refs_6_), channel_id=1, source_target_pairs={{0,4},{4,0},{8,12},{12,8},{16,20},{20,16},{24,28},{28,24},{32,36},... | collective-permute-start | bytes 589832 | tf_op jit(solution)/shard_map/ppermute | solution.py:49
  85.9 1.1 collective-permute-done.22.refs_7_
  86.9 3.1 %shard_map.54 = (f32[32,512]{1,0:T(8,128)S(1)}, f32[32,512]{1,0:T(8,128)S(1)}, f32[32,512]{1,0:T(8,128)S(1)}, f32[32,512]{1,0:T(8,128)S(1)}) custom-call(s32[80]{0:T(128)S(1)} %get-tuple-element.61.refs_0_, s32[80]{0:T(128)S(1)} %get-tuple-element.62.refs_1_, s32[80]{0:T(128)S(1)} %get-tuple-element.63.refs_2_, s32[80]{0:T(128)S(1)} %get-tuple-element.64.refs_3_, ...), custom_call_target="tpu_custom_call" | custom-call | flops 838860800 | bytes 7340032 | tf_op jit(solution)/shard_map/pallas_call | solution.py:340
  90.1 0.6 collective-permute-start.23
  90.6 2.8 %collective-permute-start.24 = (f32[32,512]{1,0:T(8,128)S(1)}, f32[32,512]{1,0:T(8,128)S(1)}, u32[]{:S(2)}, u32[]{:S(2)}) collective-permute-start(f32[32,512]{1,0:T(8,128)S(1)} %get-tuple-element.81), channel_id=1, source_target_pairs={{2,0},{3,1},{0,2},{1,3},{6,4},{7,5},{4,6},{5,7},{10,8},{11,9},{8,1... | collective-permute-start | bytes 196616 | tf_op jit(solution)/shard_map/ppermute | solution.py:41
  93.4 1.0 collective-permute-done.23.refs_1_
  94.5 1.9 %collective-permute-done.24.refs_2_ = f32[32,512]{1,0:T(8,128)S(1)} collective-permute-done((f32[32,512]{1,0:T(8,128)S(1)}, f32[32,512]{1,0:T(8,128)S(1)}, u32[]{:S(2)}, u32[]{:S(2)}) %collective-permute-start.24) | collective-permute-done | bytes 65568 | tf_op jit(solution)/shard_map/ppermute | solution.py:41
  96.4 0.8 collective-permute-done.25.refs_3_
  97.1 0.2 shard_map.55
  97.5 13.4 %all_to_all.20 = f32[32,16,128]{2,1,0:T(8,128)S(1)} all-to-all(f32[32,16,128]{2,1,0:T(8,128)S(1)} %broadcast_in_dim.13), channel_id=1, replica_groups={{0,1,2,3,4,5,6,7,8,9,10,11,12,13,14,15,16,17,18,19,20,21,22,23,24,25,26..., dimensions={0} | all-to-all | bytes 524288 | tf_op jit(solution)/shard_map/all_to_all | solution.py:79
  110.9 12.0 %all_to_all.21 = f32[8,16,128]{2,1,0:T(8,128)S(1)} all-to-all(f32[8,16,128]{2,1,0:T(8,128)S(1)} %broadcast_in_dim.28), channel_id=1, replica_groups={{0,32,64,96,128,160,192,224},{1,33,65,97,129,161,193,225},{2,34,66,98,1..., dimensions={0} | all-to-all | bytes 131072 | tf_op jit(solution)/shard_map/all_to_all | solution.py:79
  123.0 2.6 %shard_map.56 = (f32[32,512]{1,0:T(8,128)S(1)}, s32[1]{0:T(128)}) custom-call(f32[64,32]{1,0:T(8,128)S(1)} %reshape.19.grams_ref, f32[32,512]{1,0:T(8,128)S(1)} %get-tuple-element.84.image_ref), custom_call_target="tpu_custom_call" | custom-call | flops 1048576 | bytes 131072 | tf_op jit(solution)/shard_map/pallas_call | solution.py:503
  126.3 0.6 copy-done.3
  (43 shorter events, 0.8 us)
Async XLA Ops:
  0.0 44.6 %copy-start.2 = (f32[32,512]{1,0:T(8,128)S(1)}, f32[32,512]{1,0:T(8,128)}, u32[]{:S(2)}) copy-start(f32[32,512]{1,0:T(8,128)} %param.8) | copy-start | bytes 196612
  2.1 21.6 %collective-permute-start.2 = (bf16[320,512]{1,0:T(8,128)(2,1)}, bf16[320,512]{1,0:T(8,128)(2,1)S(1)}, u32[]{:S(2)}, u32[]{:S(2)}) collective-permute-start(bf16[320,512]{1,0:T(8,128)(2,1)} %get-tuple-element.52.refs_0_), channel_id=1, source_target_pairs={{3,0},{0,1},{1,2},{2,3},{7,4},{4,5},{5,6},{6,7},{11,8},{8,9},{9,10... | collective-permute-start | bytes 983048 | tf_op jit(solution)/shard_map/ppermute | solution.py:41
  4.2 19.5 %collective-permute-start.1 = (bf16[320,512]{1,0:T(8,128)(2,1)}, bf16[320,512]{1,0:T(8,128)(2,1)S(1)}, u32[]{:S(2)}, u32[]{:S(2)}) collective-permute-start(bf16[320,512]{1,0:T(8,128)(2,1)} %get-tuple-element.52.refs_0_), channel_id=1, source_target_pairs={{2,0},{3,1},{0,2},{1,3},{6,4},{7,5},{4,6},{5,7},{10,8},{11,9},{8,1... | collective-permute-start | bytes 983048 | tf_op jit(solution)/shard_map/ppermute | solution.py:41
  6.8 14.4 %collective-permute-start.4 = (bf16[304,512]{1,0:T(8,128)(2,1)}, bf16[304,512]{1,0:T(8,128)(2,1)S(1)}, u32[]{:S(2)}, u32[]{:S(2)}) collective-permute-start(bf16[304,512]{1,0:T(8,128)(2,1)} %get-tuple-element.56.refs_2_), channel_id=1, source_target_pairs={{248,0},{252,4},{0,8},{4,12},{8,16},{12,20},{16,24},{20,28},{24,32... | collective-permute-start | bytes 933896 | tf_op jit(solution)/shard_map/ppermute | solution.py:41
  8.1 13.2 %collective-permute-start.3 = (bf16[304,512]{1,0:T(8,128)(2,1)}, bf16[304,512]{1,0:T(8,128)(2,1)S(1)}, u32[]{:S(2)}, u32[]{:S(2)}) collective-permute-start(bf16[304,512]{1,0:T(8,128)(2,1)} %get-tuple-element.56.refs_2_), channel_id=1, source_target_pairs={{8,0},{12,4},{16,8},{20,12},{24,16},{28,20},{32,24},{36,28},{40,32... | collective-permute-start | bytes 933896 | tf_op jit(solution)/shard_map/ppermute | solution.py:41
  14.6 10.3 %collective-permute-start = (bf16[320,512]{1,0:T(8,128)(2,1)}, bf16[320,512]{1,0:T(8,128)(2,1)S(1)}, u32[]{:S(2)}, u32[]{:S(2)}) collective-permute-start(bf16[320,512]{1,0:T(8,128)(2,1)} %get-tuple-element.52.refs_0_), channel_id=1, source_target_pairs={{1,0},{2,1},{3,2},{0,3},{5,4},{6,5},{7,6},{4,7},{9,8},{10,9},{11,1... | collective-permute-start | bytes 983048 | tf_op jit(solution)/shard_map/ppermute | solution.py:41
  21.3 10.0 %collective-permute-start.8 = (bf16[304,512]{1,0:T(8,128)(2,1)}, bf16[304,512]{1,0:T(8,128)(2,1)S(1)}, u32[]{:S(2)}, u32[]{:S(2)}) collective-permute-start(bf16[304,512]{1,0:T(8,128)(2,1)} %get-tuple-element.56.refs_2_), channel_id=1, source_target_pairs={{0,244},{4,16},{8,252},{12,24},{16,4},{20,32},{24,12},{28,40},{32,... | collective-permute-start | bytes 933896 | tf_op jit(solution)/shard_map/ppermute | solution.py:475
  21.3 10.0 %collective-permute-start.5 = (bf16[304,512]{1,0:T(8,128)(2,1)}, bf16[304,512]{1,0:T(8,128)(2,1)S(1)}, u32[]{:S(2)}, u32[]{:S(2)}) collective-permute-start(bf16[304,512]{1,0:T(8,128)(2,1)} %get-tuple-element.56.refs_2_), channel_id=1, source_target_pairs={{0,4},{4,0},{8,12},{12,8},{16,20},{20,16},{24,28},{28,24},{32,36},... | collective-permute-start | bytes 933896 | tf_op jit(solution)/shard_map/ppermute | solution.py:49
  23.7 7.6 %collective-permute-start.6 = (bf16[304,512]{1,0:T(8,128)(2,1)S(1)}, bf16[304,512]{1,0:T(8,128)(2,1)S(1)}, u32[]{:S(2)}, u32[]{:S(2)}) collective-permute-start(bf16[304,512]{1,0:T(8,128)(2,1)S(1)} %collective-permute-done.3.refs_0_), channel_id=1, source_target_pairs={{0,4},{4,0},{8,12},{12,8},{16,20},{20,16},{24,28},{28,24},{32,36},... | collective-permute-start | bytes 933896 | tf_op jit(solution)/shard_map/ppermute | solution.py:49
  23.8 7.6 %collective-permute-start.7 = (bf16[304,512]{1,0:T(8,128)(2,1)S(1)}, bf16[304,512]{1,0:T(8,128)(2,1)S(1)}, u32[]{:S(2)}, u32[]{:S(2)}) collective-permute-start(bf16[304,512]{1,0:T(8,128)(2,1)S(1)} %collective-permute-done.4.refs_1_), channel_id=1, source_target_pairs={{0,4},{4,0},{8,12},{12,8},{16,20},{20,16},{24,28},{28,24},{32,36},... | collective-permute-start | bytes 933896 | tf_op jit(solution)/shard_map/ppermute | solution.py:49
  25.1 1.0 copy-start
  26.4 1.0 copy-start.1
  37.3 3.7 %collective-permute-start.11 = (f32[1,512]{1,0:T(1,128)S(1)}, f32[1,512]{1,0:T(1,128)S(1)}, u32[]{:S(2)}, u32[]{:S(2)}) collective-permute-start(f32[1,512]{1,0:T(1,128)S(1)} %get-tuple-element.88), channel_id=1, source_target_pairs={{1,0},{2,1},{3,2},{0,3},{5,4},{6,5},{7,6},{4,7},{9,8},{10,9},{11,1... | collective-permute-start | bytes 6152 | tf_op jit(solution)/shard_map/ppermute | solution.py:41
  39.2 3.9 %collective-permute-start.10 = (f32[1,512]{1,0:T(1,128)S(1)}, f32[1,512]{1,0:T(1,128)S(1)}, u32[]{:S(2)}, u32[]{:S(2)}) collective-permute-start(f32[1,512]{1,0:T(1,128)S(1)} %get-tuple-element.89), channel_id=1, source_target_pairs={{2,0},{3,1},{0,2},{1,3},{6,4},{7,5},{4,6},{5,7},{10,8},{11,9},{8,1... | collective-permute-start | bytes 6152 | tf_op jit(solution)/shard_map/ppermute | solution.py:41
  41.0 3.6 %collective-permute-start.9 = (f32[1,512]{1,0:T(1,128)S(1)}, f32[1,512]{1,0:T(1,128)S(1)}, u32[]{:S(2)}, u32[]{:S(2)}) collective-permute-start(f32[1,512]{1,0:T(1,128)S(1)} %get-tuple-element.90), channel_id=1, source_target_pairs={{3,0},{0,1},{1,2},{2,3},{7,4},{4,5},{5,6},{6,7},{11,8},{8,9},{9,10... | collective-permute-start | bytes 6152 | tf_op jit(solution)/shard_map/ppermute | solution.py:41
  44.6 6.2 %collective-permute-start.13 = (bf16[32,512]{1,0:T(8,128)(2,1)S(1)}, bf16[32,512]{1,0:T(8,128)(2,1)S(1)}, u32[]{:S(2)}, u32[]{:S(2)}) collective-permute-start(bf16[32,512]{1,0:T(8,128)(2,1)S(1)} %multiply_convert_fusion), channel_id=1, source_target_pairs={{8,0},{12,4},{16,8},{20,12},{24,16},{28,20},{32,24},{36,28},{40,32... | collective-permute-start | bytes 98312 | tf_op jit(solution)/shard_map/ppermute | solution.py:41
  49.8 4.8 %collective-permute-start.12 = (bf16[32,512]{1,0:T(8,128)(2,1)S(1)}, bf16[32,512]{1,0:T(8,128)(2,1)S(1)}, u32[]{:S(2)}, u32[]{:S(2)}) collective-permute-start(bf16[32,512]{1,0:T(8,128)(2,1)S(1)} %multiply_convert_fusion), channel_id=1, source_target_pairs={{0,244},{4,16},{8,252},{12,24},{16,4},{20,32},{24,12},{28,40},{32,... | collective-permute-start | bytes 98312 | tf_op jit(solution)/shard_map/ppermute | solution.py:55
  49.9 6.1 %collective-permute-start.14 = (bf16[32,512]{1,0:T(8,128)(2,1)S(1)}, bf16[32,512]{1,0:T(8,128)(2,1)S(1)}, u32[]{:S(2)}, u32[]{:S(2)}) collective-permute-start(bf16[32,512]{1,0:T(8,128)(2,1)S(1)} %multiply_convert_fusion), channel_id=1, source_target_pairs={{248,0},{252,4},{0,8},{4,12},{8,16},{12,20},{16,24},{20,28},{24,32... | collective-permute-start | bytes 98312 | tf_op jit(solution)/shard_map/ppermute | solution.py:41
  56.0 5.4 %collective-permute-start.15 = (bf16[3,32,512]{2,1,0:T(8,128)(2,1)S(1)}, bf16[3,32,512]{2,1,0:T(8,128)(2,1)S(1)}, u32[]{:S(2)}, u32[]{:S(2)}) collective-permute-start(bf16[3,32,512]{2,1,0:T(8,128)(2,1)S(1)} %pad_maximum_fusion.1.refs_6_), channel_id=1, source_target_pairs={{0,4},{4,0},{8,12},{12,8},{16,20},{20,16},{24,28},{28,24},{32,36},... | collective-permute-start | bytes 294920 | tf_op jit(solution)/shard_map/ppermute | solution.py:49
  64.4 4.4 %collective-permute-start.16 = (f32[32,512]{1,0:T(8,128)S(1)}, f32[32,512]{1,0:T(8,128)S(1)}, u32[]{:S(2)}, u32[]{:S(2)}) collective-permute-start(f32[32,512]{1,0:T(8,128)S(1)} %get-tuple-element.71), channel_id=1, source_target_pairs={{3,0},{0,1},{1,2},{2,3},{7,4},{4,5},{5,6},{6,7},{11,8},{8,9},{9,10... | collective-permute-start | bytes 196616 | tf_op jit(solution)/shard_map/ppermute | solution.py:41
  65.3 5.3 %collective-permute-start.17 = (f32[32,512]{1,0:T(8,128)S(1)}, f32[32,512]{1,0:T(8,128)S(1)}, u32[]{:S(2)}, u32[]{:S(2)}) collective-permute-start(f32[32,512]{1,0:T(8,128)S(1)} %get-tuple-element.72), channel_id=1, source_target_pairs={{2,0},{3,1},{0,2},{1,3},{6,4},{7,5},{4,6},{5,7},{10,8},{11,9},{8,1... | collective-permute-start | bytes 196616 | tf_op jit(solution)/shard_map/ppermute | solution.py:41
  67.7 3.8 %collective-permute-start.18 = (f32[32,512]{1,0:T(8,128)S(1)}, f32[32,512]{1,0:T(8,128)S(1)}, u32[]{:S(2)}, u32[]{:S(2)}) collective-permute-start(f32[32,512]{1,0:T(8,128)S(1)} %get-tuple-element.73), channel_id=1, source_target_pairs={{1,0},{2,1},{3,2},{0,3},{5,4},{6,5},{7,6},{4,7},{9,8},{10,9},{11,1... | collective-permute-start | bytes 196616 | tf_op jit(solution)/shard_map/ppermute | solution.py:41
  71.7 6.5 %collective-permute-start.21 = (f32[32,512]{1,0:T(8,128)S(1)}, f32[32,512]{1,0:T(8,128)S(1)}, u32[]{:S(2)}, u32[]{:S(2)}) collective-permute-start(f32[32,512]{1,0:T(8,128)S(1)} %get-tuple-element.75), channel_id=1, source_target_pairs={{248,0},{252,4},{0,8},{4,12},{8,16},{12,20},{16,24},{20,28},{24,32... | collective-permute-start | bytes 196616 | tf_op jit(solution)/shard_map/ppermute | solution.py:41
  71.8 6.4 %collective-permute-start.20 = (f32[32,512]{1,0:T(8,128)S(1)}, f32[32,512]{1,0:T(8,128)S(1)}, u32[]{:S(2)}, u32[]{:S(2)}) collective-permute-start(f32[32,512]{1,0:T(8,128)S(1)} %get-tuple-element.75), channel_id=1, source_target_pairs={{8,0},{12,4},{16,8},{20,12},{24,16},{28,20},{32,24},{36,28},{40,32... | collective-permute-start | bytes 196616 | tf_op jit(solution)/shard_map/ppermute | solution.py:41
  76.5 5.2 %collective-permute-start.19 = (f32[32,512]{1,0:T(8,128)S(1)}, f32[32,512]{1,0:T(8,128)S(1)}, u32[]{:S(2)}, u32[]{:S(2)}) collective-permute-start(f32[32,512]{1,0:T(8,128)S(1)} %get-tuple-element.75), channel_id=1, source_target_pairs={{0,244},{4,16},{8,252},{12,24},{16,4},{20,32},{24,12},{28,40},{32,... | collective-permute-start | bytes 196616 | tf_op jit(solution)/shard_map/ppermute | solution.py:55
  81.7 5.2 %collective-permute-start.22 = (f32[3,32,512]{2,1,0:T(8,128)S(1)}, f32[3,32,512]{2,1,0:T(8,128)S(1)}, u32[]{:S(2)}, u32[]{:S(2)}) collective-permute-start(f32[3,32,512]{2,1,0:T(8,128)S(1)} %pad_maximum_fusion.refs_6_), channel_id=1, source_target_pairs={{0,4},{4,0},{8,12},{12,8},{16,20},{20,16},{24,28},{28,24},{32,36},... | collective-permute-start | bytes 589832 | tf_op jit(solution)/shard_map/ppermute | solution.py:49
  90.1 4.4 %collective-permute-start.23 = (f32[32,512]{1,0:T(8,128)S(1)}, f32[32,512]{1,0:T(8,128)S(1)}, u32[]{:S(2)}, u32[]{:S(2)}) collective-permute-start(f32[32,512]{1,0:T(8,128)S(1)} %get-tuple-element.80), channel_id=1, source_target_pairs={{3,0},{0,1},{1,2},{2,3},{7,4},{4,5},{5,6},{6,7},{11,8},{8,9},{9,10... | collective-permute-start | bytes 196616 | tf_op jit(solution)/shard_map/ppermute | solution.py:41
  90.6 5.8 %collective-permute-start.24 = (f32[32,512]{1,0:T(8,128)S(1)}, f32[32,512]{1,0:T(8,128)S(1)}, u32[]{:S(2)}, u32[]{:S(2)}) collective-permute-start(f32[32,512]{1,0:T(8,128)S(1)} %get-tuple-element.81), channel_id=1, source_target_pairs={{2,0},{3,1},{0,2},{1,3},{6,4},{7,5},{4,6},{5,7},{10,8},{11,9},{8,1... | collective-permute-start | bytes 196616 | tf_op jit(solution)/shard_map/ppermute | solution.py:41
  93.4 3.7 %collective-permute-start.25 = (f32[32,512]{1,0:T(8,128)S(1)}, f32[32,512]{1,0:T(8,128)S(1)}, u32[]{:S(2)}, u32[]{:S(2)}) collective-permute-start(f32[32,512]{1,0:T(8,128)S(1)} %get-tuple-element.82), channel_id=1, source_target_pairs={{1,0},{2,1},{3,2},{0,3},{5,4},{6,5},{7,6},{4,7},{9,8},{10,9},{11,1... | collective-permute-start | bytes 196616 | tf_op jit(solution)/shard_map/ppermute | solution.py:41
  126.3 0.6 copy-start.3

commit v9 on v8

--- a/solution.py
+++ b/solution.py
@@ -125,7 +125,7 @@
 
 
 def prepare_columns(data_ref, first, lhs, rate_ref):
-    wide = data_ref[...].astype(jnp.float32)
+    wide = data_ref[:ROWS, :].astype(jnp.float32)
     rate = 1.0 / wide[SCALE_ROW : SCALE_ROW + 1]
     squares = wide[:FEAT] * wide[:FEAT]
     tail = ones_and_norms(jnp.sum(squares, axis=0, keepdims=True), 3, 0)
@@ -478,7 +478,7 @@
     listed = listed.reshape(N_SUB * REACH * PAIRS)
 
     tiles = []
-    carried = payload
+    carried = wide
     for at, sources in enumerate(((ahead, behind), (*there, far))):
         *tile, carried = hop_tiles(
             WINDOWS[at], at == 0, at == len(WINDOWS) - 1, listed, blocks, rate, sources, carried

time: 127 us -> 127 us (level)
  starting transfers between devices: 45.7 us -> 48.4 us
  waiting for transfers between devices: 29.9 us -> 27.8 us
    ppermute x18, waiting for transfers between devices: 20.5 us -> 18.4 us  [shifted(): lax.ppermute(value, axis, [((at + steps) % count, at) for at in range(cou...]
    ppermute x18, starting transfers between devices: 34 us -> 35.7 us  [shifted(): lax.ppermute(value, axis, [((at + steps) % count, at) for at in range(cou...]
    unnamed x8 -> x6, local copies, waits for them, and re-layouts: 2.56 us -> 1.6 us
where the time goes in v9:
time: 127 us
  starting transfers between devices  48.4 us (38%)
  waiting for transfers between devices  27.8 us (22%)
  blocking collectives  26 us (20%)
  Pallas kernels  21.3 us (17%)
  local copies, waits for them, and re-layouts  2.55 us (2%)
    ppermute x18, starting transfers between devices, shifted(): lax.ppermute(value, axis, [((at + steps) % count, at) for at in range(cou...  35.7 us
    all_to_all x2, blocking collectives, summed(): lax.all_to_all(sent, ('space', 'sub'), 0, 0, axis_index_groups=groups)  26 us
    ppermute x18, waiting for transfers between devices, shifted(): lax.ppermute(value, axis, [((at + steps) % count, at) for at in range(cou...  18.4 us
    ppermute x5, starting transfers between devices, swapped(): lax.ppermute(value, 'space', [(at, at ^ 1) for at in range(lax.axis_size(...  12.7 us
    pallas_call x2, Pallas kernels, hop_tiles(): pl.pallas_call(functools.partial(tile_kernel, windows, first, last), in_s...  9.86 us
    ppermute x2, waiting for transfers between devices, space_window(): lax.ppermute(value, 'space', far_pairs(lax.axis_size('space')))  7.36 us
    pallas_call x2, Pallas kernels, sweep(): pl.pallas_call(functools.partial(sweep_kernel, parts), in_specs=[smem] *...  6.08 us
    pallas_call x1, Pallas kernels, on_device(): pl.pallas_call(solve_both_kernel, in_specs=[pl.BlockSpec(memory_space=plt...  2.6 us
  transfers between devices with their start and end apart: 26, of which 16 were waited for; matrix products, arithmetic and copies ran while one was open for 1% of the time, Pallas kernels for 3%

profile of v9, /device:TPU:1, one launch (start us, length us, event | category | flops | bytes accessed | tf_op | source)
XLA Modules:
  0.0 127.1 jit_solution(5444593561790778466)
XLA Ops:
  0.0 2.1 %shard_map.48 = (bf16[304,512]{1,0:T(8,128)(2,1)}, bf16[320,512]{1,0:T(8,128)(2,1)}) custom-call(s32[2,24]{1,0:T(2,128)} %bitcast.29, bf16[300,512]{1,0:T(8,128)(2,1)} %data_ref.1, bf16[512]{0:T(512)(128)(2,1)} %scale_ref.1), custom_call_target="tpu_custom_call" | custom-call | flops 1048576 | bytes 131072 | tf_op jit(solution)/shard_map/pallas_call | solution.py:463
  2.1 2.1 %collective-permute-start.2 = (bf16[320,512]{1,0:T(8,128)(2,1)}, bf16[320,512]{1,0:T(8,128)(2,1)S(1)}, u32[]{:S(2)}, u32[]{:S(2)}) collective-permute-start(bf16[320,512]{1,0:T(8,128)(2,1)} %get-tuple-element.52.refs_0_.refs_2_), channel_id=1, source_target_pairs={{3,0},{0,1},{1,2},{2,3},{7,4},{4,5},{5,6},{6,7},{11,8},{8,9},{9,10... | collective-permute-start | bytes 983048 | tf_op jit(solution)/shard_map/ppermute | solution.py:41
  4.2 2.6 %collective-permute-start.1 = (bf16[320,512]{1,0:T(8,128)(2,1)}, bf16[320,512]{1,0:T(8,128)(2,1)S(1)}, u32[]{:S(2)}, u32[]{:S(2)}) collective-permute-start(bf16[320,512]{1,0:T(8,128)(2,1)} %get-tuple-element.52.refs_0_.refs_2_), channel_id=1, source_target_pairs={{2,0},{3,1},{0,2},{1,3},{6,4},{7,5},{4,6},{5,7},{10,8},{11,9},{8,1... | collective-permute-start | bytes 983048 | tf_op jit(solution)/shard_map/ppermute | solution.py:41
  6.8 1.2 collective-permute-start.4
  8.1 6.6 %collective-permute-start.3 = (bf16[304,512]{1,0:T(8,128)(2,1)}, bf16[304,512]{1,0:T(8,128)(2,1)S(1)}, u32[]{:S(2)}, u32[]{:S(2)}) collective-permute-start(bf16[304,512]{1,0:T(8,128)(2,1)} %get-tuple-element.56), channel_id=1, source_target_pairs={{8,0},{12,4},{16,8},{20,12},{24,16},{28,20},{32,24},{36,28},{40,32... | collective-permute-start | bytes 933896 | tf_op jit(solution)/shard_map/ppermute | solution.py:41
  14.6 1.1 collective-permute-start
  15.7 5.6 %collective-permute-done.4.refs_1_ = bf16[304,512]{1,0:T(8,128)(2,1)S(1)} collective-permute-done((bf16[304,512]{1,0:T(8,128)(2,1)}, bf16[304,512]{1,0:T(8,128)(2,1)S(1)}, u32[]{:S(2)}, u32[]{:S(2)}) %collective-permute-start.4) | collective-permute-done | bytes 311328 | tf_op jit(solution)/shard_map/ppermute | solution.py:41
  21.3 2.5 %collective-permute-start.5 = (bf16[304,512]{1,0:T(8,128)(2,1)}, bf16[304,512]{1,0:T(8,128)(2,1)S(1)}, u32[]{:S(2)}, u32[]{:S(2)}) collective-permute-start(bf16[304,512]{1,0:T(8,128)(2,1)} %get-tuple-element.56), channel_id=1, source_target_pairs={{0,4},{4,0},{8,12},{12,8},{16,20},{20,16},{24,28},{28,24},{32,36},... | collective-permute-start | bytes 933896 | tf_op jit(solution)/shard_map/ppermute | solution.py:49
  23.7 0.5 collective-permute-start.7
  24.3 0.7 slice.27
  25.1 1.0 copy-done
  26.0 0.3 shard_map.49
  26.4 3.9 %shard_map.50 = (bf16[40,256,256]{2,1,0:T(8,128)(2,1)S(1)}, s32[80]{0:T(128)S(1)}, s32[80]{0:T(128)S(1)}, f32[9,8,256]{2,1,0:T(8,128)S(1)}) custom-call(s32[192]{0:T(256)S(1)} %reshape.20.mine_ref, bf16[8,320,256]{2,1,0:T(8,128)(2,1)S(1)} %get-tuple-element.53.blocks_ref, f32[8,8,256]{2,1,0:T(8,128)S(1)} %get-tuple-element.54.rate_ref, ...), custom_call_target="tpu_custom_call" | custom-call | flops 671088640 | bytes 7340032 | tf_op jit(solution)/shard_map/pallas_call | solution.py:243
  30.3 5.9 %shard_map.51 = (bf16[64,256,256]{2,1,0:T(8,128)(2,1)S(1)}, s32[80]{0:T(128)S(1)}, s32[80]{0:T(128)S(1)}, f32[4,8,512]{2,1,0:T(8,128)S(1)}) custom-call(s32[192]{0:T(256)S(1)} %reshape.20.mine_ref, bf16[8,320,256]{2,1,0:T(8,128)(2,1)S(1)} %get-tuple-element.53.blocks_ref, f32[8,8,256]{2,1,0:T(8,128)S(1)} %get-tuple-element.54.rate_ref, ...), custom_call_target="tpu_custom_call" | custom-call | flops 1342177280 | bytes 7340032 | tf_op jit(solution)/shard_map/pallas_call | solution.py:243
  36.3 0.3 collective-permute-start.11
  36.6 4.3 %collective-permute-start.10 = (f32[1,512]{1,0:T(1,128)S(1)}, f32[1,512]{1,0:T(1,128)S(1)}, u32[]{:S(2)}, u32[]{:S(2)}) collective-permute-start(f32[1,512]{1,0:T(1,128)S(1)} %get-tuple-element.89), channel_id=1, source_target_pairs={{2,0},{3,1},{0,2},{1,3},{6,4},{7,5},{4,6},{5,7},{10,8},{11,9},{8,1... | collective-permute-start | bytes 6152 | tf_op jit(solution)/shard_map/ppermute | solution.py:41
  41.0 1.0 collective-permute-done.10
  41.9 2.7 %collective-permute-done.9 = f32[1,512]{1,0:T(1,128)S(1)} collective-permute-done((f32[1,512]{1,0:T(1,128)S(1)}, f32[1,512]{1,0:T(1,128)S(1)}, u32[]{:S(2)}, u32[]{:S(2)}) %collective-permute-start.9) | collective-permute-done | bytes 2080 | tf_op jit(solution)/shard_map/ppermute | solution.py:41
  44.6 4.2 %collective-permute-start.13 = (bf16[32,512]{1,0:T(8,128)(2,1)S(1)}, bf16[32,512]{1,0:T(8,128)(2,1)S(1)}, u32[]{:S(2)}, u32[]{:S(2)}) collective-permute-start(bf16[32,512]{1,0:T(8,128)(2,1)S(1)} %multiply_convert_fusion), channel_id=1, source_target_pairs={{8,0},{12,4},{16,8},{20,12},{24,16},{28,20},{32,24},{36,28},{40,32... | collective-permute-start | bytes 98312 | tf_op jit(solution)/shard_map/ppermute | solution.py:41
  48.8 1.0 collective-permute-done.13
  49.8 3.8 %collective-permute-done.12.refs_8_ = bf16[32,512]{1,0:T(8,128)(2,1)S(1)} collective-permute-done((bf16[32,512]{1,0:T(8,128)(2,1)S(1)}, bf16[32,512]{1,0:T(8,128)(2,1)S(1)}, u32[]{:S(2)}, u32[]{:S(2)}) %collective-permute-start.12) | collective-permute-done | bytes 32800 | tf_op jit(solution)/shard_map/ppermute | solution.py:55
  53.7 1.2 collective-permute-done.14
  54.9 4.8 %collective-permute-start.15 = (bf16[3,32,512]{2,1,0:T(8,128)(2,1)S(1)}, bf16[3,32,512]{2,1,0:T(8,128)(2,1)S(1)}, u32[]{:S(2)}, u32[]{:S(2)}) collective-permute-start(bf16[3,32,512]{2,1,0:T(8,128)(2,1)S(1)} %pad_maximum_fusion.1.refs_6_), channel_id=1, source_target_pairs={{0,4},{4,0},{8,12},{12,8},{16,20},{20,16},{24,28},{28,24},{32,36},... | collective-permute-start | bytes 294920 | tf_op jit(solution)/shard_map/ppermute | solution.py:49
  59.8 0.9 collective-permute-done.15.refs_7_
  60.7 3.0 %shard_map.52 = (f32[32,512]{1,0:T(8,128)S(1)}, f32[32,512]{1,0:T(8,128)S(1)}, f32[32,512]{1,0:T(8,128)S(1)}, f32[32,512]{1,0:T(8,128)S(1)}) custom-call(s32[80]{0:T(128)S(1)} %get-tuple-element.61.refs_0_, s32[80]{0:T(128)S(1)} %get-tuple-element.62.refs_1_, s32[80]{0:T(128)S(1)} %get-tuple-element.63.refs_2_, s32[80]{0:T(128)S(1)} %get-tuple-element.64.refs_3_, ...), custom_call_target="tpu_custom_call" | custom-call | flops 838860800 | bytes 7340032 | tf_op jit(solution)/shard_map/pallas_call | solution.py:340
  63.7 0.8 collective-permute-start.16
  64.5 1.6 %collective-permute-start.17 = (f32[32,512]{1,0:T(8,128)S(1)}, f32[32,512]{1,0:T(8,128)S(1)}, u32[]{:S(2)}, u32[]{:S(2)}) collective-permute-start(f32[32,512]{1,0:T(8,128)S(1)} %get-tuple-element.72), channel_id=1, source_target_pairs={{2,0},{3,1},{0,2},{1,3},{6,4},{7,5},{4,6},{5,7},{10,8},{11,9},{8,1... | collective-permute-start | bytes 196616 | tf_op jit(solution)/shard_map/ppermute | solution.py:41
  66.1 1.8 %collective-permute-start.18 = (f32[32,512]{1,0:T(8,128)S(1)}, f32[32,512]{1,0:T(8,128)S(1)}, u32[]{:S(2)}, u32[]{:S(2)}) collective-permute-start(f32[32,512]{1,0:T(8,128)S(1)} %get-tuple-element.73), channel_id=1, source_target_pairs={{1,0},{2,1},{3,2},{0,3},{5,4},{6,5},{7,6},{4,7},{9,8},{10,9},{11,1... | collective-permute-start | bytes 196616 | tf_op jit(solution)/shard_map/ppermute | solution.py:41
  68.1 1.6 %collective-permute-done.17.refs_2_ = f32[32,512]{1,0:T(8,128)S(1)} collective-permute-done((f32[32,512]{1,0:T(8,128)S(1)}, f32[32,512]{1,0:T(8,128)S(1)}, u32[]{:S(2)}, u32[]{:S(2)}) %collective-permute-start.17) | collective-permute-done | bytes 65568 | tf_op jit(solution)/shard_map/ppermute | solution.py:41
  69.6 0.2 collective-permute-done.18.refs_3_
  69.8 0.2 shard_map.53
  70.1 4.8 %collective-permute-start.20 = (f32[32,512]{1,0:T(8,128)S(1)}, f32[32,512]{1,0:T(8,128)S(1)}, u32[]{:S(2)}, u32[]{:S(2)}) collective-permute-start(f32[32,512]{1,0:T(8,128)S(1)} %get-tuple-element.75), channel_id=1, source_target_pairs={{8,0},{12,4},{16,8},{20,12},{24,16},{28,20},{32,24},{36,28},{40,32... | collective-permute-start | bytes 196616 | tf_op jit(solution)/shard_map/ppermute | solution.py:41
  74.9 1.6 %collective-permute-done.21 = f32[32,512]{1,0:T(8,128)S(1)} collective-permute-done((f32[32,512]{1,0:T(8,128)S(1)}, f32[32,512]{1,0:T(8,128)S(1)}, u32[]{:S(2)}, u32[]{:S(2)}) %collective-permute-start.21) | collective-permute-done | bytes 65568 | tf_op jit(solution)/shard_map/ppermute | solution.py:41
  76.5 3.5 %collective-permute-done.19.refs_8_ = f32[32,512]{1,0:T(8,128)S(1)} collective-permute-done((f32[32,512]{1,0:T(8,128)S(1)}, f32[32,512]{1,0:T(8,128)S(1)}, u32[]{:S(2)}, u32[]{:S(2)}) %collective-permute-start.19) | collective-permute-done | bytes 65568 | tf_op jit(solution)/shard_map/ppermute | solution.py:55
  80.1 4.9 %collective-permute-start.22 = (f32[3,32,512]{2,1,0:T(8,128)S(1)}, f32[3,32,512]{2,1,0:T(8,128)S(1)}, u32[]{:S(2)}, u32[]{:S(2)}) collective-permute-start(f32[3,32,512]{2,1,0:T(8,128)S(1)} %pad_maximum_fusion.refs_6_), channel_id=1, source_target_pairs={{0,4},{4,0},{8,12},{12,8},{16,20},{20,16},{24,28},{28,24},{32,36},... | collective-permute-start | bytes 589832 | tf_op jit(solution)/shard_map/ppermute | solution.py:49
  85.0 1.1 collective-permute-done.22.refs_7_
  86.1 3.1 %shard_map.54 = (f32[32,512]{1,0:T(8,128)S(1)}, f32[32,512]{1,0:T(8,128)S(1)}, f32[32,512]{1,0:T(8,128)S(1)}, f32[32,512]{1,0:T(8,128)S(1)}) custom-call(s32[80]{0:T(128)S(1)} %get-tuple-element.61.refs_0_, s32[80]{0:T(128)S(1)} %get-tuple-element.62.refs_1_, s32[80]{0:T(128)S(1)} %get-tuple-element.63.refs_2_, s32[80]{0:T(128)S(1)} %get-tuple-element.64.refs_3_, ...), custom_call_target="tpu_custom_call" | custom-call | flops 838860800 | bytes 7340032 | tf_op jit(solution)/shard_map/pallas_call | solution.py:340
  89.2 1.5 %collective-permute-start.23 = (f32[32,512]{1,0:T(8,128)S(1)}, f32[32,512]{1,0:T(8,128)S(1)}, u32[]{:S(2)}, u32[]{:S(2)}) collective-permute-start(f32[32,512]{1,0:T(8,128)S(1)} %get-tuple-element.80), channel_id=1, source_target_pairs={{3,0},{0,1},{1,2},{2,3},{7,4},{4,5},{5,6},{6,7},{11,8},{8,9},{9,10... | collective-permute-start | bytes 196616 | tf_op jit(solution)/shard_map/ppermute | solution.py:41
  90.7 2.1 %collective-permute-start.24 = (f32[32,512]{1,0:T(8,128)S(1)}, f32[32,512]{1,0:T(8,128)S(1)}, u32[]{:S(2)}, u32[]{:S(2)}) collective-permute-start(f32[32,512]{1,0:T(8,128)S(1)} %get-tuple-element.81), channel_id=1, source_target_pairs={{2,0},{3,1},{0,2},{1,3},{6,4},{7,5},{4,6},{5,7},{10,8},{11,9},{8,1... | collective-permute-start | bytes 196616 | tf_op jit(solution)/shard_map/ppermute | solution.py:41
  92.8 0.6 collective-permute-start.25
  93.4 0.3 collective-permute-done.23.refs_1_
  93.6 1.8 %collective-permute-done.24.refs_2_ = f32[32,512]{1,0:T(8,128)S(1)} collective-permute-done((f32[32,512]{1,0:T(8,128)S(1)}, f32[32,512]{1,0:T(8,128)S(1)}, u32[]{:S(2)}, u32[]{:S(2)}) %collective-permute-start.24) | collective-permute-done | bytes 65568 | tf_op jit(solution)/shard_map/ppermute | solution.py:41
  95.4 1.3 %collective-permute-done.25.refs_3_ = f32[32,512]{1,0:T(8,128)S(1)} collective-permute-done((f32[32,512]{1,0:T(8,128)S(1)}, f32[32,512]{1,0:T(8,128)S(1)}, u32[]{:S(2)}, u32[]{:S(2)}) %collective-permute-start.25) | collective-permute-done | bytes 65568 | tf_op jit(solution)/shard_map/ppermute | solution.py:41
  96.7 0.2 shard_map.55
  97.0 13.8 %all_to_all.20 = f32[32,16,128]{2,1,0:T(8,128)S(1)} all-to-all(f32[32,16,128]{2,1,0:T(8,128)S(1)} %broadcast_in_dim.13), channel_id=1, replica_groups={{0,1,2,3,4,5,6,7,8,9,10,11,12,13,14,15,16,17,18,19,20,21,22,23,24,25,26..., dimensions={0} | all-to-all | bytes 524288 | tf_op jit(solution)/shard_map/all_to_all | solution.py:79
  110.9 12.2 %all_to_all.21 = f32[8,16,128]{2,1,0:T(8,128)S(1)} all-to-all(f32[8,16,128]{2,1,0:T(8,128)S(1)} %broadcast_in_dim.28), channel_id=1, replica_groups={{0,32,64,96,128,160,192,224},{1,33,65,97,129,161,193,225},{2,34,66,98,1..., dimensions={0} | all-to-all | bytes 131072 | tf_op jit(solution)/shard_map/all_to_all | solution.py:79
  123.2 2.6 %shard_map.56 = (f32[32,512]{1,0:T(8,128)S(1)}, s32[1]{0:T(128)}) custom-call(f32[64,32]{1,0:T(8,128)S(1)} %reshape.19.grams_ref, f32[32,512]{1,0:T(8,128)S(1)} %get-tuple-element.84.image_ref), custom_call_target="tpu_custom_call" | custom-call | flops 1048576 | bytes 131072 | tf_op jit(solution)/shard_map/pallas_call | solution.py:503
  126.5 0.6 copy-done.2
  (41 shorter events, 0.7 us)
Async XLA Ops:
  0.0 44.6 %copy-start.1 = (f32[32,512]{1,0:T(8,128)S(1)}, f32[32,512]{1,0:T(8,128)}, u32[]{:S(2)}) copy-start(f32[32,512]{1,0:T(8,128)} %param.8) | copy-start | bytes 196612
  2.1 21.6 %collective-permute-start.2 = (bf16[320,512]{1,0:T(8,128)(2,1)}, bf16[320,512]{1,0:T(8,128)(2,1)S(1)}, u32[]{:S(2)}, u32[]{:S(2)}) collective-permute-start(bf16[320,512]{1,0:T(8,128)(2,1)} %get-tuple-element.52.refs_0_.refs_2_), channel_id=1, source_target_pairs={{3,0},{0,1},{1,2},{2,3},{7,4},{4,5},{5,6},{6,7},{11,8},{8,9},{9,10... | collective-permute-start | bytes 983048 | tf_op jit(solution)/shard_map/ppermute | solution.py:41
  4.2 19.5 %collective-permute-start.1 = (bf16[320,512]{1,0:T(8,128)(2,1)}, bf16[320,512]{1,0:T(8,128)(2,1)S(1)}, u32[]{:S(2)}, u32[]{:S(2)}) collective-permute-start(bf16[320,512]{1,0:T(8,128)(2,1)} %get-tuple-element.52.refs_0_.refs_2_), channel_id=1, source_target_pairs={{2,0},{3,1},{0,2},{1,3},{6,4},{7,5},{4,6},{5,7},{10,8},{11,9},{8,1... | collective-permute-start | bytes 983048 | tf_op jit(solution)/shard_map/ppermute | solution.py:41
  6.8 14.4 %collective-permute-start.4 = (bf16[304,512]{1,0:T(8,128)(2,1)}, bf16[304,512]{1,0:T(8,128)(2,1)S(1)}, u32[]{:S(2)}, u32[]{:S(2)}) collective-permute-start(bf16[304,512]{1,0:T(8,128)(2,1)} %get-tuple-element.56), channel_id=1, source_target_pairs={{248,0},{252,4},{0,8},{4,12},{8,16},{12,20},{16,24},{20,28},{24,32... | collective-permute-start | bytes 933896 | tf_op jit(solution)/shard_map/ppermute | solution.py:41
  8.1 13.2 %collective-permute-start.3 = (bf16[304,512]{1,0:T(8,128)(2,1)}, bf16[304,512]{1,0:T(8,128)(2,1)S(1)}, u32[]{:S(2)}, u32[]{:S(2)}) collective-permute-start(bf16[304,512]{1,0:T(8,128)(2,1)} %get-tuple-element.56), channel_id=1, source_target_pairs={{8,0},{12,4},{16,8},{20,12},{24,16},{28,20},{32,24},{36,28},{40,32... | collective-permute-start | bytes 933896 | tf_op jit(solution)/shard_map/ppermute | solution.py:41
  14.6 10.3 %collective-permute-start = (bf16[320,512]{1,0:T(8,128)(2,1)}, bf16[320,512]{1,0:T(8,128)(2,1)S(1)}, u32[]{:S(2)}, u32[]{:S(2)}) collective-permute-start(bf16[320,512]{1,0:T(8,128)(2,1)} %get-tuple-element.52.refs_0_.refs_2_), channel_id=1, source_target_pairs={{1,0},{2,1},{3,2},{0,3},{5,4},{6,5},{7,6},{4,7},{9,8},{10,9},{11,1... | collective-permute-start | bytes 983048 | tf_op jit(solution)/shard_map/ppermute | solution.py:41
  21.3 9.0 %collective-permute-start.8 = (bf16[304,512]{1,0:T(8,128)(2,1)}, bf16[304,512]{1,0:T(8,128)(2,1)S(1)}, u32[]{:S(2)}, u32[]{:S(2)}) collective-permute-start(bf16[304,512]{1,0:T(8,128)(2,1)} %get-tuple-element.56), channel_id=1, source_target_pairs={{0,244},{4,16},{8,252},{12,24},{16,4},{20,32},{24,12},{28,40},{32,... | collective-permute-start | bytes 933896 | tf_op jit(solution)/shard_map/ppermute | solution.py:475
  21.3 9.0 %collective-permute-start.5 = (bf16[304,512]{1,0:T(8,128)(2,1)}, bf16[304,512]{1,0:T(8,128)(2,1)S(1)}, u32[]{:S(2)}, u32[]{:S(2)}) collective-permute-start(bf16[304,512]{1,0:T(8,128)(2,1)} %get-tuple-element.56), channel_id=1, source_target_pairs={{0,4},{4,0},{8,12},{12,8},{16,20},{20,16},{24,28},{28,24},{32,36},... | collective-permute-start | bytes 933896 | tf_op jit(solution)/shard_map/ppermute | solution.py:49
  23.7 6.6 %collective-permute-start.6 = (bf16[304,512]{1,0:T(8,128)(2,1)S(1)}, bf16[304,512]{1,0:T(8,128)(2,1)S(1)}, u32[]{:S(2)}, u32[]{:S(2)}) collective-permute-start(bf16[304,512]{1,0:T(8,128)(2,1)S(1)} %collective-permute-done.3.refs_0_), channel_id=1, source_target_pairs={{0,4},{4,0},{8,12},{12,8},{16,20},{20,16},{24,28},{28,24},{32,36},... | collective-permute-start | bytes 933896 | tf_op jit(solution)/shard_map/ppermute | solution.py:49
  23.7 6.6 %collective-permute-start.7 = (bf16[304,512]{1,0:T(8,128)(2,1)S(1)}, bf16[304,512]{1,0:T(8,128)(2,1)S(1)}, u32[]{:S(2)}, u32[]{:S(2)}) collective-permute-start(bf16[304,512]{1,0:T(8,128)(2,1)S(1)} %collective-permute-done.4.refs_1_), channel_id=1, source_target_pairs={{0,4},{4,0},{8,12},{12,8},{16,20},{20,16},{24,28},{28,24},{32,36},... | collective-permute-start | bytes 933896 | tf_op jit(solution)/shard_map/ppermute | solution.py:49
  25.1 1.0 copy-start
  36.3 4.7 %collective-permute-start.11 = (f32[1,512]{1,0:T(1,128)S(1)}, f32[1,512]{1,0:T(1,128)S(1)}, u32[]{:S(2)}, u32[]{:S(2)}) collective-permute-start(f32[1,512]{1,0:T(1,128)S(1)} %get-tuple-element.88), channel_id=1, source_target_pairs={{1,0},{2,1},{3,2},{0,3},{5,4},{6,5},{7,6},{4,7},{9,8},{10,9},{11,1... | collective-permute-start | bytes 6152 | tf_op jit(solution)/shard_map/ppermute | solution.py:41
  36.6 5.3 %collective-permute-start.10 = (f32[1,512]{1,0:T(1,128)S(1)}, f32[1,512]{1,0:T(1,128)S(1)}, u32[]{:S(2)}, u32[]{:S(2)}) collective-permute-start(f32[1,512]{1,0:T(1,128)S(1)} %get-tuple-element.89), channel_id=1, source_target_pairs={{2,0},{3,1},{0,2},{1,3},{6,4},{7,5},{4,6},{5,7},{10,8},{11,9},{8,1... | collective-permute-start | bytes 6152 | tf_op jit(solution)/shard_map/ppermute | solution.py:41
  41.0 3.6 %collective-permute-start.9 = (f32[1,512]{1,0:T(1,128)S(1)}, f32[1,512]{1,0:T(1,128)S(1)}, u32[]{:S(2)}, u32[]{:S(2)}) collective-permute-start(f32[1,512]{1,0:T(1,128)S(1)} %get-tuple-element.90), channel_id=1, source_target_pairs={{3,0},{0,1},{1,2},{2,3},{7,4},{4,5},{5,6},{6,7},{11,8},{8,9},{9,10... | collective-permute-start | bytes 6152 | tf_op jit(solution)/shard_map/ppermute | solution.py:41
  44.6 5.2 %collective-permute-start.13 = (bf16[32,512]{1,0:T(8,128)(2,1)S(1)}, bf16[32,512]{1,0:T(8,128)(2,1)S(1)}, u32[]{:S(2)}, u32[]{:S(2)}) collective-permute-start(bf16[32,512]{1,0:T(8,128)(2,1)S(1)} %multiply_convert_fusion), channel_id=1, source_target_pairs={{8,0},{12,4},{16,8},{20,12},{24,16},{28,20},{32,24},{36,28},{40,32... | collective-permute-start | bytes 98312 | tf_op jit(solution)/shard_map/ppermute | solution.py:41
  48.8 4.8 %collective-permute-start.12 = (bf16[32,512]{1,0:T(8,128)(2,1)S(1)}, bf16[32,512]{1,0:T(8,128)(2,1)S(1)}, u32[]{:S(2)}, u32[]{:S(2)}) collective-permute-start(bf16[32,512]{1,0:T(8,128)(2,1)S(1)} %multiply_convert_fusion), channel_id=1, source_target_pairs={{0,244},{4,16},{8,252},{12,24},{16,4},{20,32},{24,12},{28,40},{32,... | collective-permute-start | bytes 98312 | tf_op jit(solution)/shard_map/ppermute | solution.py:55
  48.8 6.1 %collective-permute-start.14 = (bf16[32,512]{1,0:T(8,128)(2,1)S(1)}, bf16[32,512]{1,0:T(8,128)(2,1)S(1)}, u32[]{:S(2)}, u32[]{:S(2)}) collective-permute-start(bf16[32,512]{1,0:T(8,128)(2,1)S(1)} %multiply_convert_fusion), channel_id=1, source_target_pairs={{248,0},{252,4},{0,8},{4,12},{8,16},{12,20},{16,24},{20,28},{24,32... | collective-permute-start | bytes 98312 | tf_op jit(solution)/shard_map/ppermute | solution.py:41
  54.9 5.8 %collective-permute-start.15 = (bf16[3,32,512]{2,1,0:T(8,128)(2,1)S(1)}, bf16[3,32,512]{2,1,0:T(8,128)(2,1)S(1)}, u32[]{:S(2)}, u32[]{:S(2)}) collective-permute-start(bf16[3,32,512]{2,1,0:T(8,128)(2,1)S(1)} %pad_maximum_fusion.1.refs_6_), channel_id=1, source_target_pairs={{0,4},{4,0},{8,12},{12,8},{16,20},{20,16},{24,28},{28,24},{32,36},... | collective-permute-start | bytes 294920 | tf_op jit(solution)/shard_map/ppermute | solution.py:49
  63.7 4.4 %collective-permute-start.16 = (f32[32,512]{1,0:T(8,128)S(1)}, f32[32,512]{1,0:T(8,128)S(1)}, u32[]{:S(2)}, u32[]{:S(2)}) collective-permute-start(f32[32,512]{1,0:T(8,128)S(1)} %get-tuple-element.71), channel_id=1, source_target_pairs={{3,0},{0,1},{1,2},{2,3},{7,4},{4,5},{5,6},{6,7},{11,8},{8,9},{9,10... | collective-permute-start | bytes 196616 | tf_op jit(solution)/shard_map/ppermute | solution.py:41
  64.5 5.1 %collective-permute-start.17 = (f32[32,512]{1,0:T(8,128)S(1)}, f32[32,512]{1,0:T(8,128)S(1)}, u32[]{:S(2)}, u32[]{:S(2)}) collective-permute-start(f32[32,512]{1,0:T(8,128)S(1)} %get-tuple-element.72), channel_id=1, source_target_pairs={{2,0},{3,1},{0,2},{1,3},{6,4},{7,5},{4,6},{5,7},{10,8},{11,9},{8,1... | collective-permute-start | bytes 196616 | tf_op jit(solution)/shard_map/ppermute | solution.py:41
  66.1 3.7 %collective-permute-start.18 = (f32[32,512]{1,0:T(8,128)S(1)}, f32[32,512]{1,0:T(8,128)S(1)}, u32[]{:S(2)}, u32[]{:S(2)}) collective-permute-start(f32[32,512]{1,0:T(8,128)S(1)} %get-tuple-element.73), channel_id=1, source_target_pairs={{1,0},{2,1},{3,2},{0,3},{5,4},{6,5},{7,6},{4,7},{9,8},{10,9},{11,1... | collective-permute-start | bytes 196616 | tf_op jit(solution)/shard_map/ppermute | solution.py:41
  70.1 6.5 %collective-permute-start.21 = (f32[32,512]{1,0:T(8,128)S(1)}, f32[32,512]{1,0:T(8,128)S(1)}, u32[]{:S(2)}, u32[]{:S(2)}) collective-permute-start(f32[32,512]{1,0:T(8,128)S(1)} %get-tuple-element.75), channel_id=1, source_target_pairs={{248,0},{252,4},{0,8},{4,12},{8,16},{12,20},{16,24},{20,28},{24,32... | collective-permute-start | bytes 196616 | tf_op jit(solution)/shard_map/ppermute | solution.py:41
  70.1 6.4 %collective-permute-start.20 = (f32[32,512]{1,0:T(8,128)S(1)}, f32[32,512]{1,0:T(8,128)S(1)}, u32[]{:S(2)}, u32[]{:S(2)}) collective-permute-start(f32[32,512]{1,0:T(8,128)S(1)} %get-tuple-element.75), channel_id=1, source_target_pairs={{8,0},{12,4},{16,8},{20,12},{24,16},{28,20},{32,24},{36,28},{40,32... | collective-permute-start | bytes 196616 | tf_op jit(solution)/shard_map/ppermute | solution.py:41
  74.9 5.2 %collective-permute-start.19 = (f32[32,512]{1,0:T(8,128)S(1)}, f32[32,512]{1,0:T(8,128)S(1)}, u32[]{:S(2)}, u32[]{:S(2)}) collective-permute-start(f32[32,512]{1,0:T(8,128)S(1)} %get-tuple-element.75), channel_id=1, source_target_pairs={{0,244},{4,16},{8,252},{12,24},{16,4},{20,32},{24,12},{28,40},{32,... | collective-permute-start | bytes 196616 | tf_op jit(solution)/shard_map/ppermute | solution.py:55
  80.1 6.0 %collective-permute-start.22 = (f32[3,32,512]{2,1,0:T(8,128)S(1)}, f32[3,32,512]{2,1,0:T(8,128)S(1)}, u32[]{:S(2)}, u32[]{:S(2)}) collective-permute-start(f32[3,32,512]{2,1,0:T(8,128)S(1)} %pad_maximum_fusion.refs_6_), channel_id=1, source_target_pairs={{0,4},{4,0},{8,12},{12,8},{16,20},{20,16},{24,28},{28,24},{32,36},... | collective-permute-start | bytes 589832 | tf_op jit(solution)/shard_map/ppermute | solution.py:49
  89.2 4.4 %collective-permute-start.23 = (f32[32,512]{1,0:T(8,128)S(1)}, f32[32,512]{1,0:T(8,128)S(1)}, u32[]{:S(2)}, u32[]{:S(2)}) collective-permute-start(f32[32,512]{1,0:T(8,128)S(1)} %get-tuple-element.80), channel_id=1, source_target_pairs={{3,0},{0,1},{1,2},{2,3},{7,4},{4,5},{5,6},{6,7},{11,8},{8,9},{9,10... | collective-permute-start | bytes 196616 | tf_op jit(solution)/shard_map/ppermute | solution.py:41
  90.7 4.7 %collective-permute-start.24 = (f32[32,512]{1,0:T(8,128)S(1)}, f32[32,512]{1,0:T(8,128)S(1)}, u32[]{:S(2)}, u32[]{:S(2)}) collective-permute-start(f32[32,512]{1,0:T(8,128)S(1)} %get-tuple-element.81), channel_id=1, source_target_pairs={{2,0},{3,1},{0,2},{1,3},{6,4},{7,5},{4,6},{5,7},{10,8},{11,9},{8,1... | collective-permute-start | bytes 196616 | tf_op jit(solution)/shard_map/ppermute | solution.py:41
  92.8 3.9 %collective-permute-start.25 = (f32[32,512]{1,0:T(8,128)S(1)}, f32[32,512]{1,0:T(8,128)S(1)}, u32[]{:S(2)}, u32[]{:S(2)}) collective-permute-start(f32[32,512]{1,0:T(8,128)S(1)} %get-tuple-element.82), channel_id=1, source_target_pairs={{1,0},{2,1},{3,2},{0,3},{5,4},{6,5},{7,6},{4,7},{9,8},{10,9},{11,1... | collective-permute-start | bytes 196616 | tf_op jit(solution)/shard_map/ppermute | solution.py:41
  126.5 0.6 copy-start.2

commit v10 on v9

--- a/solution.py
+++ b/solution.py
@@ -72,7 +72,7 @@
     n_space, n_sub = lax.axis_size("space"), lax.axis_size("sub")
     shape = value.shape
     value = value.reshape(-1, 128)
-    for key in (lambda s, y: (s // 8, 0), lambda s, y: (s % 8, y)):
+    for key in (lambda s, y: (s % 8, y), lambda s, y: (s // 8, 0)):
         groups = groups_by(key, n_space, n_sub)
         sent = jnp.broadcast_to(value[None], (len(groups[0]),) + value.shape)
         value = jnp.sum(

time: 127 us -> 129 us (1.016)
  starting transfers between devices: 48.4 us -> 46.3 us
  Pallas kernels: 21.3 us -> 22.9 us
    ppermute x5, starting transfers between devices: 12.7 us -> 11 us  [swapped(): lax.ppermute(value, 'space', [(at, at ^ 1) for at in range(lax.axis_size(...]
  transfers between devices with their start and end apart: 26 -> 26, of which waited for: 16 -> 17; matrix products, arithmetic and copies ran while one was open for 1% -> 1% of each run, Pallas kernels for 3% -> 4%
where the time goes in v10:
time: 129 us
  starting transfers between devices  46.3 us (36%)
  waiting for transfers between devices  29 us (22%)
  blocking collectives  27.2 us (21%)
  Pallas kernels  22.9 us (18%)
  local copies, waits for them, and re-layouts  2.55 us (2%)
    ppermute x18, starting transfers between devices, shifted(): lax.ppermute(value, axis, [((at + steps) % count, at) for at in range(cou...  35.2 us
    all_to_all x2, blocking collectives, summed(): lax.all_to_all(sent, ('space', 'sub'), 0, 0, axis_index_groups=groups)  27.2 us
    ppermute x18, waiting for transfers between devices, shifted(): lax.ppermute(value, axis, [((at + steps) % count, at) for at in range(cou...  19.6 us
    ppermute x5, starting transfers between devices, swapped(): lax.ppermute(value, 'space', [(at, at ^ 1) for at in range(lax.axis_size(...  11 us
    pallas_call x2, Pallas kernels, hop_tiles(): pl.pallas_call(functools.partial(tile_kernel, windows, first, last), in_s...  10.7 us
    ppermute x2, waiting for transfers between devices, space_window(): lax.ppermute(value, 'space', far_pairs(lax.axis_size('space')))  7.36 us
    pallas_call x2, Pallas kernels, sweep(): pl.pallas_call(functools.partial(sweep_kernel, parts), in_specs=[smem] *...  6.84 us
    pallas_call x1, Pallas kernels, on_device(): pl.pallas_call(solve_both_kernel, in_specs=[pl.BlockSpec(memory_space=plt...  2.6 us
  transfers between devices with their start and end apart: 26, of which 17 were waited for; matrix products, arithmetic and copies ran while one was open for 1% of the time, Pallas kernels for 4%

profile of v10, /device:TPU:1, one launch (start us, length us, event | category | flops | bytes accessed | tf_op | source)
XLA Modules:
  0.0 129.0 jit_solution(13945150475525170513)
XLA Ops:
  0.0 2.1 %shard_map.48 = (bf16[304,512]{1,0:T(8,128)(2,1)}, bf16[320,512]{1,0:T(8,128)(2,1)}) custom-call(s32[2,24]{1,0:T(2,128)} %bitcast.29, bf16[300,512]{1,0:T(8,128)(2,1)} %data_ref.1, bf16[512]{0:T(512)(128)(2,1)} %scale_ref.1), custom_call_target="tpu_custom_call" | custom-call | flops 1048576 | bytes 131072 | tf_op jit(solution)/shard_map/pallas_call | solution.py:463
  2.1 2.1 %collective-permute-start.2 = (bf16[320,512]{1,0:T(8,128)(2,1)}, bf16[320,512]{1,0:T(8,128)(2,1)S(1)}, u32[]{:S(2)}, u32[]{:S(2)}) collective-permute-start(bf16[320,512]{1,0:T(8,128)(2,1)} %get-tuple-element.52.refs_0_.refs_2_), channel_id=1, source_target_pairs={{3,0},{0,1},{1,2},{2,3},{7,4},{4,5},{5,6},{6,7},{11,8},{8,9},{9,10... | collective-permute-start | bytes 983048 | tf_op jit(solution)/shard_map/ppermute | solution.py:41
  4.2 2.6 %collective-permute-start.1 = (bf16[320,512]{1,0:T(8,128)(2,1)}, bf16[320,512]{1,0:T(8,128)(2,1)S(1)}, u32[]{:S(2)}, u32[]{:S(2)}) collective-permute-start(bf16[320,512]{1,0:T(8,128)(2,1)} %get-tuple-element.52.refs_0_.refs_2_), channel_id=1, source_target_pairs={{2,0},{3,1},{0,2},{1,3},{6,4},{7,5},{4,6},{5,7},{10,8},{11,9},{8,1... | collective-permute-start | bytes 983048 | tf_op jit(solution)/shard_map/ppermute | solution.py:41
  6.8 1.2 collective-permute-start.4
  8.1 6.6 %collective-permute-start.3 = (bf16[304,512]{1,0:T(8,128)(2,1)}, bf16[304,512]{1,0:T(8,128)(2,1)S(1)}, u32[]{:S(2)}, u32[]{:S(2)}) collective-permute-start(bf16[304,512]{1,0:T(8,128)(2,1)} %get-tuple-element.56), channel_id=1, source_target_pairs={{8,0},{12,4},{16,8},{20,12},{24,16},{28,20},{32,24},{36,28},{40,32... | collective-permute-start | bytes 933896 | tf_op jit(solution)/shard_map/ppermute | solution.py:41
  14.6 1.1 collective-permute-start
  15.7 5.6 %collective-permute-done.4.refs_1_ = bf16[304,512]{1,0:T(8,128)(2,1)S(1)} collective-permute-done((bf16[304,512]{1,0:T(8,128)(2,1)}, bf16[304,512]{1,0:T(8,128)(2,1)S(1)}, u32[]{:S(2)}, u32[]{:S(2)}) %collective-permute-start.4) | collective-permute-done | bytes 311328 | tf_op jit(solution)/shard_map/ppermute | solution.py:41
  21.3 2.5 %collective-permute-start.5 = (bf16[304,512]{1,0:T(8,128)(2,1)}, bf16[304,512]{1,0:T(8,128)(2,1)S(1)}, u32[]{:S(2)}, u32[]{:S(2)}) collective-permute-start(bf16[304,512]{1,0:T(8,128)(2,1)} %get-tuple-element.56), channel_id=1, source_target_pairs={{0,4},{4,0},{8,12},{12,8},{16,20},{20,16},{24,28},{28,24},{32,36},... | collective-permute-start | bytes 933896 | tf_op jit(solution)/shard_map/ppermute | solution.py:49
  23.7 0.5 collective-permute-start.7
  24.3 0.7 slice.27
  25.1 1.0 copy-done
  26.0 0.3 shard_map.49
  26.4 4.8 %shard_map.50 = (bf16[40,256,256]{2,1,0:T(8,128)(2,1)S(1)}, s32[80]{0:T(128)S(1)}, s32[80]{0:T(128)S(1)}, f32[9,8,256]{2,1,0:T(8,128)S(1)}) custom-call(s32[192]{0:T(256)S(1)} %reshape.20.mine_ref, bf16[8,320,256]{2,1,0:T(8,128)(2,1)S(1)} %get-tuple-element.53.blocks_ref, f32[8,8,256]{2,1,0:T(8,128)S(1)} %get-tuple-element.54.rate_ref, ...), custom_call_target="tpu_custom_call" | custom-call | flops 671088640 | bytes 7340032 | tf_op jit(solution)/shard_map/pallas_call | solution.py:243
  31.2 5.9 %shard_map.51 = (bf16[64,256,256]{2,1,0:T(8,128)(2,1)S(1)}, s32[80]{0:T(128)S(1)}, s32[80]{0:T(128)S(1)}, f32[4,8,512]{2,1,0:T(8,128)S(1)}) custom-call(s32[192]{0:T(256)S(1)} %reshape.20.mine_ref, bf16[8,320,256]{2,1,0:T(8,128)(2,1)S(1)} %get-tuple-element.53.blocks_ref, f32[8,8,256]{2,1,0:T(8,128)S(1)} %get-tuple-element.54.rate_ref, ...), custom_call_target="tpu_custom_call" | custom-call | flops 1342177280 | bytes 7340032 | tf_op jit(solution)/shard_map/pallas_call | solution.py:243
  37.1 1.1 collective-permute-start.11
  38.3 1.1 collective-permute-start.10
  39.3 0.3 collective-permute-done.11
  39.6 2.6 %collective-permute-done.10 = f32[1,512]{1,0:T(1,128)S(1)} collective-permute-done((f32[1,512]{1,0:T(1,128)S(1)}, f32[1,512]{1,0:T(1,128)S(1)}, u32[]{:S(2)}, u32[]{:S(2)}) %collective-permute-start.10) | collective-permute-done | bytes 2080 | tf_op jit(solution)/shard_map/ppermute | solution.py:41
  42.2 0.8 collective-permute-done.9
  43.0 7.4 %collective-permute-start.13 = (bf16[32,512]{1,0:T(8,128)(2,1)S(1)}, bf16[32,512]{1,0:T(8,128)(2,1)S(1)}, u32[]{:S(2)}, u32[]{:S(2)}) collective-permute-start(bf16[32,512]{1,0:T(8,128)(2,1)S(1)} %multiply_convert_fusion), channel_id=1, source_target_pairs={{8,0},{12,4},{16,8},{20,12},{24,16},{28,20},{32,24},{36,28},{40,32... | collective-permute-start | bytes 98312 | tf_op jit(solution)/shard_map/ppermute | solution.py:41
  50.4 1.0 collective-permute-done.13
  51.4 3.8 %collective-permute-done.12.refs_8_ = bf16[32,512]{1,0:T(8,128)(2,1)S(1)} collective-permute-done((bf16[32,512]{1,0:T(8,128)(2,1)S(1)}, bf16[32,512]{1,0:T(8,128)(2,1)S(1)}, u32[]{:S(2)}, u32[]{:S(2)}) %collective-permute-start.12) | collective-permute-done | bytes 32800 | tf_op jit(solution)/shard_map/ppermute | solution.py:55
  55.3 1.2 collective-permute-done.14
  56.5 3.3 %collective-permute-start.15 = (bf16[3,32,512]{2,1,0:T(8,128)(2,1)S(1)}, bf16[3,32,512]{2,1,0:T(8,128)(2,1)S(1)}, u32[]{:S(2)}, u32[]{:S(2)}) collective-permute-start(bf16[3,32,512]{2,1,0:T(8,128)(2,1)S(1)} %pad_maximum_fusion.1.refs_6_), channel_id=1, source_target_pairs={{0,4},{4,0},{8,12},{12,8},{16,20},{20,16},{24,28},{28,24},{32,36},... | collective-permute-start | bytes 294920 | tf_op jit(solution)/shard_map/ppermute | solution.py:49
  59.8 0.9 collective-permute-done.15.refs_7_
  60.8 3.3 %shard_map.52 = (f32[32,512]{1,0:T(8,128)S(1)}, f32[32,512]{1,0:T(8,128)S(1)}, f32[32,512]{1,0:T(8,128)S(1)}, f32[32,512]{1,0:T(8,128)S(1)}) custom-call(s32[80]{0:T(128)S(1)} %get-tuple-element.61.refs_0_, s32[80]{0:T(128)S(1)} %get-tuple-element.62.refs_1_, s32[80]{0:T(128)S(1)} %get-tuple-element.63.refs_2_, s32[80]{0:T(128)S(1)} %get-tuple-element.64.refs_3_, ...), custom_call_target="tpu_custom_call" | custom-call | flops 838860800 | bytes 7340032 | tf_op jit(solution)/shard_map/pallas_call | solution.py:340
  64.2 2.6 %collective-permute-start.17 = (f32[32,512]{1,0:T(8,128)S(1)}, f32[32,512]{1,0:T(8,128)S(1)}, u32[]{:S(2)}, u32[]{:S(2)}) collective-permute-start(f32[32,512]{1,0:T(8,128)S(1)} %get-tuple-element.72), channel_id=1, source_target_pairs={{2,0},{3,1},{0,2},{1,3},{6,4},{7,5},{4,6},{5,7},{10,8},{11,9},{8,1... | collective-permute-start | bytes 196616 | tf_op jit(solution)/shard_map/ppermute | solution.py:41
  66.9 1.1 collective-permute-start.18
  67.9 0.6 collective-permute-done.16.refs_1_
  68.6 0.8 collective-permute-done.17.refs_2_
  69.4 1.0 collective-permute-done.18.refs_3_
  70.4 0.2 shard_map.53
  70.7 4.8 %collective-permute-start.20 = (f32[32,512]{1,0:T(8,128)S(1)}, f32[32,512]{1,0:T(8,128)S(1)}, u32[]{:S(2)}, u32[]{:S(2)}) collective-permute-start(f32[32,512]{1,0:T(8,128)S(1)} %get-tuple-element.75), channel_id=1, source_target_pairs={{8,0},{12,4},{16,8},{20,12},{24,16},{28,20},{32,24},{36,28},{40,32... | collective-permute-start | bytes 196616 | tf_op jit(solution)/shard_map/ppermute | solution.py:41
  75.5 1.6 %collective-permute-done.21 = f32[32,512]{1,0:T(8,128)S(1)} collective-permute-done((f32[32,512]{1,0:T(8,128)S(1)}, f32[32,512]{1,0:T(8,128)S(1)}, u32[]{:S(2)}, u32[]{:S(2)}) %collective-permute-start.21) | collective-permute-done | bytes 65568 | tf_op jit(solution)/shard_map/ppermute | solution.py:41
  77.1 3.5 %collective-permute-done.19.refs_8_ = f32[32,512]{1,0:T(8,128)S(1)} collective-permute-done((f32[32,512]{1,0:T(8,128)S(1)}, f32[32,512]{1,0:T(8,128)S(1)}, u32[]{:S(2)}, u32[]{:S(2)}) %collective-permute-start.19) | collective-permute-done | bytes 65568 | tf_op jit(solution)/shard_map/ppermute | solution.py:55
  80.7 4.8 %collective-permute-start.22 = (f32[3,32,512]{2,1,0:T(8,128)S(1)}, f32[3,32,512]{2,1,0:T(8,128)S(1)}, u32[]{:S(2)}, u32[]{:S(2)}) collective-permute-start(f32[3,32,512]{2,1,0:T(8,128)S(1)} %pad_maximum_fusion.refs_6_), channel_id=1, source_target_pairs={{0,4},{4,0},{8,12},{12,8},{16,20},{20,16},{24,28},{28,24},{32,36},... | collective-permute-start | bytes 589832 | tf_op jit(solution)/shard_map/ppermute | solution.py:49
  85.5 1.1 collective-permute-done.22.refs_7_
  86.5 3.5 %shard_map.54 = (f32[32,512]{1,0:T(8,128)S(1)}, f32[32,512]{1,0:T(8,128)S(1)}, f32[32,512]{1,0:T(8,128)S(1)}, f32[32,512]{1,0:T(8,128)S(1)}) custom-call(s32[80]{0:T(128)S(1)} %get-tuple-element.61.refs_0_, s32[80]{0:T(128)S(1)} %get-tuple-element.62.refs_1_, s32[80]{0:T(128)S(1)} %get-tuple-element.63.refs_2_, s32[80]{0:T(128)S(1)} %get-tuple-element.64.refs_3_, ...), custom_call_target="tpu_custom_call" | custom-call | flops 838860800 | bytes 7340032 | tf_op jit(solution)/shard_map/pallas_call | solution.py:340
  90.0 0.3 collective-permute-start.23
  90.3 3.0 %collective-permute-start.24 = (f32[32,512]{1,0:T(8,128)S(1)}, f32[32,512]{1,0:T(8,128)S(1)}, u32[]{:S(2)}, u32[]{:S(2)}) collective-permute-start(f32[32,512]{1,0:T(8,128)S(1)} %get-tuple-element.81), channel_id=1, source_target_pairs={{2,0},{3,1},{0,2},{1,3},{6,4},{7,5},{4,6},{5,7},{10,8},{11,9},{8,1... | collective-permute-start | bytes 196616 | tf_op jit(solution)/shard_map/ppermute | solution.py:41
  93.4 1.0 collective-permute-done.23.refs_1_
  94.4 1.4 %collective-permute-done.24.refs_2_ = f32[32,512]{1,0:T(8,128)S(1)} collective-permute-done((f32[32,512]{1,0:T(8,128)S(1)}, f32[32,512]{1,0:T(8,128)S(1)}, u32[]{:S(2)}, u32[]{:S(2)}) %collective-permute-start.24) | collective-permute-done | bytes 65568 | tf_op jit(solution)/shard_map/ppermute | solution.py:41
  95.8 1.5 %collective-permute-done.25.refs_3_ = f32[32,512]{1,0:T(8,128)S(1)} collective-permute-done((f32[32,512]{1,0:T(8,128)S(1)}, f32[32,512]{1,0:T(8,128)S(1)}, u32[]{:S(2)}, u32[]{:S(2)}) %collective-permute-start.25) | collective-permute-done | bytes 65568 | tf_op jit(solution)/shard_map/ppermute | solution.py:41
  97.4 0.2 shard_map.55
  97.7 12.4 %all_to_all.20 = f32[8,16,128]{2,1,0:T(8,128)S(1)} all-to-all(f32[8,16,128]{2,1,0:T(8,128)S(1)} %broadcast_in_dim.13), channel_id=1, replica_groups={{0,32,64,96,128,160,192,224},{1,33,65,97,129,161,193,225},{2,34,66,98,1..., dimensions={0} | all-to-all | bytes 131072 | tf_op jit(solution)/shard_map/all_to_all | solution.py:79
  110.1 14.8 %all_to_all.21 = f32[32,16,128]{2,1,0:T(8,128)S(1)} all-to-all(f32[32,16,128]{2,1,0:T(8,128)S(1)} %broadcast_in_dim.28), channel_id=1, replica_groups={{0,1,2,3,4,5,6,7,8,9,10,11,12,13,14,15,16,17,18,19,20,21,22,23,24,25,26..., dimensions={0} | all-to-all | bytes 524288 | tf_op jit(solution)/shard_map/all_to_all | solution.py:79
  125.0 2.6 %shard_map.56 = (f32[32,512]{1,0:T(8,128)S(1)}, s32[1]{0:T(128)}) custom-call(f32[64,32]{1,0:T(8,128)S(1)} %reshape.19.grams_ref, f32[32,512]{1,0:T(8,128)S(1)} %get-tuple-element.84.image_ref), custom_call_target="tpu_custom_call" | custom-call | flops 1048576 | bytes 131072 | tf_op jit(solution)/shard_map/pallas_call | solution.py:503
  128.3 0.6 copy-done.2
  (41 shorter events, 0.7 us)
Async XLA Ops:
  0.0 43.0 %copy-start.1 = (f32[32,512]{1,0:T(8,128)S(1)}, f32[32,512]{1,0:T(8,128)}, u32[]{:S(2)}) copy-start(f32[32,512]{1,0:T(8,128)} %param.8) | copy-start | bytes 196612
  2.1 21.6 %collective-permute-start.2 = (bf16[320,512]{1,0:T(8,128)(2,1)}, bf16[320,512]{1,0:T(8,128)(2,1)S(1)}, u32[]{:S(2)}, u32[]{:S(2)}) collective-permute-start(bf16[320,512]{1,0:T(8,128)(2,1)} %get-tuple-element.52.refs_0_.refs_2_), channel_id=1, source_target_pairs={{3,0},{0,1},{1,2},{2,3},{7,4},{4,5},{5,6},{6,7},{11,8},{8,9},{9,10... | collective-permute-start | bytes 983048 | tf_op jit(solution)/shard_map/ppermute | solution.py:41
  4.2 19.5 %collective-permute-start.1 = (bf16[320,512]{1,0:T(8,128)(2,1)}, bf16[320,512]{1,0:T(8,128)(2,1)S(1)}, u32[]{:S(2)}, u32[]{:S(2)}) collective-permute-start(bf16[320,512]{1,0:T(8,128)(2,1)} %get-tuple-element.52.refs_0_.refs_2_), channel_id=1, source_target_pairs={{2,0},{3,1},{0,2},{1,3},{6,4},{7,5},{4,6},{5,7},{10,8},{11,9},{8,1... | collective-permute-start | bytes 983048 | tf_op jit(solution)/shard_map/ppermute | solution.py:41
  6.8 14.4 %collective-permute-start.4 = (bf16[304,512]{1,0:T(8,128)(2,1)}, bf16[304,512]{1,0:T(8,128)(2,1)S(1)}, u32[]{:S(2)}, u32[]{:S(2)}) collective-permute-start(bf16[304,512]{1,0:T(8,128)(2,1)} %get-tuple-element.56), channel_id=1, source_target_pairs={{248,0},{252,4},{0,8},{4,12},{8,16},{12,20},{16,24},{20,28},{24,32... | collective-permute-start | bytes 933896 | tf_op jit(solution)/shard_map/ppermute | solution.py:41
  8.1 13.2 %collective-permute-start.3 = (bf16[304,512]{1,0:T(8,128)(2,1)}, bf16[304,512]{1,0:T(8,128)(2,1)S(1)}, u32[]{:S(2)}, u32[]{:S(2)}) collective-permute-start(bf16[304,512]{1,0:T(8,128)(2,1)} %get-tuple-element.56), channel_id=1, source_target_pairs={{8,0},{12,4},{16,8},{20,12},{24,16},{28,20},{32,24},{36,28},{40,32... | collective-permute-start | bytes 933896 | tf_op jit(solution)/shard_map/ppermute | solution.py:41
  14.6 10.3 %collective-permute-start = (bf16[320,512]{1,0:T(8,128)(2,1)}, bf16[320,512]{1,0:T(8,128)(2,1)S(1)}, u32[]{:S(2)}, u32[]{:S(2)}) collective-permute-start(bf16[320,512]{1,0:T(8,128)(2,1)} %get-tuple-element.52.refs_0_.refs_2_), channel_id=1, source_target_pairs={{1,0},{2,1},{3,2},{0,3},{5,4},{6,5},{7,6},{4,7},{9,8},{10,9},{11,1... | collective-permute-start | bytes 983048 | tf_op jit(solution)/shard_map/ppermute | solution.py:41
  21.3 9.9 %collective-permute-start.8 = (bf16[304,512]{1,0:T(8,128)(2,1)}, bf16[304,512]{1,0:T(8,128)(2,1)S(1)}, u32[]{:S(2)}, u32[]{:S(2)}) collective-permute-start(bf16[304,512]{1,0:T(8,128)(2,1)} %get-tuple-element.56), channel_id=1, source_target_pairs={{0,244},{4,16},{8,252},{12,24},{16,4},{20,32},{24,12},{28,40},{32,... | collective-permute-start | bytes 933896 | tf_op jit(solution)/shard_map/ppermute | solution.py:475
  21.3 9.9 %collective-permute-start.5 = (bf16[304,512]{1,0:T(8,128)(2,1)}, bf16[304,512]{1,0:T(8,128)(2,1)S(1)}, u32[]{:S(2)}, u32[]{:S(2)}) collective-permute-start(bf16[304,512]{1,0:T(8,128)(2,1)} %get-tuple-element.56), channel_id=1, source_target_pairs={{0,4},{4,0},{8,12},{12,8},{16,20},{20,16},{24,28},{28,24},{32,36},... | collective-permute-start | bytes 933896 | tf_op jit(solution)/shard_map/ppermute | solution.py:49
  23.7 7.4 %collective-permute-start.6 = (bf16[304,512]{1,0:T(8,128)(2,1)S(1)}, bf16[304,512]{1,0:T(8,128)(2,1)S(1)}, u32[]{:S(2)}, u32[]{:S(2)}) collective-permute-start(bf16[304,512]{1,0:T(8,128)(2,1)S(1)} %collective-permute-done.3.refs_0_), channel_id=1, source_target_pairs={{0,4},{4,0},{8,12},{12,8},{16,20},{20,16},{24,28},{28,24},{32,36},... | collective-permute-start | bytes 933896 | tf_op jit(solution)/shard_map/ppermute | solution.py:49
  23.7 7.4 %collective-permute-start.7 = (bf16[304,512]{1,0:T(8,128)(2,1)S(1)}, bf16[304,512]{1,0:T(8,128)(2,1)S(1)}, u32[]{:S(2)}, u32[]{:S(2)}) collective-permute-start(bf16[304,512]{1,0:T(8,128)(2,1)S(1)} %collective-permute-done.4.refs_1_), channel_id=1, source_target_pairs={{0,4},{4,0},{8,12},{12,8},{16,20},{20,16},{24,28},{28,24},{32,36},... | collective-permute-start | bytes 933896 | tf_op jit(solution)/shard_map/ppermute | solution.py:49
  25.1 1.0 copy-start
  37.1 2.5 %collective-permute-start.11 = (f32[1,512]{1,0:T(1,128)S(1)}, f32[1,512]{1,0:T(1,128)S(1)}, u32[]{:S(2)}, u32[]{:S(2)}) collective-permute-start(f32[1,512]{1,0:T(1,128)S(1)} %get-tuple-element.88), channel_id=1, source_target_pairs={{1,0},{2,1},{3,2},{0,3},{5,4},{6,5},{7,6},{4,7},{9,8},{10,9},{11,1... | collective-permute-start | bytes 6152 | tf_op jit(solution)/shard_map/ppermute | solution.py:41
  38.3 3.9 %collective-permute-start.10 = (f32[1,512]{1,0:T(1,128)S(1)}, f32[1,512]{1,0:T(1,128)S(1)}, u32[]{:S(2)}, u32[]{:S(2)}) collective-permute-start(f32[1,512]{1,0:T(1,128)S(1)} %get-tuple-element.89), channel_id=1, source_target_pairs={{2,0},{3,1},{0,2},{1,3},{6,4},{7,5},{4,6},{5,7},{10,8},{11,9},{8,1... | collective-permute-start | bytes 6152 | tf_op jit(solution)/shard_map/ppermute | solution.py:41
  39.3 3.6 %collective-permute-start.9 = (f32[1,512]{1,0:T(1,128)S(1)}, f32[1,512]{1,0:T(1,128)S(1)}, u32[]{:S(2)}, u32[]{:S(2)}) collective-permute-start(f32[1,512]{1,0:T(1,128)S(1)} %get-tuple-element.90), channel_id=1, source_target_pairs={{3,0},{0,1},{1,2},{2,3},{7,4},{4,5},{5,6},{6,7},{11,8},{8,9},{9,10... | collective-permute-start | bytes 6152 | tf_op jit(solution)/shard_map/ppermute | solution.py:41
  43.0 8.4 %collective-permute-start.13 = (bf16[32,512]{1,0:T(8,128)(2,1)S(1)}, bf16[32,512]{1,0:T(8,128)(2,1)S(1)}, u32[]{:S(2)}, u32[]{:S(2)}) collective-permute-start(bf16[32,512]{1,0:T(8,128)(2,1)S(1)} %multiply_convert_fusion), channel_id=1, source_target_pairs={{8,0},{12,4},{16,8},{20,12},{24,16},{28,20},{32,24},{36,28},{40,32... | collective-permute-start | bytes 98312 | tf_op jit(solution)/shard_map/ppermute | solution.py:41
  50.4 4.8 %collective-permute-start.12 = (bf16[32,512]{1,0:T(8,128)(2,1)S(1)}, bf16[32,512]{1,0:T(8,128)(2,1)S(1)}, u32[]{:S(2)}, u32[]{:S(2)}) collective-permute-start(bf16[32,512]{1,0:T(8,128)(2,1)S(1)} %multiply_convert_fusion), channel_id=1, source_target_pairs={{0,244},{4,16},{8,252},{12,24},{16,4},{20,32},{24,12},{28,40},{32,... | collective-permute-start | bytes 98312 | tf_op jit(solution)/shard_map/ppermute | solution.py:55
  50.4 6.1 %collective-permute-start.14 = (bf16[32,512]{1,0:T(8,128)(2,1)S(1)}, bf16[32,512]{1,0:T(8,128)(2,1)S(1)}, u32[]{:S(2)}, u32[]{:S(2)}) collective-permute-start(bf16[32,512]{1,0:T(8,128)(2,1)S(1)} %multiply_convert_fusion), channel_id=1, source_target_pairs={{248,0},{252,4},{0,8},{4,12},{8,16},{12,20},{16,24},{20,28},{24,32... | collective-permute-start | bytes 98312 | tf_op jit(solution)/shard_map/ppermute | solution.py:41
  56.5 4.3 %collective-permute-start.15 = (bf16[3,32,512]{2,1,0:T(8,128)(2,1)S(1)}, bf16[3,32,512]{2,1,0:T(8,128)(2,1)S(1)}, u32[]{:S(2)}, u32[]{:S(2)}) collective-permute-start(bf16[3,32,512]{2,1,0:T(8,128)(2,1)S(1)} %pad_maximum_fusion.1.refs_6_), channel_id=1, source_target_pairs={{0,4},{4,0},{8,12},{12,8},{16,20},{20,16},{24,28},{28,24},{32,36},... | collective-permute-start | bytes 294920 | tf_op jit(solution)/shard_map/ppermute | solution.py:49
  64.1 4.4 %collective-permute-start.16 = (f32[32,512]{1,0:T(8,128)S(1)}, f32[32,512]{1,0:T(8,128)S(1)}, u32[]{:S(2)}, u32[]{:S(2)}) collective-permute-start(f32[32,512]{1,0:T(8,128)S(1)} %get-tuple-element.71), channel_id=1, source_target_pairs={{3,0},{0,1},{1,2},{2,3},{7,4},{4,5},{5,6},{6,7},{11,8},{8,9},{9,10... | collective-permute-start | bytes 196616 | tf_op jit(solution)/shard_map/ppermute | solution.py:41
  64.2 5.2 %collective-permute-start.17 = (f32[32,512]{1,0:T(8,128)S(1)}, f32[32,512]{1,0:T(8,128)S(1)}, u32[]{:S(2)}, u32[]{:S(2)}) collective-permute-start(f32[32,512]{1,0:T(8,128)S(1)} %get-tuple-element.72), channel_id=1, source_target_pairs={{2,0},{3,1},{0,2},{1,3},{6,4},{7,5},{4,6},{5,7},{10,8},{11,9},{8,1... | collective-permute-start | bytes 196616 | tf_op jit(solution)/shard_map/ppermute | solution.py:41
  66.9 3.6 %collective-permute-start.18 = (f32[32,512]{1,0:T(8,128)S(1)}, f32[32,512]{1,0:T(8,128)S(1)}, u32[]{:S(2)}, u32[]{:S(2)}) collective-permute-start(f32[32,512]{1,0:T(8,128)S(1)} %get-tuple-element.73), channel_id=1, source_target_pairs={{1,0},{2,1},{3,2},{0,3},{5,4},{6,5},{7,6},{4,7},{9,8},{10,9},{11,1... | collective-permute-start | bytes 196616 | tf_op jit(solution)/shard_map/ppermute | solution.py:41
  70.6 6.5 %collective-permute-start.21 = (f32[32,512]{1,0:T(8,128)S(1)}, f32[32,512]{1,0:T(8,128)S(1)}, u32[]{:S(2)}, u32[]{:S(2)}) collective-permute-start(f32[32,512]{1,0:T(8,128)S(1)} %get-tuple-element.75), channel_id=1, source_target_pairs={{248,0},{252,4},{0,8},{4,12},{8,16},{12,20},{16,24},{20,28},{24,32... | collective-permute-start | bytes 196616 | tf_op jit(solution)/shard_map/ppermute | solution.py:41
  70.7 6.4 %collective-permute-start.20 = (f32[32,512]{1,0:T(8,128)S(1)}, f32[32,512]{1,0:T(8,128)S(1)}, u32[]{:S(2)}, u32[]{:S(2)}) collective-permute-start(f32[32,512]{1,0:T(8,128)S(1)} %get-tuple-element.75), channel_id=1, source_target_pairs={{8,0},{12,4},{16,8},{20,12},{24,16},{28,20},{32,24},{36,28},{40,32... | collective-permute-start | bytes 196616 | tf_op jit(solution)/shard_map/ppermute | solution.py:41
  75.5 5.2 %collective-permute-start.19 = (f32[32,512]{1,0:T(8,128)S(1)}, f32[32,512]{1,0:T(8,128)S(1)}, u32[]{:S(2)}, u32[]{:S(2)}) collective-permute-start(f32[32,512]{1,0:T(8,128)S(1)} %get-tuple-element.75), channel_id=1, source_target_pairs={{0,244},{4,16},{8,252},{12,24},{16,4},{20,32},{24,12},{28,40},{32,... | collective-permute-start | bytes 196616 | tf_op jit(solution)/shard_map/ppermute | solution.py:55
  80.7 5.8 %collective-permute-start.22 = (f32[3,32,512]{2,1,0:T(8,128)S(1)}, f32[3,32,512]{2,1,0:T(8,128)S(1)}, u32[]{:S(2)}, u32[]{:S(2)}) collective-permute-start(f32[3,32,512]{2,1,0:T(8,128)S(1)} %pad_maximum_fusion.refs_6_), channel_id=1, source_target_pairs={{0,4},{4,0},{8,12},{12,8},{16,20},{20,16},{24,28},{28,24},{32,36},... | collective-permute-start | bytes 589832 | tf_op jit(solution)/shard_map/ppermute | solution.py:49
  90.0 4.4 %collective-permute-start.23 = (f32[32,512]{1,0:T(8,128)S(1)}, f32[32,512]{1,0:T(8,128)S(1)}, u32[]{:S(2)}, u32[]{:S(2)}) collective-permute-start(f32[32,512]{1,0:T(8,128)S(1)} %get-tuple-element.80), channel_id=1, source_target_pairs={{3,0},{0,1},{1,2},{2,3},{7,4},{4,5},{5,6},{6,7},{11,8},{8,9},{9,10... | collective-permute-start | bytes 196616 | tf_op jit(solution)/shard_map/ppermute | solution.py:41
  90.3 5.5 %collective-permute-start.24 = (f32[32,512]{1,0:T(8,128)S(1)}, f32[32,512]{1,0:T(8,128)S(1)}, u32[]{:S(2)}, u32[]{:S(2)}) collective-permute-start(f32[32,512]{1,0:T(8,128)S(1)} %get-tuple-element.81), channel_id=1, source_target_pairs={{2,0},{3,1},{0,2},{1,3},{6,4},{7,5},{4,6},{5,7},{10,8},{11,9},{8,1... | collective-permute-start | bytes 196616 | tf_op jit(solution)/shard_map/ppermute | solution.py:41
  93.3 4.0 %collective-permute-start.25 = (f32[32,512]{1,0:T(8,128)S(1)}, f32[32,512]{1,0:T(8,128)S(1)}, u32[]{:S(2)}, u32[]{:S(2)}) collective-permute-start(f32[32,512]{1,0:T(8,128)S(1)} %get-tuple-element.82), channel_id=1, source_target_pairs={{1,0},{2,1},{3,2},{0,3},{5,4},{6,5},{7,6},{4,7},{9,8},{10,9},{11,1... | collective-permute-start | bytes 196616 | tf_op jit(solution)/shard_map/ppermute | solution.py:41
  128.3 0.6 copy-start.2
